TPU v7x, 32 devices: a whole 2x2x4 slice. The times are simulated.
32 devices in a mesh: frame: 8 (over z, x), row: 4 (over y, core).
Axes of the slice: x: 2, y: 2, z: 4, core: 2. Of those that a mesh axis runs over, the one named last changes fastest.
Arguments:
- frames_in: bfloat16 [8, 64, 64, 1152], P('frame', 'row'), may hold values from -6 to 6
- spatial_qkv: bfloat16 [1152, 1728], replicated
- spatial_out: bfloat16 [576, 1152], replicated, may hold values from -0.8984375 to 0.8984375
- temporal_qkv: bfloat16 [1152, 1728], replicated
- temporal_out: bfloat16 [576, 1152], replicated, may hold values from -0.8984375 to 0.8984375
- key_tiles: int32 [8, 64, 9], P('frame', 'row'), may hold values from 0 to 63, as said below
- tile_counts: int32 [8, 64], P('frame', 'row'), may hold values from 1 to 9, as said below
Outputs:
- frames_out: bfloat16 [8, 64, 64, 1152], P('frame', 'row')
Inputs may be any that keep to these rules, and one draw needn't show every extreme that they name: `key_tiles`: for query tile t, whose tile row is t // 4 and tile column t % 4, the first tile_counts entries name distinct tiles whose tile row and tile column each differ from t's by at most one; later entries equal t. `tile_counts`: at most the number of tiles within one tile row and one tile column of the query tile.
All inputs are finite; a program needn't handle non-finite values.
Results may differ from a plain program's by a relative error of at most 0.019.
Values may be sent and summed in bfloat16 or wider, within the bound.
No kernel may reach another device: no remote copies, remote signals or barrier semaphores. Data moves between devices by JAX's collectives and lax.ppermute only.
A program may use at most 128 MiB of HBM per device.

v0:
```python
import jax
import jax.numpy as jnp
from jax import lax
from jax.sharding import PartitionSpec as P

HEADS = 8
HD = 72
TH = 4
TW = 16


NORM_EPS = 1e-06


def padded(x, sides, width):
    for axis, dim in sides:
        size, length = (lax.axis_size(axis), x.shape[dim])
        up = [(i, (i + 1) % size) for i in range(size - 1)]
        down = [(j, i) for i, j in up]
        last = lax.slice_in_dim(x, length - width, length, axis=dim)
        first = lax.slice_in_dim(x, 0, width, axis=dim)
        before = lax.ppermute(last, axis, up)
        after = lax.ppermute(first, axis, down)
        x = jnp.concatenate([before, x, after], axis=dim)
    return x


def layer_norm(values):
    values = values.astype(jnp.float32)
    centred = values - jnp.mean(values, axis=-1, keepdims=True)
    spread = jnp.mean(centred * centred, axis=-1, keepdims=True)
    return (centred * lax.rsqrt(spread + NORM_EPS)).astype(jnp.bfloat16)


def softmax_rows(scores):
    top = jnp.max(scores, axis=-1, keepdims=True)
    expo = jnp.exp(scores - top)
    return (expo / jnp.sum(expo, axis=-1, keepdims=True)).astype(jnp.bfloat16)


def temporal_core(item_set):
    frame_num, pos_num = (item_set.shape[0], item_set.shape[2])
    pieces = item_set.reshape(frame_num, pos_num, 3, HEADS, HD)
    scores = jnp.einsum(
        "fphd,gphd->phfg", pieces[:, :, 0], pieces[:, :, 1], preferred_element_type=jnp.float32
    ) * HD ** (-0.5)
    weights = softmax_rows(scores)
    result = jnp.einsum(
        "phfg,gphd->fphd", weights, pieces[:, :, 2], preferred_element_type=jnp.float32
    )
    return result.astype(jnp.bfloat16).reshape(frame_num, 1, pos_num, HEADS * HD)


def body(frames_in, spatial_qkv, spatial_out, temporal_qkv, temporal_out, key_tiles, tile_counts):
    inner_dim = HEADS * HD
    rows_dev = frames_in.shape[1]
    columns = frames_in.shape[2]
    feat_num = frames_in.shape[3]
    tile_rows = rows_dev // TH
    tile_cols = columns // TW
    slab = TH * columns
    pixels = rows_dev * columns
    frame_in = frames_in[0]
    normed = layer_norm(frame_in).reshape(pixels, feat_num)
    qkv_heads = spatial_qkv.reshape(feat_num, 3, HEADS, HD)
    projected = jnp.einsum(
        "te,echk->chkt", normed, qkv_heads, preferred_element_type=jnp.float32
    ).astype(jnp.bfloat16)
    queries = projected[0]
    keyval = projected[1:]
    extended = padded(keyval, (("row", 3),), slab)
    targets = key_tiles[0]
    counts = tile_counts[0]
    tile_num = targets.shape[0]
    slot_num = targets.shape[1]
    ext_row = targets // tile_cols - lax.axis_index("row") * tile_rows + 1
    own_row = jnp.arange(tile_num, dtype=jnp.int32) // tile_cols
    cand_id = (ext_row - own_row[:, None]) * tile_cols + targets % tile_cols
    live = jnp.arange(slot_num, dtype=jnp.int32)[None, :] < counts[:, None]
    cand_all = jnp.arange(3 * tile_cols, dtype=jnp.int32)
    allowed = jnp.any(live[:, :, None] & (cand_id[:, :, None] == cand_all[None, None, :]), axis=1)
    allowed = allowed.astype(jnp.float32).reshape(tile_rows, tile_cols, 3 * tile_cols)
    query_pos = jnp.arange(slab, dtype=jnp.int32)
    query_pick = (query_pos % columns // TW)[:, None] == jnp.arange(tile_cols, dtype=jnp.int32)[
        None, :
    ]
    query_pick = query_pick.astype(jnp.float32)
    key_pos = jnp.arange(3 * slab, dtype=jnp.int32)
    key_tile = key_pos // columns // TH * tile_cols + key_pos % columns // TW
    key_pick = (key_tile[None, :] == cand_all[:, None]).astype(jnp.float32)
    out_heads = spatial_out.reshape(HEADS, HD, feat_num)

    def tile_row_attend(row_num):
        query_blk = lax.dynamic_slice_in_dim(queries, row_num * slab, slab, 2)
        kv_blk = lax.dynamic_slice_in_dim(extended, row_num * slab, 3 * slab, 3)
        table = lax.dynamic_index_in_dim(allowed, row_num, 0, keepdims=False)
        visible = jnp.dot(jnp.dot(query_pick, table), key_pick) > 0.5
        scores = jnp.einsum(
            "hdq,hdk->hqk", query_blk, kv_blk[0], preferred_element_type=jnp.float32
        ) * HD ** (-0.5)
        scores = jnp.where(visible[None], scores, -1e30)
        weights = softmax_rows(scores)
        heads_out = jnp.einsum(
            "hqk,hdk->hdq", weights, kv_blk[1], preferred_element_type=jnp.float32
        ).astype(jnp.bfloat16)
        return jnp.einsum("hdq,hde->qe", heads_out, out_heads, preferred_element_type=jnp.float32)

    branch = lax.map(tile_row_attend, jnp.arange(tile_rows, dtype=jnp.int32))
    mixed_one = (frame_in.astype(jnp.float32) + branch.reshape(rows_dev, columns, feat_num)).astype(
        jnp.bfloat16
    )
    peer_count = lax.axis_size("frame")
    group_len = pixels // peer_count
    normed_two = layer_norm(mixed_one).reshape(1, peer_count, group_len, -1)
    item_set = lax.all_to_all(normed_two, "frame", split_axis=1, concat_axis=0, tiled=True)
    frame_num = item_set.shape[0]
    pos_num = item_set.shape[2]
    width_num = item_set.shape[3]
    proj_items = jnp.dot(
        item_set.reshape(frame_num * pos_num, width_num),
        temporal_qkv,
        preferred_element_type=jnp.float32,
    )
    regrouped = temporal_core(
        proj_items.astype(jnp.bfloat16).reshape(frame_num, 1, pos_num, 3 * inner_dim)
    )
    returned = lax.all_to_all(regrouped, "frame", split_axis=0, concat_axis=1, tiled=True)
    branch_two = jnp.dot(
        returned.reshape(pixels, inner_dim), temporal_out, preferred_element_type=jnp.float32
    )
    result = (mixed_one.astype(jnp.float32) + branch_two.reshape(rows_dev, columns, -1)).astype(
        jnp.bfloat16
    )
    return result[None]


def solution(mesh):
    in_specs = (
        P("frame", "row", None, None),
        P(),
        P(),
        P(),
        P(),
        P("frame", "row", None),
        P("frame", "row"),
    )
    out_specs = P("frame", "row", None, None)
    return jax.shard_map(body, mesh=mesh, in_specs=in_specs, out_specs=out_specs, check_vma=False)
```

profile of v0, /device:TPU:0, one launch (start us, length us, event | category | flops | bytes accessed | tf_op | source)
XLA Modules:
  0.0 271.5 jit_solution(1863293847540468216)
XLA Ops:
  0.0 2.2 convert_reduce_fusion.1
  4.4 4.8 %fusion.89 = f32[1024,1728]{0,1:S(1)} fusion(bf16[1024,1152]{1,0:T(8,128)(2,1)S(1)} %bitcast.124, bf16[1152,1728]{0,1:T(8,128)(2,1)S(1)} %copy-done.6), kind=kOutput, calls=%fused_computation.137 | convolution fusion | flops 4076863488 | bytes 13418496
  10.9 2.4 collective-permute-start
  14.9 4.3 %convert_element_type.118 = f32[1,16,64,1152]{3,2,1,0:T(8,128)} convert(bf16[1,16,64,1152]{3,2,1,0:T(8,128)(2,1)} %param.9) | non-fusion elementwise | flops 1179648 | bytes 7077888 | tf_op jit(solution)/shard_map/convert_element_type | solution.py:109
  21.3 2.9 %pad_maximum_fusion = bf16[2,8,72,1536]{3,2,1,0:T(8,128)(2,1)} fusion(bf16[2,8,72,256]{3,2,1,0:T(8,128)(2,1)} %collective-permute-done.1, bf16[2,8,72,1024]{3,2,1,0:T(8,128)(2,1)S(1)} %slice-done, bf16[2,8,72,256]{3,2,1,0:T(8,128)(2,1)S(1)} %collective-permute-done), kind=kLoop, calls=%fused_computation.54 | loop fusion | flops 10616832 | bytes 7077888 | tf_op jit(solution)/shard_map/concatenate | solution.py:24
  24.2 99.4 %while.11 = (s32[]{:T(128)}, f32[4,256,1152]{2,1,0:T(8,128)}, s32[4]{0:T(128)S(1)}, bf16[2,8,72,1536]{3,2,1,0:T(8,128)(2,1)}, bf16[4,4,12]{2,1,0:T(4,128)(2,1)S(...) while((s32[]{:T(128)}, f32[4,256,1152]{2,1,0:T(8,128)}, ...), condition=%wide.region_6.7_spmd.clone, body=%wide.region_3.6_spmd.clone.sunk | while | flops 810414848 | bytes 30153512 | solution.py:108
  25.4 4.9 %fusion.111 = f32[8,256,768]{2,1,0:T(8,128)} fusion(bf16[2,8,72,1536]{3,2,1,0:T(8,128)(2,1)} %get-tuple-element.199, s32[]{:T(128)S(6)} %select_n.184, bf16[8,72,1024]{2,1,0:T(8,128)(2,1)S(1)} %get-tuple-element.201, s32[]{:T(128)S(6)} %select_n.185), kind=kOutput, calls=%fused_computation.17.clone.1 | convolution fusion | flops 226492416 | bytes 7471112 | tf_op jit(solution)/shard_map/while/body/eval_jaxpr/hdq,hdk->hqk/dot_general | solution.py:98
  32.8 10.2 %fusion.112 = (f32[8,256]{1,0:T(8,128)S(1)}, f32[8,256,768]{2,1,0:T(8,128)}) fusion(f32[8,256,768]{2,1,0:T(8,128)} %fusion.111, pred[256,768]{1,0:T(8,128)(4,1)S(1)} %convolution_compare_fusion.2), kind=kOutput, calls=%fused_computation.133.clone.1 | output fusion | flops 9437951 | bytes 12787712 | tf_op jit(solution)/shard_map/while/body/eval_jaxpr/sub | solution.py:37
  43.0 6.1 %fusion.113 = f32[4,256,1152]{2,1,0:T(8,128)} fusion(f32[4,256,1152]{2,1,0:T(8,128)} %get-tuple-element.181, s32[]{:T(128)} %get-tuple-element.180, bf16[8,72,1152]{2,1,0:T(8,128)(2,1)} %get-tuple-element.202, f32[8,256,768]{2,1,0:T(8,128)} %get-tuple-element.162, f32[8,256]{1,0:T(8,128)S(1)} %get-tuple-element.163, ...), kind=kOutput, calls=%fused_computation.12.clone.1 | convolution fusion | flops 569524224 | bytes 9691656 | tf_op jit(solution)/shard_map/while/body/eval_jaxpr/hdq,hde->qe/dot_general | solution.py:106
  50.3 4.9 %fusion.111 = f32[8,256,768]{2,1,0:T(8,128)} fusion(bf16[2,8,72,1536]{3,2,1,0:T(8,128)(2,1)} %get-tuple-element.199, s32[]{:T(128)S(6)} %select_n.184, bf16[8,72,1024]{2,1,0:T(8,128)(2,1)S(1)} %get-tuple-element.201, s32[]{:T(128)S(6)} %select_n.185), kind=kOutput, calls=%fused_computation.17.clone.1 | convolution fusion | flops 226492416 | bytes 7471112 | tf_op jit(solution)/shard_map/while/body/eval_jaxpr/hdq,hdk->hqk/dot_general | solution.py:98
  57.6 10.2 %fusion.112 = (f32[8,256]{1,0:T(8,128)S(1)}, f32[8,256,768]{2,1,0:T(8,128)}) fusion(f32[8,256,768]{2,1,0:T(8,128)} %fusion.111, pred[256,768]{1,0:T(8,128)(4,1)S(1)} %convolution_compare_fusion.2), kind=kOutput, calls=%fused_computation.133.clone.1 | output fusion | flops 9437951 | bytes 12787712 | tf_op jit(solution)/shard_map/while/body/eval_jaxpr/sub | solution.py:37
  67.8 6.1 %fusion.113 = f32[4,256,1152]{2,1,0:T(8,128)} fusion(f32[4,256,1152]{2,1,0:T(8,128)} %get-tuple-element.181, s32[]{:T(128)} %get-tuple-element.180, bf16[8,72,1152]{2,1,0:T(8,128)(2,1)} %get-tuple-element.202, f32[8,256,768]{2,1,0:T(8,128)} %get-tuple-element.162, f32[8,256]{1,0:T(8,128)S(1)} %get-tuple-element.163, ...), kind=kOutput, calls=%fused_computation.12.clone.1 | convolution fusion | flops 569524224 | bytes 9691656 | tf_op jit(solution)/shard_map/while/body/eval_jaxpr/hdq,hde->qe/dot_general | solution.py:106
  75.1 4.9 %fusion.111 = f32[8,256,768]{2,1,0:T(8,128)} fusion(bf16[2,8,72,1536]{3,2,1,0:T(8,128)(2,1)} %get-tuple-element.199, s32[]{:T(128)S(6)} %select_n.184, bf16[8,72,1024]{2,1,0:T(8,128)(2,1)S(1)} %get-tuple-element.201, s32[]{:T(128)S(6)} %select_n.185), kind=kOutput, calls=%fused_computation.17.clone.1 | convolution fusion | flops 226492416 | bytes 7471112 | tf_op jit(solution)/shard_map/while/body/eval_jaxpr/hdq,hdk->hqk/dot_general | solution.py:98
  82.5 10.2 %fusion.112 = (f32[8,256]{1,0:T(8,128)S(1)}, f32[8,256,768]{2,1,0:T(8,128)}) fusion(f32[8,256,768]{2,1,0:T(8,128)} %fusion.111, pred[256,768]{1,0:T(8,128)(4,1)S(1)} %convolution_compare_fusion.2), kind=kOutput, calls=%fused_computation.133.clone.1 | output fusion | flops 9437951 | bytes 12787712 | tf_op jit(solution)/shard_map/while/body/eval_jaxpr/sub | solution.py:37
  92.7 6.1 %fusion.113 = f32[4,256,1152]{2,1,0:T(8,128)} fusion(f32[4,256,1152]{2,1,0:T(8,128)} %get-tuple-element.181, s32[]{:T(128)} %get-tuple-element.180, bf16[8,72,1152]{2,1,0:T(8,128)(2,1)} %get-tuple-element.202, f32[8,256,768]{2,1,0:T(8,128)} %get-tuple-element.162, f32[8,256]{1,0:T(8,128)S(1)} %get-tuple-element.163, ...), kind=kOutput, calls=%fused_computation.12.clone.1 | convolution fusion | flops 569524224 | bytes 9691656 | tf_op jit(solution)/shard_map/while/body/eval_jaxpr/hdq,hde->qe/dot_general | solution.py:106
  100.0 4.9 %fusion.111 = f32[8,256,768]{2,1,0:T(8,128)} fusion(bf16[2,8,72,1536]{3,2,1,0:T(8,128)(2,1)} %get-tuple-element.199, s32[]{:T(128)S(6)} %select_n.184, bf16[8,72,1024]{2,1,0:T(8,128)(2,1)S(1)} %get-tuple-element.201, s32[]{:T(128)S(6)} %select_n.185), kind=kOutput, calls=%fused_computation.17.clone.1 | convolution fusion | flops 226492416 | bytes 7471112 | tf_op jit(solution)/shard_map/while/body/eval_jaxpr/hdq,hdk->hqk/dot_general | solution.py:98
  107.3 10.2 %fusion.112 = (f32[8,256]{1,0:T(8,128)S(1)}, f32[8,256,768]{2,1,0:T(8,128)}) fusion(f32[8,256,768]{2,1,0:T(8,128)} %fusion.111, pred[256,768]{1,0:T(8,128)(4,1)S(1)} %convolution_compare_fusion.2), kind=kOutput, calls=%fused_computation.133.clone.1 | output fusion | flops 9437951 | bytes 12787712 | tf_op jit(solution)/shard_map/while/body/eval_jaxpr/sub | solution.py:37
  117.5 6.1 %fusion.113 = f32[4,256,1152]{2,1,0:T(8,128)} fusion(f32[4,256,1152]{2,1,0:T(8,128)} %get-tuple-element.181, s32[]{:T(128)} %get-tuple-element.180, bf16[8,72,1152]{2,1,0:T(8,128)(2,1)} %get-tuple-element.202, f32[8,256,768]{2,1,0:T(8,128)} %get-tuple-element.162, f32[8,256]{1,0:T(8,128)S(1)} %get-tuple-element.163, ...), kind=kOutput, calls=%fused_computation.12.clone.1 | convolution fusion | flops 569524224 | bytes 9691656 | tf_op jit(solution)/shard_map/while/body/eval_jaxpr/hdq,hde->qe/dot_general | solution.py:106
  123.6 5.6 %convert_reduce_fusion = (f32[4,256]{1,0:T(4,128)S(1)}, bf16[4,256,1152]{2,1,0:T(8,128)(2,1)}) fusion(f32[4,256,1152]{2,1,0:T(8,128)} %bitcast.117, f32[4,256,1152]{2,1,0:T(8,128)} %get-tuple-element.52), kind=kLoop, calls=%fused_computation.35 | loop fusion | flops 4717568 | bytes 11800576 | tf_op jit(solution)/shard_map/reduce_sum | solution.py:30
  129.2 2.4 fusion.35
  131.7 4.5 %multiply_convert_fusion = bf16[1,8,128,1152]{3,2,0,1:T(8,128)(2,1)S(1)} fusion(f32[1,8,128,1152]{3,2,0,1:T(8,128)} %bitcast.118, f32[1,8,128,1152]{3,2,0,1:T(8,128)} %bitcast.119, f32[8,128]{1,0:T(8,128)S(1)} %rsqrt.21, f32[8,128]{1,0:T(8,128)S(1)} %div.110), kind=kLoop, calls=%fused_computation.44 | loop fusion | flops 7077888 | bytes 11804672 | tf_op jit(solution)/shard_map/convert_element_type | solution.py:32
  136.1 59.7 %all_to_all.8 = bf16[1,8,128,1152]{3,2,0,1:T(8,128)(2,1)S(1)} all-to-all(bf16[1,8,128,1152]{3,2,0,1:T(8,128)(2,1)S(1)} %multiply_convert_fusion), channel_id=1, replica_groups=mesh['frame'=8,'row'=4] {'frame'}, dimensions={1} | all-to-all | bytes 4718592 | tf_op jit(solution)/shard_map/all_to_all | solution.py:115
  195.8 5.0 %fusion.50 = bf16[216,8,8,128]{3,1,2,0:T(8,128)(2,1)S(1)} fusion(bf16[1024,1152]{1,0:T(8,128)(2,1)S(1)} %bitcast.125, bf16[1152,1728]{0,1:T(8,128)(2,1)S(1)} %copy-done.7), kind=kOutput, calls=%fused_computation.65 | convolution fusion | flops 4078632960 | bytes 9879552 | tf_op jit(solution)/shard_map/dot_general | solution.py:119
  203.6 3.4 %copy.38 = bf16[8,128,1,8,72]{4,0,3,1,2:T(8,128)(2,1)S(1)} copy(bf16[8,128,1,8,72]{1,0,4,3,2:T(8,128)(2,1)} %get-tuple-element.99) | data formatting | bytes 2359296
  207.0 4.1 %copy.39 = bf16[8,128,1,8,72]{4,0,3,1,2:T(8,128)(2,1)} copy(bf16[8,128,1,8,72]{1,0,4,3,2:T(8,128)(2,1)} %get-tuple-element.100) | data formatting | bytes 2359296
  211.1 2.8 %fusion.44 = f32[128,8,8,8]{2,3,1,0:T(8,128)S(1)} fusion(bf16[8,128,1,8,72]{4,0,3,1,2:T(8,128)(2,1)} %copy.39, bf16[8,128,1,8,72]{4,0,3,1,2:T(8,128)(2,1)S(1)} %copy.38), kind=kOutput, calls=%fused_computation.58 | convolution fusion | flops 9437184 | bytes 2621440 | tf_op jit(solution)/shard_map/fphd,gphd->phfg/dot_general | solution.py:44
  213.9 3.8 %fusion.88 = (f32[128,8,8]{2,1,0:T(8,128)S(1)}, f32[128,8,8,8]{2,3,1,0:T(8,128)}) fusion(f32[128,8,8,8]{2,3,1,0:T(8,128)S(1)} %fusion.44), kind=kOutput, calls=%fused_computation.136 | output fusion | flops 262151 | bytes 557056 | tf_op jit(solution)/shard_map/sub | solution.py:37
  217.8 3.0 %copy.37 = bf16[8,128,1,8,72]{4,0,3,1,2:T(8,128)(2,1)} copy(bf16[8,128,1,8,72]{1,0,4,3,2:T(8,128)(2,1)S(1)} %copy-done.3) | data formatting | bytes 2359296
  220.8 4.7 %convert_bitcast_fusion.1 = bf16[8,128,8,72]{3,0,2,1:T(8,128)(2,1)} fusion(f32[128,8,8,8]{2,3,1,0:T(8,128)} %get-tuple-element.104, f32[128,8,8]{2,1,0:T(8,128)S(1)} %get-tuple-element.103, bf16[8,128,1,8,72]{4,0,3,1,2:T(8,128)(2,1)} %copy.37), kind=kOutput, calls=%fused_computation.62 | convolution fusion | flops 10158080 | bytes 2654208 | tf_op jit(solution)/shard_map/phfg,gphd->fphd/dot_general | solution.py:48
  225.5 3.2 %copy.33 = bf16[8,128,8,72]{1,3,2,0:T(8,128)(2,1)S(1)} copy(bf16[8,128,8,72]{3,0,2,1:T(8,128)(2,1)} %convert_bitcast_fusion.1) | data formatting | bytes 2359296 | tf_op jit(solution)/shard_map/convert_element_type | solution.py:51
  228.7 34.4 %all_to_all.9 = bf16[8,1,128,576]{2,3,1,0:T(8,128)(2,1)} all-to-all(bf16[8,1,128,576]{2,3,1,0:T(8,128)(2,1)S(1)} %bitcast.123), channel_id=1, replica_groups=mesh['frame'=8,'row'=4] {'frame'}, dimensions={0} | all-to-all | bytes 2359296 | tf_op jit(solution)/shard_map/all_to_all | solution.py:127
  264.8 6.6 %fusion.40 = bf16[1,16,64,1152]{3,2,1,0:T(8,128)(2,1)} fusion(bf16[16,64,576]{2,1,0:T(8,128)(2,1)S(1)} %bitcast.126, f32[16,64,1152]{2,1,0:T(8,128)} %bitcast.120, bf16[1,16,64,1152]{3,2,1,0:T(8,128)(2,1)} %param.9, bf16[576,1152]{1,0:T(8,128)(2,1)S(1)} %copy-done), kind=kOutput, calls=%fused_computation.56 | convolution fusion | flops 1366032384 | bytes 11943936 | tf_op jit(solution)/shard_map/dot_general | solution.py:128
  (52 shorter events, 16.6 us)
Async XLA Ops:
  0.0 264.8 %copy-start = (bf16[576,1152]{1,0:T(8,128)(2,1)S(1)}, bf16[576,1152]{1,0:T(8,128)(2,1)}, u32[]{:S(2)}) copy-start(bf16[576,1152]{1,0:T(8,128)(2,1)} %param.13) | copy-start | bytes 3981316
  0.0 2.5 copy-start.1
  2.2 2.2 copy-start.6
  9.7 5.1 %copy-start.2 = (bf16[3,8,72,1024]{3,2,1,0:T(8,128)(2,1)}, bf16[3,8,72,1024]{3,2,1,0:T(8,128)(2,1)S(1)}, u32[]{:S(2)}) copy-start(bf16[3,8,72,1024]{3,2,1,0:T(8,128)(2,1)S(1)} %convert_bitcast_fusion) | copy-start | bytes 10616836
  10.9 9.9 %collective-permute-start = (bf16[2,8,72,256]{3,2,1,0:T(8,128)(2,1)}, bf16[2,8,72,256]{3,2,1,0:T(8,128)(2,1)S(1)}, u32[]{:S(2)}, u32[]{:S(2)}) collective-permute-start(bf16[2,8,72,256]{3,2,1,0:T(8,128)(2,1)} %get-tuple-element.101), channel_id=1, source_target_pairs={{0,1},{1,2},{2,3},{4,5},{5,6},{6,7},{8,9},{9,10},{10,11},{12,13},{... | collective-permute-start | bytes 1769480 | tf_op jit(solution)/shard_map/ppermute | solution.py:22
  13.3 7.5 %collective-permute-start.1 = (bf16[2,8,72,256]{3,2,1,0:T(8,128)(2,1)}, bf16[2,8,72,256]{3,2,1,0:T(8,128)(2,1)}, u32[]{:S(2)}, u32[]{:S(2)}) collective-permute-start(bf16[2,8,72,256]{3,2,1,0:T(8,128)(2,1)} %get-tuple-element.102), channel_id=1, source_target_pairs={{1,0},{2,1},{3,2},{5,4},{6,5},{7,6},{9,8},{10,9},{11,10},{13,12},{... | collective-permute-start | bytes 1769480 | tf_op jit(solution)/shard_map/ppermute | solution.py:23
  14.8 4.3 %copy-start.5 = (s32[1,16]{1,0:T(1,128)S(1)}, s32[1,16]{1,0:T(1,128)}, u32[]{:S(2)}) copy-start(s32[1,16]{1,0:T(1,128)} %param.15) | copy-start | bytes 196
  14.8 4.3 %copy-start.4 = (s32[1,16,9]{1,0,2:T(1,128)S(1)}, s32[1,16,9]{1,0,2:T(1,128)}, u32[]{:S(2)}) copy-start(s32[1,16,9]{1,0,2:T(1,128)} %param.14) | copy-start | bytes 1732
  19.3 2.0 slice-start
  136.1 59.7 %copy-start.7 = (bf16[1152,1728]{0,1:T(8,128)(2,1)S(1)}, bf16[1152,1728]{0,1:T(8,128)(2,1)}, u32[]{:S(2)}) copy-start(bf16[1152,1728]{0,1:T(8,128)(2,1)} %param.12) | copy-start | bytes 11943940
  213.9 3.8 %copy-start.3 = (bf16[8,128,1,8,72]{1,0,4,3,2:T(8,128)(2,1)S(1)}, bf16[8,128,1,8,72]{1,0,4,3,2:T(8,128)(2,1)}, u32[]{:S(2)}) copy-start(bf16[8,128,1,8,72]{1,0,4,3,2:T(8,128)(2,1)} %get-tuple-element.98) | copy-start | bytes 3538948
where the time goes:
time: 272 us; the launch traced here: 271 us
  blocking collectives  94.1 us (35%)
  matrix products  69.9 us (26%)
  other arithmetic  68.4 us (25%)
  local copies, waits for them, and re-layouts  24.5 us (9%)
  loops' own time  10.4 us (4%)
  starting transfers between devices  3.86 us (1%)
    all_to_all x1, blocking collectives, body(): lax.all_to_all(normed_two, 'frame', split_axis=1, concat_axis=0, tiled=True)  59.7 us
    sub x5, other arithmetic, softmax_rows(): expo = jnp.exp(scores - top)  44.4 us
    all_to_all x1, blocking collectives, body(): lax.all_to_all(regrouped, 'frame', split_axis=0, concat_axis=1, tiled=True)  34.4 us
    dot_general x4, matrix products, tile_row_attend(): jnp.einsum('hdq,hde->qe', heads_out, out_heads, preferred_element_type=jn...  24.4 us
    dot_general x4, matrix products, tile_row_attend(): jnp.einsum('hdq,hdk->hqk', query_blk, kv_blk[0], preferred_element_type=j...  19.4 us
    unnamed x20, local copies, waits for them, and re-layouts  12.2 us
    another operation x1, loops' own time, body(): branch = lax.map(tile_row_attend, jnp.arange(tile_rows, dtype=jnp.int32))  10.4 us
    reduce_sum x2, other arithmetic, layer_norm(): centred = values - jnp.mean(values, axis=-1, keepdims=True)  7.79 us
  transfers between devices with their start and end apart: 2, of which 0 were waited for; matrix products, arithmetic and copies ran while one was open for 2% of the time, Pallas kernels for 0%

commit v1 on v0

v1 whole, which is shorter than its diff:
```python
import functools

import jax
import jax.numpy as jnp
from jax import lax
from jax.experimental import pallas as pl
from jax.experimental.pallas import tpu as pltpu
from jax.sharding import PartitionSpec as P

HEADS = 8
HD = 72
TH = 4
TW = 16
LANES = 128
PACK = 16
NORM_EPS = 1e-06
NEG = -1e30
LOG2E = 1.4426950408889634
F32 = jnp.float32
BF16 = jnp.bfloat16
INNER = HEADS * HD
SHIFT = INNER % LANES
KEY_LO = INNER - SHIFT
EXT = INNER + SHIFT
VMEM_LIMIT = 48 * 1024 * 1024


def layer_norm(values):
    values = values.astype(F32)
    centred = values - jnp.mean(values, axis=-1, keepdims=True)
    spread = jnp.mean(centred * centred, axis=-1, keepdims=True)
    return (centred * lax.rsqrt(spread + NORM_EPS)).astype(BF16)


def window(start):
    return start // LANES * LANES, -(-(start + HD) // LANES) * LANES


def head_lanes(rows, lo, hi, start):
    lane = lax.broadcasted_iota(jnp.int32, (rows, hi - lo), 1) + lo
    return (lane >= start) & (lane < start + HD)


def scaled_queries(prod):
    shifted = pltpu.roll(prod[:, :EXT], SHIFT, 1) if SHIFT else prod[:, :EXT]
    return (shifted * (LOG2E * HD**-0.5)).astype(BF16)


def nt_dot(a, b):
    return lax.dot_general(a, b, (((1,), (1,)), ((), ())), preferred_element_type=F32)


def project_kernel(steps, x_ref, w_ref, q_ref, kv_ref, top_ref, bot_ref):
    step = pl.program_id(0)
    prod = jnp.dot(layer_norm(x_ref[...]), w_ref[...], preferred_element_type=F32)
    q_ref[...] = scaled_queries(prod)
    kv_ref[:, :EXT] = prod[:, KEY_LO : 2 * INNER].astype(BF16)
    kv_ref[:, EXT:] = prod[:, 2 * INNER :].astype(BF16)

    @pl.when(step == 0)
    def _():
        top_ref[...] = kv_ref[...]

    @pl.when(step == steps - 1)
    def _():
        bot_ref[...] = kv_ref[...]


def project(x, w, slab):
    pixels, feat = x.shape
    steps = pixels // slab
    kv_dim = EXT + INNER
    return pl.pallas_call(
        functools.partial(project_kernel, steps),
        grid=(steps,),
        in_specs=[
            pl.BlockSpec((slab, feat), lambda i: (i, 0)),
            pl.BlockSpec(w.shape, lambda i: (0, 0)),
        ],
        out_specs=[
            pl.BlockSpec((slab, EXT), lambda i: (i, 0)),
            pl.BlockSpec((slab, kv_dim), lambda i: (i, 0)),
            pl.BlockSpec((slab, kv_dim), lambda i: (0, 0)),
            pl.BlockSpec((slab, kv_dim), lambda i: (0, 0)),
        ],
        out_shape=[
            jax.ShapeDtypeStruct((pixels, EXT), BF16),
            jax.ShapeDtypeStruct((pixels, kv_dim), BF16),
            jax.ShapeDtypeStruct((slab, kv_dim), BF16),
            jax.ShapeDtypeStruct((slab, kv_dim), BF16),
        ],
        compiler_params=pltpu.CompilerParams(vmem_limit_bytes=VMEM_LIMIT),
        cost_estimate=pl.CostEstimate(
            flops=2 * pixels * feat * 3 * INNER, bytes_accessed=12 * 2**20, transcendentals=0
        ),
        name="project",
    )(x, w)


def fill_bias(bias_ref, tile_row, global_row, tile_cols, slot_num, targets_ref, counts_ref):
    slab, key_num = bias_ref.shape
    columns = tile_cols * TW
    key = lax.broadcasted_iota(jnp.int32, (1, key_num), 1)
    key_tile = key // slab * tile_cols + key % columns // TW
    for col in range(tile_cols):
        tile = tile_row * tile_cols + col
        count = counts_ref[0, tile]
        seen = jnp.zeros((1, key_num), jnp.bool_)
        for slot in range(slot_num):
            target = targets_ref[0, tile, slot]
            cand = lax.div(target, tile_cols) - global_row + 1
            cand = cand * tile_cols + lax.rem(target, tile_cols)
            cand = jnp.where(slot < count, cand, -1)
            seen = seen | (key_tile == cand)
        line = jnp.broadcast_to(jnp.where(seen, 0.0, NEG).astype(F32), (TW, key_num))
        for row in range(slab // columns):
            bias_ref[pl.ds(row * columns + col * TW, TW), :] = line


def spatial_kernel(
    edges, rows_of, group, frame_axis, row_axis, tile_rows, peers, xor,
    targets_ref, counts_ref, x_ref, q_ref, prev_ref, mid_ref, next_ref, *rest,
):
    if edges:
        top_ref, bot_ref, w_ref = rest[:3]
        rest = rest[3:]
    else:
        w_ref = rest[0]
        rest = rest[1:]
    mixed_ref = rest[0]
    send_refs = rest[1 : 1 + peers]
    bias_ref, acc_ref, normed_ref = rest[1 + peers : 4 + peers]
    step = pl.program_id(0)
    steps = len(rows_of)
    slab = x_ref.shape[0]
    if edges:
        prev_s, next_s = rest[4 + peers :]

        @pl.when(step == 0)
        def _():
            prev_s[...] = top_ref[...]
            next_s[...] = next_ref[...]

        @pl.when(step != 0)
        def _():
            prev_s[...] = prev_ref[...]
            next_s[...] = bot_ref[...]

        kv_refs = (prev_s, mid_ref, next_s)
        tile_row = step * (tile_rows - 1)
    else:
        kv_refs = (prev_ref, mid_ref, next_ref)
        tile_row = step + rows_of[0]
    global_row = lax.axis_index(row_axis) * tile_rows + tile_row
    tile_cols = targets_ref.shape[1] // tile_rows
    fill_bias(
        bias_ref, tile_row, global_row, tile_cols, targets_ref.shape[2], targets_ref, counts_ref
    )

    for head in range(HEADS):
        start = SHIFT + head * HD
        lo, hi = window(start)
        queries = jnp.where(head_lanes(slab, lo, hi, start), q_ref[:, lo:hi], 0)
        scores = [
            nt_dot(queries, ref[:, lo:hi]) + bias_ref[:, i * slab : (i + 1) * slab]
            for i, ref in enumerate(kv_refs)
        ]
        top = jnp.max(jnp.maximum(jnp.maximum(scores[0], scores[1]), scores[2]), axis=-1, keepdims=True)
        expo = [jnp.exp2(s - top) for s in scores]
        total = jnp.sum(expo[0] + expo[1] + expo[2], axis=-1, keepdims=True)
        start = head * HD
        lo, hi = window(start)
        hi = min(hi, INNER)
        out = sum(
            jnp.dot(e.astype(BF16), ref[:, EXT + lo : EXT + hi], preferred_element_type=F32)
            for e, ref in zip(expo, kv_refs)
        )
        out = (out / total).astype(BF16)
        if head == 0:
            acc_ref[:, lo:hi] = out
        else:
            mask = head_lanes(slab, lo, hi, start)
            if lo // LANES * LANES < start:
                acc_ref[:, lo:hi] = jnp.where(mask, out, acc_ref[:, lo:hi])
            else:
                acc_ref[:, lo:hi] = out

    branch = jnp.dot(acc_ref[...], w_ref[...], preferred_element_type=F32)
    mixed = (x_ref[...].astype(F32) + branch).astype(BF16)
    mixed_ref[...] = mixed
    normed_ref[pl.ds(pl.multiple_of(step * slab, slab), slab), :] = layer_norm(mixed)

    @pl.when(step == steps - 1)
    def _():
        me = lax.axis_index(frame_axis)
        for j in range(peers):
            peer = me ^ j if xor else lax.rem(me + j, peers)
            begin = pl.multiple_of(peer * group, PACK)
            send_refs[j][...] = normed_ref[pl.ds(begin, group), :]


def spatial(edges, x, q, kv, halos, w, targets, counts, slab, peers, xor):
    pixels, feat = x.shape
    tile_rows = pixels // slab
    rows_of = (0, tile_rows - 1) if edges else tuple(range(1, tile_rows - 1))
    steps = len(rows_of)
    group = steps * slab // peers
    kv_dim = kv.shape[1]
    if edges:
        at = lambda i: i * (tile_rows - 1)
        prev_at = lambda i: tile_rows - 2
        next_at = lambda i: 1
    else:
        at = lambda i: i + 1
        prev_at = lambda i: i
        next_at = lambda i: i + 2
    smem = pl.BlockSpec(memory_space=pltpu.SMEM)
    in_specs = [
        smem,
        smem,
        pl.BlockSpec((slab, feat), lambda i: (at(i), 0)),
        pl.BlockSpec((slab, EXT), lambda i: (at(i), 0)),
        pl.BlockSpec((slab, kv_dim), lambda i: (prev_at(i), 0)),
        pl.BlockSpec((slab, kv_dim), lambda i: (at(i), 0)),
        pl.BlockSpec((slab, kv_dim), lambda i: (next_at(i), 0)),
    ]
    args = [targets, counts, x, q, kv, kv, kv]
    scratch = [
        pltpu.VMEM((slab, 3 * slab), F32),
        pltpu.VMEM((slab, INNER), BF16),
        pltpu.VMEM((steps * slab, feat), BF16),
    ]
    if edges:
        in_specs += [pl.BlockSpec((slab, kv_dim), lambda i: (0, 0))] * 2
        args += list(halos)
        scratch += [pltpu.VMEM((slab, kv_dim), BF16)] * 2
    in_specs.append(pl.BlockSpec(w.shape, lambda i: (0, 0)))
    args.append(w)
    outs = pl.pallas_call(
        functools.partial(
            spatial_kernel, edges, rows_of, group, "frame", "row", tile_rows, peers, xor
        ),
        grid=(steps,),
        in_specs=in_specs,
        out_specs=[pl.BlockSpec((slab, feat), lambda i: (i, 0))]
        + [pl.BlockSpec((group, feat), lambda i: (0, 0))] * peers,
        out_shape=[jax.ShapeDtypeStruct((steps * slab, feat), BF16)]
        + [jax.ShapeDtypeStruct((group, feat), BF16)] * peers,
        scratch_shapes=scratch,
        compiler_params=pltpu.CompilerParams(vmem_limit_bytes=VMEM_LIMIT),
        cost_estimate=pl.CostEstimate(
            flops=8 * 10**9, bytes_accessed=8 * 2**20, transcendentals=0
        ),
        name="spatial_edges" if edges else "spatial_inner",
    )(*args)
    return outs[0], outs[1:]


def temporal_kernel(peers, group, *refs):
    in_refs = refs[:peers]
    w_ref = refs[peers]
    out_refs = refs[peers + 1 : 2 * peers + 1]
    x_ref, q_ref, kv_ref, acc_ref = refs[2 * peers + 1 :]
    block = peers * PACK
    parts = group // PACK
    for part in range(parts):
        for j in range(peers):
            x_ref[pl.ds(part * block + j * PACK, PACK), :] = in_refs[j][pl.ds(part * PACK, PACK), :]
    prod = jnp.dot(x_ref[...], w_ref[...], preferred_element_type=F32)
    q_ref[...] = scaled_queries(prod)
    kv_ref[:, :EXT] = prod[:, KEY_LO : 2 * INNER].astype(BF16)
    kv_ref[:, EXT:] = prod[:, 2 * INNER :].astype(BF16)
    row = lax.broadcasted_iota(jnp.int32, (block, block), 0)
    col = lax.broadcasted_iota(jnp.int32, (block, block), 1)
    bias = jnp.where(row % PACK == col % PACK, 0.0, NEG).astype(F32)
    for part in range(parts):
        rows = pl.ds(part * block, block)
        for head in range(HEADS):
            start = SHIFT + head * HD
            lo, hi = window(start)
            queries = jnp.where(head_lanes(block, lo, hi, start), q_ref[rows, lo:hi], 0)
            scores = nt_dot(queries, kv_ref[rows, lo:hi]) + bias
            expo = jnp.exp2(scores - jnp.max(scores, axis=-1, keepdims=True))
            total = jnp.sum(expo, axis=-1, keepdims=True)
            start = head * HD
            lo, hi = window(start)
            hi = min(hi, INNER)
            out = jnp.dot(expo.astype(BF16), kv_ref[rows, EXT + lo : EXT + hi], preferred_element_type=F32)
            out = (out / total).astype(BF16)
            if lo < start:
                out = jnp.where(head_lanes(block, lo, hi, start), out, acc_ref[rows, lo:hi])
            acc_ref[rows, lo:hi] = out
        for j in range(peers):
            out_refs[j][pl.ds(part * PACK, PACK), :] = acc_ref[pl.ds(part * block + j * PACK, PACK), :]


def temporal(pieces, w):
    peers = len(pieces)
    group, feat = pieces[0].shape
    tokens = peers * group
    return pl.pallas_call(
        functools.partial(temporal_kernel, peers, group),
        out_shape=[jax.ShapeDtypeStruct((group, INNER), BF16)] * peers,
        scratch_shapes=[
            pltpu.VMEM((tokens, feat), BF16),
            pltpu.VMEM((tokens, EXT), BF16),
            pltpu.VMEM((tokens, EXT + INNER), BF16),
            pltpu.VMEM((tokens, INNER), BF16),
        ],
        compiler_params=pltpu.CompilerParams(vmem_limit_bytes=VMEM_LIMIT),
        cost_estimate=pl.CostEstimate(
            flops=4 * 10**9, bytes_accessed=6 * 2**20, transcendentals=0
        ),
        name="temporal",
    )(*pieces, w)


def final_kernel(aliased, peers, group, frame_axis, xor, slab, *refs):
    in_refs = refs[:peers]
    mixed_ref, w_ref = refs[peers : peers + 2]
    out_ref, heads_ref = refs[-2:]
    step = pl.program_id(0)

    @pl.when(step == 0)
    def _():
        me = lax.axis_index(frame_axis)
        for j in range(peers):
            peer = me ^ j if xor else lax.rem(me + j, peers)
            heads_ref[pl.ds(pl.multiple_of(peer * group, PACK), group), :] = in_refs[j][...]

    heads = heads_ref[pl.ds(pl.multiple_of(step * slab, slab), slab), :]
    branch = jnp.dot(heads, w_ref[...], preferred_element_type=F32)
    out_ref[...] = (mixed_ref[...].astype(F32) + branch).astype(BF16)


def final(edges, pieces, mixed, w, slab, pixels, xor, base):
    peers = len(pieces)
    group = pieces[0].shape[0]
    feat = mixed.shape[1]
    steps = mixed.shape[0] // slab
    tile_rows = pixels // slab
    at = (lambda i: i * (tile_rows - 1)) if edges else (lambda i: i + 1)
    in_specs = [pl.BlockSpec((group, INNER), lambda i: (0, 0))] * peers + [
        pl.BlockSpec((slab, feat), lambda i: (i, 0)),
        pl.BlockSpec(w.shape, lambda i: (0, 0)),
    ]
    args = list(pieces) + [mixed, w]
    aliases = {}
    if base is not None:
        in_specs.append(pl.BlockSpec(memory_space=pl.ANY))
        aliases = {len(args): 0}
        args.append(base)
    return pl.pallas_call(
        functools.partial(final_kernel, base is not None, peers, group, "frame", xor, slab),
        grid=(steps,),
        in_specs=in_specs,
        out_specs=pl.BlockSpec((slab, feat), lambda i: (at(i), 0)),
        out_shape=jax.ShapeDtypeStruct((pixels, feat), BF16),
        scratch_shapes=[pltpu.VMEM((peers * group, INNER), BF16)],
        input_output_aliases=aliases,
        compiler_params=pltpu.CompilerParams(vmem_limit_bytes=VMEM_LIMIT),
        cost_estimate=pl.CostEstimate(
            flops=10**9, bytes_accessed=4 * 2**20, transcendentals=0
        ),
        name="final",
    )(*args)


def neighbours(kv_top, kv_bot):
    size = lax.axis_size("row")
    up = [(i, i + 1) for i in range(size - 1)]
    down = [(j, i) for i, j in up]
    return lax.ppermute(kv_bot, "row", up), lax.ppermute(kv_top, "row", down)


def exchange(pieces, xor, back):
    size = lax.axis_size("frame")
    result = [pieces[0]]
    for j in range(1, size):
        if xor:
            pairs = [(i, i ^ j) for i in range(size)]
        else:
            pairs = [(i, (i - j if back else i + j) % size) for i in range(size)]
        result.append(lax.ppermute(pieces[j], "frame", pairs))
    return result


def body(frames_in, spatial_qkv, spatial_out, temporal_qkv, temporal_out, key_tiles, tile_counts):
    _, rows_dev, columns, feat = frames_in.shape
    slab = TH * columns
    pixels = rows_dev * columns
    peers = lax.axis_size("frame")
    xor = peers & (peers - 1) == 0
    x = frames_in.reshape(pixels, feat)
    q, kv, kv_top, kv_bot = project(x, spatial_qkv, slab)
    halos = neighbours(kv_top, kv_bot)
    mixed_a, send_a = spatial(
        False, x, q, kv, None, spatial_out, key_tiles, tile_counts, slab, peers, xor
    )
    got_a = exchange(send_a, xor, False)
    mixed_b, send_b = spatial(
        True, x, q, kv, halos, spatial_out, key_tiles, tile_counts, slab, peers, xor
    )
    got_b = exchange(send_b, xor, False)
    ret_a = exchange(temporal(got_a, temporal_qkv), xor, True)
    ret_b = exchange(temporal(got_b, temporal_qkv), xor, True)
    out = final(False, ret_a, mixed_a, temporal_out, slab, pixels, xor, None)
    out = final(True, ret_b, mixed_b, temporal_out, slab, pixels, xor, out)
    return out.reshape(frames_in.shape)


def solution(mesh):
    in_specs = (
        P("frame", "row", None, None),
        P(),
        P(),
        P(),
        P(),
        P("frame", "row", None),
        P("frame", "row"),
    )
    out_specs = P("frame", "row", None, None)
    return jax.shard_map(body, mesh=mesh, in_specs=in_specs, out_specs=out_specs, check_vma=False)
```

time: 272 us -> 146 us (0.54)
  blocking collectives: 94.1 us -> 0 us
  matrix products: 69.9 us -> 0 us
  other arithmetic: 68.4 us -> 0 us
  Pallas kernels: 0 us -> 54.3 us
  starting transfers between devices: 3.86 us -> 55 us
  loops' own time: 10.4 us -> 0 us
  local copies, waits for them, and re-layouts: 24.5 us -> 31.7 us
  waiting for transfers between devices: 0.01 us -> 3.99 us
    all_to_all x2 -> x0, blocking collectives: 94.1 us -> none  [the longest x1 59.7 us: body(): lax.all_to_all(normed_two, 'frame', split_axis=1, concat_axis=0, tiled=True)]
    dot_general x16 -> x0, matrix products: 65.1 us -> none  [the longest x4 24.4 us: tile_row_attend(): jnp.einsum('hdq,hde->qe', heads_out, out_heads, preferred_element_type=jn...]
    pallas_call x0 -> x7, Pallas kernels: none -> 54.3 us  [the longest x2 21.6 us: spatial(): pl.pallas_call(functools.partial(spatial_kernel, edges, rows_of, group, '...]
    ppermute x2 -> x30, starting transfers between devices: 3.86 us -> 55 us  [the longest x28 50.3 us: exchange(): result.append(lax.ppermute(pieces[j], 'frame', pairs))]
    sub x5 -> x0, other arithmetic: 44.4 us -> none  [softmax_rows(): expo = jnp.exp(scores - top)]
    unnamed x20 -> x47, local copies, waits for them, and re-layouts: 12.2 us -> 26 us
    reduce_sum x4 -> x0, other arithmetic: 11 us -> none  [the longest x2 7.79 us: layer_norm(): centred = values - jnp.mean(values, axis=-1, keepdims=True)]
    another operation x1 -> x0, loops' own time: 10.4 us -> none  [body(): branch = lax.map(tile_row_attend, jnp.arange(tile_rows, dtype=jnp.int32))]
  transfers between devices with their start and end apart: 2 -> 30, of which waited for: 0 -> 3; matrix products, arithmetic and copies ran while one was open for 2% -> 8% of each run, Pallas kernels for 0% -> 29%
where the time goes in v1:
time: 146 us; the launch traced here: 145 us
  starting transfers between devices  55 us (38%)
  Pallas kernels  54.3 us (37%)
  local copies, waits for them, and re-layouts  31.7 us (22%)
  waiting for transfers between devices  3.99 us (3%)
    ppermute x28, starting transfers between devices, exchange(): result.append(lax.ppermute(pieces[j], 'frame', pairs))  50.3 us
    unnamed x47, local copies, waits for them, and re-layouts  26 us
    pallas_call x2, Pallas kernels, spatial(): pl.pallas_call(functools.partial(spatial_kernel, edges, rows_of, group, '...  21.6 us
    pallas_call x2, Pallas kernels, temporal(): pl.pallas_call(functools.partial(temporal_kernel, peers, group), out_shap...  18.6 us
    pallas_call x1, Pallas kernels, project(): pl.pallas_call(functools.partial(project_kernel, steps), grid=(steps,), i...  9.65 us
    ppermute x2, starting transfers between devices, neighbours(): return (lax.ppermute(kv_bot, 'row', up), lax.ppermute(kv_top, 'row', down))  4.66 us
    pallas_call x2, Pallas kernels, final(): pl.pallas_call(functools.partial(final_kernel, base is not None, peers, g...  4.44 us
    ppermute x28, waiting for transfers between devices, exchange(): result.append(lax.ppermute(pieces[j], 'frame', pairs))  3.98 us
  transfers between devices with their start and end apart: 30, of which 3 were waited for; matrix products, arithmetic and copies ran while one was open for 8% of the time, Pallas kernels for 29%

profile of v1, /device:TPU:0, one launch (start us, length us, event | category | flops | bytes accessed | tf_op | source)
XLA Modules:
  0.0 145.0 jit_solution(3860308727405050467)
XLA Ops:
  0.0 6.5 %copy.14.w_ref = bf16[1152,1728]{1,0:T(8,128)(2,1)} copy(bf16[1152,1728]{0,1:T(8,128)(2,1)} %param.8) | data formatting | bytes 7962624 | tf_op args[1]
  6.5 1.7 %copy-done.4 = bf16[1,16,64,1152]{3,2,1,0:T(8,128)(2,1)S(1)} copy-done((bf16[1,16,64,1152]{3,2,1,0:T(8,128)(2,1)S(1)}, bf16[1,16,64,1152]{3,2,1,0:T(8,128)(2,1)}, u32[]{:S(2)}) %copy-start.4) | copy-done | bytes 2359320
  8.1 9.7 %project.1 = (bf16[1024,640]{1,0:T(8,128)(2,1)S(1)}, bf16[1024,1216]{1,0:T(8,128)(2,1)}, bf16[256,1216]{1,0:T(8,128)(2,1)S(1)}, bf16[256,1216]{1,0:T(8,128)(2,1)S(1)}) custom-call(bf16[1024,1152]{1,0:T(8,128)(2,1)S(1)} %bitcast.4, bf16[1152,1728]{1,0:T(8,128)(2,1)} %copy.14.w_ref), custom_call_target="tpu_custom_call" | custom-call | flops 4076863488 | bytes 12582912 | tf_op jit(solution)/shard_map/project/pallas_call | solution.py:73
  19.9 3.2 %collective-permute-start = (bf16[256,1216]{0,1:T(8,128)(2,1)}, bf16[256,1216]{0,1:T(8,128)(2,1)}, u32[]{:S(2)}, u32[]{:S(2)}) collective-permute-start(bf16[256,1216]{0,1:T(8,128)(2,1)} %copy.15), channel_id=1, source_target_pairs={{0,1},{1,2},{2,3},{4,5},{5,6},{6,7},{8,9},{9,10},{10,11},{12,13},{... | collective-permute-start | bytes 1867784 | tf_op jit(solution)/shard_map/ppermute | solution.py:373
  24.2 1.5 %collective-permute-start.1 = (bf16[256,1216]{0,1:T(8,128)(2,1)}, bf16[256,1216]{0,1:T(8,128)(2,1)}, u32[]{:S(2)}, u32[]{:S(2)}) collective-permute-start(bf16[256,1216]{0,1:T(8,128)(2,1)} %copy.16), channel_id=1, source_target_pairs={{1,0},{2,1},{3,2},{5,4},{6,5},{7,6},{9,8},{10,9},{11,10},{13,12},{... | collective-permute-start | bytes 1867784 | tf_op jit(solution)/shard_map/ppermute | solution.py:373
  27.1 10.7 %spatial_inner.1 = (bf16[512,1152]{1,0:T(8,128)(2,1)S(1)}, bf16[64,1152]{1,0:T(8,128)(2,1)S(1)}, bf16[64,1152]{1,0:T(8,128)(2,1)}, bf16[64,1152]{1,0:T(8,128)(2,...) custom-call(s32[1,16,9]{2,1,0:T(8,128)S(1)} %copy.17.targets_ref, ...), custom_call_target="tpu_custom_call" | custom-call | flops 8000000000 | bytes 8388608 | tf_op jit(solution)/shard_map/spatial_inner/pallas_call | solution.py:239
  38.4 2.3 %collective-permute-start.16 = (bf16[64,1152]{1,0:T(8,128)(2,1)}, bf16[64,1152]{1,0:T(8,128)(2,1)S(1)}, u32[]{:S(2)}, u32[]{:S(2)}) collective-permute-start(bf16[64,1152]{1,0:T(8,128)(2,1)} %get-tuple-element.65), channel_id=1, source_target_pairs={{0,4},{4,0},{8,12},{12,8},{16,20},{20,16},{24,28},{28,24},{1,5},{5... | collective-permute-start | bytes 442376 | tf_op jit(solution)/shard_map/ppermute | solution.py:384
  40.7 1.6 %collective-permute-start.17 = (bf16[64,1152]{1,0:T(8,128)(2,1)}, bf16[64,1152]{1,0:T(8,128)(2,1)S(1)}, u32[]{:S(2)}, u32[]{:S(2)}) collective-permute-start(bf16[64,1152]{1,0:T(8,128)(2,1)} %get-tuple-element.66), channel_id=1, source_target_pairs={{0,8},{4,12},{8,0},{12,4},{16,24},{20,28},{24,16},{28,20},{1,9},{5... | collective-permute-start | bytes 442376 | tf_op jit(solution)/shard_map/ppermute | solution.py:384
  42.3 3.0 %collective-permute-start.19 = (bf16[64,1152]{1,0:T(8,128)(2,1)}, bf16[64,1152]{1,0:T(8,128)(2,1)}, u32[]{:S(2)}, u32[]{:S(2)}) collective-permute-start(bf16[64,1152]{1,0:T(8,128)(2,1)} %get-tuple-element.68), channel_id=1, source_target_pairs={{0,16},{4,20},{8,24},{12,28},{16,0},{20,4},{24,8},{28,12},{1,17},{... | collective-permute-start | bytes 442376 | tf_op jit(solution)/shard_map/ppermute | solution.py:384
  46.6 1.3 collective-permute-start.20
  48.0 2.2 %copy.19.rest_1_ = bf16[256,1216]{1,0:T(8,128)(2,1)} copy(bf16[256,1216]{0,1:T(8,128)(2,1)} %collective-permute-done.1) | data formatting | bytes 1245184 | tf_op jit(solution)/shard_map/ppermute | solution.py:373
  52.6 10.9 %spatial_edges.1 = (bf16[512,1152]{1,0:T(8,128)(2,1)S(1)}, bf16[64,1152]{1,0:T(8,128)(2,1)S(1)}, bf16[64,1152]{1,0:T(8,128)(2,1)}, bf16[64,1152]{1,0:T(8,128)(2,...) custom-call(s32[1,16,9]{2,1,0:T(8,128)S(1)} %copy.17.targets_ref, ...), custom_call_target="tpu_custom_call" | custom-call | flops 8000000000 | bytes 8388608 | tf_op jit(solution)/shard_map/spatial_edges/pallas_call | solution.py:239
  66.2 3.6 %collective-permute-start.21 = (bf16[64,1152]{1,0:T(8,128)(2,1)}, bf16[64,1152]{1,0:T(8,128)(2,1)}, u32[]{:S(2)}, u32[]{:S(2)}) collective-permute-start(bf16[64,1152]{1,0:T(8,128)(2,1)} %get-tuple-element.70), channel_id=1, source_target_pairs={{0,24},{4,28},{8,16},{12,20},{16,8},{20,12},{24,0},{28,4},{1,25},{... | collective-permute-start | bytes 442376 | tf_op jit(solution)/shard_map/ppermute | solution.py:384
  69.8 1.6 %collective-permute-start.2 = (bf16[64,1152]{1,0:T(8,128)(2,1)}, bf16[64,1152]{1,0:T(8,128)(2,1)S(1)}, u32[]{:S(2)}, u32[]{:S(2)}) collective-permute-start(bf16[64,1152]{1,0:T(8,128)(2,1)} %get-tuple-element.48), channel_id=1, source_target_pairs={{0,4},{4,0},{8,12},{12,8},{16,20},{20,16},{24,28},{28,24},{1,5},{5... | collective-permute-start | bytes 442376 | tf_op jit(solution)/shard_map/ppermute | solution.py:384
  71.6 6.6 %copy.20.refs_8_ = bf16[1152,1728]{1,0:T(8,128)(2,1)} copy(bf16[1152,1728]{0,1:T(8,128)(2,1)} %param.10) | data formatting | bytes 7962624 | tf_op args[3]
  78.1 1.7 %collective-permute-start.4 = (bf16[64,1152]{1,0:T(8,128)(2,1)}, bf16[64,1152]{1,0:T(8,128)(2,1)S(1)}, u32[]{:S(2)}, u32[]{:S(2)}) collective-permute-start(bf16[64,1152]{1,0:T(8,128)(2,1)} %copy-done.12), channel_id=1, source_target_pairs={{0,12},{4,8},{8,4},{12,0},{16,28},{20,24},{24,20},{28,16},{1,13},{... | collective-permute-start | bytes 442376 | tf_op jit(solution)/shard_map/ppermute | solution.py:384
  79.9 2.4 %collective-permute-start.5 = (bf16[64,1152]{1,0:T(8,128)(2,1)S(1)}, bf16[64,1152]{1,0:T(8,128)(2,1)S(1)}, u32[]{:S(2)}, u32[]{:S(2)}) collective-permute-start(bf16[64,1152]{1,0:T(8,128)(2,1)S(1)} %copy-done.11), channel_id=1, source_target_pairs={{0,16},{4,20},{8,24},{12,28},{16,0},{20,4},{24,8},{28,12},{1,17},{... | collective-permute-start | bytes 442376 | tf_op jit(solution)/shard_map/ppermute | solution.py:384
  82.3 3.5 %collective-permute-start.6 = (bf16[64,1152]{1,0:T(8,128)(2,1)S(1)}, bf16[64,1152]{1,0:T(8,128)(2,1)S(1)}, u32[]{:S(2)}, u32[]{:S(2)}) collective-permute-start(bf16[64,1152]{1,0:T(8,128)(2,1)S(1)} %copy-done.9), channel_id=1, source_target_pairs={{0,20},{4,16},{8,28},{12,24},{16,4},{20,0},{24,12},{28,8},{1,21},{... | collective-permute-start | bytes 442376 | tf_op jit(solution)/shard_map/ppermute | solution.py:384
  85.8 2.2 %collective-permute-start.7 = (bf16[64,1152]{1,0:T(8,128)(2,1)S(1)}, bf16[64,1152]{1,0:T(8,128)(2,1)S(1)}, u32[]{:S(2)}, u32[]{:S(2)}) collective-permute-start(bf16[64,1152]{1,0:T(8,128)(2,1)S(1)} %copy-done.7), channel_id=1, source_target_pairs={{0,24},{4,28},{8,16},{12,20},{16,8},{20,12},{24,0},{28,4},{1,25},{... | collective-permute-start | bytes 442376 | tf_op jit(solution)/shard_map/ppermute | solution.py:384
  89.2 2.2 %copy-done.1 = bf16[1152,1728]{1,0:T(8,128)(2,1)S(1)} copy-done((bf16[1152,1728]{1,0:T(8,128)(2,1)S(1)}, bf16[1152,1728]{1,0:T(8,128)(2,1)}, u32[]{:S(2)}) %copy-start.1) | copy-done | bytes 3981336
  92.3 9.5 %temporal.3 = (bf16[64,576]{1,0:T(8,128)(2,1)S(1)}, bf16[64,576]{1,0:T(8,128)(2,1)S(1)}, bf16[64,576]{1,0:T(8,128)(2,1)S(1)}, bf16[64,576]{1,0:T(8,128)(2,1)S(1)...) custom-call(bf16[64,1152]{1,0:T(8,128)(2,1)S(1)} %copy-done.20, ...), custom_call_target="tpu_custom_call" | custom-call | flops 4000000000 | bytes 6291456 | tf_op jit(solution)/shard_map/temporal/pallas_call | solution.py:301
  101.8 1.9 %collective-permute-start.23 = (bf16[64,576]{1,0:T(8,128)(2,1)S(1)}, bf16[64,576]{1,0:T(8,128)(2,1)S(1)}, u32[]{:S(2)}, u32[]{:S(2)}) collective-permute-start(bf16[64,576]{1,0:T(8,128)(2,1)S(1)} %get-tuple-element.73), channel_id=1, source_target_pairs={{0,4},{4,0},{8,12},{12,8},{16,20},{20,16},{24,28},{28,24},{1,5},{5... | collective-permute-start | bytes 221192 | tf_op jit(solution)/shard_map/ppermute | solution.py:384
  105.3 3.4 %collective-permute-start.26 = (bf16[64,576]{1,0:T(8,128)(2,1)S(1)}, bf16[64,576]{1,0:T(8,128)(2,1)S(1)}, u32[]{:S(2)}, u32[]{:S(2)}) collective-permute-start(bf16[64,576]{1,0:T(8,128)(2,1)S(1)} %get-tuple-element.76), channel_id=1, source_target_pairs={{0,16},{4,20},{8,24},{12,28},{16,0},{20,4},{24,8},{28,12},{1,17},{... | collective-permute-start | bytes 221192 | tf_op jit(solution)/shard_map/ppermute | solution.py:384
  108.7 4.9 %collective-permute-start.27 = (bf16[64,576]{1,0:T(8,128)(2,1)S(1)}, bf16[64,576]{1,0:T(8,128)(2,1)S(1)}, u32[]{:S(2)}, u32[]{:S(2)}) collective-permute-start(bf16[64,576]{1,0:T(8,128)(2,1)S(1)} %get-tuple-element.77), channel_id=1, source_target_pairs={{0,20},{4,16},{8,28},{12,24},{16,4},{20,0},{24,12},{28,8},{1,21},{... | collective-permute-start | bytes 221192 | tf_op jit(solution)/shard_map/ppermute | solution.py:384
  113.7 9.2 %temporal.2 = (bf16[64,576]{1,0:T(8,128)(2,1)S(1)}, bf16[64,576]{1,0:T(8,128)(2,1)S(1)}, bf16[64,576]{1,0:T(8,128)(2,1)S(1)}, bf16[64,576]{1,0:T(8,128)(2,1)S(1)...) custom-call(bf16[64,1152]{1,0:T(8,128)(2,1)S(1)} %copy-done.18, ...), custom_call_target="tpu_custom_call" | custom-call | flops 4000000000 | bytes 6291456 | tf_op jit(solution)/shard_map/temporal/pallas_call | solution.py:301
  123.4 3.8 %collective-permute-start.29 = (bf16[64,576]{1,0:T(8,128)(2,1)S(1)}, bf16[64,576]{1,0:T(8,128)(2,1)S(1)}, u32[]{:S(2)}, u32[]{:S(2)}) collective-permute-start(bf16[64,576]{1,0:T(8,128)(2,1)S(1)} %get-tuple-element.79), channel_id=1, source_target_pairs={{0,28},{4,24},{8,20},{12,16},{16,12},{20,8},{24,4},{28,0},{1,29},{... | collective-permute-start | bytes 221192 | tf_op jit(solution)/shard_map/ppermute | solution.py:384
  128.2 2.4 %collective-permute-start.11 = (bf16[64,576]{1,0:T(8,128)(2,1)S(1)}, bf16[64,576]{1,0:T(8,128)(2,1)S(1)}, u32[]{:S(2)}, u32[]{:S(2)}) collective-permute-start(bf16[64,576]{1,0:T(8,128)(2,1)S(1)} %get-tuple-element.58), channel_id=1, source_target_pairs={{0,12},{4,8},{8,4},{12,0},{16,28},{20,24},{24,20},{28,16},{1,13},{... | collective-permute-start | bytes 221192 | tf_op jit(solution)/shard_map/ppermute | solution.py:384
  131.9 2.2 %collective-permute-start.13 = (bf16[64,576]{1,0:T(8,128)(2,1)S(1)}, bf16[64,576]{1,0:T(8,128)(2,1)S(1)}, u32[]{:S(2)}, u32[]{:S(2)}) collective-permute-start(bf16[64,576]{1,0:T(8,128)(2,1)S(1)} %get-tuple-element.60), channel_id=1, source_target_pairs={{0,20},{4,16},{8,28},{12,24},{16,4},{20,0},{24,12},{28,8},{1,21},{... | collective-permute-start | bytes 221192 | tf_op jit(solution)/shard_map/ppermute | solution.py:384
  134.5 3.8 %collective-permute-start.15 = (bf16[64,576]{1,0:T(8,128)(2,1)S(1)}, bf16[64,576]{1,0:T(8,128)(2,1)S(1)}, u32[]{:S(2)}, u32[]{:S(2)}) collective-permute-start(bf16[64,576]{1,0:T(8,128)(2,1)S(1)} %get-tuple-element.62), channel_id=1, source_target_pairs={{0,28},{4,24},{8,20},{12,16},{16,12},{20,8},{24,4},{28,0},{1,29},{... | collective-permute-start | bytes 221192 | tf_op jit(solution)/shard_map/ppermute | solution.py:384
  138.3 2.2 %final.2.refs_10_ = bf16[1024,1152]{1,0:T(8,128)(2,1)} custom-call(bf16[64,576]{1,0:T(8,128)(2,1)S(1)} %get-tuple-element.72.refs_0_, bf16[64,576]{1,0:T(8,128)(2,1)S(1)} %collective-permute-done.23.refs_1_, bf16[64,576]{1,0:T(8,128)(2,1)S(1)} %collective-permute-done.24.refs_2_, bf16[64,576]{1,0:T(8,128)(2,1)S(1)} %collective-permute-done.25.refs_3_, ...), custom_call_target="tpu_custom_call" | custom-call | flops 1000000000 | bytes 4194304 | tf_op jit(solution)/shard_map/final/pallas_call | solution.py:353
  140.5 2.2 %collective-permute-done.13.refs_5_ = bf16[64,576]{1,0:T(8,128)(2,1)S(1)} collective-permute-done((bf16[64,576]{1,0:T(8,128)(2,1)S(1)}, bf16[64,576]{1,0:T(8,128)(2,1)S(1)}, u32[]{:S(2)}, u32[]{:S(2)}) %collective-permute-start.13) | collective-permute-done | bytes 73760 | tf_op jit(solution)/shard_map/ppermute | solution.py:384
  142.8 2.2 %final.3 = bf16[1024,1152]{1,0:T(8,128)(2,1)} custom-call(bf16[64,576]{1,0:T(8,128)(2,1)S(1)} %get-tuple-element.55.refs_0_, bf16[64,576]{1,0:T(8,128)(2,1)S(1)} %collective-permute-done.9.refs_1_, bf16[64,576]{1,0:T(8,128)(2,1)S(1)} %collective-permute-done.10.refs_2_, ...), custom_call_target="tpu_custom_call", output_to_operand_aliasing={{}: (10, {})} | custom-call | flops 1000000000 | bytes 4194304 | tf_op jit(solution)/shard_map/final/pallas_call | solution.py:353
  (86 shorter events, 18.9 us)
Async XLA Ops:
  19.9 22.4 %collective-permute-start = (bf16[256,1216]{0,1:T(8,128)(2,1)}, bf16[256,1216]{0,1:T(8,128)(2,1)}, u32[]{:S(2)}, u32[]{:S(2)}) collective-permute-start(bf16[256,1216]{0,1:T(8,128)(2,1)} %copy.15), channel_id=1, source_target_pairs={{0,1},{1,2},{2,3},{4,5},{5,6},{6,7},{8,9},{9,10},{10,11},{12,13},{... | collective-permute-start | bytes 1867784 | tf_op jit(solution)/shard_map/ppermute | solution.py:373
  24.2 22.4 %collective-permute-start.1 = (bf16[256,1216]{0,1:T(8,128)(2,1)}, bf16[256,1216]{0,1:T(8,128)(2,1)}, u32[]{:S(2)}, u32[]{:S(2)}) collective-permute-start(bf16[256,1216]{0,1:T(8,128)(2,1)} %copy.16), channel_id=1, source_target_pairs={{1,0},{2,1},{3,2},{5,4},{6,5},{7,6},{9,8},{10,9},{11,10},{13,12},{... | collective-permute-start | bytes 1867784 | tf_op jit(solution)/shard_map/ppermute | solution.py:373
  38.4 27.8 %collective-permute-start.16 = (bf16[64,1152]{1,0:T(8,128)(2,1)}, bf16[64,1152]{1,0:T(8,128)(2,1)S(1)}, u32[]{:S(2)}, u32[]{:S(2)}) collective-permute-start(bf16[64,1152]{1,0:T(8,128)(2,1)} %get-tuple-element.65), channel_id=1, source_target_pairs={{0,4},{4,0},{8,12},{12,8},{16,20},{20,16},{24,28},{28,24},{1,5},{5... | collective-permute-start | bytes 442376 | tf_op jit(solution)/shard_map/ppermute | solution.py:384
  40.7 29.1 %collective-permute-start.17 = (bf16[64,1152]{1,0:T(8,128)(2,1)}, bf16[64,1152]{1,0:T(8,128)(2,1)S(1)}, u32[]{:S(2)}, u32[]{:S(2)}) collective-permute-start(bf16[64,1152]{1,0:T(8,128)(2,1)} %get-tuple-element.66), channel_id=1, source_target_pairs={{0,8},{4,12},{8,0},{12,4},{16,24},{20,28},{24,16},{28,20},{1,9},{5... | collective-permute-start | bytes 442376 | tf_op jit(solution)/shard_map/ppermute | solution.py:384
  42.3 27.5 %collective-permute-start.18 = (bf16[64,1152]{1,0:T(8,128)(2,1)}, bf16[64,1152]{1,0:T(8,128)(2,1)}, u32[]{:S(2)}, u32[]{:S(2)}) collective-permute-start(bf16[64,1152]{1,0:T(8,128)(2,1)} %get-tuple-element.67), channel_id=1, source_target_pairs={{0,12},{4,8},{8,4},{12,0},{16,28},{20,24},{24,20},{28,16},{1,13},{... | collective-permute-start | bytes 442376 | tf_op jit(solution)/shard_map/ppermute | solution.py:384
  42.3 29.2 %collective-permute-start.19 = (bf16[64,1152]{1,0:T(8,128)(2,1)}, bf16[64,1152]{1,0:T(8,128)(2,1)}, u32[]{:S(2)}, u32[]{:S(2)}) collective-permute-start(bf16[64,1152]{1,0:T(8,128)(2,1)} %get-tuple-element.68), channel_id=1, source_target_pairs={{0,16},{4,20},{8,24},{12,28},{16,0},{20,4},{24,8},{28,12},{1,17},{... | collective-permute-start | bytes 442376 | tf_op jit(solution)/shard_map/ppermute | solution.py:384
  46.6 31.5 %collective-permute-start.20 = (bf16[64,1152]{1,0:T(8,128)(2,1)}, bf16[64,1152]{1,0:T(8,128)(2,1)}, u32[]{:S(2)}, u32[]{:S(2)}) collective-permute-start(bf16[64,1152]{1,0:T(8,128)(2,1)} %get-tuple-element.69), channel_id=1, source_target_pairs={{0,20},{4,16},{8,28},{12,24},{16,4},{20,0},{24,12},{28,8},{1,21},{... | collective-permute-start | bytes 442376 | tf_op jit(solution)/shard_map/ppermute | solution.py:384
  66.2 13.7 %collective-permute-start.21 = (bf16[64,1152]{1,0:T(8,128)(2,1)}, bf16[64,1152]{1,0:T(8,128)(2,1)}, u32[]{:S(2)}, u32[]{:S(2)}) collective-permute-start(bf16[64,1152]{1,0:T(8,128)(2,1)} %get-tuple-element.70), channel_id=1, source_target_pairs={{0,24},{4,28},{8,16},{12,20},{16,8},{20,12},{24,0},{28,4},{1,25},{... | collective-permute-start | bytes 442376 | tf_op jit(solution)/shard_map/ppermute | solution.py:384
  69.8 12.5 %collective-permute-start.22 = (bf16[64,1152]{1,0:T(8,128)(2,1)}, bf16[64,1152]{1,0:T(8,128)(2,1)}, u32[]{:S(2)}, u32[]{:S(2)}) collective-permute-start(bf16[64,1152]{1,0:T(8,128)(2,1)} %get-tuple-element.71), channel_id=1, source_target_pairs={{0,28},{4,24},{8,20},{12,16},{16,12},{20,8},{24,4},{28,0},{1,29},{... | collective-permute-start | bytes 442376 | tf_op jit(solution)/shard_map/ppermute | solution.py:384
  69.8 15.9 %collective-permute-start.2 = (bf16[64,1152]{1,0:T(8,128)(2,1)}, bf16[64,1152]{1,0:T(8,128)(2,1)S(1)}, u32[]{:S(2)}, u32[]{:S(2)}) collective-permute-start(bf16[64,1152]{1,0:T(8,128)(2,1)} %get-tuple-element.48), channel_id=1, source_target_pairs={{0,4},{4,0},{8,12},{12,8},{16,20},{20,16},{24,28},{28,24},{1,5},{5... | collective-permute-start | bytes 442376 | tf_op jit(solution)/shard_map/ppermute | solution.py:384
  71.5 16.4 %collective-permute-start.3 = (bf16[64,1152]{1,0:T(8,128)(2,1)}, bf16[64,1152]{1,0:T(8,128)(2,1)}, u32[]{:S(2)}, u32[]{:S(2)}) collective-permute-start(bf16[64,1152]{1,0:T(8,128)(2,1)} %get-tuple-element.49), channel_id=1, source_target_pairs={{0,8},{4,12},{8,0},{12,4},{16,24},{20,28},{24,16},{28,20},{1,9},{5... | collective-permute-start | bytes 442376 | tf_op jit(solution)/shard_map/ppermute | solution.py:384
  78.1 23.6 %collective-permute-start.4 = (bf16[64,1152]{1,0:T(8,128)(2,1)}, bf16[64,1152]{1,0:T(8,128)(2,1)S(1)}, u32[]{:S(2)}, u32[]{:S(2)}) collective-permute-start(bf16[64,1152]{1,0:T(8,128)(2,1)} %copy-done.12), channel_id=1, source_target_pairs={{0,12},{4,8},{8,4},{12,0},{16,28},{20,24},{24,20},{28,16},{1,13},{... | collective-permute-start | bytes 442376 | tf_op jit(solution)/shard_map/ppermute | solution.py:384
  79.9 23.8 %collective-permute-start.5 = (bf16[64,1152]{1,0:T(8,128)(2,1)S(1)}, bf16[64,1152]{1,0:T(8,128)(2,1)S(1)}, u32[]{:S(2)}, u32[]{:S(2)}) collective-permute-start(bf16[64,1152]{1,0:T(8,128)(2,1)S(1)} %copy-done.11), channel_id=1, source_target_pairs={{0,16},{4,20},{8,24},{12,28},{16,0},{20,4},{24,8},{28,12},{1,17},{... | collective-permute-start | bytes 442376 | tf_op jit(solution)/shard_map/ppermute | solution.py:384
  82.3 21.9 %collective-permute-start.6 = (bf16[64,1152]{1,0:T(8,128)(2,1)S(1)}, bf16[64,1152]{1,0:T(8,128)(2,1)S(1)}, u32[]{:S(2)}, u32[]{:S(2)}) collective-permute-start(bf16[64,1152]{1,0:T(8,128)(2,1)S(1)} %copy-done.9), channel_id=1, source_target_pairs={{0,20},{4,16},{8,28},{12,24},{16,4},{20,0},{24,12},{28,8},{1,21},{... | collective-permute-start | bytes 442376 | tf_op jit(solution)/shard_map/ppermute | solution.py:384
  85.8 19.6 %collective-permute-start.7 = (bf16[64,1152]{1,0:T(8,128)(2,1)S(1)}, bf16[64,1152]{1,0:T(8,128)(2,1)S(1)}, u32[]{:S(2)}, u32[]{:S(2)}) collective-permute-start(bf16[64,1152]{1,0:T(8,128)(2,1)S(1)} %copy-done.7), channel_id=1, source_target_pairs={{0,24},{4,28},{8,16},{12,20},{16,8},{20,12},{24,0},{28,4},{1,25},{... | collective-permute-start | bytes 442376 | tf_op jit(solution)/shard_map/ppermute | solution.py:384
  87.9 20.8 %collective-permute-start.8 = (bf16[64,1152]{1,0:T(8,128)(2,1)S(1)}, bf16[64,1152]{1,0:T(8,128)(2,1)S(1)}, u32[]{:S(2)}, u32[]{:S(2)}) collective-permute-start(bf16[64,1152]{1,0:T(8,128)(2,1)S(1)} %get-tuple-element.54), channel_id=1, source_target_pairs={{0,28},{4,24},{8,20},{12,16},{16,12},{20,8},{24,4},{28,0},{1,29},{... | collective-permute-start | bytes 442376 | tf_op jit(solution)/shard_map/ppermute | solution.py:384
  92.3 21.4 %copy-start.18 = (bf16[64,1152]{1,0:T(8,128)(2,1)S(1)}, bf16[64,1152]{1,0:T(8,128)(2,1)}, u32[]{:S(2)}) copy-start(bf16[64,1152]{1,0:T(8,128)(2,1)} %copy-done.17) | copy-start | bytes 442372
  101.8 21.1 %collective-permute-start.23 = (bf16[64,576]{1,0:T(8,128)(2,1)S(1)}, bf16[64,576]{1,0:T(8,128)(2,1)S(1)}, u32[]{:S(2)}, u32[]{:S(2)}) collective-permute-start(bf16[64,576]{1,0:T(8,128)(2,1)S(1)} %get-tuple-element.73), channel_id=1, source_target_pairs={{0,4},{4,0},{8,12},{12,8},{16,20},{20,16},{24,28},{28,24},{1,5},{5... | collective-permute-start | bytes 221192 | tf_op jit(solution)/shard_map/ppermute | solution.py:384
  103.7 19.6 %collective-permute-start.24 = (bf16[64,576]{1,0:T(8,128)(2,1)S(1)}, bf16[64,576]{1,0:T(8,128)(2,1)S(1)}, u32[]{:S(2)}, u32[]{:S(2)}) collective-permute-start(bf16[64,576]{1,0:T(8,128)(2,1)S(1)} %get-tuple-element.74), channel_id=1, source_target_pairs={{0,8},{4,12},{8,0},{12,4},{16,24},{20,28},{24,16},{28,20},{1,9},{5... | collective-permute-start | bytes 221192 | tf_op jit(solution)/shard_map/ppermute | solution.py:384
  104.2 23.0 %collective-permute-start.25 = (bf16[64,576]{1,0:T(8,128)(2,1)S(1)}, bf16[64,576]{1,0:T(8,128)(2,1)S(1)}, u32[]{:S(2)}, u32[]{:S(2)}) collective-permute-start(bf16[64,576]{1,0:T(8,128)(2,1)S(1)} %get-tuple-element.75), channel_id=1, source_target_pairs={{0,12},{4,8},{8,4},{12,0},{16,28},{20,24},{24,20},{28,16},{1,13},{... | collective-permute-start | bytes 221192 | tf_op jit(solution)/shard_map/ppermute | solution.py:384
  105.3 22.9 %collective-permute-start.26 = (bf16[64,576]{1,0:T(8,128)(2,1)S(1)}, bf16[64,576]{1,0:T(8,128)(2,1)S(1)}, u32[]{:S(2)}, u32[]{:S(2)}) collective-permute-start(bf16[64,576]{1,0:T(8,128)(2,1)S(1)} %get-tuple-element.76), channel_id=1, source_target_pairs={{0,16},{4,20},{8,24},{12,28},{16,0},{20,4},{24,8},{28,12},{1,17},{... | collective-permute-start | bytes 221192 | tf_op jit(solution)/shard_map/ppermute | solution.py:384
  108.7 19.5 %collective-permute-start.27 = (bf16[64,576]{1,0:T(8,128)(2,1)S(1)}, bf16[64,576]{1,0:T(8,128)(2,1)S(1)}, u32[]{:S(2)}, u32[]{:S(2)}) collective-permute-start(bf16[64,576]{1,0:T(8,128)(2,1)S(1)} %get-tuple-element.77), channel_id=1, source_target_pairs={{0,20},{4,16},{8,28},{12,24},{16,4},{20,0},{24,12},{28,8},{1,21},{... | collective-permute-start | bytes 221192 | tf_op jit(solution)/shard_map/ppermute | solution.py:384
  113.7 24.7 %copy-start = (bf16[576,1152]{1,0:T(8,128)(2,1)S(1)}, bf16[576,1152]{1,0:T(8,128)(2,1)}, u32[]{:S(2)}) copy-start(bf16[576,1152]{1,0:T(8,128)(2,1)} %refs_9_.3) | copy-start | bytes 3981316
  122.9 7.8 %collective-permute-start.28 = (bf16[64,576]{1,0:T(8,128)(2,1)S(1)}, bf16[64,576]{1,0:T(8,128)(2,1)S(1)}, u32[]{:S(2)}, u32[]{:S(2)}) collective-permute-start(bf16[64,576]{1,0:T(8,128)(2,1)S(1)} %get-tuple-element.78), channel_id=1, source_target_pairs={{0,24},{4,28},{8,16},{12,20},{16,8},{20,12},{24,0},{28,4},{1,25},{... | collective-permute-start | bytes 221192 | tf_op jit(solution)/shard_map/ppermute | solution.py:384
  123.4 8.5 %collective-permute-start.29 = (bf16[64,576]{1,0:T(8,128)(2,1)S(1)}, bf16[64,576]{1,0:T(8,128)(2,1)S(1)}, u32[]{:S(2)}, u32[]{:S(2)}) collective-permute-start(bf16[64,576]{1,0:T(8,128)(2,1)S(1)} %get-tuple-element.79), channel_id=1, source_target_pairs={{0,28},{4,24},{8,20},{12,16},{16,12},{20,8},{24,4},{28,0},{1,29},{... | collective-permute-start | bytes 221192 | tf_op jit(solution)/shard_map/ppermute | solution.py:384
  127.2 6.9 %collective-permute-start.9 = (bf16[64,576]{1,0:T(8,128)(2,1)S(1)}, bf16[64,576]{1,0:T(8,128)(2,1)S(1)}, u32[]{:S(2)}, u32[]{:S(2)}) collective-permute-start(bf16[64,576]{1,0:T(8,128)(2,1)S(1)} %get-tuple-element.56), channel_id=1, source_target_pairs={{0,4},{4,0},{8,12},{12,8},{16,20},{20,16},{24,28},{28,24},{1,5},{5... | collective-permute-start | bytes 221192 | tf_op jit(solution)/shard_map/ppermute | solution.py:384
  128.2 6.3 %collective-permute-start.10 = (bf16[64,576]{1,0:T(8,128)(2,1)S(1)}, bf16[64,576]{1,0:T(8,128)(2,1)S(1)}, u32[]{:S(2)}, u32[]{:S(2)}) collective-permute-start(bf16[64,576]{1,0:T(8,128)(2,1)S(1)} %get-tuple-element.57), channel_id=1, source_target_pairs={{0,8},{4,12},{8,0},{12,4},{16,24},{20,28},{24,16},{28,20},{1,9},{5... | collective-permute-start | bytes 221192 | tf_op jit(solution)/shard_map/ppermute | solution.py:384
  128.2 12.3 %collective-permute-start.11 = (bf16[64,576]{1,0:T(8,128)(2,1)S(1)}, bf16[64,576]{1,0:T(8,128)(2,1)S(1)}, u32[]{:S(2)}, u32[]{:S(2)}) collective-permute-start(bf16[64,576]{1,0:T(8,128)(2,1)S(1)} %get-tuple-element.58), channel_id=1, source_target_pairs={{0,12},{4,8},{8,4},{12,0},{16,28},{20,24},{24,20},{28,16},{1,13},{... | collective-permute-start | bytes 221192 | tf_op jit(solution)/shard_map/ppermute | solution.py:384
  130.7 9.9 %collective-permute-start.12 = (bf16[64,576]{1,0:T(8,128)(2,1)S(1)}, bf16[64,576]{1,0:T(8,128)(2,1)S(1)}, u32[]{:S(2)}, u32[]{:S(2)}) collective-permute-start(bf16[64,576]{1,0:T(8,128)(2,1)S(1)} %get-tuple-element.59), channel_id=1, source_target_pairs={{0,16},{4,20},{8,24},{12,28},{16,0},{20,4},{24,8},{28,12},{1,17},{... | collective-permute-start | bytes 221192 | tf_op jit(solution)/shard_map/ppermute | solution.py:384
  131.9 10.9 %collective-permute-start.13 = (bf16[64,576]{1,0:T(8,128)(2,1)S(1)}, bf16[64,576]{1,0:T(8,128)(2,1)S(1)}, u32[]{:S(2)}, u32[]{:S(2)}) collective-permute-start(bf16[64,576]{1,0:T(8,128)(2,1)S(1)} %get-tuple-element.60), channel_id=1, source_target_pairs={{0,20},{4,16},{8,28},{12,24},{16,4},{20,0},{24,12},{28,8},{1,21},{... | collective-permute-start | bytes 221192 | tf_op jit(solution)/shard_map/ppermute | solution.py:384
  134.1 8.7 %collective-permute-start.14 = (bf16[64,576]{1,0:T(8,128)(2,1)S(1)}, bf16[64,576]{1,0:T(8,128)(2,1)S(1)}, u32[]{:S(2)}, u32[]{:S(2)}) collective-permute-start(bf16[64,576]{1,0:T(8,128)(2,1)S(1)} %get-tuple-element.61), channel_id=1, source_target_pairs={{0,24},{4,28},{8,16},{12,20},{16,8},{20,12},{24,0},{28,4},{1,25},{... | collective-permute-start | bytes 221192 | tf_op jit(solution)/shard_map/ppermute | solution.py:384
  134.5 8.3 %collective-permute-start.15 = (bf16[64,576]{1,0:T(8,128)(2,1)S(1)}, bf16[64,576]{1,0:T(8,128)(2,1)S(1)}, u32[]{:S(2)}, u32[]{:S(2)}) collective-permute-start(bf16[64,576]{1,0:T(8,128)(2,1)S(1)} %get-tuple-element.62), channel_id=1, source_target_pairs={{0,28},{4,24},{8,20},{12,16},{16,12},{20,8},{24,4},{28,0},{1,29},{... | collective-permute-start | bytes 221192 | tf_op jit(solution)/shard_map/ppermute | solution.py:384
  (20 other events, 93.8 us)

commit v2 on v1

v2 whole, which is shorter than its diff:
```python
import functools

import jax
import jax.numpy as jnp
from jax import lax
from jax.experimental import pallas as pl
from jax.experimental.pallas import tpu as pltpu
from jax.sharding import PartitionSpec as P

HEADS = 8
HD = 72
TH = 4
TW = 16
LANES = 128
PACK = 16
NORM_EPS = 1e-06
NEG = -1e30
LOG2E = 1.4426950408889634
F32 = jnp.float32
BF16 = jnp.bfloat16
INNER = HEADS * HD
WIDE = -(-INNER // LANES) * LANES
PAIR = 2 * HD
PAIRS = HEADS // 2
PAIR_ROWS = PAIR + PACK
TILE = TH * TW
SPLIT = (True, True, True, True)
VMEM_LIMIT = 48 * 1024 * 1024


def params():
    return pltpu.CompilerParams(vmem_limit_bytes=VMEM_LIMIT)


def cost(flops, bytes_accessed):
    return pl.CostEstimate(flops=flops, bytes_accessed=bytes_accessed, transcendentals=0)


def nt_dot(a, b):
    return lax.dot_general(a, b, (((1,), (1,)), ((), ())), preferred_element_type=F32)


def nn_dot(a, b):
    return jnp.dot(a, b, preferred_element_type=F32)


def moments(x):
    x = x.astype(F32)
    mean = jnp.mean(x, axis=-1, keepdims=True)
    centred = x - mean
    spread = jnp.mean(centred * centred, axis=-1, keepdims=True)
    return mean, lax.rsqrt(spread + NORM_EPS)


def as_rows(column):
    return jnp.broadcast_to(column, (column.shape[0], LANES)).T[:1]


def normed_dot(x, mean, scale, w):
    ones = jnp.ones((PACK, w.shape[1]), BF16)
    return (nt_dot(x, w) - mean * nt_dot(ones, w)[:1]) * scale


def normed_dot_t(x, mean_row, scale_row, w):
    ones = jnp.ones((LANES, w.shape[1]), BF16)
    return (nt_dot(w, x) - nt_dot(w, ones)[:, :1] * mean_row) * scale_row


def tile_order(rows, columns):
    for col in range(columns // TW):
        for row in range(TH):
            yield (col * TH + row) * TW, row * columns + col * TW


def pair_window(pair):
    return pair * PAIR // LANES * LANES, -(-(pair + 1) * PAIR // LANES) * LANES


def two_heads(queries, pair):
    lo, hi = pair_window(pair)
    lane = lax.broadcasted_iota(jnp.int32, queries.shape, 1) + lo
    start = pair * PAIR
    first = jnp.where((lane >= start) & (lane < start + HD), queries, 0)
    second = jnp.where((lane >= start + HD) & (lane < start + PAIR), queries, 0)
    return jnp.concatenate([first, second], axis=0)


def project_kernel(slab, columns, x_ref, w_ref, q_ref, kv_ref, top_ref, bot_ref, xp_ref, mean_ref, rstd_ref):
    step = pl.program_id(0)
    pixels = x_ref.shape[0]

    @pl.when(step == 0)
    def _():
        for base in range(0, pixels, slab):
            for to, at in tile_order(slab, columns):
                xp_ref[pl.ds(base + to, TW), :] = x_ref[pl.ds(base + at, TW), :]
        mean, rstd = moments(xp_ref[...])
        mean_ref[...] = mean
        rstd_ref[...] = rstd
        q = normed_dot(xp_ref[...], mean, rstd * (LOG2E * HD**-0.5), w_ref[...])
        q_ref[:, :INNER] = q.astype(BF16)
        q_ref[:, INNER:] = jnp.zeros((pixels, WIDE - INNER), BF16)

    @pl.when(step == 1)
    def _():
        k = normed_dot(xp_ref[...], mean_ref[...], rstd_ref[...], w_ref[...])
        kv_ref[:, :INNER] = k.astype(BF16)
        kv_ref[:, INNER:WIDE] = jnp.zeros((pixels, WIDE - INNER), BF16)

    @pl.when(step == 2)
    def _():
        mean, rstd = as_rows(mean_ref[...]), as_rows(rstd_ref[...])
        v = normed_dot_t(xp_ref[...], mean, rstd, w_ref[...]).astype(BF16)
        for base in range(0, pixels, slab):
            for part, row in enumerate(range(0, INNER, slab)):
                rows = min(slab, INNER - row)
                at = WIDE + part * slab
                kv_ref[pl.ds(base, rows), at : at + slab] = v[row : row + rows, base : base + slab]
                if rows < slab:
                    kv_ref[pl.ds(base + rows, slab - rows), at : at + slab] = jnp.zeros(
                        (slab - rows, slab), BF16
                    )
        top_ref[...] = kv_ref[:slab, :]
        bot_ref[...] = kv_ref[pixels - slab :, :]


def project(x, w, slab, columns):
    pixels, feat = x.shape
    kv_dim = WIDE + -(-INNER // slab) * slab
    whole = lambda *shape: pl.BlockSpec(shape, lambda i: (0, 0))
    return pl.pallas_call(
        functools.partial(project_kernel, slab, columns),
        grid=(3,),
        in_specs=[whole(pixels, feat), pl.BlockSpec((INNER, feat), lambda i: (i, 0))],
        out_specs=[
            whole(pixels, WIDE),
            whole(pixels, kv_dim),
            whole(slab, kv_dim),
            whole(slab, kv_dim),
        ],
        out_shape=[
            jax.ShapeDtypeStruct((pixels, WIDE), BF16),
            jax.ShapeDtypeStruct((pixels, kv_dim), BF16),
            jax.ShapeDtypeStruct((slab, kv_dim), BF16),
            jax.ShapeDtypeStruct((slab, kv_dim), BF16),
        ],
        scratch_shapes=[
            pltpu.VMEM((pixels, feat), BF16),
            pltpu.VMEM((pixels, 1), F32),
            pltpu.VMEM((pixels, 1), F32),
        ],
        compiler_params=params(),
        cost_estimate=cost(5 * 10**9, 12 * 2**20),
        name="project",
    )(x, w)


def visible_bits(tile, count, global_row, tile_cols, slot_num, targets_ref):
    bits = jnp.int32(0)
    for slot in range(slot_num):
        target = targets_ref[0, tile, slot]
        cand = (lax.div(target, tile_cols) - global_row + 1) * tile_cols + lax.rem(target, tile_cols)
        bits = bits | jnp.where(slot < count, jnp.left_shift(1, cand), 0)
    return bits


def hidden(bits, index):
    return (1 - (jnp.right_shift(bits, index) & 1)).astype(F32) * NEG


def spatial_kernel(
    edges, first_row, group, peers, xor, split, tile_rows, columns,
    targets_ref, counts_ref, x_ref, q_ref, prev_ref, mid_ref, next_ref, *rest,
):
    if edges:
        top_ref, bot_ref = rest[:2]
        rest = rest[2:]
    w_ref, mixed_ref = rest[:2]
    rest = rest[2:]
    if split:
        send_refs, rest = rest[:peers], rest[peers:]
    p_ref, v_ref, acc_ref, out_ref = rest[:4]
    rest = rest[4:]
    step = pl.program_id(0)
    steps = pl.num_programs(0)
    slab, feat = x_ref.shape
    tile_cols = columns // TW
    slot_num = targets_ref.shape[2]

    @pl.when(step == 0)
    def _():
        p_ref[...] = jnp.zeros(p_ref.shape, BF16)
        for pair in range(PAIRS):
            v_ref[:, pair * PAIR_ROWS + PAIR : (pair + 1) * PAIR_ROWS, :] = jnp.ones(
                (3, PACK, slab), BF16
            )

    if edges:
        prev_s, next_s = rest

        @pl.when(step == 0)
        def _():
            prev_s[...] = top_ref[...]
            next_s[...] = next_ref[...]

        @pl.when(step != 0)
        def _():
            prev_s[...] = prev_ref[...]
            next_s[...] = bot_ref[...]

        kv_refs = (prev_s, mid_ref, next_s)
        tile_row = step * (tile_rows - 1)
    else:
        kv_refs = (prev_ref, mid_ref, next_ref)
        tile_row = step + first_row
    global_row = lax.axis_index("row") * tile_rows + tile_row

    for j, ref in enumerate(kv_refs):
        for pair in range(PAIRS):
            done = 0
            while done < PAIR:
                row = pair * PAIR + done
                part, inside = row // slab, row % slab
                rows = min(PAIR - done, slab - inside)
                at = WIDE + part * slab
                v_ref[j, pl.ds(pair * PAIR_ROWS + done, rows), :] = ref[
                    pl.ds(inside, rows), at : at + slab
                ]
                done += rows

    left = lax.broadcasted_iota(jnp.int32, (1, 4 * TILE), 1) % (2 * TILE) < TILE
    for duo in range(tile_cols // 2):
        bits = []
        for tile in (2 * duo, 2 * duo + 1):
            tile = tile_row * tile_cols + tile
            bits.append(
                visible_bits(tile, counts_ref[0, tile], global_row, tile_cols, slot_num, targets_ref)
            )
        lowest, highest = max(2 * duo - 1, 0), min(2 * duo + 2, tile_cols - 1)
        span = range(lowest, highest + 1)
        bias = {}
        for j in range(3):
            for col in span:
                at = j * tile_cols + col
                bias[j, col] = jnp.where(left, hidden(bits[0], at), hidden(bits[1], at))
        for pair in range(PAIRS):
            lo, hi = pair_window(pair)
            queries = two_heads(q_ref[2 * duo * TILE : (2 * duo + 2) * TILE, lo:hi], pair)
            scores = {}
            for j, ref in enumerate(kv_refs):
                part = nt_dot(ref[lowest * TILE : (highest + 1) * TILE, lo:hi], queries)
                for col in span:
                    at = (col - lowest) * TILE
                    scores[j, col] = part[at : at + TILE] + bias[j, col]
            top = functools.reduce(jnp.maximum, scores.values())
            top = jnp.max(top, axis=0, keepdims=True)
            for (j, col), score in scores.items():
                at = j * slab + col * TILE
                p_ref[duo, at : at + TILE, :] = jnp.exp2(score - top).astype(BF16)
            out = sum(
                nn_dot(
                    v_ref[j, pair * PAIR_ROWS : (pair + 1) * PAIR_ROWS, :],
                    p_ref[duo, j * slab : (j + 1) * slab, :],
                )
                for j in range(3)
            )
            out = out[:PAIR] / out[PAIR : PAIR + 1]
            lanes = slice(2 * duo * TILE, (2 * duo + 2) * TILE)
            acc_ref[pair * PAIR : pair * PAIR + HD, lanes] = out[:HD, : 2 * TILE]
            acc_ref[pair * PAIR + HD : (pair + 1) * PAIR, lanes] = out[HD:, 2 * TILE :]

    branch = nn_dot(acc_ref[...].T.astype(BF16), w_ref[...])
    base = step * slab
    for to, at in tile_order(slab, columns):
        mixed = (x_ref[pl.ds(at, TW), :].astype(F32) + branch[to : to + TW]).astype(BF16)
        mixed_ref[pl.ds(to, TW), :] = mixed
        if split:
            out_ref[pl.ds(pl.multiple_of(base + to, TW), TW), :] = mixed

    if split:

        @pl.when(step == steps - 1)
        def _():
            me = lax.axis_index("frame")
            for j in range(peers):
                peer = me ^ j if xor else lax.rem(me + j, peers)
                send_refs[j][...] = out_ref[pl.ds(pl.multiple_of(peer * group, PACK), group), :]


def spatial(edges, split, x, q, kv, halos, w, targets, counts, slab, columns, peers, xor):
    pixels, feat = x.shape
    tile_rows = pixels // slab
    steps = 2 if edges else tile_rows - 2
    group = steps * slab // peers
    kv_dim = kv.shape[1]
    if edges:
        at = lambda i: i * (tile_rows - 1)
        prev_at = lambda i: tile_rows - 2
        next_at = lambda i: 1
    else:
        at = lambda i: i + 1
        prev_at = lambda i: i
        next_at = lambda i: i + 2
    smem = pl.BlockSpec(memory_space=pltpu.SMEM)
    whole = lambda *shape: pl.BlockSpec(shape, lambda i: (0, 0))
    in_specs = [
        smem,
        smem,
        pl.BlockSpec((slab, feat), lambda i: (at(i), 0)),
        pl.BlockSpec((slab, WIDE), lambda i: (at(i), 0)),
        pl.BlockSpec((slab, kv_dim), lambda i: (prev_at(i), 0)),
        pl.BlockSpec((slab, kv_dim), lambda i: (at(i), 0)),
        pl.BlockSpec((slab, kv_dim), lambda i: (next_at(i), 0)),
    ]
    args = [targets, counts, x, q, kv, kv, kv]
    scratch = [
        pltpu.VMEM((columns // TW // 2, 3 * slab, 4 * TILE), BF16),
        pltpu.VMEM((3, PAIRS * PAIR_ROWS, slab), BF16),
        pltpu.VMEM((INNER, slab), F32),
        pltpu.VMEM((steps * slab, feat), BF16),
    ]
    if edges:
        in_specs += [whole(slab, kv_dim)] * 2
        args += list(halos)
        scratch += [pltpu.VMEM((slab, kv_dim), BF16)] * 2
    in_specs.append(whole(*w.shape))
    args.append(w)
    out_specs = [pl.BlockSpec((slab, feat), lambda i: (i, 0))]
    out_shape = [jax.ShapeDtypeStruct((steps * slab, feat), BF16)]
    if split:
        out_specs += [whole(group, feat)] * peers
        out_shape += [jax.ShapeDtypeStruct((group, feat), BF16)] * peers
    outs = pl.pallas_call(
        functools.partial(
            spatial_kernel, edges, 0 if edges else 1, group, peers, xor, split, tile_rows, columns
        ),
        grid=(steps,),
        in_specs=in_specs,
        out_specs=out_specs,
        out_shape=out_shape,
        scratch_shapes=scratch,
        compiler_params=params(),
        cost_estimate=cost(6 * 10**9, 8 * 2**20),
        name="spatial_edges" if edges else "spatial_inner",
    )(*args)
    return outs[0], outs[1:] if split else [outs[0]]


def temporal_kernel(peers, group, split_in, split_out, *refs):
    count = peers if split_in else 1
    in_refs, w_ref, refs = refs[:count], refs[count], refs[count + 1 :]
    count = peers if split_out else 1
    out_refs = refs[:count]
    x_ref, q_ref, k_ref, v_ref, acc_ref = refs[count:]
    block = peers * PACK
    parts = group // PACK
    tokens = peers * group
    for part in range(parts):
        for j in range(peers):
            to = pl.ds(part * block + j * PACK, PACK)
            if split_in:
                x_ref[to, :] = in_refs[j][pl.ds(part * PACK, PACK), :]
            else:
                x_ref[to, :] = in_refs[0][pl.ds(j * group + part * PACK, PACK), :]
    x = x_ref[...]
    mean, rstd = moments(x)
    q = normed_dot(x, mean, rstd * (LOG2E * HD**-0.5), w_ref[:INNER, :])
    q_ref[:, :INNER] = q.astype(BF16)
    q_ref[:, INNER:] = jnp.zeros((tokens, WIDE - INNER), BF16)
    k_ref[:, :INNER] = normed_dot(x, mean, rstd, w_ref[INNER : 2 * INNER, :]).astype(BF16)
    k_ref[:, INNER:] = jnp.zeros((tokens, WIDE - INNER), BF16)
    v = normed_dot_t(x, as_rows(mean), as_rows(rstd), w_ref[2 * INNER :, :]).astype(BF16)
    for pair in range(PAIRS):
        at = pair * PAIR_ROWS
        v_ref[at : at + PAIR, :] = v[pair * PAIR : (pair + 1) * PAIR]
        v_ref[at + PAIR : at + PAIR_ROWS, :] = jnp.ones((PACK, tokens), BF16)
    row = lax.broadcasted_iota(jnp.int32, (block, 2 * block), 0)
    col = lax.broadcasted_iota(jnp.int32, (block, 2 * block), 1)
    bias = jnp.where(row % PACK == col % PACK, 0.0, NEG).astype(F32)
    for part in range(parts):
        at = part * block
        for pair in range(PAIRS):
            lo, hi = pair_window(pair)
            queries = two_heads(q_ref[at : at + block, lo:hi], pair)
            scores = nt_dot(k_ref[at : at + block, lo:hi], queries) + bias
            expo = jnp.exp2(scores - jnp.max(scores, axis=0, keepdims=True)).astype(BF16)
            out = nn_dot(v_ref[pair * PAIR_ROWS : (pair + 1) * PAIR_ROWS, at : at + block], expo)
            out = out[:PAIR] / out[PAIR : PAIR + 1]
            acc_ref[pair * PAIR : pair * PAIR + HD, at : at + block] = out[:HD, :block]
            acc_ref[pair * PAIR + HD : (pair + 1) * PAIR, at : at + block] = out[HD:, block:]
        heads = acc_ref[:, at : at + block].T.astype(BF16)
        for j in range(peers):
            rows = heads[j * PACK : (j + 1) * PACK]
            if split_out:
                out_refs[j][pl.ds(part * PACK, PACK), :] = rows
            else:
                out_refs[0][pl.ds(j * group + part * PACK, PACK), :] = rows


def temporal(pieces, w, peers, split_out):
    split_in = len(pieces) > 1
    feat = pieces[0].shape[1]
    tokens = sum(piece.shape[0] for piece in pieces)
    group = tokens // peers
    if split_out:
        out_shape = [jax.ShapeDtypeStruct((group, INNER), BF16)] * peers
    else:
        out_shape = [jax.ShapeDtypeStruct((tokens, INNER), BF16)]
    return pl.pallas_call(
        functools.partial(temporal_kernel, peers, group, split_in, split_out),
        out_shape=out_shape,
        scratch_shapes=[
            pltpu.VMEM((tokens, feat), BF16),
            pltpu.VMEM((tokens, WIDE), BF16),
            pltpu.VMEM((tokens, WIDE), BF16),
            pltpu.VMEM((PAIRS * PAIR_ROWS, tokens), BF16),
            pltpu.VMEM((INNER, tokens), F32),
        ],
        compiler_params=params(),
        cost_estimate=cost(4 * 10**9, 6 * 2**20),
        name="temporal",
    )(*pieces, w)


def final_kernel(peers, group, xor, split, columns, *refs):
    count = peers if split else 1
    in_refs = refs[:count]
    mixed_ref, w_ref = refs[count : count + 2]
    out_ref, heads_ref = refs[-2:]
    step = pl.program_id(0)
    slab = mixed_ref.shape[0]

    if split:

        @pl.when(step == 0)
        def _():
            me = lax.axis_index("frame")
            for j in range(peers):
                peer = me ^ j if xor else lax.rem(me + j, peers)
                heads_ref[pl.ds(pl.multiple_of(peer * group, PACK), group), :] = in_refs[j][...]

        heads = heads_ref[pl.ds(pl.multiple_of(step * slab, slab), slab), :]
    else:
        heads = in_refs[0][pl.ds(pl.multiple_of(step * slab, slab), slab), :]
    result = mixed_ref[...].astype(F32) + nn_dot(heads, w_ref[...])
    for to, at in tile_order(slab, columns):
        out_ref[pl.ds(at, TW), :] = result[to : to + TW].astype(BF16)


def final(edges, pieces, mixed, w, slab, columns, pixels, peers, xor, base):
    split = len(pieces) > 1
    group = mixed.shape[0] // peers
    feat = mixed.shape[1]
    steps = mixed.shape[0] // slab
    tile_rows = pixels // slab
    at = (lambda i: i * (tile_rows - 1)) if edges else (lambda i: i + 1)
    whole = lambda *shape: pl.BlockSpec(shape, lambda i: (0, 0))
    in_specs = [whole(*piece.shape) for piece in pieces] + [
        pl.BlockSpec((slab, feat), lambda i: (i, 0)),
        whole(*w.shape),
    ]
    args = list(pieces) + [mixed, w]
    aliases = {}
    if base is not None:
        in_specs.append(pl.BlockSpec(memory_space=pl.ANY))
        aliases = {len(args): 0}
        args.append(base)
    return pl.pallas_call(
        functools.partial(final_kernel, peers, group, xor, split, columns),
        grid=(steps,),
        in_specs=in_specs,
        out_specs=pl.BlockSpec((slab, feat), lambda i: (at(i), 0)),
        out_shape=jax.ShapeDtypeStruct((pixels, feat), BF16),
        scratch_shapes=[pltpu.VMEM((peers * group, INNER), BF16)],
        input_output_aliases=aliases,
        compiler_params=params(),
        cost_estimate=cost(10**9, 4 * 2**20),
        name="final",
    )(*args)


def neighbours(kv_top, kv_bot):
    size = lax.axis_size("row")
    up = [(i, i + 1) for i in range(size - 1)]
    down = [(j, i) for i, j in up]
    return lax.ppermute(kv_bot, "row", up), lax.ppermute(kv_top, "row", down)


def exchange(pieces, xor, back):
    size = lax.axis_size("frame")
    if len(pieces) == 1:
        whole = pieces[0].reshape(size, -1, pieces[0].shape[-1])
        got = lax.all_to_all(whole, "frame", split_axis=0, concat_axis=0)
        return [got.reshape(pieces[0].shape)]
    result = [pieces[0]]
    for j in range(1, size):
        if xor:
            pairs = [(i, i ^ j) for i in range(size)]
        else:
            pairs = [(i, (i - j if back else i + j) % size) for i in range(size)]
        result.append(lax.ppermute(pieces[j], "frame", pairs))
    return result


def body(frames_in, spatial_qkv, spatial_out, temporal_qkv, temporal_out, key_tiles, tile_counts):
    _, rows_dev, columns, feat = frames_in.shape
    slab = TH * columns
    pixels = rows_dev * columns
    peers = lax.axis_size("frame")
    xor = peers & (peers - 1) == 0
    x = frames_in.reshape(pixels, feat)
    q, kv, kv_top, kv_bot = project(x, spatial_qkv.T, slab, columns)
    halos = neighbours(kv_top, kv_bot)
    tiles = (spatial_out, key_tiles, tile_counts, slab, columns, peers, xor)
    mixed_a, send_a = spatial(False, SPLIT[0], x, q, kv, None, *tiles)
    got_a = exchange(send_a, xor, False)
    mixed_b, send_b = spatial(True, SPLIT[1], x, q, kv, halos, *tiles)
    got_b = exchange(send_b, xor, False)
    ret_a = exchange(temporal(got_a, temporal_qkv.T, peers, SPLIT[2]), xor, True)
    ret_b = exchange(temporal(got_b, temporal_qkv.T, peers, SPLIT[3]), xor, True)
    sizes = (temporal_out, slab, columns, pixels, peers, xor)
    out = final(False, ret_a, mixed_a, *sizes, None)
    out = final(True, ret_b, mixed_b, *sizes, out)
    return out.reshape(frames_in.shape)


def solution(mesh):
    in_specs = (
        P("frame", "row", None, None),
        P(),
        P(),
        P(),
        P(),
        P("frame", "row", None),
        P("frame", "row"),
    )
    out_specs = P("frame", "row", None, None)
    return jax.shard_map(body, mesh=mesh, in_specs=in_specs, out_specs=out_specs, check_vma=False)
```

time: 146 us -> 135 us (0.925)
  local copies, waits for them, and re-layouts: 31.7 us -> 6.92 us
  starting transfers between devices: 55 us -> 62.8 us
  waiting for transfers between devices: 3.99 us -> 7.34 us
  Pallas kernels: 54.3 us -> 56.7 us
    unnamed x47 -> x25, local copies, waits for them, and re-layouts: 26 us -> 6.92 us
    ppermute x28, starting transfers between devices: 50.3 us -> 58.9 us  [exchange(): result.append(lax.ppermute(pieces[j], 'frame', pairs))]
    ppermute x2 -> x0, local copies, waits for them, and re-layouts: 3.5 us -> none  [neighbours(): return (lax.ppermute(kv_bot, 'row', up), lax.ppermute(kv_top, 'row', down))]
    ppermute x28, waiting for transfers between devices: 3.98 us -> 7.34 us  [exchange(): result.append(lax.ppermute(pieces[j], 'frame', pairs))]
    pallas_call x7, Pallas kernels: 54.3 us -> 56.7 us  [the longest x2 22.3 us: spatial(): pl.pallas_call(functools.partial(spatial_kernel, edges, 0 if edges else 1...]
    pallas_call x2 -> x0, local copies, waits for them, and re-layouts: 2.16 us -> none  [project(): pl.pallas_call(functools.partial(project_kernel, steps), grid=(steps,), i...]
  transfers between devices with their start and end apart: 30 -> 30, of which waited for: 3 -> 6; matrix products, arithmetic and copies ran while one was open for 8% -> 0% of each run, Pallas kernels for 29% -> 31%
where the time goes in v2:
time: 135 us; the launch traced here: 134 us
  starting transfers between devices  62.8 us (47%)
  Pallas kernels  56.7 us (42%)
  waiting for transfers between devices  7.34 us (5%)
  local copies, waits for them, and re-layouts  6.92 us (5%)
    ppermute x28, starting transfers between devices, exchange(): result.append(lax.ppermute(pieces[j], 'frame', pairs))  58.9 us
    pallas_call x2, Pallas kernels, spatial(): pl.pallas_call(functools.partial(spatial_kernel, edges, 0 if edges else 1...  22.3 us
    pallas_call x2, Pallas kernels, temporal(): pl.pallas_call(functools.partial(temporal_kernel, peers, group, split_in,...  17.5 us
    pallas_call x1, Pallas kernels, project(): pl.pallas_call(functools.partial(project_kernel, slab, columns), grid=(3,...  12.5 us
    ppermute x28, waiting for transfers between devices, exchange(): result.append(lax.ppermute(pieces[j], 'frame', pairs))  7.34 us
    unnamed x25, local copies, waits for them, and re-layouts  6.92 us
    pallas_call x2, Pallas kernels, final(): pl.pallas_call(functools.partial(final_kernel, peers, group, xor, split,...  4.43 us
    ppermute x2, starting transfers between devices, neighbours(): return (lax.ppermute(kv_bot, 'row', up), lax.ppermute(kv_top, 'row', down))  3.85 us
  transfers between devices with their start and end apart: 30, of which 6 were waited for; matrix products, arithmetic and copies ran while one was open for 0% of the time, Pallas kernels for 31%

profile of v2, /device:TPU:0, one launch (start us, length us, event | category | flops | bytes accessed | tf_op | source)
XLA Modules:
  0.0 133.9 jit_solution(17567197076763501211)
XLA Ops:
  0.0 1.7 %copy-done.3 = bf16[1,16,64,1152]{3,2,1,0:T(8,128)(2,1)S(1)} copy-done((bf16[1,16,64,1152]{3,2,1,0:T(8,128)(2,1)S(1)}, bf16[1,16,64,1152]{3,2,1,0:T(8,128)(2,1)}, u32[]{:S(2)}) %copy-start.3) | copy-done | bytes 2359320
  1.7 12.5 %project.1 = (bf16[1024,640]{1,0:T(8,128)(2,1)S(1)}, bf16[1024,1408]{1,0:T(8,128)(2,1)}, bf16[256,1408]{1,0:T(8,128)(2,1)S(1)}, bf16[256,1408]{1,0:T(8,128)(2,1)}) custom-call(bf16[1024,1152]{1,0:T(8,128)(2,1)S(1)} %bitcast.8, bf16[1728,1152]{1,0:T(8,128)(2,1)} %bitcast.9), custom_call_target="tpu_custom_call" | custom-call | flops 5000000000 | bytes 12582912 | tf_op jit(solution)/shard_map/project/pallas_call | solution.py:131
  15.2 2.4 %collective-permute-start = (bf16[256,1408]{1,0:T(8,128)(2,1)}, bf16[256,1408]{1,0:T(8,128)(2,1)S(1)}, u32[]{:S(2)}, u32[]{:S(2)}) collective-permute-start(bf16[256,1408]{1,0:T(8,128)(2,1)} %get-tuple-element.45), channel_id=1, source_target_pairs={{0,1},{1,2},{2,3},{4,5},{5,6},{6,7},{8,9},{9,10},{10,11},{12,13},{... | collective-permute-start | bytes 2162696 | tf_op jit(solution)/shard_map/ppermute | solution.py:486
  17.6 1.5 %collective-permute-start.1 = (bf16[256,1408]{1,0:T(8,128)(2,1)S(1)}, bf16[256,1408]{1,0:T(8,128)(2,1)S(1)}, u32[]{:S(2)}, u32[]{:S(2)}) collective-permute-start(bf16[256,1408]{1,0:T(8,128)(2,1)S(1)} %get-tuple-element.46), channel_id=1, source_target_pairs={{1,0},{2,1},{3,2},{5,4},{6,5},{7,6},{9,8},{10,9},{11,10},{13,12},{... | collective-permute-start | bytes 2162696 | tf_op jit(solution)/shard_map/ppermute | solution.py:486
  20.5 10.8 %spatial_inner.1 = (bf16[512,1152]{1,0:T(8,128)(2,1)S(1)}, bf16[64,1152]{1,0:T(8,128)(2,1)S(1)}, bf16[64,1152]{1,0:T(8,128)(2,1)S(1)}, bf16[64,1152]{1,0:T(8,128...) custom-call(s32[1,16,9]{2,1,0:T(8,128)S(1)} %copy.9.targets_ref, ...), custom_call_target="tpu_custom_call" | custom-call | flops 6000000000 | bytes 8388608 | tf_op jit(solution)/shard_map/spatial_inner/pallas_call | solution.py:333
  32.0 2.3 %collective-permute-start.16 = (bf16[64,1152]{1,0:T(8,128)(2,1)S(1)}, bf16[64,1152]{1,0:T(8,128)(2,1)S(1)}, u32[]{:S(2)}, u32[]{:S(2)}) collective-permute-start(bf16[64,1152]{1,0:T(8,128)(2,1)S(1)} %get-tuple-element.65), channel_id=1, source_target_pairs={{0,4},{4,0},{8,12},{12,8},{16,20},{20,16},{24,28},{28,24},{1,5},{5... | collective-permute-start | bytes 442376 | tf_op jit(solution)/shard_map/ppermute | solution.py:501
  34.3 1.6 %collective-permute-start.17 = (bf16[64,1152]{1,0:T(8,128)(2,1)S(1)}, bf16[64,1152]{1,0:T(8,128)(2,1)S(1)}, u32[]{:S(2)}, u32[]{:S(2)}) collective-permute-start(bf16[64,1152]{1,0:T(8,128)(2,1)S(1)} %get-tuple-element.66), channel_id=1, source_target_pairs={{0,8},{4,12},{8,0},{12,4},{16,24},{20,28},{24,16},{28,20},{1,9},{5... | collective-permute-start | bytes 442376 | tf_op jit(solution)/shard_map/ppermute | solution.py:501
  35.9 3.0 %collective-permute-start.19 = (bf16[64,1152]{1,0:T(8,128)(2,1)S(1)}, bf16[64,1152]{1,0:T(8,128)(2,1)S(1)}, u32[]{:S(2)}, u32[]{:S(2)}) collective-permute-start(bf16[64,1152]{1,0:T(8,128)(2,1)S(1)} %get-tuple-element.68), channel_id=1, source_target_pairs={{0,16},{4,20},{8,24},{12,28},{16,0},{20,4},{24,8},{28,12},{1,17},{... | collective-permute-start | bytes 442376 | tf_op jit(solution)/shard_map/ppermute | solution.py:501
  40.2 11.4 %spatial_edges.1 = (bf16[512,1152]{1,0:T(8,128)(2,1)S(1)}, bf16[64,1152]{1,0:T(8,128)(2,1)S(1)}, bf16[64,1152]{1,0:T(8,128)(2,1)S(1)}, bf16[64,1152]{1,0:T(8,128...) custom-call(s32[1,16,9]{2,1,0:T(8,128)S(1)} %copy.9.targets_ref, ...), custom_call_target="tpu_custom_call" | custom-call | flops 6000000000 | bytes 8388608 | tf_op jit(solution)/shard_map/spatial_edges/pallas_call | solution.py:333
  51.7 3.7 %collective-permute-start.21 = (bf16[64,1152]{1,0:T(8,128)(2,1)S(1)}, bf16[64,1152]{1,0:T(8,128)(2,1)S(1)}, u32[]{:S(2)}, u32[]{:S(2)}) collective-permute-start(bf16[64,1152]{1,0:T(8,128)(2,1)S(1)} %get-tuple-element.70), channel_id=1, source_target_pairs={{0,24},{4,28},{8,16},{12,20},{16,8},{20,12},{24,0},{28,4},{1,25},{... | collective-permute-start | bytes 442376 | tf_op jit(solution)/shard_map/ppermute | solution.py:501
  55.4 1.6 %collective-permute-start.2 = (bf16[64,1152]{1,0:T(8,128)(2,1)S(1)}, bf16[64,1152]{1,0:T(8,128)(2,1)S(1)}, u32[]{:S(2)}, u32[]{:S(2)}) collective-permute-start(bf16[64,1152]{1,0:T(8,128)(2,1)S(1)} %get-tuple-element.48), channel_id=1, source_target_pairs={{0,4},{4,0},{8,12},{12,8},{16,20},{20,16},{24,28},{28,24},{1,5},{5... | collective-permute-start | bytes 442376 | tf_op jit(solution)/shard_map/ppermute | solution.py:501
  57.0 1.9 %collective-permute-start.4 = (bf16[64,1152]{1,0:T(8,128)(2,1)S(1)}, bf16[64,1152]{1,0:T(8,128)(2,1)S(1)}, u32[]{:S(2)}, u32[]{:S(2)}) collective-permute-start(bf16[64,1152]{1,0:T(8,128)(2,1)S(1)} %get-tuple-element.50), channel_id=1, source_target_pairs={{0,12},{4,8},{8,4},{12,0},{16,28},{20,24},{24,20},{28,16},{1,13},{... | collective-permute-start | bytes 442376 | tf_op jit(solution)/shard_map/ppermute | solution.py:501
  58.9 1.4 %collective-permute-done.21.refs_6_ = bf16[64,1152]{1,0:T(8,128)(2,1)S(1)} collective-permute-done((bf16[64,1152]{1,0:T(8,128)(2,1)S(1)}, bf16[64,1152]{1,0:T(8,128)(2,1)S(1)}, u32[]{:S(2)}, u32[]{:S(2)}) %collective-permute-start.21) | collective-permute-done | bytes 147488 | tf_op jit(solution)/shard_map/ppermute | solution.py:501
  60.3 7.0 %collective-permute-start.5 = (bf16[64,1152]{1,0:T(8,128)(2,1)S(1)}, bf16[64,1152]{1,0:T(8,128)(2,1)S(1)}, u32[]{:S(2)}, u32[]{:S(2)}) collective-permute-start(bf16[64,1152]{1,0:T(8,128)(2,1)S(1)} %get-tuple-element.51), channel_id=1, source_target_pairs={{0,16},{4,20},{8,24},{12,28},{16,0},{20,4},{24,8},{28,12},{1,17},{... | collective-permute-start | bytes 442376 | tf_op jit(solution)/shard_map/ppermute | solution.py:501
  67.3 7.0 %collective-permute-start.6 = (bf16[64,1152]{1,0:T(8,128)(2,1)S(1)}, bf16[64,1152]{1,0:T(8,128)(2,1)S(1)}, u32[]{:S(2)}, u32[]{:S(2)}) collective-permute-start(bf16[64,1152]{1,0:T(8,128)(2,1)S(1)} %get-tuple-element.52), channel_id=1, source_target_pairs={{0,20},{4,16},{8,28},{12,24},{16,4},{20,0},{24,12},{28,8},{1,21},{... | collective-permute-start | bytes 442376 | tf_op jit(solution)/shard_map/ppermute | solution.py:501
  74.4 3.0 %collective-permute-start.8 = (bf16[64,1152]{1,0:T(8,128)(2,1)S(1)}, bf16[64,1152]{1,0:T(8,128)(2,1)S(1)}, u32[]{:S(2)}, u32[]{:S(2)}) collective-permute-start(bf16[64,1152]{1,0:T(8,128)(2,1)S(1)} %get-tuple-element.54), channel_id=1, source_target_pairs={{0,28},{4,24},{8,20},{12,16},{16,12},{20,8},{24,4},{28,0},{1,29},{... | collective-permute-start | bytes 442376 | tf_op jit(solution)/shard_map/ppermute | solution.py:501
  77.4 2.1 %copy-done.1 = bf16[1152,1728]{0,1:T(8,128)(2,1)S(1)} copy-done((bf16[1152,1728]{0,1:T(8,128)(2,1)S(1)}, bf16[1152,1728]{0,1:T(8,128)(2,1)}, u32[]{:S(2)}) %copy-start.1) | copy-done | bytes 3981336
  79.6 8.6 %temporal.3 = (bf16[64,576]{1,0:T(8,128)(2,1)S(1)}, bf16[64,576]{1,0:T(8,128)(2,1)S(1)}, bf16[64,576]{1,0:T(8,128)(2,1)S(1)}, bf16[64,576]{1,0:T(8,128)(2,1)S(1)...) custom-call(bf16[64,1152]{1,0:T(8,128)(2,1)S(1)} %copy-done.10, ...), custom_call_target="tpu_custom_call" | custom-call | flops 4000000000 | bytes 6291456 | tf_op jit(solution)/shard_map/temporal/pallas_call | solution.py:409
  88.2 2.3 %collective-permute-start.23 = (bf16[64,576]{1,0:T(8,128)(2,1)S(1)}, bf16[64,576]{1,0:T(8,128)(2,1)S(1)}, u32[]{:S(2)}, u32[]{:S(2)}) collective-permute-start(bf16[64,576]{1,0:T(8,128)(2,1)S(1)} %get-tuple-element.73), channel_id=1, source_target_pairs={{0,4},{4,0},{8,12},{12,8},{16,20},{20,16},{24,28},{28,24},{1,5},{5... | collective-permute-start | bytes 221192 | tf_op jit(solution)/shard_map/ppermute | solution.py:501
  90.5 1.5 %collective-permute-start.25 = (bf16[64,576]{1,0:T(8,128)(2,1)S(1)}, bf16[64,576]{1,0:T(8,128)(2,1)S(1)}, u32[]{:S(2)}, u32[]{:S(2)}) collective-permute-start(bf16[64,576]{1,0:T(8,128)(2,1)S(1)} %get-tuple-element.75), channel_id=1, source_target_pairs={{0,12},{4,8},{8,4},{12,0},{16,28},{20,24},{24,20},{28,16},{1,13},{... | collective-permute-start | bytes 221192 | tf_op jit(solution)/shard_map/ppermute | solution.py:501
  92.1 2.6 %collective-permute-start.26 = (bf16[64,576]{1,0:T(8,128)(2,1)S(1)}, bf16[64,576]{1,0:T(8,128)(2,1)S(1)}, u32[]{:S(2)}, u32[]{:S(2)}) collective-permute-start(bf16[64,576]{1,0:T(8,128)(2,1)S(1)} %get-tuple-element.76), channel_id=1, source_target_pairs={{0,16},{4,20},{8,24},{12,28},{16,0},{20,4},{24,8},{28,12},{1,17},{... | collective-permute-start | bytes 221192 | tf_op jit(solution)/shard_map/ppermute | solution.py:501
  94.6 6.6 %collective-permute-start.27 = (bf16[64,576]{1,0:T(8,128)(2,1)S(1)}, bf16[64,576]{1,0:T(8,128)(2,1)S(1)}, u32[]{:S(2)}, u32[]{:S(2)}) collective-permute-start(bf16[64,576]{1,0:T(8,128)(2,1)S(1)} %get-tuple-element.77), channel_id=1, source_target_pairs={{0,20},{4,16},{8,28},{12,24},{16,4},{20,0},{24,12},{28,8},{1,21},{... | collective-permute-start | bytes 221192 | tf_op jit(solution)/shard_map/ppermute | solution.py:501
  101.3 8.9 %temporal.2 = (bf16[64,576]{1,0:T(8,128)(2,1)S(1)}, bf16[64,576]{1,0:T(8,128)(2,1)S(1)}, bf16[64,576]{1,0:T(8,128)(2,1)S(1)}, bf16[64,576]{1,0:T(8,128)(2,1)S(1)...) custom-call(bf16[64,1152]{1,0:T(8,128)(2,1)S(1)} %get-tuple-element., ...), custom_call_target="tpu_custom_call" | custom-call | flops 4000000000 | bytes 6291456 | tf_op jit(solution)/shard_map/temporal/pallas_call | solution.py:409
  110.3 2.2 %collective-permute-start.29 = (bf16[64,576]{1,0:T(8,128)(2,1)S(1)}, bf16[64,576]{1,0:T(8,128)(2,1)S(1)}, u32[]{:S(2)}, u32[]{:S(2)}) collective-permute-start(bf16[64,576]{1,0:T(8,128)(2,1)S(1)} %get-tuple-element.79), channel_id=1, source_target_pairs={{0,28},{4,24},{8,20},{12,16},{16,12},{20,8},{24,4},{28,0},{1,29},{... | collective-permute-start | bytes 221192 | tf_op jit(solution)/shard_map/ppermute | solution.py:501
  112.5 3.1 %collective-permute-start.9 = (bf16[64,576]{1,0:T(8,128)(2,1)S(1)}, bf16[64,576]{1,0:T(8,128)(2,1)S(1)}, u32[]{:S(2)}, u32[]{:S(2)}) collective-permute-start(bf16[64,576]{1,0:T(8,128)(2,1)S(1)} %get-tuple-element.56), channel_id=1, source_target_pairs={{0,4},{4,0},{8,12},{12,8},{16,20},{20,16},{24,28},{28,24},{1,5},{5... | collective-permute-start | bytes 221192 | tf_op jit(solution)/shard_map/ppermute | solution.py:501
  115.5 1.5 %collective-permute-start.11 = (bf16[64,576]{1,0:T(8,128)(2,1)S(1)}, bf16[64,576]{1,0:T(8,128)(2,1)S(1)}, u32[]{:S(2)}, u32[]{:S(2)}) collective-permute-start(bf16[64,576]{1,0:T(8,128)(2,1)S(1)} %get-tuple-element.58), channel_id=1, source_target_pairs={{0,12},{4,8},{8,4},{12,0},{16,28},{20,24},{24,20},{28,16},{1,13},{... | collective-permute-start | bytes 221192 | tf_op jit(solution)/shard_map/ppermute | solution.py:501
  118.2 3.2 %collective-permute-start.13 = (bf16[64,576]{1,0:T(8,128)(2,1)S(1)}, bf16[64,576]{1,0:T(8,128)(2,1)S(1)}, u32[]{:S(2)}, u32[]{:S(2)}) collective-permute-start(bf16[64,576]{1,0:T(8,128)(2,1)S(1)} %get-tuple-element.60), channel_id=1, source_target_pairs={{0,20},{4,16},{8,28},{12,24},{16,4},{20,0},{24,12},{28,8},{1,21},{... | collective-permute-start | bytes 221192 | tf_op jit(solution)/shard_map/ppermute | solution.py:501
  122.1 2.9 %collective-permute-start.15 = (bf16[64,576]{1,0:T(8,128)(2,1)S(1)}, bf16[64,576]{1,0:T(8,128)(2,1)S(1)}, u32[]{:S(2)}, u32[]{:S(2)}) collective-permute-start(bf16[64,576]{1,0:T(8,128)(2,1)S(1)} %get-tuple-element.62), channel_id=1, source_target_pairs={{0,28},{4,24},{8,20},{12,16},{16,12},{20,8},{24,4},{28,0},{1,29},{... | collective-permute-start | bytes 221192 | tf_op jit(solution)/shard_map/ppermute | solution.py:501
  125.0 2.2 %final.2.refs_10_ = bf16[1024,1152]{1,0:T(8,128)(2,1)} custom-call(bf16[64,576]{1,0:T(8,128)(2,1)S(1)} %get-tuple-element.72.refs_0_, bf16[64,576]{1,0:T(8,128)(2,1)S(1)} %collective-permute-done.23.refs_1_, bf16[64,576]{1,0:T(8,128)(2,1)S(1)} %collective-permute-done.24.refs_2_, bf16[64,576]{1,0:T(8,128)(2,1)S(1)} %collective-permute-done.25.refs_3_, ...), custom_call_target="tpu_custom_call" | custom-call | flops 1000000000 | bytes 4194304 | tf_op jit(solution)/shard_map/final/pallas_call | solution.py:468
  127.2 2.7 %collective-permute-done.12.refs_4_ = bf16[64,576]{1,0:T(8,128)(2,1)S(1)} collective-permute-done((bf16[64,576]{1,0:T(8,128)(2,1)S(1)}, bf16[64,576]{1,0:T(8,128)(2,1)S(1)}, u32[]{:S(2)}, u32[]{:S(2)}) %collective-permute-start.12) | collective-permute-done | bytes 73760 | tf_op jit(solution)/shard_map/ppermute | solution.py:501
  129.9 1.8 %collective-permute-done.13.refs_5_ = bf16[64,576]{1,0:T(8,128)(2,1)S(1)} collective-permute-done((bf16[64,576]{1,0:T(8,128)(2,1)S(1)}, bf16[64,576]{1,0:T(8,128)(2,1)S(1)}, u32[]{:S(2)}, u32[]{:S(2)}) %collective-permute-start.13) | collective-permute-done | bytes 73760 | tf_op jit(solution)/shard_map/ppermute | solution.py:501
  131.7 2.2 %final.3 = bf16[1024,1152]{1,0:T(8,128)(2,1)} custom-call(bf16[64,576]{1,0:T(8,128)(2,1)S(1)} %get-tuple-element.55.refs_0_, bf16[64,576]{1,0:T(8,128)(2,1)S(1)} %collective-permute-done.9.refs_1_, bf16[64,576]{1,0:T(8,128)(2,1)S(1)} %collective-permute-done.10.refs_2_, ...), custom_call_target="tpu_custom_call", output_to_operand_aliasing={{}: (10, {})} | custom-call | flops 1000000000 | bytes 4194304 | tf_op jit(solution)/shard_map/final/pallas_call | solution.py:468
  (60 shorter events, 6.4 us)
Async XLA Ops:
  15.2 20.7 %collective-permute-start = (bf16[256,1408]{1,0:T(8,128)(2,1)}, bf16[256,1408]{1,0:T(8,128)(2,1)S(1)}, u32[]{:S(2)}, u32[]{:S(2)}) collective-permute-start(bf16[256,1408]{1,0:T(8,128)(2,1)} %get-tuple-element.45), channel_id=1, source_target_pairs={{0,1},{1,2},{2,3},{4,5},{5,6},{6,7},{8,9},{9,10},{10,11},{12,13},{... | collective-permute-start | bytes 2162696 | tf_op jit(solution)/shard_map/ppermute | solution.py:486
  17.6 21.3 %collective-permute-start.1 = (bf16[256,1408]{1,0:T(8,128)(2,1)S(1)}, bf16[256,1408]{1,0:T(8,128)(2,1)S(1)}, u32[]{:S(2)}, u32[]{:S(2)}) collective-permute-start(bf16[256,1408]{1,0:T(8,128)(2,1)S(1)} %get-tuple-element.46), channel_id=1, source_target_pairs={{1,0},{2,1},{3,2},{5,4},{6,5},{7,6},{9,8},{10,9},{11,10},{13,12},{... | collective-permute-start | bytes 2162696 | tf_op jit(solution)/shard_map/ppermute | solution.py:486
  32.0 19.7 %collective-permute-start.16 = (bf16[64,1152]{1,0:T(8,128)(2,1)S(1)}, bf16[64,1152]{1,0:T(8,128)(2,1)S(1)}, u32[]{:S(2)}, u32[]{:S(2)}) collective-permute-start(bf16[64,1152]{1,0:T(8,128)(2,1)S(1)} %get-tuple-element.65), channel_id=1, source_target_pairs={{0,4},{4,0},{8,12},{12,8},{16,20},{20,16},{24,28},{28,24},{1,5},{5... | collective-permute-start | bytes 442376 | tf_op jit(solution)/shard_map/ppermute | solution.py:501
  34.3 21.0 %collective-permute-start.17 = (bf16[64,1152]{1,0:T(8,128)(2,1)S(1)}, bf16[64,1152]{1,0:T(8,128)(2,1)S(1)}, u32[]{:S(2)}, u32[]{:S(2)}) collective-permute-start(bf16[64,1152]{1,0:T(8,128)(2,1)S(1)} %get-tuple-element.66), channel_id=1, source_target_pairs={{0,8},{4,12},{8,0},{12,4},{16,24},{20,28},{24,16},{28,20},{1,9},{5... | collective-permute-start | bytes 442376 | tf_op jit(solution)/shard_map/ppermute | solution.py:501
  35.9 19.5 %collective-permute-start.18 = (bf16[64,1152]{1,0:T(8,128)(2,1)S(1)}, bf16[64,1152]{1,0:T(8,128)(2,1)S(1)}, u32[]{:S(2)}, u32[]{:S(2)}) collective-permute-start(bf16[64,1152]{1,0:T(8,128)(2,1)S(1)} %get-tuple-element.67), channel_id=1, source_target_pairs={{0,12},{4,8},{8,4},{12,0},{16,28},{20,24},{24,20},{28,16},{1,13},{... | collective-permute-start | bytes 442376 | tf_op jit(solution)/shard_map/ppermute | solution.py:501
  35.9 21.1 %collective-permute-start.19 = (bf16[64,1152]{1,0:T(8,128)(2,1)S(1)}, bf16[64,1152]{1,0:T(8,128)(2,1)S(1)}, u32[]{:S(2)}, u32[]{:S(2)}) collective-permute-start(bf16[64,1152]{1,0:T(8,128)(2,1)S(1)} %get-tuple-element.68), channel_id=1, source_target_pairs={{0,16},{4,20},{8,24},{12,28},{16,0},{20,4},{24,8},{28,12},{1,17},{... | collective-permute-start | bytes 442376 | tf_op jit(solution)/shard_map/ppermute | solution.py:501
  38.9 38.5 %copy-start.10 = (bf16[64,1152]{1,0:T(8,128)(2,1)S(1)}, bf16[64,1152]{1,0:T(8,128)(2,1)}, u32[]{:S(2)}) copy-start(bf16[64,1152]{1,0:T(8,128)(2,1)} %copy-done.9) | copy-start | bytes 442372
  38.9 18.1 %collective-permute-start.20 = (bf16[64,1152]{1,0:T(8,128)(2,1)S(1)}, bf16[64,1152]{1,0:T(8,128)(2,1)S(1)}, u32[]{:S(2)}, u32[]{:S(2)}) collective-permute-start(bf16[64,1152]{1,0:T(8,128)(2,1)S(1)} %get-tuple-element.69), channel_id=1, source_target_pairs={{0,20},{4,16},{8,28},{12,24},{16,4},{20,0},{24,12},{28,8},{1,21},{... | collective-permute-start | bytes 442376 | tf_op jit(solution)/shard_map/ppermute | solution.py:501
  51.7 8.6 %collective-permute-start.21 = (bf16[64,1152]{1,0:T(8,128)(2,1)S(1)}, bf16[64,1152]{1,0:T(8,128)(2,1)S(1)}, u32[]{:S(2)}, u32[]{:S(2)}) collective-permute-start(bf16[64,1152]{1,0:T(8,128)(2,1)S(1)} %get-tuple-element.70), channel_id=1, source_target_pairs={{0,24},{4,28},{8,16},{12,20},{16,8},{20,12},{24,0},{28,4},{1,25},{... | collective-permute-start | bytes 442376 | tf_op jit(solution)/shard_map/ppermute | solution.py:501
  55.3 12.0 %collective-permute-start.22 = (bf16[64,1152]{1,0:T(8,128)(2,1)S(1)}, bf16[64,1152]{1,0:T(8,128)(2,1)S(1)}, u32[]{:S(2)}, u32[]{:S(2)}) collective-permute-start(bf16[64,1152]{1,0:T(8,128)(2,1)S(1)} %get-tuple-element.71), channel_id=1, source_target_pairs={{0,28},{4,24},{8,20},{12,16},{16,12},{20,8},{24,4},{28,0},{1,29},{... | collective-permute-start | bytes 442376 | tf_op jit(solution)/shard_map/ppermute | solution.py:501
  55.4 19.0 %collective-permute-start.2 = (bf16[64,1152]{1,0:T(8,128)(2,1)S(1)}, bf16[64,1152]{1,0:T(8,128)(2,1)S(1)}, u32[]{:S(2)}, u32[]{:S(2)}) collective-permute-start(bf16[64,1152]{1,0:T(8,128)(2,1)S(1)} %get-tuple-element.48), channel_id=1, source_target_pairs={{0,4},{4,0},{8,12},{12,8},{16,20},{20,16},{24,28},{28,24},{1,5},{5... | collective-permute-start | bytes 442376 | tf_op jit(solution)/shard_map/ppermute | solution.py:501
  57.0 17.4 %collective-permute-start.3 = (bf16[64,1152]{1,0:T(8,128)(2,1)S(1)}, bf16[64,1152]{1,0:T(8,128)(2,1)S(1)}, u32[]{:S(2)}, u32[]{:S(2)}) collective-permute-start(bf16[64,1152]{1,0:T(8,128)(2,1)S(1)} %get-tuple-element.49), channel_id=1, source_target_pairs={{0,8},{4,12},{8,0},{12,4},{16,24},{20,28},{24,16},{28,20},{1,9},{5... | collective-permute-start | bytes 442376 | tf_op jit(solution)/shard_map/ppermute | solution.py:501
  57.0 31.1 %collective-permute-start.4 = (bf16[64,1152]{1,0:T(8,128)(2,1)S(1)}, bf16[64,1152]{1,0:T(8,128)(2,1)S(1)}, u32[]{:S(2)}, u32[]{:S(2)}) collective-permute-start(bf16[64,1152]{1,0:T(8,128)(2,1)S(1)} %get-tuple-element.50), channel_id=1, source_target_pairs={{0,12},{4,8},{8,4},{12,0},{16,28},{20,24},{24,20},{28,16},{1,13},{... | collective-permute-start | bytes 442376 | tf_op jit(solution)/shard_map/ppermute | solution.py:501
  60.3 30.2 %collective-permute-start.5 = (bf16[64,1152]{1,0:T(8,128)(2,1)S(1)}, bf16[64,1152]{1,0:T(8,128)(2,1)S(1)}, u32[]{:S(2)}, u32[]{:S(2)}) collective-permute-start(bf16[64,1152]{1,0:T(8,128)(2,1)S(1)} %get-tuple-element.51), channel_id=1, source_target_pairs={{0,16},{4,20},{8,24},{12,28},{16,0},{20,4},{24,8},{28,12},{1,17},{... | collective-permute-start | bytes 442376 | tf_op jit(solution)/shard_map/ppermute | solution.py:501
  67.3 23.2 %collective-permute-start.6 = (bf16[64,1152]{1,0:T(8,128)(2,1)S(1)}, bf16[64,1152]{1,0:T(8,128)(2,1)S(1)}, u32[]{:S(2)}, u32[]{:S(2)}) collective-permute-start(bf16[64,1152]{1,0:T(8,128)(2,1)S(1)} %get-tuple-element.52), channel_id=1, source_target_pairs={{0,20},{4,16},{8,28},{12,24},{16,4},{20,0},{24,12},{28,8},{1,21},{... | collective-permute-start | bytes 442376 | tf_op jit(solution)/shard_map/ppermute | solution.py:501
  74.4 17.7 %collective-permute-start.7 = (bf16[64,1152]{1,0:T(8,128)(2,1)S(1)}, bf16[64,1152]{1,0:T(8,128)(2,1)S(1)}, u32[]{:S(2)}, u32[]{:S(2)}) collective-permute-start(bf16[64,1152]{1,0:T(8,128)(2,1)S(1)} %get-tuple-element.53), channel_id=1, source_target_pairs={{0,24},{4,28},{8,16},{12,20},{16,8},{20,12},{24,0},{28,4},{1,25},{... | collective-permute-start | bytes 442376 | tf_op jit(solution)/shard_map/ppermute | solution.py:501
  74.4 20.3 %collective-permute-start.8 = (bf16[64,1152]{1,0:T(8,128)(2,1)S(1)}, bf16[64,1152]{1,0:T(8,128)(2,1)S(1)}, u32[]{:S(2)}, u32[]{:S(2)}) collective-permute-start(bf16[64,1152]{1,0:T(8,128)(2,1)S(1)} %get-tuple-element.54), channel_id=1, source_target_pairs={{0,28},{4,24},{8,20},{12,16},{16,12},{20,8},{24,4},{28,0},{1,29},{... | collective-permute-start | bytes 442376 | tf_op jit(solution)/shard_map/ppermute | solution.py:501
  88.2 22.0 %collective-permute-start.23 = (bf16[64,576]{1,0:T(8,128)(2,1)S(1)}, bf16[64,576]{1,0:T(8,128)(2,1)S(1)}, u32[]{:S(2)}, u32[]{:S(2)}) collective-permute-start(bf16[64,576]{1,0:T(8,128)(2,1)S(1)} %get-tuple-element.73), channel_id=1, source_target_pairs={{0,4},{4,0},{8,12},{12,8},{16,20},{20,16},{24,28},{28,24},{1,5},{5... | collective-permute-start | bytes 221192 | tf_op jit(solution)/shard_map/ppermute | solution.py:501
  90.5 19.7 %collective-permute-start.24 = (bf16[64,576]{1,0:T(8,128)(2,1)S(1)}, bf16[64,576]{1,0:T(8,128)(2,1)S(1)}, u32[]{:S(2)}, u32[]{:S(2)}) collective-permute-start(bf16[64,576]{1,0:T(8,128)(2,1)S(1)} %get-tuple-element.74), channel_id=1, source_target_pairs={{0,8},{4,12},{8,0},{12,4},{16,24},{20,28},{24,16},{28,20},{1,9},{5... | collective-permute-start | bytes 221192 | tf_op jit(solution)/shard_map/ppermute | solution.py:501
  90.5 21.9 %collective-permute-start.25 = (bf16[64,576]{1,0:T(8,128)(2,1)S(1)}, bf16[64,576]{1,0:T(8,128)(2,1)S(1)}, u32[]{:S(2)}, u32[]{:S(2)}) collective-permute-start(bf16[64,576]{1,0:T(8,128)(2,1)S(1)} %get-tuple-element.75), channel_id=1, source_target_pairs={{0,12},{4,8},{8,4},{12,0},{16,28},{20,24},{24,20},{28,16},{1,13},{... | collective-permute-start | bytes 221192 | tf_op jit(solution)/shard_map/ppermute | solution.py:501
  92.1 23.5 %collective-permute-start.26 = (bf16[64,576]{1,0:T(8,128)(2,1)S(1)}, bf16[64,576]{1,0:T(8,128)(2,1)S(1)}, u32[]{:S(2)}, u32[]{:S(2)}) collective-permute-start(bf16[64,576]{1,0:T(8,128)(2,1)S(1)} %get-tuple-element.76), channel_id=1, source_target_pairs={{0,16},{4,20},{8,24},{12,28},{16,0},{20,4},{24,8},{28,12},{1,17},{... | collective-permute-start | bytes 221192 | tf_op jit(solution)/shard_map/ppermute | solution.py:501
  94.6 20.9 %collective-permute-start.27 = (bf16[64,576]{1,0:T(8,128)(2,1)S(1)}, bf16[64,576]{1,0:T(8,128)(2,1)S(1)}, u32[]{:S(2)}, u32[]{:S(2)}) collective-permute-start(bf16[64,576]{1,0:T(8,128)(2,1)S(1)} %get-tuple-element.77), channel_id=1, source_target_pairs={{0,20},{4,16},{8,28},{12,24},{16,4},{20,0},{24,12},{28,8},{1,21},{... | collective-permute-start | bytes 221192 | tf_op jit(solution)/shard_map/ppermute | solution.py:501
  101.3 23.8 %copy-start = (bf16[576,1152]{1,0:T(8,128)(2,1)S(1)}, bf16[576,1152]{1,0:T(8,128)(2,1)}, u32[]{:S(2)}) copy-start(bf16[576,1152]{1,0:T(8,128)(2,1)} %refs_9_.3) | copy-start | bytes 3981316
  110.2 7.2 %collective-permute-start.28 = (bf16[64,576]{1,0:T(8,128)(2,1)S(1)}, bf16[64,576]{1,0:T(8,128)(2,1)S(1)}, u32[]{:S(2)}, u32[]{:S(2)}) collective-permute-start(bf16[64,576]{1,0:T(8,128)(2,1)S(1)} %get-tuple-element.78), channel_id=1, source_target_pairs={{0,24},{4,28},{8,16},{12,20},{16,8},{20,12},{24,0},{28,4},{1,25},{... | collective-permute-start | bytes 221192 | tf_op jit(solution)/shard_map/ppermute | solution.py:501
  110.3 8.0 %collective-permute-start.29 = (bf16[64,576]{1,0:T(8,128)(2,1)S(1)}, bf16[64,576]{1,0:T(8,128)(2,1)S(1)}, u32[]{:S(2)}, u32[]{:S(2)}) collective-permute-start(bf16[64,576]{1,0:T(8,128)(2,1)S(1)} %get-tuple-element.79), channel_id=1, source_target_pairs={{0,28},{4,24},{8,20},{12,16},{16,12},{20,8},{24,4},{28,0},{1,29},{... | collective-permute-start | bytes 221192 | tf_op jit(solution)/shard_map/ppermute | solution.py:501
  112.5 8.9 %collective-permute-start.9 = (bf16[64,576]{1,0:T(8,128)(2,1)S(1)}, bf16[64,576]{1,0:T(8,128)(2,1)S(1)}, u32[]{:S(2)}, u32[]{:S(2)}) collective-permute-start(bf16[64,576]{1,0:T(8,128)(2,1)S(1)} %get-tuple-element.56), channel_id=1, source_target_pairs={{0,4},{4,0},{8,12},{12,8},{16,20},{20,16},{24,28},{28,24},{1,5},{5... | collective-permute-start | bytes 221192 | tf_op jit(solution)/shard_map/ppermute | solution.py:501
  115.5 6.5 %collective-permute-start.10 = (bf16[64,576]{1,0:T(8,128)(2,1)S(1)}, bf16[64,576]{1,0:T(8,128)(2,1)S(1)}, u32[]{:S(2)}, u32[]{:S(2)}) collective-permute-start(bf16[64,576]{1,0:T(8,128)(2,1)S(1)} %get-tuple-element.57), channel_id=1, source_target_pairs={{0,8},{4,12},{8,0},{12,4},{16,24},{20,28},{24,16},{28,20},{1,9},{5... | collective-permute-start | bytes 221192 | tf_op jit(solution)/shard_map/ppermute | solution.py:501
  115.5 11.7 %collective-permute-start.11 = (bf16[64,576]{1,0:T(8,128)(2,1)S(1)}, bf16[64,576]{1,0:T(8,128)(2,1)S(1)}, u32[]{:S(2)}, u32[]{:S(2)}) collective-permute-start(bf16[64,576]{1,0:T(8,128)(2,1)S(1)} %get-tuple-element.58), channel_id=1, source_target_pairs={{0,12},{4,8},{8,4},{12,0},{16,28},{20,24},{24,20},{28,16},{1,13},{... | collective-permute-start | bytes 221192 | tf_op jit(solution)/shard_map/ppermute | solution.py:501
  117.4 12.5 %collective-permute-start.12 = (bf16[64,576]{1,0:T(8,128)(2,1)S(1)}, bf16[64,576]{1,0:T(8,128)(2,1)S(1)}, u32[]{:S(2)}, u32[]{:S(2)}) collective-permute-start(bf16[64,576]{1,0:T(8,128)(2,1)S(1)} %get-tuple-element.59), channel_id=1, source_target_pairs={{0,16},{4,20},{8,24},{12,28},{16,0},{20,4},{24,8},{28,12},{1,17},{... | collective-permute-start | bytes 221192 | tf_op jit(solution)/shard_map/ppermute | solution.py:501
  118.2 13.4 %collective-permute-start.13 = (bf16[64,576]{1,0:T(8,128)(2,1)S(1)}, bf16[64,576]{1,0:T(8,128)(2,1)S(1)}, u32[]{:S(2)}, u32[]{:S(2)}) collective-permute-start(bf16[64,576]{1,0:T(8,128)(2,1)S(1)} %get-tuple-element.60), channel_id=1, source_target_pairs={{0,20},{4,16},{8,28},{12,24},{16,4},{20,0},{24,12},{28,8},{1,21},{... | collective-permute-start | bytes 221192 | tf_op jit(solution)/shard_map/ppermute | solution.py:501
  121.4 10.3 %collective-permute-start.14 = (bf16[64,576]{1,0:T(8,128)(2,1)S(1)}, bf16[64,576]{1,0:T(8,128)(2,1)S(1)}, u32[]{:S(2)}, u32[]{:S(2)}) collective-permute-start(bf16[64,576]{1,0:T(8,128)(2,1)S(1)} %get-tuple-element.61), channel_id=1, source_target_pairs={{0,24},{4,28},{8,16},{12,20},{16,8},{20,12},{24,0},{28,4},{1,25},{... | collective-permute-start | bytes 221192 | tf_op jit(solution)/shard_map/ppermute | solution.py:501
  122.1 9.6 %collective-permute-start.15 = (bf16[64,576]{1,0:T(8,128)(2,1)S(1)}, bf16[64,576]{1,0:T(8,128)(2,1)S(1)}, u32[]{:S(2)}, u32[]{:S(2)}) collective-permute-start(bf16[64,576]{1,0:T(8,128)(2,1)S(1)} %get-tuple-element.62), channel_id=1, source_target_pairs={{0,28},{4,24},{8,20},{12,16},{16,12},{20,8},{24,4},{28,0},{1,29},{... | collective-permute-start | bytes 221192 | tf_op jit(solution)/shard_map/ppermute | solution.py:501
  (10 other events, 100.7 us)

commit v3 on v2

--- a/solution.py
+++ b/solution.py
@@ -56,16 +56,6 @@
     return jnp.broadcast_to(column, (column.shape[0], LANES)).T[:1]
 
 
-def normed_dot(x, mean, scale, w):
-    ones = jnp.ones((PACK, w.shape[1]), BF16)
-    return (nt_dot(x, w) - mean * nt_dot(ones, w)[:1]) * scale
-
-
-def normed_dot_t(x, mean_row, scale_row, w):
-    ones = jnp.ones((LANES, w.shape[1]), BF16)
-    return (nt_dot(w, x) - nt_dot(w, ones)[:, :1] * mean_row) * scale_row
-
-
 def tile_order(rows, columns):
     for col in range(columns // TW):
         for row in range(TH):
@@ -85,69 +75,134 @@
     return jnp.concatenate([first, second], axis=0)
 
 
-def project_kernel(slab, columns, x_ref, w_ref, q_ref, kv_ref, top_ref, bot_ref, xp_ref, mean_ref, rstd_ref):
+def split_queries_keys(prod):
+    keys = prod[:, INNER // LANES * LANES :]
+    shift = INNER % LANES
+    if shift:
+        keys = pltpu.roll(keys, keys.shape[1] - shift, 1)
+    return prod[:, :WIDE], keys
+
+
+def column_sums(w):
+    return nt_dot(jnp.ones((PACK, w.shape[1]), BF16), w)[:1]
+
+
+def store_values(v_ref, values, lanes):
+    for pair in range(PAIRS):
+        at = pair * PAIR_ROWS
+        v_ref[at : at + PAIR, lanes] = values[pair * PAIR : (pair + 1) * PAIR]
+        v_ref[at + PAIR : at + PAIR_ROWS, lanes] = jnp.ones((PACK, values.shape[1]), BF16)
+
+
+def packed_keys(slab):
+    per = slab // LANES
+    for piece in range(WIDE // LANES):
+        lanes = slice(piece * LANES, (piece + 1) * LANES)
+        if piece < WIDE // slab * per:
+            yield slice(0, slab), lanes, piece // per * slab, piece % per * LANES
+        else:
+            at = WIDE // slab * slab
+            for part in range(per):
+                rows = slab // per
+                yield slice(part * rows, (part + 1) * rows), lanes, at, part * LANES
+
+
+def pack_halo(halo_ref, k_ref, v_ref):
+    slab = k_ref.shape[0]
+    size = v_ref.shape[0]
+    halo_ref[:size, :] = v_ref[...]
+    for rows, lanes, row, lane in packed_keys(slab):
+        count = rows.stop - rows.start
+        halo_ref[size + row : size + row + count, lane : lane + LANES] = k_ref[rows, lanes]
+
+
+def unpack_halo(halo_ref, k_ref, v_ref):
+    slab = k_ref.shape[0]
+    size = v_ref.shape[0]
+    v_ref[...] = halo_ref[:size, :]
+    for rows, lanes, row, lane in packed_keys(slab):
+        count = rows.stop - rows.start
+        k_ref[rows, lanes] = halo_ref[size + row : size + row + count, lane : lane + LANES]
+
+
+def project_kernel(
+    columns, x_ref, w_hbm, q_ref, k_ref, v_ref, top_ref, bot_ref, w_ref, xp_ref, sum_ref, col_ref, sem
+):
     step = pl.program_id(0)
-    pixels = x_ref.shape[0]
+    slab = x_ref.shape[0]
+    first = pltpu.make_async_copy(
+        w_hbm.at[pl.ds(0, 2 * INNER)], w_ref.at[pl.ds(0, 2 * INNER)], sem.at[0]
+    )
+    second = pltpu.make_async_copy(
+        w_hbm.at[pl.ds(2 * INNER, INNER)], w_ref.at[pl.ds(2 * INNER, INNER)], sem.at[1]
+    )
 
     @pl.when(step == 0)
     def _():
-        for base in range(0, pixels, slab):
-            for to, at in tile_order(slab, columns):
-                xp_ref[pl.ds(base + to, TW), :] = x_ref[pl.ds(base + at, TW), :]
-        mean, rstd = moments(xp_ref[...])
-        mean_ref[...] = mean
-        rstd_ref[...] = rstd
-        q = normed_dot(xp_ref[...], mean, rstd * (LOG2E * HD**-0.5), w_ref[...])
-        q_ref[:, :INNER] = q.astype(BF16)
-        q_ref[:, INNER:] = jnp.zeros((pixels, WIDE - INNER), BF16)
-
-    @pl.when(step == 1)
+        first.start()
+        second.start()
+
+    for to, at in tile_order(slab, columns):
+        xp_ref[pl.ds(to, TW), :] = x_ref[pl.ds(at, TW), :]
+
+    @pl.when(step == 0)
     def _():
-        k = normed_dot(xp_ref[...], mean_ref[...], rstd_ref[...], w_ref[...])
-        kv_ref[:, :INNER] = k.astype(BF16)
-        kv_ref[:, INNER:WIDE] = jnp.zeros((pixels, WIDE - INNER), BF16)
-
-    @pl.when(step == 2)
+        first.wait()
+        second.wait()
+        sum_ref[...] = column_sums(w_ref[: 2 * INNER, :])
+        ones = jnp.ones((LANES, w_ref.shape[1]), BF16)
+        col_ref[...] = nt_dot(w_ref[2 * INNER :, :], ones)[:, :1]
+
+    x = xp_ref[...]
+    mean, rstd = moments(x)
+    prod = (nt_dot(x, w_ref[: 2 * INNER, :]) - mean * sum_ref[...]) * rstd
+    q, k = split_queries_keys(prod)
+    q_ref[...] = (q * (LOG2E * HD**-0.5)).astype(BF16)
+    k_ref[...] = k.astype(BF16)
+    values = nt_dot(w_ref[2 * INNER :, :], x) - col_ref[...] * as_rows(mean)
+    store_values(v_ref, (values * as_rows(rstd)).astype(BF16), slice(None))
+
+    @pl.when(step == 0)
     def _():
-        mean, rstd = as_rows(mean_ref[...]), as_rows(rstd_ref[...])
-        v = normed_dot_t(xp_ref[...], mean, rstd, w_ref[...]).astype(BF16)
-        for base in range(0, pixels, slab):
-            for part, row in enumerate(range(0, INNER, slab)):
-                rows = min(slab, INNER - row)
-                at = WIDE + part * slab
-                kv_ref[pl.ds(base, rows), at : at + slab] = v[row : row + rows, base : base + slab]
-                if rows < slab:
-                    kv_ref[pl.ds(base + rows, slab - rows), at : at + slab] = jnp.zeros(
-                        (slab - rows, slab), BF16
-                    )
-        top_ref[...] = kv_ref[:slab, :]
-        bot_ref[...] = kv_ref[pixels - slab :, :]
+        pack_halo(top_ref, k_ref, v_ref)
+
+    @pl.when(step == pl.num_programs(0) - 1)
+    def _():
+        pack_halo(bot_ref, k_ref, v_ref)
 
 
 def project(x, w, slab, columns):
     pixels, feat = x.shape
-    kv_dim = WIDE + -(-INNER // slab) * slab
-    whole = lambda *shape: pl.BlockSpec(shape, lambda i: (0, 0))
+    steps = pixels // slab
+    v_rows = PAIRS * PAIR_ROWS
+    halo_rows = v_rows + WIDE
     return pl.pallas_call(
-        functools.partial(project_kernel, slab, columns),
-        grid=(3,),
-        in_specs=[whole(pixels, feat), pl.BlockSpec((INNER, feat), lambda i: (i, 0))],
+        functools.partial(project_kernel, columns),
+        grid=(steps,),
+        in_specs=[
+            pl.BlockSpec((slab, feat), lambda i: (i, 0)),
+            pl.BlockSpec(memory_space=pl.ANY),
+        ],
         out_specs=[
-            whole(pixels, WIDE),
-            whole(pixels, kv_dim),
-            whole(slab, kv_dim),
-            whole(slab, kv_dim),
+            pl.BlockSpec((slab, WIDE), lambda i: (i, 0)),
+            pl.BlockSpec((slab, WIDE), lambda i: (i, 0)),
+            pl.BlockSpec((v_rows, slab), lambda i: (i, 0)),
+            pl.BlockSpec((halo_rows, slab), lambda i: (0, 0)),
+            pl.BlockSpec((halo_rows, slab), lambda i: (0, 0)),
         ],
         out_shape=[
             jax.ShapeDtypeStruct((pixels, WIDE), BF16),
-            jax.ShapeDtypeStruct((pixels, kv_dim), BF16),
-            jax.ShapeDtypeStruct((slab, kv_dim), BF16),
-            jax.ShapeDtypeStruct((slab, kv_dim), BF16),
+            jax.ShapeDtypeStruct((pixels, WIDE), BF16),
+            jax.ShapeDtypeStruct((steps * v_rows, slab), BF16),
+            jax.ShapeDtypeStruct((halo_rows, slab), BF16),
+            jax.ShapeDtypeStruct((halo_rows, slab), BF16),
         ],
         scratch_shapes=[
-            pltpu.VMEM((pixels, feat), BF16),
-            pltpu.VMEM((pixels, 1), F32),
-            pltpu.VMEM((pixels, 1), F32),
+            pltpu.VMEM(w.shape, BF16),
+            pltpu.VMEM((slab, feat), BF16),
+            pltpu.VMEM((1, 2 * INNER), F32),
+            pltpu.VMEM((INNER, 1), F32),
+            pltpu.SemaphoreType.DMA((2,)),
         ],
         compiler_params=params(),
         cost_estimate=cost(5 * 10**9, 12 * 2**20),
@@ -170,8 +225,9 @@
 
 def spatial_kernel(
     edges, first_row, group, peers, xor, split, tile_rows, columns,
-    targets_ref, counts_ref, x_ref, q_ref, prev_ref, mid_ref, next_ref, *rest,
+    targets_ref, counts_ref, x_ref, q_ref, *rest,
 ):
+    k_refs, v_refs, rest = rest[:3], rest[3:6], rest[6:]
     if edges:
         top_ref, bot_ref = rest[:2]
         rest = rest[2:]
@@ -179,8 +235,8 @@
     rest = rest[2:]
     if split:
         send_refs, rest = rest[:peers], rest[peers:]
-    p_ref, v_ref, acc_ref, out_ref = rest[:4]
-    rest = rest[4:]
+    p_ref, acc_ref, out_ref = rest[:3]
+    rest = rest[3:]
     step = pl.program_id(0)
     steps = pl.num_programs(0)
     slab, feat = x_ref.shape
@@ -190,43 +246,28 @@
     @pl.when(step == 0)
     def _():
         p_ref[...] = jnp.zeros(p_ref.shape, BF16)
-        for pair in range(PAIRS):
-            v_ref[:, pair * PAIR_ROWS + PAIR : (pair + 1) * PAIR_ROWS, :] = jnp.ones(
-                (3, PACK, slab), BF16
-            )
 
     if edges:
-        prev_s, next_s = rest
+        (k_prev, k_next, v_prev, v_next) = rest
 
         @pl.when(step == 0)
         def _():
-            prev_s[...] = top_ref[...]
-            next_s[...] = next_ref[...]
+            unpack_halo(top_ref, k_prev, v_prev)
+            k_next[...] = k_refs[2][...]
+            v_next[...] = v_refs[2][...]
 
         @pl.when(step != 0)
         def _():
-            prev_s[...] = prev_ref[...]
-            next_s[...] = bot_ref[...]
-
-        kv_refs = (prev_s, mid_ref, next_s)
+            k_prev[...] = k_refs[0][...]
+            v_prev[...] = v_refs[0][...]
+            unpack_halo(bot_ref, k_next, v_next)
+
+        k_refs = (k_prev, k_refs[1], k_next)
+        v_refs = (v_prev, v_refs[1], v_next)
         tile_row = step * (tile_rows - 1)
     else:
-        kv_refs = (prev_ref, mid_ref, next_ref)
         tile_row = step + first_row
     global_row = lax.axis_index("row") * tile_rows + tile_row
-
-    for j, ref in enumerate(kv_refs):
-        for pair in range(PAIRS):
-            done = 0
-            while done < PAIR:
-                row = pair * PAIR + done
-                part, inside = row // slab, row % slab
-                rows = min(PAIR - done, slab - inside)
-                at = WIDE + part * slab
-                v_ref[j, pl.ds(pair * PAIR_ROWS + done, rows), :] = ref[
-                    pl.ds(inside, rows), at : at + slab
-                ]
-                done += rows
 
     left = lax.broadcasted_iota(jnp.int32, (1, 4 * TILE), 1) % (2 * TILE) < TILE
     for duo in range(tile_cols // 2):
@@ -247,7 +288,7 @@
             lo, hi = pair_window(pair)
             queries = two_heads(q_ref[2 * duo * TILE : (2 * duo + 2) * TILE, lo:hi], pair)
             scores = {}
-            for j, ref in enumerate(kv_refs):
+            for j, ref in enumerate(k_refs):
                 part = nt_dot(ref[lowest * TILE : (highest + 1) * TILE, lo:hi], queries)
                 for col in span:
                     at = (col - lowest) * TILE
@@ -256,15 +297,18 @@
             top = jnp.max(top, axis=0, keepdims=True)
             for (j, col), score in scores.items():
                 at = j * slab + col * TILE
-                p_ref[duo, at : at + TILE, :] = jnp.exp2(score - top).astype(BF16)
+                p_ref[duo * PAIRS + pair, at : at + TILE, :] = jnp.exp2(score - top).astype(BF16)
+
+    for duo in range(tile_cols // 2):
+        for pair in range(PAIRS):
             out = sum(
                 nn_dot(
-                    v_ref[j, pair * PAIR_ROWS : (pair + 1) * PAIR_ROWS, :],
-                    p_ref[duo, j * slab : (j + 1) * slab, :],
+                    ref[pair * PAIR_ROWS : (pair + 1) * PAIR_ROWS, :],
+                    p_ref[duo * PAIRS + pair, j * slab : (j + 1) * slab, :],
                 )
-                for j in range(3)
+                for j, ref in enumerate(v_refs)
             )
-            out = out[:PAIR] / out[PAIR : PAIR + 1]
+            out = out[:PAIR] * (1.0 / out[PAIR : PAIR + 1])
             lanes = slice(2 * duo * TILE, (2 * duo + 2) * TILE)
             acc_ref[pair * PAIR : pair * PAIR + HD, lanes] = out[:HD, : 2 * TILE]
             acc_ref[pair * PAIR + HD : (pair + 1) * PAIR, lanes] = out[HD:, 2 * TILE :]
@@ -287,12 +331,12 @@
                 send_refs[j][...] = out_ref[pl.ds(pl.multiple_of(peer * group, PACK), group), :]
 
 
-def spatial(edges, split, x, q, kv, halos, w, targets, counts, slab, columns, peers, xor):
+def spatial(edges, split, x, q, k, v, halos, w, targets, counts, slab, columns, peers, xor):
     pixels, feat = x.shape
     tile_rows = pixels // slab
     steps = 2 if edges else tile_rows - 2
     group = steps * slab // peers
-    kv_dim = kv.shape[1]
+    v_rows = PAIRS * PAIR_ROWS
     if edges:
         at = lambda i: i * (tile_rows - 1)
         prev_at = lambda i: tile_rows - 2
@@ -308,21 +352,23 @@
         smem,
         pl.BlockSpec((slab, feat), lambda i: (at(i), 0)),
         pl.BlockSpec((slab, WIDE), lambda i: (at(i), 0)),
-        pl.BlockSpec((slab, kv_dim), lambda i: (prev_at(i), 0)),
-        pl.BlockSpec((slab, kv_dim), lambda i: (at(i), 0)),
-        pl.BlockSpec((slab, kv_dim), lambda i: (next_at(i), 0)),
     ]
-    args = [targets, counts, x, q, kv, kv, kv]
+    for block in ((slab, WIDE), (v_rows, slab)):
+        in_specs += [
+            pl.BlockSpec(block, lambda i: (prev_at(i), 0)),
+            pl.BlockSpec(block, lambda i: (at(i), 0)),
+            pl.BlockSpec(block, lambda i: (next_at(i), 0)),
+        ]
+    args = [targets, counts, x, q, k, k, k, v, v, v]
     scratch = [
-        pltpu.VMEM((columns // TW // 2, 3 * slab, 4 * TILE), BF16),
-        pltpu.VMEM((3, PAIRS * PAIR_ROWS, slab), BF16),
+        pltpu.VMEM((columns // TW // 2 * PAIRS, 3 * slab, 4 * TILE), BF16),
         pltpu.VMEM((INNER, slab), F32),
         pltpu.VMEM((steps * slab, feat), BF16),
     ]
     if edges:
-        in_specs += [whole(slab, kv_dim)] * 2
+        in_specs += [whole(*halos[0].shape)] * 2
         args += list(halos)
-        scratch += [pltpu.VMEM((slab, kv_dim), BF16)] * 2
+        scratch += [pltpu.VMEM((slab, WIDE), BF16)] * 2 + [pltpu.VMEM((v_rows, slab), BF16)] * 2
     in_specs.append(whole(*w.shape))
     args.append(w)
     out_specs = [pl.BlockSpec((slab, feat), lambda i: (i, 0))]
@@ -351,7 +397,7 @@
     in_refs, w_ref, refs = refs[:count], refs[count], refs[count + 1 :]
     count = peers if split_out else 1
     out_refs = refs[:count]
-    x_ref, q_ref, k_ref, v_ref, acc_ref = refs[count:]
+    x_ref, q_ref, k_ref, v_ref, p_ref, acc_ref = refs[count:]
     block = peers * PACK
     parts = group // PACK
     tokens = peers * group
@@ -364,16 +410,14 @@
                 x_ref[to, :] = in_refs[0][pl.ds(j * group + part * PACK, PACK), :]
     x = x_ref[...]
     mean, rstd = moments(x)
-    q = normed_dot(x, mean, rstd * (LOG2E * HD**-0.5), w_ref[:INNER, :])
-    q_ref[:, :INNER] = q.astype(BF16)
-    q_ref[:, INNER:] = jnp.zeros((tokens, WIDE - INNER), BF16)
-    k_ref[:, :INNER] = normed_dot(x, mean, rstd, w_ref[INNER : 2 * INNER, :]).astype(BF16)
-    k_ref[:, INNER:] = jnp.zeros((tokens, WIDE - INNER), BF16)
-    v = normed_dot_t(x, as_rows(mean), as_rows(rstd), w_ref[2 * INNER :, :]).astype(BF16)
-    for pair in range(PAIRS):
-        at = pair * PAIR_ROWS
-        v_ref[at : at + PAIR, :] = v[pair * PAIR : (pair + 1) * PAIR]
-        v_ref[at + PAIR : at + PAIR_ROWS, :] = jnp.ones((PACK, tokens), BF16)
+    prod = (nt_dot(x, w_ref[: 2 * INNER, :]) - mean * column_sums(w_ref[: 2 * INNER, :])) * rstd
+    q, k = split_queries_keys(prod)
+    q_ref[...] = (q * (LOG2E * HD**-0.5)).astype(BF16)
+    k_ref[...] = k.astype(BF16)
+    w_values = w_ref[2 * INNER :, :]
+    col = nt_dot(w_values, jnp.ones((LANES, w_values.shape[1]), BF16))[:, :1]
+    values = (nt_dot(w_values, x) - col * as_rows(mean)) * as_rows(rstd)
+    store_values(v_ref, values.astype(BF16), slice(None))
     row = lax.broadcasted_iota(jnp.int32, (block, 2 * block), 0)
     col = lax.broadcasted_iota(jnp.int32, (block, 2 * block), 1)
     bias = jnp.where(row % PACK == col % PACK, 0.0, NEG).astype(F32)
@@ -383,11 +427,18 @@
             lo, hi = pair_window(pair)
             queries = two_heads(q_ref[at : at + block, lo:hi], pair)
             scores = nt_dot(k_ref[at : at + block, lo:hi], queries) + bias
-            expo = jnp.exp2(scores - jnp.max(scores, axis=0, keepdims=True)).astype(BF16)
-            out = nn_dot(v_ref[pair * PAIR_ROWS : (pair + 1) * PAIR_ROWS, at : at + block], expo)
-            out = out[:PAIR] / out[PAIR : PAIR + 1]
+            expo = jnp.exp2(scores - jnp.max(scores, axis=0, keepdims=True))
+            p_ref[part * PAIRS + pair] = expo.astype(BF16)
+    for part in range(parts):
+        at = part * block
+        for pair in range(PAIRS):
+            weights = v_ref[pair * PAIR_ROWS : (pair + 1) * PAIR_ROWS, at : at + block]
+            out = nn_dot(weights, p_ref[part * PAIRS + pair])
+            out = out[:PAIR] * (1.0 / out[PAIR : PAIR + 1])
             acc_ref[pair * PAIR : pair * PAIR + HD, at : at + block] = out[:HD, :block]
             acc_ref[pair * PAIR + HD : (pair + 1) * PAIR, at : at + block] = out[HD:, block:]
+    for part in range(parts):
+        at = part * block
         heads = acc_ref[:, at : at + block].T.astype(BF16)
         for j in range(peers):
             rows = heads[j * PACK : (j + 1) * PACK]
@@ -414,6 +465,7 @@
             pltpu.VMEM((tokens, WIDE), BF16),
             pltpu.VMEM((tokens, WIDE), BF16),
             pltpu.VMEM((PAIRS * PAIR_ROWS, tokens), BF16),
+            pltpu.VMEM((group // PACK * PAIRS, peers * PACK, 2 * peers * PACK), BF16),
             pltpu.VMEM((INNER, tokens), F32),
         ],
         compiler_params=params(),
@@ -479,11 +531,11 @@
     )(*args)
 
 
-def neighbours(kv_top, kv_bot):
+def neighbours(top, bot):
     size = lax.axis_size("row")
     up = [(i, i + 1) for i in range(size - 1)]
     down = [(j, i) for i, j in up]
-    return lax.ppermute(kv_bot, "row", up), lax.ppermute(kv_top, "row", down)
+    return lax.ppermute(bot, "row", up), lax.ppermute(top, "row", down)
 
 
 def exchange(pieces, xor, back):
@@ -509,12 +561,12 @@
     peers = lax.axis_size("frame")
     xor = peers & (peers - 1) == 0
     x = frames_in.reshape(pixels, feat)
-    q, kv, kv_top, kv_bot = project(x, spatial_qkv.T, slab, columns)
-    halos = neighbours(kv_top, kv_bot)
+    q, k, v, top, bot = project(x, spatial_qkv.T, slab, columns)
+    halos = neighbours(top, bot)
     tiles = (spatial_out, key_tiles, tile_counts, slab, columns, peers, xor)
-    mixed_a, send_a = spatial(False, SPLIT[0], x, q, kv, None, *tiles)
+    mixed_a, send_a = spatial(False, SPLIT[0], x, q, k, v, None, *tiles)
     got_a = exchange(send_a, xor, False)
-    mixed_b, send_b = spatial(True, SPLIT[1], x, q, kv, halos, *tiles)
+    mixed_b, send_b = spatial(True, SPLIT[1], x, q, k, v, halos, *tiles)
     got_b = exchange(send_b, xor, False)
     ret_a = exchange(temporal(got_a, temporal_qkv.T, peers, SPLIT[2]), xor, True)
     ret_b = exchange(temporal(got_b, temporal_qkv.T, peers, SPLIT[3]), xor, True)

time: 135 us -> 125 us (0.926)
  Pallas kernels: 56.7 us -> 40.6 us
  waiting for transfers between devices: 7.34 us -> 13.5 us
    pallas_call x2, Pallas kernels: 17.5 us -> 9.84 us  [temporal(): pl.pallas_call(functools.partial(temporal_kernel, peers, group, split_in,...]
    pallas_call x2, Pallas kernels: 22.3 us -> 15.5 us  [spatial(): pl.pallas_call(functools.partial(spatial_kernel, edges, 0 if edges else 1...]
    ppermute x28, waiting for transfers between devices: 7.34 us -> 13.5 us  [exchange(): result.append(lax.ppermute(pieces[j], 'frame', pairs))]
    pallas_call x1, Pallas kernels: 12.5 us -> 10.8 us  [project(): pl.pallas_call(functools.partial(project_kernel, columns), grid=(steps,),...]
    unnamed x25 -> x21, local copies, waits for them, and re-layouts: 6.92 us -> 8.07 us
  transfers between devices with their start and end apart: 30 -> 30, of which waited for: 6 -> 5; matrix products, arithmetic and copies ran while one was open for 0% -> 0% of each run, Pallas kernels for 31% -> 22%
where the time goes in v3:
time: 125 us; the launch traced here: 124 us
  starting transfers between devices  61.5 us (49%)
  Pallas kernels  40.6 us (32%)
  waiting for transfers between devices  13.5 us (11%)
  local copies, waits for them, and re-layouts  8.07 us (6%)
    ppermute x28, starting transfers between devices, exchange(): result.append(lax.ppermute(pieces[j], 'frame', pairs))  57.8 us
    pallas_call x2, Pallas kernels, spatial(): pl.pallas_call(functools.partial(spatial_kernel, edges, 0 if edges else 1...  15.5 us
    ppermute x28, waiting for transfers between devices, exchange(): result.append(lax.ppermute(pieces[j], 'frame', pairs))  13.5 us
    pallas_call x1, Pallas kernels, project(): pl.pallas_call(functools.partial(project_kernel, columns), grid=(steps,),...  10.8 us
    pallas_call x2, Pallas kernels, temporal(): pl.pallas_call(functools.partial(temporal_kernel, peers, group, split_in,...  9.84 us
    unnamed x21, local copies, waits for them, and re-layouts  8.07 us
    pallas_call x2, Pallas kernels, final(): pl.pallas_call(functools.partial(final_kernel, peers, group, xor, split,...  4.45 us
    ppermute x2, starting transfers between devices, neighbours(): return (lax.ppermute(bot, 'row', up), lax.ppermute(top, 'row', down))  3.67 us
  transfers between devices with their start and end apart: 30, of which 5 were waited for; matrix products, arithmetic and copies ran while one was open for 0% of the time, Pallas kernels for 22%

profile of v3, /device:TPU:0, one launch (start us, length us, event | category | flops | bytes accessed | tf_op | source)
XLA Modules:
  0.0 123.8 jit_solution(2790057447501903109)
XLA Ops:
  0.0 10.8 %project.1 = (bf16[1024,640]{1,0:T(8,128)(2,1)S(1)}, bf16[1024,640]{1,0:T(8,128)(2,1)S(1)}, bf16[2560,256]{1,0:T(8,128)(2,1)S(1)}, bf16[1280,256]{1,0:T(8,128)(2,1)S(1)}, bf16[1280,256]{1,0:T(8,128)(2,1)S(1)}) custom-call(bf16[1024,1152]{1,0:T(8,128)(2,1)} %bitcast.7, bf16[1728,1152]{1,0:T(8,128)(2,1)} %bitcast.6), custom_call_target="tpu_custom_call" | custom-call | flops 5000000000 | bytes 12582912 | tf_op jit(solution)/shard_map/project/pallas_call | solution.py:179
  14.0 2.4 %collective-permute-start = (bf16[1280,256]{1,0:T(8,128)(2,1)S(1)}, bf16[1280,256]{1,0:T(8,128)(2,1)S(1)}, u32[]{:S(2)}, u32[]{:S(2)}) collective-permute-start(bf16[1280,256]{1,0:T(8,128)(2,1)S(1)} %get-tuple-element.47), channel_id=1, source_target_pairs={{0,1},{1,2},{2,3},{4,5},{5,6},{6,7},{8,9},{9,10},{10,11},{12,13},{... | collective-permute-start | bytes 1966088 | tf_op jit(solution)/shard_map/ppermute | solution.py:538
  16.4 1.3 %collective-permute-start.1 = (bf16[1280,256]{1,0:T(8,128)(2,1)S(1)}, bf16[1280,256]{1,0:T(8,128)(2,1)S(1)}, u32[]{:S(2)}, u32[]{:S(2)}) collective-permute-start(bf16[1280,256]{1,0:T(8,128)(2,1)S(1)} %get-tuple-element.48), channel_id=1, source_target_pairs={{1,0},{2,1},{3,2},{5,4},{6,5},{7,6},{9,8},{10,9},{11,10},{13,12},{... | collective-permute-start | bytes 1966088 | tf_op jit(solution)/shard_map/ppermute | solution.py:538
  17.8 1.3 %copy-done.5 = bf16[1024,640]{1,0:T(8,128)(2,1)S(1)} copy-done((bf16[1024,640]{1,0:T(8,128)(2,1)S(1)}, bf16[1024,640]{1,0:T(8,128)(2,1)}, u32[]{:S(2)}) %copy-start.5) | copy-done | bytes 1310744
  19.1 1.3 %copy-done.7 = bf16[1024,640]{1,0:T(8,128)(2,1)S(1)} copy-done((bf16[1024,640]{1,0:T(8,128)(2,1)S(1)}, bf16[1024,640]{1,0:T(8,128)(2,1)}, u32[]{:S(2)}) %copy-start.7) | copy-done | bytes 1310744
  20.5 7.5 %spatial_inner.1 = (bf16[512,1152]{1,0:T(8,128)(2,1)S(1)}, bf16[64,1152]{1,0:T(8,128)(2,1)S(1)}, bf16[64,1152]{1,0:T(8,128)(2,1)S(1)}, bf16[64,1152]{1,0:T(8,128...) custom-call(s32[1,16,9]{2,1,0:T(8,128)S(1)} %copy.9.targets_ref, ...), custom_call_target="tpu_custom_call" | custom-call | flops 6000000000 | bytes 8388608 | tf_op jit(solution)/shard_map/spatial_inner/pallas_call | solution.py:379
  28.0 2.4 %collective-permute-start.16 = (bf16[64,1152]{1,0:T(8,128)(2,1)S(1)}, bf16[64,1152]{1,0:T(8,128)(2,1)S(1)}, u32[]{:S(2)}, u32[]{:S(2)}) collective-permute-start(bf16[64,1152]{1,0:T(8,128)(2,1)S(1)} %get-tuple-element.67), channel_id=1, source_target_pairs={{0,4},{4,0},{8,12},{12,8},{16,20},{20,16},{24,28},{28,24},{1,5},{5... | collective-permute-start | bytes 442376 | tf_op jit(solution)/shard_map/ppermute | solution.py:553
  30.4 1.6 %collective-permute-start.17 = (bf16[64,1152]{1,0:T(8,128)(2,1)S(1)}, bf16[64,1152]{1,0:T(8,128)(2,1)S(1)}, u32[]{:S(2)}, u32[]{:S(2)}) collective-permute-start(bf16[64,1152]{1,0:T(8,128)(2,1)S(1)} %get-tuple-element.68), channel_id=1, source_target_pairs={{0,8},{4,12},{8,0},{12,4},{16,24},{20,28},{24,16},{28,20},{1,9},{5... | collective-permute-start | bytes 442376 | tf_op jit(solution)/shard_map/ppermute | solution.py:553
  32.0 3.0 %collective-permute-start.19 = (bf16[64,1152]{1,0:T(8,128)(2,1)S(1)}, bf16[64,1152]{1,0:T(8,128)(2,1)S(1)}, u32[]{:S(2)}, u32[]{:S(2)}) collective-permute-start(bf16[64,1152]{1,0:T(8,128)(2,1)S(1)} %get-tuple-element.70), channel_id=1, source_target_pairs={{0,16},{4,20},{8,24},{12,28},{16,0},{20,4},{24,8},{28,12},{1,17},{... | collective-permute-start | bytes 442376 | tf_op jit(solution)/shard_map/ppermute | solution.py:553
  36.2 8.0 %spatial_edges.1 = (bf16[512,1152]{1,0:T(8,128)(2,1)S(1)}, bf16[64,1152]{1,0:T(8,128)(2,1)S(1)}, bf16[64,1152]{1,0:T(8,128)(2,1)S(1)}, bf16[64,1152]{1,0:T(8,128...) custom-call(s32[1,16,9]{2,1,0:T(8,128)S(1)} %copy.9.targets_ref, ...), custom_call_target="tpu_custom_call" | custom-call | flops 6000000000 | bytes 8388608 | tf_op jit(solution)/shard_map/spatial_edges/pallas_call | solution.py:379
  44.3 3.7 %collective-permute-start.21 = (bf16[64,1152]{1,0:T(8,128)(2,1)S(1)}, bf16[64,1152]{1,0:T(8,128)(2,1)S(1)}, u32[]{:S(2)}, u32[]{:S(2)}) collective-permute-start(bf16[64,1152]{1,0:T(8,128)(2,1)S(1)} %get-tuple-element.72), channel_id=1, source_target_pairs={{0,24},{4,28},{8,16},{12,20},{16,8},{20,12},{24,0},{28,4},{1,25},{... | collective-permute-start | bytes 442376 | tf_op jit(solution)/shard_map/ppermute | solution.py:553
  48.0 1.6 %collective-permute-start.2 = (bf16[64,1152]{1,0:T(8,128)(2,1)S(1)}, bf16[64,1152]{1,0:T(8,128)(2,1)S(1)}, u32[]{:S(2)}, u32[]{:S(2)}) collective-permute-start(bf16[64,1152]{1,0:T(8,128)(2,1)S(1)} %get-tuple-element.50), channel_id=1, source_target_pairs={{0,4},{4,0},{8,12},{12,8},{16,20},{20,16},{24,28},{28,24},{1,5},{5... | collective-permute-start | bytes 442376 | tf_op jit(solution)/shard_map/ppermute | solution.py:553
  49.6 3.6 %collective-permute-done.20.refs_5_ = bf16[64,1152]{1,0:T(8,128)(2,1)S(1)} collective-permute-done((bf16[64,1152]{1,0:T(8,128)(2,1)S(1)}, bf16[64,1152]{1,0:T(8,128)(2,1)S(1)}, u32[]{:S(2)}, u32[]{:S(2)}) %collective-permute-start.20) | collective-permute-done | bytes 147488 | tf_op jit(solution)/shard_map/ppermute | solution.py:553
  53.2 8.0 %collective-permute-start.5 = (bf16[64,1152]{1,0:T(8,128)(2,1)S(1)}, bf16[64,1152]{1,0:T(8,128)(2,1)S(1)}, u32[]{:S(2)}, u32[]{:S(2)}) collective-permute-start(bf16[64,1152]{1,0:T(8,128)(2,1)S(1)} %get-tuple-element.53), channel_id=1, source_target_pairs={{0,16},{4,20},{8,24},{12,28},{16,0},{20,4},{24,8},{28,12},{1,17},{... | collective-permute-start | bytes 442376 | tf_op jit(solution)/shard_map/ppermute | solution.py:553
  61.2 6.2 %collective-permute-start.6 = (bf16[64,1152]{1,0:T(8,128)(2,1)S(1)}, bf16[64,1152]{1,0:T(8,128)(2,1)S(1)}, u32[]{:S(2)}, u32[]{:S(2)}) collective-permute-start(bf16[64,1152]{1,0:T(8,128)(2,1)S(1)} %get-tuple-element.54), channel_id=1, source_target_pairs={{0,20},{4,16},{8,28},{12,24},{16,4},{20,0},{24,12},{28,8},{1,21},{... | collective-permute-start | bytes 442376 | tf_op jit(solution)/shard_map/ppermute | solution.py:553
  67.7 3.7 %collective-permute-start.8 = (bf16[64,1152]{1,0:T(8,128)(2,1)S(1)}, bf16[64,1152]{1,0:T(8,128)(2,1)S(1)}, u32[]{:S(2)}, u32[]{:S(2)}) collective-permute-start(bf16[64,1152]{1,0:T(8,128)(2,1)S(1)} %get-tuple-element.56), channel_id=1, source_target_pairs={{0,28},{4,24},{8,20},{12,16},{16,12},{20,8},{24,4},{28,0},{1,29},{... | collective-permute-start | bytes 442376 | tf_op jit(solution)/shard_map/ppermute | solution.py:553
  71.4 2.1 %copy-done.1 = bf16[1152,1728]{0,1:T(8,128)(2,1)S(1)} copy-done((bf16[1152,1728]{0,1:T(8,128)(2,1)S(1)}, bf16[1152,1728]{0,1:T(8,128)(2,1)}, u32[]{:S(2)}) %copy-start.1) | copy-done | bytes 3981336
  73.5 4.9 %temporal.3 = (bf16[64,576]{1,0:T(8,128)(2,1)S(1)}, bf16[64,576]{1,0:T(8,128)(2,1)S(1)}, bf16[64,576]{1,0:T(8,128)(2,1)S(1)}, bf16[64,576]{1,0:T(8,128)(2,1)S(1)...) custom-call(bf16[64,1152]{1,0:T(8,128)(2,1)S(1)} %get-tuple-element., ...), custom_call_target="tpu_custom_call" | custom-call | flops 4000000000 | bytes 6291456 | tf_op jit(solution)/shard_map/temporal/pallas_call | solution.py:460
  78.5 1.4 %collective-permute-start.23 = (bf16[64,576]{1,0:T(8,128)(2,1)S(1)}, bf16[64,576]{1,0:T(8,128)(2,1)S(1)}, u32[]{:S(2)}, u32[]{:S(2)}) collective-permute-start(bf16[64,576]{1,0:T(8,128)(2,1)S(1)} %get-tuple-element.75), channel_id=1, source_target_pairs={{0,4},{4,0},{8,12},{12,8},{16,20},{20,16},{24,28},{28,24},{1,5},{5... | collective-permute-start | bytes 221192 | tf_op jit(solution)/shard_map/ppermute | solution.py:553
  79.9 3.0 %collective-permute-done.6.refs_5_ = bf16[64,1152]{1,0:T(8,128)(2,1)S(1)} collective-permute-done((bf16[64,1152]{1,0:T(8,128)(2,1)S(1)}, bf16[64,1152]{1,0:T(8,128)(2,1)S(1)}, u32[]{:S(2)}, u32[]{:S(2)}) %collective-permute-start.6) | collective-permute-done | bytes 147488 | tf_op jit(solution)/shard_map/ppermute | solution.py:553
  83.7 4.0 %collective-permute-start.26 = (bf16[64,576]{1,0:T(8,128)(2,1)S(1)}, bf16[64,576]{1,0:T(8,128)(2,1)S(1)}, u32[]{:S(2)}, u32[]{:S(2)}) collective-permute-start(bf16[64,576]{1,0:T(8,128)(2,1)S(1)} %get-tuple-element.78), channel_id=1, source_target_pairs={{0,16},{4,20},{8,24},{12,28},{16,0},{20,4},{24,8},{28,12},{1,17},{... | collective-permute-start | bytes 221192 | tf_op jit(solution)/shard_map/ppermute | solution.py:553
  87.7 5.8 %collective-permute-start.27 = (bf16[64,576]{1,0:T(8,128)(2,1)S(1)}, bf16[64,576]{1,0:T(8,128)(2,1)S(1)}, u32[]{:S(2)}, u32[]{:S(2)}) collective-permute-start(bf16[64,576]{1,0:T(8,128)(2,1)S(1)} %get-tuple-element.79), channel_id=1, source_target_pairs={{0,20},{4,16},{8,28},{12,24},{16,4},{20,0},{24,12},{28,8},{1,21},{... | collective-permute-start | bytes 221192 | tf_op jit(solution)/shard_map/ppermute | solution.py:553
  93.5 4.9 %temporal.2 = (bf16[64,576]{1,0:T(8,128)(2,1)S(1)}, bf16[64,576]{1,0:T(8,128)(2,1)S(1)}, bf16[64,576]{1,0:T(8,128)(2,1)S(1)}, bf16[64,576]{1,0:T(8,128)(2,1)S(1)...) custom-call(bf16[64,1152]{1,0:T(8,128)(2,1)S(1)} %get-tuple-element., ...), custom_call_target="tpu_custom_call" | custom-call | flops 4000000000 | bytes 6291456 | tf_op jit(solution)/shard_map/temporal/pallas_call | solution.py:460
  99.4 3.3 %collective-permute-start.29 = (bf16[64,576]{1,0:T(8,128)(2,1)S(1)}, bf16[64,576]{1,0:T(8,128)(2,1)S(1)}, u32[]{:S(2)}, u32[]{:S(2)}) collective-permute-start(bf16[64,576]{1,0:T(8,128)(2,1)S(1)} %get-tuple-element.81), channel_id=1, source_target_pairs={{0,28},{4,24},{8,20},{12,16},{16,12},{20,8},{24,4},{28,0},{1,29},{... | collective-permute-start | bytes 221192 | tf_op jit(solution)/shard_map/ppermute | solution.py:553
  103.8 2.4 %collective-permute-start.11 = (bf16[64,576]{1,0:T(8,128)(2,1)S(1)}, bf16[64,576]{1,0:T(8,128)(2,1)S(1)}, u32[]{:S(2)}, u32[]{:S(2)}) collective-permute-start(bf16[64,576]{1,0:T(8,128)(2,1)S(1)} %get-tuple-element.60), channel_id=1, source_target_pairs={{0,12},{4,8},{8,4},{12,0},{16,28},{20,24},{24,20},{28,16},{1,13},{... | collective-permute-start | bytes 221192 | tf_op jit(solution)/shard_map/ppermute | solution.py:553
  106.2 1.3 %collective-permute-done.29.refs_7_ = bf16[64,576]{1,0:T(8,128)(2,1)S(1)} collective-permute-done((bf16[64,576]{1,0:T(8,128)(2,1)S(1)}, bf16[64,576]{1,0:T(8,128)(2,1)S(1)}, u32[]{:S(2)}, u32[]{:S(2)}) %collective-permute-start.29) | collective-permute-done | bytes 73760 | tf_op jit(solution)/shard_map/ppermute | solution.py:553
  107.5 2.1 %collective-permute-start.13 = (bf16[64,576]{1,0:T(8,128)(2,1)S(1)}, bf16[64,576]{1,0:T(8,128)(2,1)S(1)}, u32[]{:S(2)}, u32[]{:S(2)}) collective-permute-start(bf16[64,576]{1,0:T(8,128)(2,1)S(1)} %get-tuple-element.62), channel_id=1, source_target_pairs={{0,20},{4,16},{8,28},{12,24},{16,4},{20,0},{24,12},{28,8},{1,21},{... | collective-permute-start | bytes 221192 | tf_op jit(solution)/shard_map/ppermute | solution.py:553
  110.6 3.3 %collective-permute-start.15 = (bf16[64,576]{1,0:T(8,128)(2,1)S(1)}, bf16[64,576]{1,0:T(8,128)(2,1)S(1)}, u32[]{:S(2)}, u32[]{:S(2)}) collective-permute-start(bf16[64,576]{1,0:T(8,128)(2,1)S(1)} %get-tuple-element.64), channel_id=1, source_target_pairs={{0,28},{4,24},{8,20},{12,16},{16,12},{20,8},{24,4},{28,0},{1,29},{... | collective-permute-start | bytes 221192 | tf_op jit(solution)/shard_map/ppermute | solution.py:553
  113.9 2.2 %final.2.refs_10_ = bf16[1024,1152]{1,0:T(8,128)(2,1)} custom-call(bf16[64,576]{1,0:T(8,128)(2,1)S(1)} %get-tuple-element.74.refs_0_, bf16[64,576]{1,0:T(8,128)(2,1)S(1)} %collective-permute-done.23.refs_1_, bf16[64,576]{1,0:T(8,128)(2,1)S(1)} %collective-permute-done.24.refs_2_, bf16[64,576]{1,0:T(8,128)(2,1)S(1)} %collective-permute-done.25.refs_3_, ...), custom_call_target="tpu_custom_call" | custom-call | flops 1000000000 | bytes 4194304 | tf_op jit(solution)/shard_map/final/pallas_call | solution.py:520
  116.1 3.1 %collective-permute-done.12.refs_4_ = bf16[64,576]{1,0:T(8,128)(2,1)S(1)} collective-permute-done((bf16[64,576]{1,0:T(8,128)(2,1)S(1)}, bf16[64,576]{1,0:T(8,128)(2,1)S(1)}, u32[]{:S(2)}, u32[]{:S(2)}) %collective-permute-start.12) | collective-permute-done | bytes 73760 | tf_op jit(solution)/shard_map/ppermute | solution.py:553
  119.2 2.4 %collective-permute-done.13.refs_5_ = bf16[64,576]{1,0:T(8,128)(2,1)S(1)} collective-permute-done((bf16[64,576]{1,0:T(8,128)(2,1)S(1)}, bf16[64,576]{1,0:T(8,128)(2,1)S(1)}, u32[]{:S(2)}, u32[]{:S(2)}) %collective-permute-start.13) | collective-permute-done | bytes 73760 | tf_op jit(solution)/shard_map/ppermute | solution.py:553
  121.6 2.2 %final.3 = bf16[1024,1152]{1,0:T(8,128)(2,1)} custom-call(bf16[64,576]{1,0:T(8,128)(2,1)S(1)} %get-tuple-element.57.refs_0_, bf16[64,576]{1,0:T(8,128)(2,1)S(1)} %collective-permute-done.9.refs_1_, bf16[64,576]{1,0:T(8,128)(2,1)S(1)} %collective-permute-done.10.refs_2_, ...), custom_call_target="tpu_custom_call", output_to_operand_aliasing={{}: (10, {})} | custom-call | flops 1000000000 | bytes 4194304 | tf_op jit(solution)/shard_map/final/pallas_call | solution.py:520
  (56 shorter events, 8.7 us)
Async XLA Ops:
  14.0 17.9 %collective-permute-start = (bf16[1280,256]{1,0:T(8,128)(2,1)S(1)}, bf16[1280,256]{1,0:T(8,128)(2,1)S(1)}, u32[]{:S(2)}, u32[]{:S(2)}) collective-permute-start(bf16[1280,256]{1,0:T(8,128)(2,1)S(1)} %get-tuple-element.47), channel_id=1, source_target_pairs={{0,1},{1,2},{2,3},{4,5},{5,6},{6,7},{8,9},{9,10},{10,11},{12,13},{... | collective-permute-start | bytes 1966088 | tf_op jit(solution)/shard_map/ppermute | solution.py:538
  16.4 18.5 %collective-permute-start.1 = (bf16[1280,256]{1,0:T(8,128)(2,1)S(1)}, bf16[1280,256]{1,0:T(8,128)(2,1)S(1)}, u32[]{:S(2)}, u32[]{:S(2)}) collective-permute-start(bf16[1280,256]{1,0:T(8,128)(2,1)S(1)} %get-tuple-element.48), channel_id=1, source_target_pairs={{1,0},{2,1},{3,2},{5,4},{6,5},{7,6},{9,8},{10,9},{11,10},{13,12},{... | collective-permute-start | bytes 1966088 | tf_op jit(solution)/shard_map/ppermute | solution.py:538
  28.0 16.3 %collective-permute-start.16 = (bf16[64,1152]{1,0:T(8,128)(2,1)S(1)}, bf16[64,1152]{1,0:T(8,128)(2,1)S(1)}, u32[]{:S(2)}, u32[]{:S(2)}) collective-permute-start(bf16[64,1152]{1,0:T(8,128)(2,1)S(1)} %get-tuple-element.67), channel_id=1, source_target_pairs={{0,4},{4,0},{8,12},{12,8},{16,20},{20,16},{24,28},{28,24},{1,5},{5... | collective-permute-start | bytes 442376 | tf_op jit(solution)/shard_map/ppermute | solution.py:553
  30.4 17.6 %collective-permute-start.17 = (bf16[64,1152]{1,0:T(8,128)(2,1)S(1)}, bf16[64,1152]{1,0:T(8,128)(2,1)S(1)}, u32[]{:S(2)}, u32[]{:S(2)}) collective-permute-start(bf16[64,1152]{1,0:T(8,128)(2,1)S(1)} %get-tuple-element.68), channel_id=1, source_target_pairs={{0,8},{4,12},{8,0},{12,4},{16,24},{20,28},{24,16},{28,20},{1,9},{5... | collective-permute-start | bytes 442376 | tf_op jit(solution)/shard_map/ppermute | solution.py:553
  32.0 16.0 %collective-permute-start.18 = (bf16[64,1152]{1,0:T(8,128)(2,1)S(1)}, bf16[64,1152]{1,0:T(8,128)(2,1)S(1)}, u32[]{:S(2)}, u32[]{:S(2)}) collective-permute-start(bf16[64,1152]{1,0:T(8,128)(2,1)S(1)} %get-tuple-element.69), channel_id=1, source_target_pairs={{0,12},{4,8},{8,4},{12,0},{16,28},{20,24},{24,20},{28,16},{1,13},{... | collective-permute-start | bytes 442376 | tf_op jit(solution)/shard_map/ppermute | solution.py:553
  32.0 17.7 %collective-permute-start.19 = (bf16[64,1152]{1,0:T(8,128)(2,1)S(1)}, bf16[64,1152]{1,0:T(8,128)(2,1)S(1)}, u32[]{:S(2)}, u32[]{:S(2)}) collective-permute-start(bf16[64,1152]{1,0:T(8,128)(2,1)S(1)} %get-tuple-element.70), channel_id=1, source_target_pairs={{0,16},{4,20},{8,24},{12,28},{16,0},{20,4},{24,8},{28,12},{1,17},{... | collective-permute-start | bytes 442376 | tf_op jit(solution)/shard_map/ppermute | solution.py:553
  35.0 18.3 %collective-permute-start.20 = (bf16[64,1152]{1,0:T(8,128)(2,1)S(1)}, bf16[64,1152]{1,0:T(8,128)(2,1)S(1)}, u32[]{:S(2)}, u32[]{:S(2)}) collective-permute-start(bf16[64,1152]{1,0:T(8,128)(2,1)S(1)} %get-tuple-element.71), channel_id=1, source_target_pairs={{0,20},{4,16},{8,28},{12,24},{16,4},{20,0},{24,12},{28,8},{1,21},{... | collective-permute-start | bytes 442376 | tf_op jit(solution)/shard_map/ppermute | solution.py:553
  44.3 9.0 %collective-permute-start.21 = (bf16[64,1152]{1,0:T(8,128)(2,1)S(1)}, bf16[64,1152]{1,0:T(8,128)(2,1)S(1)}, u32[]{:S(2)}, u32[]{:S(2)}) collective-permute-start(bf16[64,1152]{1,0:T(8,128)(2,1)S(1)} %get-tuple-element.72), channel_id=1, source_target_pairs={{0,24},{4,28},{8,16},{12,20},{16,8},{20,12},{24,0},{28,4},{1,25},{... | collective-permute-start | bytes 442376 | tf_op jit(solution)/shard_map/ppermute | solution.py:553
  48.0 13.3 %collective-permute-start.22 = (bf16[64,1152]{1,0:T(8,128)(2,1)S(1)}, bf16[64,1152]{1,0:T(8,128)(2,1)S(1)}, u32[]{:S(2)}, u32[]{:S(2)}) collective-permute-start(bf16[64,1152]{1,0:T(8,128)(2,1)S(1)} %get-tuple-element.73), channel_id=1, source_target_pairs={{0,28},{4,24},{8,20},{12,16},{16,12},{20,8},{24,4},{28,0},{1,29},{... | collective-permute-start | bytes 442376 | tf_op jit(solution)/shard_map/ppermute | solution.py:553
  48.0 19.5 %collective-permute-start.2 = (bf16[64,1152]{1,0:T(8,128)(2,1)S(1)}, bf16[64,1152]{1,0:T(8,128)(2,1)S(1)}, u32[]{:S(2)}, u32[]{:S(2)}) collective-permute-start(bf16[64,1152]{1,0:T(8,128)(2,1)S(1)} %get-tuple-element.50), channel_id=1, source_target_pairs={{0,4},{4,0},{8,12},{12,8},{16,20},{20,16},{24,28},{28,24},{1,5},{5... | collective-permute-start | bytes 442376 | tf_op jit(solution)/shard_map/ppermute | solution.py:553
  49.6 18.1 %collective-permute-start.3 = (bf16[64,1152]{1,0:T(8,128)(2,1)S(1)}, bf16[64,1152]{1,0:T(8,128)(2,1)S(1)}, u32[]{:S(2)}, u32[]{:S(2)}) collective-permute-start(bf16[64,1152]{1,0:T(8,128)(2,1)S(1)} %get-tuple-element.51), channel_id=1, source_target_pairs={{0,8},{4,12},{8,0},{12,4},{16,24},{20,28},{24,16},{28,20},{1,9},{5... | collective-permute-start | bytes 442376 | tf_op jit(solution)/shard_map/ppermute | solution.py:553
  53.2 25.2 %collective-permute-start.4 = (bf16[64,1152]{1,0:T(8,128)(2,1)S(1)}, bf16[64,1152]{1,0:T(8,128)(2,1)S(1)}, u32[]{:S(2)}, u32[]{:S(2)}) collective-permute-start(bf16[64,1152]{1,0:T(8,128)(2,1)S(1)} %get-tuple-element.52), channel_id=1, source_target_pairs={{0,12},{4,8},{8,4},{12,0},{16,28},{20,24},{24,20},{28,16},{1,13},{... | collective-permute-start | bytes 442376 | tf_op jit(solution)/shard_map/ppermute | solution.py:553
  53.2 26.6 %collective-permute-start.5 = (bf16[64,1152]{1,0:T(8,128)(2,1)S(1)}, bf16[64,1152]{1,0:T(8,128)(2,1)S(1)}, u32[]{:S(2)}, u32[]{:S(2)}) collective-permute-start(bf16[64,1152]{1,0:T(8,128)(2,1)S(1)} %get-tuple-element.53), channel_id=1, source_target_pairs={{0,16},{4,20},{8,24},{12,28},{16,0},{20,4},{24,8},{28,12},{1,17},{... | collective-permute-start | bytes 442376 | tf_op jit(solution)/shard_map/ppermute | solution.py:553
  61.2 21.7 %collective-permute-start.6 = (bf16[64,1152]{1,0:T(8,128)(2,1)S(1)}, bf16[64,1152]{1,0:T(8,128)(2,1)S(1)}, u32[]{:S(2)}, u32[]{:S(2)}) collective-permute-start(bf16[64,1152]{1,0:T(8,128)(2,1)S(1)} %get-tuple-element.54), channel_id=1, source_target_pairs={{0,20},{4,16},{8,28},{12,24},{16,4},{20,0},{24,12},{28,8},{1,21},{... | collective-permute-start | bytes 442376 | tf_op jit(solution)/shard_map/ppermute | solution.py:553
  67.5 16.2 %collective-permute-start.7 = (bf16[64,1152]{1,0:T(8,128)(2,1)S(1)}, bf16[64,1152]{1,0:T(8,128)(2,1)S(1)}, u32[]{:S(2)}, u32[]{:S(2)}) collective-permute-start(bf16[64,1152]{1,0:T(8,128)(2,1)S(1)} %get-tuple-element.55), channel_id=1, source_target_pairs={{0,24},{4,28},{8,16},{12,20},{16,8},{20,12},{24,0},{28,4},{1,25},{... | collective-permute-start | bytes 442376 | tf_op jit(solution)/shard_map/ppermute | solution.py:553
  67.7 20.0 %collective-permute-start.8 = (bf16[64,1152]{1,0:T(8,128)(2,1)S(1)}, bf16[64,1152]{1,0:T(8,128)(2,1)S(1)}, u32[]{:S(2)}, u32[]{:S(2)}) collective-permute-start(bf16[64,1152]{1,0:T(8,128)(2,1)S(1)} %get-tuple-element.56), channel_id=1, source_target_pairs={{0,28},{4,24},{8,20},{12,16},{16,12},{20,8},{24,4},{28,0},{1,29},{... | collective-permute-start | bytes 442376 | tf_op jit(solution)/shard_map/ppermute | solution.py:553
  73.5 19.9 %copy-start.2 = (bf16[1152,1728]{0,1:T(8,128)(2,1)S(1)}, bf16[1152,1728]{0,1:T(8,128)(2,1)}, u32[]{:S(2)}) copy-start(bf16[1152,1728]{0,1:T(8,128)(2,1)} %param.10) | copy-start | bytes 11943940
  78.5 19.9 %collective-permute-start.23 = (bf16[64,576]{1,0:T(8,128)(2,1)S(1)}, bf16[64,576]{1,0:T(8,128)(2,1)S(1)}, u32[]{:S(2)}, u32[]{:S(2)}) collective-permute-start(bf16[64,576]{1,0:T(8,128)(2,1)S(1)} %get-tuple-element.75), channel_id=1, source_target_pairs={{0,4},{4,0},{8,12},{12,8},{16,20},{20,16},{24,28},{28,24},{1,5},{5... | collective-permute-start | bytes 221192 | tf_op jit(solution)/shard_map/ppermute | solution.py:553
  79.9 19.5 %collective-permute-start.24 = (bf16[64,576]{1,0:T(8,128)(2,1)S(1)}, bf16[64,576]{1,0:T(8,128)(2,1)S(1)}, u32[]{:S(2)}, u32[]{:S(2)}) collective-permute-start(bf16[64,576]{1,0:T(8,128)(2,1)S(1)} %get-tuple-element.76), channel_id=1, source_target_pairs={{0,8},{4,12},{8,0},{12,4},{16,24},{20,28},{24,16},{28,20},{1,9},{5... | collective-permute-start | bytes 221192 | tf_op jit(solution)/shard_map/ppermute | solution.py:553
  82.9 19.8 %collective-permute-start.25 = (bf16[64,576]{1,0:T(8,128)(2,1)S(1)}, bf16[64,576]{1,0:T(8,128)(2,1)S(1)}, u32[]{:S(2)}, u32[]{:S(2)}) collective-permute-start(bf16[64,576]{1,0:T(8,128)(2,1)S(1)} %get-tuple-element.77), channel_id=1, source_target_pairs={{0,12},{4,8},{8,4},{12,0},{16,28},{20,24},{24,20},{28,16},{1,13},{... | collective-permute-start | bytes 221192 | tf_op jit(solution)/shard_map/ppermute | solution.py:553
  83.7 20.1 %collective-permute-start.26 = (bf16[64,576]{1,0:T(8,128)(2,1)S(1)}, bf16[64,576]{1,0:T(8,128)(2,1)S(1)}, u32[]{:S(2)}, u32[]{:S(2)}) collective-permute-start(bf16[64,576]{1,0:T(8,128)(2,1)S(1)} %get-tuple-element.78), channel_id=1, source_target_pairs={{0,16},{4,20},{8,24},{12,28},{16,0},{20,4},{24,8},{28,12},{1,17},{... | collective-permute-start | bytes 221192 | tf_op jit(solution)/shard_map/ppermute | solution.py:553
  87.7 16.1 %collective-permute-start.27 = (bf16[64,576]{1,0:T(8,128)(2,1)S(1)}, bf16[64,576]{1,0:T(8,128)(2,1)S(1)}, u32[]{:S(2)}, u32[]{:S(2)}) collective-permute-start(bf16[64,576]{1,0:T(8,128)(2,1)S(1)} %get-tuple-element.79), channel_id=1, source_target_pairs={{0,20},{4,16},{8,28},{12,24},{16,4},{20,0},{24,12},{28,8},{1,21},{... | collective-permute-start | bytes 221192 | tf_op jit(solution)/shard_map/ppermute | solution.py:553
  93.5 20.4 %copy-start = (bf16[576,1152]{1,0:T(8,128)(2,1)S(1)}, bf16[576,1152]{1,0:T(8,128)(2,1)}, u32[]{:S(2)}) copy-start(bf16[576,1152]{1,0:T(8,128)(2,1)} %refs_9_.3) | copy-start | bytes 3981316
  98.4 7.8 %collective-permute-start.28 = (bf16[64,576]{1,0:T(8,128)(2,1)S(1)}, bf16[64,576]{1,0:T(8,128)(2,1)S(1)}, u32[]{:S(2)}, u32[]{:S(2)}) collective-permute-start(bf16[64,576]{1,0:T(8,128)(2,1)S(1)} %get-tuple-element.80), channel_id=1, source_target_pairs={{0,24},{4,28},{8,16},{12,20},{16,8},{20,12},{24,0},{28,4},{1,25},{... | collective-permute-start | bytes 221192 | tf_op jit(solution)/shard_map/ppermute | solution.py:553
  99.4 8.1 %collective-permute-start.29 = (bf16[64,576]{1,0:T(8,128)(2,1)S(1)}, bf16[64,576]{1,0:T(8,128)(2,1)S(1)}, u32[]{:S(2)}, u32[]{:S(2)}) collective-permute-start(bf16[64,576]{1,0:T(8,128)(2,1)S(1)} %get-tuple-element.81), channel_id=1, source_target_pairs={{0,28},{4,24},{8,20},{12,16},{16,12},{20,8},{24,4},{28,0},{1,29},{... | collective-permute-start | bytes 221192 | tf_op jit(solution)/shard_map/ppermute | solution.py:553
  102.7 6.9 %collective-permute-start.9 = (bf16[64,576]{1,0:T(8,128)(2,1)S(1)}, bf16[64,576]{1,0:T(8,128)(2,1)S(1)}, u32[]{:S(2)}, u32[]{:S(2)}) collective-permute-start(bf16[64,576]{1,0:T(8,128)(2,1)S(1)} %get-tuple-element.58), channel_id=1, source_target_pairs={{0,4},{4,0},{8,12},{12,8},{16,20},{20,16},{24,28},{28,24},{1,5},{5... | collective-permute-start | bytes 221192 | tf_op jit(solution)/shard_map/ppermute | solution.py:553
  103.8 6.8 %collective-permute-start.10 = (bf16[64,576]{1,0:T(8,128)(2,1)S(1)}, bf16[64,576]{1,0:T(8,128)(2,1)S(1)}, u32[]{:S(2)}, u32[]{:S(2)}) collective-permute-start(bf16[64,576]{1,0:T(8,128)(2,1)S(1)} %get-tuple-element.59), channel_id=1, source_target_pairs={{0,8},{4,12},{8,0},{12,4},{16,24},{20,28},{24,16},{28,20},{1,9},{5... | collective-permute-start | bytes 221192 | tf_op jit(solution)/shard_map/ppermute | solution.py:553
  103.8 12.3 %collective-permute-start.11 = (bf16[64,576]{1,0:T(8,128)(2,1)S(1)}, bf16[64,576]{1,0:T(8,128)(2,1)S(1)}, u32[]{:S(2)}, u32[]{:S(2)}) collective-permute-start(bf16[64,576]{1,0:T(8,128)(2,1)S(1)} %get-tuple-element.60), channel_id=1, source_target_pairs={{0,12},{4,8},{8,4},{12,0},{16,28},{20,24},{24,20},{28,16},{1,13},{... | collective-permute-start | bytes 221192 | tf_op jit(solution)/shard_map/ppermute | solution.py:553
  106.2 13.0 %collective-permute-start.12 = (bf16[64,576]{1,0:T(8,128)(2,1)S(1)}, bf16[64,576]{1,0:T(8,128)(2,1)S(1)}, u32[]{:S(2)}, u32[]{:S(2)}) collective-permute-start(bf16[64,576]{1,0:T(8,128)(2,1)S(1)} %get-tuple-element.61), channel_id=1, source_target_pairs={{0,16},{4,20},{8,24},{12,28},{16,0},{20,4},{24,8},{28,12},{1,17},{... | collective-permute-start | bytes 221192 | tf_op jit(solution)/shard_map/ppermute | solution.py:553
  107.5 14.1 %collective-permute-start.13 = (bf16[64,576]{1,0:T(8,128)(2,1)S(1)}, bf16[64,576]{1,0:T(8,128)(2,1)S(1)}, u32[]{:S(2)}, u32[]{:S(2)}) collective-permute-start(bf16[64,576]{1,0:T(8,128)(2,1)S(1)} %get-tuple-element.62), channel_id=1, source_target_pairs={{0,20},{4,16},{8,28},{12,24},{16,4},{20,0},{24,12},{28,8},{1,21},{... | collective-permute-start | bytes 221192 | tf_op jit(solution)/shard_map/ppermute | solution.py:553
  109.6 11.9 %collective-permute-start.14 = (bf16[64,576]{1,0:T(8,128)(2,1)S(1)}, bf16[64,576]{1,0:T(8,128)(2,1)S(1)}, u32[]{:S(2)}, u32[]{:S(2)}) collective-permute-start(bf16[64,576]{1,0:T(8,128)(2,1)S(1)} %get-tuple-element.63), channel_id=1, source_target_pairs={{0,24},{4,28},{8,16},{12,20},{16,8},{20,12},{24,0},{28,4},{1,25},{... | collective-permute-start | bytes 221192 | tf_op jit(solution)/shard_map/ppermute | solution.py:553
  110.6 11.0 %collective-permute-start.15 = (bf16[64,576]{1,0:T(8,128)(2,1)S(1)}, bf16[64,576]{1,0:T(8,128)(2,1)S(1)}, u32[]{:S(2)}, u32[]{:S(2)}) collective-permute-start(bf16[64,576]{1,0:T(8,128)(2,1)S(1)} %get-tuple-element.64), channel_id=1, source_target_pairs={{0,28},{4,24},{8,20},{12,16},{16,12},{20,8},{24,4},{28,0},{1,29},{... | collective-permute-start | bytes 221192 | tf_op jit(solution)/shard_map/ppermute | solution.py:553
  (8 other events, 43.5 us)

commit v4 on v3

v4 whole, which is shorter than its diff:
```python
import functools

import jax
import jax.numpy as jnp
from jax import lax
from jax.experimental import pallas as pl
from jax.experimental.pallas import tpu as pltpu
from jax.sharding import PartitionSpec as P

HEADS = 8
HD = 72
TH = 4
TW = 16
LANES = 128
PACK = 16
NORM_EPS = 1e-06
NEG = -1e30
LOG2E = 1.4426950408889634
F32 = jnp.float32
BF16 = jnp.bfloat16
INNER = HEADS * HD
WIDE = -(-INNER // LANES) * LANES
PAIR = 2 * HD
PAIRS = HEADS // 2
PAIR_ROWS = PAIR + PACK
TILE = TH * TW
VMEM_LIMIT = 28 * 1024 * 1024
VMEM_WHOLE = 57 * 1024 * 1024


def params(limit=VMEM_LIMIT):
    return pltpu.CompilerParams(vmem_limit_bytes=limit)


def cost(flops, bytes_accessed):
    return pl.CostEstimate(flops=flops, bytes_accessed=bytes_accessed, transcendentals=0)


def nt_dot(a, b):
    return lax.dot_general(a, b, (((1,), (1,)), ((), ())), preferred_element_type=F32)


def nn_dot(a, b):
    return jnp.dot(a, b, preferred_element_type=F32)


def moments(x):
    x = x.astype(F32)
    mean = jnp.mean(x, axis=-1, keepdims=True)
    centred = x - mean
    spread = jnp.mean(centred * centred, axis=-1, keepdims=True)
    return mean, lax.rsqrt(spread + NORM_EPS)


def as_rows(column):
    return jnp.broadcast_to(column, (column.shape[0], LANES)).T[:1]


def tile_order(rows, columns):
    for col in range(columns // TW):
        for row in range(TH):
            yield (col * TH + row) * TW, row * columns + col * TW


def pair_window(pair):
    return pair * PAIR // LANES * LANES, -(-(pair + 1) * PAIR // LANES) * LANES


def two_heads(queries, pair):
    lo, hi = pair_window(pair)
    lane = lax.broadcasted_iota(jnp.int32, queries.shape, 1) + lo
    start = pair * PAIR
    first = jnp.where((lane >= start) & (lane < start + HD), queries, 0)
    second = jnp.where((lane >= start + HD) & (lane < start + PAIR), queries, 0)
    return jnp.concatenate([first, second], axis=0)


def split_queries_keys(prod):
    keys = prod[:, INNER // LANES * LANES :]
    shift = INNER % LANES
    if shift:
        keys = pltpu.roll(keys, keys.shape[1] - shift, 1)
    return prod[:, :WIDE], keys


def column_sums(w):
    return nt_dot(jnp.ones((PACK, w.shape[1]), BF16), w)[:1]


def store_values(v_ref, values, lanes):
    for pair in range(PAIRS):
        at = pair * PAIR_ROWS
        v_ref[at : at + PAIR, lanes] = values[pair * PAIR : (pair + 1) * PAIR]
        v_ref[at + PAIR : at + PAIR_ROWS, lanes] = jnp.ones((PACK, values.shape[1]), BF16)


def keys_values(x, mean, rstd, w_keys, w_values, k_ref, v_ref):
    k = (nt_dot(x, w_keys) - mean * column_sums(w_keys)) * rstd
    k_ref[:, :INNER] = k.astype(BF16)
    if WIDE > INNER:
        k_ref[:, INNER:] = jnp.zeros((x.shape[0], WIDE - INNER), BF16)
    col = nt_dot(w_values, jnp.ones((LANES, x.shape[1]), BF16))[:, :1]
    values = (nt_dot(w_values, x) - col * as_rows(mean)) * as_rows(rstd)
    store_values(v_ref, values.astype(BF16), slice(None))


def halo_kernel(columns, top_ref, bot_ref, wk_ref, wv_ref, k_ref, v_ref, x_ref):
    slab = top_ref.shape[0]
    v_rows = v_ref.shape[0] // 2
    for part, ref in enumerate((top_ref, bot_ref)):
        for to, at in tile_order(slab, columns):
            x_ref[pl.ds(to, TW), :] = ref[pl.ds(at, TW), :]
        x = x_ref[...]
        mean, rstd = moments(x)
        keys_values(
            x, mean, rstd, wk_ref[...], wv_ref[...],
            k_ref.at[pl.ds(part * slab, slab)], v_ref.at[pl.ds(part * v_rows, v_rows)],
        )


def project_halos(top, bot, w, columns):
    slab, feat = top.shape
    v_rows = PAIRS * PAIR_ROWS
    whole = lambda *shape: pl.BlockSpec(shape, lambda i: (0, 0))
    return pl.pallas_call(
        functools.partial(halo_kernel, columns),
        grid=(1,),
        in_specs=[
            whole(slab, feat),
            whole(slab, feat),
            pl.BlockSpec((INNER, feat), lambda i: (1, 0)),
            pl.BlockSpec((INNER, feat), lambda i: (2, 0)),
        ],
        out_specs=[whole(2 * slab, WIDE), whole(2 * v_rows, slab)],
        out_shape=[
            jax.ShapeDtypeStruct((2 * slab, WIDE), BF16),
            jax.ShapeDtypeStruct((2 * v_rows, slab), BF16),
        ],
        scratch_shapes=[pltpu.VMEM((slab, feat), BF16)],
        compiler_params=params(),
        cost_estimate=cost(2 * 10**9, 4 * 2**20),
        name="project_halos",
    )(top, bot, w, w)


def visible_bits(tile, count, global_row, tile_cols, slot_num, targets_ref):
    bits = jnp.int32(0)
    for slot in range(slot_num):
        target = targets_ref[0, tile, slot]
        cand = (lax.div(target, tile_cols) - global_row + 1) * tile_cols + lax.rem(target, tile_cols)
        bits = bits | jnp.where(slot < count, jnp.left_shift(1, cand), 0)
    return bits


def hidden(bits, index):
    return (1 - (jnp.right_shift(bits, index) & 1)).astype(F32) * NEG


def attend_tile_row(
    tile_row, tile_rows, columns, targets_ref, counts_ref, q_ref, k_refs, v_refs, p_ref, acc_ref
):
    slab = q_ref.shape[0]
    tile_cols = columns // TW
    slot_num = targets_ref.shape[2]
    global_row = lax.axis_index("row") * tile_rows + tile_row
    left = lax.broadcasted_iota(jnp.int32, (1, 4 * TILE), 1) % (2 * TILE) < TILE
    for duo in range(tile_cols // 2):
        bits = []
        for tile in (2 * duo, 2 * duo + 1):
            tile = tile_row * tile_cols + tile
            bits.append(
                visible_bits(tile, counts_ref[0, tile], global_row, tile_cols, slot_num, targets_ref)
            )
        lowest, highest = max(2 * duo - 1, 0), min(2 * duo + 2, tile_cols - 1)
        span = range(lowest, highest + 1)
        bias = {}
        for j in range(3):
            for col in span:
                at = j * tile_cols + col
                bias[j, col] = jnp.where(left, hidden(bits[0], at), hidden(bits[1], at))
        for pair in range(PAIRS):
            lo, hi = pair_window(pair)
            queries = two_heads(q_ref[2 * duo * TILE : (2 * duo + 2) * TILE, lo:hi], pair)
            scores = {}
            for j, ref in enumerate(k_refs):
                part = nt_dot(ref[lowest * TILE : (highest + 1) * TILE, lo:hi], queries)
                for col in span:
                    at = (col - lowest) * TILE
                    scores[j, col] = part[at : at + TILE] + bias[j, col]
            top = functools.reduce(jnp.maximum, scores.values())
            top = jnp.max(top, axis=0, keepdims=True)
            for (j, col), score in scores.items():
                at = j * slab + col * TILE
                p_ref[duo * PAIRS + pair, at : at + TILE, :] = jnp.exp2(score - top).astype(BF16)

    for duo in range(tile_cols // 2):
        for pair in range(PAIRS):
            out = sum(
                nn_dot(
                    ref[pair * PAIR_ROWS : (pair + 1) * PAIR_ROWS, :],
                    p_ref[duo * PAIRS + pair, j * slab : (j + 1) * slab, :],
                )
                for j, ref in enumerate(v_refs)
            )
            out = out[:PAIR] * (1.0 / out[PAIR : PAIR + 1])
            lanes = slice(2 * duo * TILE, (2 * duo + 2) * TILE)
            acc_ref[pair * PAIR : pair * PAIR + HD, lanes] = out[:HD, : 2 * TILE]
            acc_ref[pair * PAIR + HD : (pair + 1) * PAIR, lanes] = out[HD:, 2 * TILE :]


def peer_of(slot, peers, xor):
    me, j = lax.axis_index("frame"), (peers - slot) % peers
    return me ^ j if xor else lax.rem(me + j, peers)


def hand_out(send_refs, out_ref, group, xor):
    for slot, ref in enumerate(send_refs):
        peer = peer_of(slot, len(send_refs), xor)
        ref[...] = out_ref[pl.ds(pl.multiple_of(peer * group, PACK), group), :]


def inner_kernel(
    group, peers, xor,
    targets_ref, counts_ref, x_hbm, w_hbm, wo_hbm, q_hbm, k_hbm, v_hbm, mixed_ref, *rest,
):
    send_refs, rest = rest[:peers], rest[peers:]
    (w_ref, wo_ref, x_ref, q_ref, k_ref, v_ref, sum_ref, col_ref, p_ref, acc_ref, out_ref) = rest[:11]
    x_sem, w_sem, out_sem = rest[11:]
    step = pl.program_id(0)
    tile_rows, tile_cols = x_ref.shape[:2]
    columns = tile_cols * TW
    feat = x_ref.shape[-1]
    slab = tile_cols * TILE
    v_rows = PAIRS * PAIR_ROWS
    low = INNER // LANES * LANES
    bounds = (0, low, 2 * INNER, 3 * INNER)

    def x_copy(at, col):
        return pltpu.make_async_copy(
            x_hbm.at[pl.ds(at * TH, TH), pl.ds(col * TW, TW), :], x_ref.at[at, col], x_sem.at[at, col]
        )

    def w_copy(part):
        if part == 3:
            return pltpu.make_async_copy(wo_hbm, wo_ref, w_sem.at[3])
        rows = pl.ds(bounds[part], bounds[part + 1] - bounds[part])
        return pltpu.make_async_copy(w_hbm.at[rows], w_ref.at[rows], w_sem.at[part])

    def out_copies(at):
        rows, wide = pl.ds(at * slab, slab), pl.ds(at * v_rows, v_rows)
        return (
            pltpu.make_async_copy(q_ref.at[at], q_hbm.at[rows], out_sem.at[0, at]),
            pltpu.make_async_copy(k_ref.at[at], k_hbm.at[rows], out_sem.at[1, at]),
            pltpu.make_async_copy(v_ref.at[at], v_hbm.at[wide], out_sem.at[2, at]),
        )

    def work(first):
        for col in range(tile_cols):
            x_copy(step, col).wait()
        x = x_ref[step].reshape(slab, feat)
        mean, rstd = moments(x)
        if first:
            w_copy(0).wait()
            sum_ref[:, :low] = column_sums(w_ref[:low, :])
        scale = rstd * (LOG2E * HD**-0.5)
        q = (nt_dot(x, w_ref[:low, :]) - mean * sum_ref[:, :low]) * scale
        q_ref[step, :, :low] = q.astype(BF16)
        if first:
            w_copy(1).wait()
            sum_ref[:, low:] = column_sums(w_ref[low : 2 * INNER, :])
        k = (nt_dot(x, w_ref[low : 2 * INNER, :]) - mean * sum_ref[:, low:]) * rstd
        if INNER > low:
            q_ref[step, :, low:] = (k[:, : WIDE - low] * (LOG2E * HD**-0.5)).astype(BF16)
            k = pltpu.roll(k, k.shape[1] - (INNER - low), 1)
        k_ref[step] = k.astype(BF16)
        if first:
            w_copy(2).wait()
            ones = jnp.ones((LANES, feat), BF16)
            col_ref[...] = nt_dot(w_ref[2 * INNER :, :], ones)[:, :1]
        values = nt_dot(w_ref[2 * INNER :, :], x) - col_ref[...] * as_rows(mean)
        store_values(v_ref.at[step], (values * as_rows(rstd)).astype(BF16), slice(None))
        for copy in out_copies(step):
            copy.start()

    @pl.when(step == 0)
    def _():
        for col in range(tile_cols):
            x_copy(0, col).start()
        for part in range(3):
            w_copy(part).start()
        for at in range(1, tile_rows):
            for col in range(tile_cols):
                x_copy(at, col).start()
        w_copy(3).start()
        work(True)

    @pl.when((step > 0) & (step < tile_rows))
    def _():
        work(False)

    @pl.when(step == tile_rows)
    def _():
        w_copy(3).wait()
        p_ref[...] = jnp.zeros(p_ref.shape, BF16)

    @pl.when(step >= tile_rows)
    def _():
        tile_row = step - tile_rows + 1
        k_refs = [k_ref.at[tile_row + j] for j in (-1, 0, 1)]
        v_refs = [v_ref.at[tile_row + j] for j in (-1, 0, 1)]
        attend_tile_row(
            tile_row, tile_rows, columns, targets_ref, counts_ref, q_ref.at[tile_row],
            k_refs, v_refs, p_ref, acc_ref,
        )
        branch = nn_dot(acc_ref[...].T.astype(BF16), wo_ref[...])
        mixed = (x_ref[tile_row].reshape(slab, feat).astype(F32) + branch).astype(BF16)
        mixed_ref[...] = mixed
        out_ref[pl.ds(pl.multiple_of((tile_row - 1) * slab, slab), slab), :] = mixed

    @pl.when(step == 2 * tile_rows - 3)
    def _():
        hand_out(send_refs, out_ref, group, xor)
        for at in range(tile_rows):
            for copy in out_copies(at):
                copy.wait()


def spatial_inner(x, w, wo, targets, counts, peers, xor):
    rows, columns, feat = x.shape
    tile_rows = rows // TH
    slab = TH * columns
    v_rows = PAIRS * PAIR_ROWS
    group = (tile_rows - 2) * slab // peers
    smem = pl.BlockSpec(memory_space=pltpu.SMEM)
    hbm = pl.BlockSpec(memory_space=pltpu.HBM)
    outs = pl.pallas_call(
        functools.partial(inner_kernel, group, peers, xor),
        grid=(2 * tile_rows - 2,),
        in_specs=[smem, smem, hbm, hbm, hbm],
        out_specs=[hbm, hbm, hbm, pl.BlockSpec((slab, feat), lambda i: (jnp.maximum(i - tile_rows, 0), 0))]
        + [pl.BlockSpec((group, feat), lambda i: (0, 0))] * peers,
        out_shape=[
            jax.ShapeDtypeStruct((tile_rows * slab, WIDE), BF16),
            jax.ShapeDtypeStruct((tile_rows * slab, WIDE), BF16),
            jax.ShapeDtypeStruct((tile_rows * v_rows, slab), BF16),
            jax.ShapeDtypeStruct((tile_rows * slab, feat), BF16),
        ]
        + [jax.ShapeDtypeStruct((group, feat), BF16)] * peers,
        scratch_shapes=[
            pltpu.VMEM(w.shape, BF16),
            pltpu.VMEM(wo.shape, BF16),
            pltpu.VMEM((tile_rows, columns // TW, TH, TW, feat), BF16),
            pltpu.VMEM((tile_rows, slab, WIDE), BF16),
            pltpu.VMEM((tile_rows, slab, WIDE), BF16),
            pltpu.VMEM((tile_rows, v_rows, slab), BF16),
            pltpu.VMEM((1, 2 * INNER), F32),
            pltpu.VMEM((INNER, 1), F32),
            pltpu.VMEM((columns // TW // 2 * PAIRS, 3 * slab, 4 * TILE), BF16),
            pltpu.VMEM((INNER, slab), F32),
            pltpu.VMEM(((tile_rows - 2) * slab, feat), BF16),
            pltpu.SemaphoreType.DMA((tile_rows, columns // TW)),
            pltpu.SemaphoreType.DMA((4,)),
            pltpu.SemaphoreType.DMA((3, tile_rows)),
        ],
        compiler_params=params(VMEM_WHOLE),
        cost_estimate=cost(12 * 10**9, 16 * 2**20),
        name="spatial_inner",
    )(targets, counts, x, w, wo)
    return outs[:3], outs[3], outs[4:]


def edges_kernel(
    group, peers, xor, tile_rows, columns,
    targets_ref, counts_ref, x_ref, q_ref, k0, k1, k2, v0, v1, v2, k_halo, v_halo, _, w_ref, mixed_ref, *rest,
):
    send_refs, rest = rest[:peers], rest[peers:]
    p_ref, acc_ref, out_ref, k_prev, k_next, v_prev, v_next = rest
    step = pl.program_id(0)
    slab = x_ref.shape[0]
    v_rows = v_prev.shape[0]

    @pl.when(step == 0)
    def _():
        p_ref[...] = jnp.zeros(p_ref.shape, BF16)
        k_prev[...] = k_halo[:slab, :]
        v_prev[...] = v_halo[:v_rows, :]
        k_next[...] = k2[...]
        v_next[...] = v2[...]

    @pl.when(step != 0)
    def _():
        k_prev[...] = k0[...]
        v_prev[...] = v0[...]
        k_next[...] = k_halo[slab:, :]
        v_next[...] = v_halo[v_rows:, :]

    attend_tile_row(
        step * (tile_rows - 1), tile_rows, columns, targets_ref, counts_ref, q_ref,
        (k_prev, k1, k_next), (v_prev, v1, v_next), p_ref, acc_ref,
    )
    branch = nn_dot(acc_ref[...].T.astype(BF16), w_ref[...])
    base = step * slab
    for to, at in tile_order(slab, columns):
        mixed = (x_ref[pl.ds(at, TW), :].astype(F32) + branch[to : to + TW]).astype(BF16)
        mixed_ref[pl.ds(to, TW), :] = mixed
        out_ref[pl.ds(pl.multiple_of(base + to, TW), TW), :] = mixed

    @pl.when(step == 1)
    def _():
        hand_out(send_refs, out_ref, group, xor)


def spatial_edges(x, q, k, v, halos, base, w, targets, counts, slab, columns, peers, xor):
    pixels, feat = x.shape
    tile_rows = pixels // slab
    group = 2 * slab // peers
    v_rows = PAIRS * PAIR_ROWS
    at = lambda i: i * (tile_rows - 1)
    smem = pl.BlockSpec(memory_space=pltpu.SMEM)
    whole = lambda *shape: pl.BlockSpec(shape, lambda i: (0, 0))
    in_specs = [
        smem,
        smem,
        pl.BlockSpec((slab, feat), lambda i: (at(i), 0)),
        pl.BlockSpec((slab, WIDE), lambda i: (at(i), 0)),
    ]
    for block in ((slab, WIDE), (v_rows, slab)):
        in_specs += [
            pl.BlockSpec(block, lambda i: (tile_rows - 2, 0)),
            pl.BlockSpec(block, lambda i: (at(i), 0)),
            pl.BlockSpec(block, lambda i: (1, 0)),
        ]
    in_specs += [whole(*halo.shape) for halo in halos]
    in_specs += [pl.BlockSpec(memory_space=pl.ANY), whole(*w.shape)]
    outs = pl.pallas_call(
        functools.partial(edges_kernel, group, peers, xor, tile_rows, columns),
        grid=(2,),
        in_specs=in_specs,
        out_specs=[pl.BlockSpec((slab, feat), lambda i: (tile_rows - 2 + i, 0))]
        + [whole(group, feat)] * peers,
        out_shape=[jax.ShapeDtypeStruct((pixels, feat), BF16)]
        + [jax.ShapeDtypeStruct((group, feat), BF16)] * peers,
        scratch_shapes=[
            pltpu.VMEM((columns // TW // 2 * PAIRS, 3 * slab, 4 * TILE), BF16),
            pltpu.VMEM((INNER, slab), F32),
            pltpu.VMEM((2 * slab, feat), BF16),
            pltpu.VMEM((slab, WIDE), BF16),
            pltpu.VMEM((slab, WIDE), BF16),
            pltpu.VMEM((v_rows, slab), BF16),
            pltpu.VMEM((v_rows, slab), BF16),
        ],
        input_output_aliases={12: 0},
        compiler_params=params(),
        cost_estimate=cost(6 * 10**9, 8 * 2**20),
        name="spatial_edges",
    )(targets, counts, x, q, k, k, k, v, v, v, *halos, base, w)
    return outs[0], outs[1:]


def temporal_kernel(peers, group, earlier, *refs):
    in_refs, w_ref, refs = refs[:peers], refs[peers], refs[peers + 1 :]
    if earlier:
        early_refs, refs = refs[:peers], refs[peers:]
    out_refs = refs[:peers]
    x_ref, q_ref, k_ref, v_ref, p_ref, acc_ref = refs[peers:]
    if earlier:
        for j in range(peers):
            out_refs[j][:earlier, :] = early_refs[j][...]
    block = peers * PACK
    parts = group // PACK
    tokens = peers * group
    for part in range(parts):
        for j in range(peers):
            to = pl.ds(part * block + j * PACK, PACK)
            x_ref[to, :] = in_refs[j][pl.ds(part * PACK, PACK), :]
    x = x_ref[...]
    mean, rstd = moments(x)
    prod = (nt_dot(x, w_ref[: 2 * INNER, :]) - mean * column_sums(w_ref[: 2 * INNER, :])) * rstd
    q, k = split_queries_keys(prod)
    q_ref[...] = (q * (LOG2E * HD**-0.5)).astype(BF16)
    k_ref[...] = k.astype(BF16)
    w_values = w_ref[2 * INNER :, :]
    col = nt_dot(w_values, jnp.ones((LANES, w_values.shape[1]), BF16))[:, :1]
    values = (nt_dot(w_values, x) - col * as_rows(mean)) * as_rows(rstd)
    store_values(v_ref, values.astype(BF16), slice(None))
    row = lax.broadcasted_iota(jnp.int32, (block, 2 * block), 0)
    col = lax.broadcasted_iota(jnp.int32, (block, 2 * block), 1)
    bias = jnp.where(row % PACK == col % PACK, 0.0, NEG).astype(F32)
    for part in range(parts):
        at = part * block
        for pair in range(PAIRS):
            lo, hi = pair_window(pair)
            queries = two_heads(q_ref[at : at + block, lo:hi], pair)
            scores = nt_dot(k_ref[at : at + block, lo:hi], queries) + bias
            expo = jnp.exp2(scores - jnp.max(scores, axis=0, keepdims=True))
            p_ref[part * PAIRS + pair] = expo.astype(BF16)
    for part in range(parts):
        at = part * block
        for pair in range(PAIRS):
            weights = v_ref[pair * PAIR_ROWS : (pair + 1) * PAIR_ROWS, at : at + block]
            out = nn_dot(weights, p_ref[part * PAIRS + pair])
            out = out[:PAIR] * (1.0 / out[PAIR : PAIR + 1])
            acc_ref[pair * PAIR : pair * PAIR + HD, at : at + block] = out[:HD, :block]
            acc_ref[pair * PAIR + HD : (pair + 1) * PAIR, at : at + block] = out[HD:, block:]
    for part in range(parts):
        at = part * block
        heads = acc_ref[:, at : at + block].T.astype(BF16)
        for j in range(peers):
            rows = heads[j * PACK : (j + 1) * PACK]
            out_refs[j][pl.ds(earlier + part * PACK, PACK), :] = rows


def temporal(pieces, w, early):
    peers = len(pieces)
    group, feat = pieces[0].shape
    tokens = peers * group
    earlier = early[0].shape[0] if early else 0
    return pl.pallas_call(
        functools.partial(temporal_kernel, peers, group, earlier),
        out_shape=[jax.ShapeDtypeStruct((earlier + group, INNER), BF16)] * peers,
        scratch_shapes=[
            pltpu.VMEM((tokens, feat), BF16),
            pltpu.VMEM((tokens, WIDE), BF16),
            pltpu.VMEM((tokens, WIDE), BF16),
            pltpu.VMEM((PAIRS * PAIR_ROWS, tokens), BF16),
            pltpu.VMEM((group // PACK * PAIRS, peers * PACK, 2 * peers * PACK), BF16),
            pltpu.VMEM((INNER, tokens), F32),
        ],
        compiler_params=params(),
        cost_estimate=cost(4 * 10**9, 6 * 2**20),
        name="temporal",
    )(*pieces, w, *early)


def final_kernel(groups, xor, columns, *refs):
    in_refs, (mixed_ref, w_ref, out_ref, heads_ref) = refs[:-4], refs[-4:]
    step = pl.program_id(0)
    slab = mixed_ref.shape[0]
    peers = len(in_refs)

    @pl.when(step == 0)
    def _():
        for j in range(peers):
            peer = peer_of(j, peers, xor)
            base = start = 0
            for group in groups:
                to = pl.multiple_of(base + peer * group, PACK)
                heads_ref[pl.ds(to, group), :] = in_refs[j][start : start + group, :]
                base += peers * group
                start += group

    heads = heads_ref[pl.ds(pl.multiple_of(step * slab, slab), slab), :]
    result = mixed_ref[...].astype(F32) + nn_dot(heads, w_ref[...])
    for to, at in tile_order(slab, columns):
        out_ref[pl.ds(at, TW), :] = result[to : to + TW].astype(BF16)


def final(pieces, groups, mixed, w, slab, columns, xor):
    pixels, feat = mixed.shape
    tile_rows = pixels // slab
    inner = tile_rows - 2
    at = lambda i: jnp.where(i < inner, i + 1, (i - inner) * (tile_rows - 1))
    whole = lambda *shape: pl.BlockSpec(shape, lambda i: (0, 0))
    return pl.pallas_call(
        functools.partial(final_kernel, groups, xor, columns),
        grid=(tile_rows,),
        in_specs=[whole(*piece.shape) for piece in pieces]
        + [pl.BlockSpec((slab, feat), lambda i: (i, 0)), whole(*w.shape)],
        out_specs=pl.BlockSpec((slab, feat), lambda i: (at(i), 0)),
        out_shape=jax.ShapeDtypeStruct((pixels, feat), BF16),
        scratch_shapes=[pltpu.VMEM((pixels, INNER), BF16)],
        compiler_params=params(),
        cost_estimate=cost(2 * 10**9, 6 * 2**20),
        name="final",
    )(*pieces, mixed, w)


def neighbours(x, slab):
    size = lax.axis_size("row")
    up = [(i, i + 1) for i in range(size - 1)]
    down = [(j, i) for i, j in up]
    return lax.ppermute(x[-slab:], "row", up), lax.ppermute(x[:slab], "row", down)


def exchange(pieces, xor, back):
    size = lax.axis_size("frame")
    result = [pieces[0]]
    for slot in range(1, size):
        j = size - slot
        if xor:
            pairs = [(i, i ^ j) for i in range(size)]
        else:
            pairs = [(i, (i - j if back else i + j) % size) for i in range(size)]
        result.append(lax.ppermute(pieces[slot], "frame", pairs))
    return result


def body(frames_in, spatial_qkv, spatial_out, temporal_qkv, temporal_out, key_tiles, tile_counts):
    _, rows_dev, columns, feat = frames_in.shape
    slab = TH * columns
    pixels = rows_dev * columns
    peers = lax.axis_size("frame")
    xor = peers & (peers - 1) == 0
    x = frames_in.reshape(pixels, feat)
    top, bot = neighbours(x, slab)
    qkv, mixed, send_a = spatial_inner(
        frames_in[0], spatial_qkv.T, spatial_out, key_tiles, tile_counts, peers, xor
    )
    got_a = exchange(send_a, xor, False)
    top, bot, mixed = lax.optimization_barrier((top, bot, mixed))
    halos = project_halos(top, bot, spatial_qkv.T, columns)
    mixed, send_b = spatial_edges(
        x, *qkv, halos, mixed, spatial_out, key_tiles, tile_counts, slab, columns, peers, xor
    )
    got_b = exchange(send_b, xor, False)
    heads_a = temporal(got_a, temporal_qkv.T, ())
    heads = temporal(got_b, temporal_qkv.T, heads_a)
    groups = (got_a[0].shape[0], got_b[0].shape[0])
    out = final(exchange(heads, xor, True), groups, mixed, temporal_out, slab, columns, xor)
    return out.reshape(frames_in.shape)


def solution(mesh):
    in_specs = (
        P("frame", "row", None, None),
        P(),
        P(),
        P(),
        P(),
        P("frame", "row", None),
        P("frame", "row"),
    )
    out_specs = P("frame", "row", None, None)
    return jax.shard_map(body, mesh=mesh, in_specs=in_specs, out_specs=out_specs, check_vma=False)
```

time: 125 us -> 122 us (0.976)
  starting transfers between devices: 61.5 us -> 43.5 us
  waiting for transfers between devices: 13.5 us -> 30.9 us
  local copies, waits for them, and re-layouts: 8.07 us -> 3.4 us
  Pallas kernels: 40.6 us -> 42.5 us
    ppermute x30 -> x23, starting transfers between devices: 61.5 us -> 43.5 us  [the longest x21 39.8 us: exchange(): result.append(lax.ppermute(pieces[slot], 'frame', pairs))]
    ppermute x30 -> x23, waiting for transfers between devices: 13.5 us -> 30.9 us  [the longest x21 30.9 us: exchange(): result.append(lax.ppermute(pieces[slot], 'frame', pairs))]
    unnamed x21 -> x31, local copies, waits for them, and re-layouts: 8.07 us -> 2.04 us
    pallas_call x7 -> x6, Pallas kernels: 40.6 us -> 42.5 us  [the longest x1 18.2 us: spatial_inner(): pl.pallas_call(functools.partial(inner_kernel, group, peers, xor), grid=(...]
    slice x0 -> x1, local copies, waits for them, and re-layouts: none -> 1.35 us  [neighbours(): x[:slab]]
  transfers between devices with their start and end apart: 30 -> 23, of which waited for: 5 -> 9; matrix products, arithmetic and copies ran while one was open for 0% -> 1% of each run, Pallas kernels for 22% -> 28%
where the time goes in v4:
time: 122 us; the launch traced here: 121 us
  starting transfers between devices  43.5 us (36%)
  Pallas kernels  42.5 us (35%)
  waiting for transfers between devices  30.9 us (25%)
  local copies, waits for them, and re-layouts  3.4 us (3%)
    ppermute x21, starting transfers between devices, exchange(): result.append(lax.ppermute(pieces[slot], 'frame', pairs))  39.8 us
    ppermute x21, waiting for transfers between devices, exchange(): result.append(lax.ppermute(pieces[slot], 'frame', pairs))  30.9 us
    pallas_call x1, Pallas kernels, spatial_inner(): pl.pallas_call(functools.partial(inner_kernel, group, peers, xor), grid=(...  18.2 us
    pallas_call x2, Pallas kernels, temporal(): pl.pallas_call(functools.partial(temporal_kernel, peers, group, earlier),...  10.2 us
    pallas_call x1, Pallas kernels, spatial_edges(): pl.pallas_call(functools.partial(edges_kernel, group, peers, xor, tile_ro...  6.54 us
    pallas_call x1, Pallas kernels, project_halos(): pl.pallas_call(functools.partial(halo_kernel, columns), grid=(1,), in_spe...  3.82 us
    pallas_call x1, Pallas kernels, final(): pl.pallas_call(functools.partial(final_kernel, groups, xor, columns), gri...  3.76 us
  transfers between devices with their start and end apart: 23, of which 9 were waited for; matrix products, arithmetic and copies ran while one was open for 1% of the time, Pallas kernels for 28%

profile of v4, /device:TPU:0, one launch (start us, length us, event | category | flops | bytes accessed | tf_op | source)
XLA Modules:
  0.0 120.5 jit_solution(10012068854665622778)
XLA Ops:
  0.0 1.4 %fusion = (bf16[1,4,64,1152]{3,2,1,0:T(8,128)(2,1)S(1)}, bf16[1,4,64,1152]{3,2,1,0:T(8,128)(2,1)S(1)}) fusion(bf16[1,16,64,1152]{3,2,1,0:T(8,128)(2,1)} %param.7), kind=kLoop, calls=%fused_computation | loop fusion | bytes 2359296 | tf_op jit(solution)/shard_map/slice | solution.py:582
  1.4 2.4 %collective-permute-start = (bf16[256,1152]{1,0:T(8,128)(2,1)S(1)}, bf16[256,1152]{1,0:T(8,128)(2,1)S(1)}, u32[]{:S(2)}, u32[]{:S(2)}) collective-permute-start(bf16[256,1152]{1,0:T(8,128)(2,1)S(1)} %bitcast.15), channel_id=1, source_target_pairs={{0,1},{1,2},{2,3},{4,5},{5,6},{6,7},{8,9},{9,10},{10,11},{12,13},{... | collective-permute-start | bytes 1769480 | tf_op jit(solution)/shard_map/ppermute | solution.py:582
  3.8 1.3 %collective-permute-start.1 = (bf16[256,1152]{1,0:T(8,128)(2,1)S(1)}, bf16[256,1152]{1,0:T(8,128)(2,1)S(1)}, u32[]{:S(2)}, u32[]{:S(2)}) collective-permute-start(bf16[256,1152]{1,0:T(8,128)(2,1)S(1)} %bitcast.14), channel_id=1, source_target_pairs={{1,0},{2,1},{3,2},{5,4},{6,5},{7,6},{9,8},{10,9},{11,10},{13,12},{... | collective-permute-start | bytes 1769480 | tf_op jit(solution)/shard_map/ppermute | solution.py:582
  5.1 0.7 copy.10.targets_ref
  5.8 18.2 %spatial_inner.1 = (bf16[1024,640]{1,0:T(8,128)(2,1)}, bf16[1024,640]{1,0:T(8,128)(2,1)}, bf16[2560,256]{1,0:T(8,128)(2,1)}, bf16[1024,1152]{1,0:T(8,128)(2,1)},...) custom-call(s32[1,16,9]{2,1,0:T(8,128)} %copy.10.targets_ref, ...), custom_call_target="tpu_custom_call" | custom-call | flops 12000000000 | bytes 16777216 | tf_op jit(solution)/shard_map/spatial_inner/pallas_call | solution.py:336
  23.9 5.4 %collective-permute-start.9 = (bf16[64,1152]{1,0:T(8,128)(2,1)}, bf16[64,1152]{1,0:T(8,128)(2,1)S(1)}, u32[]{:S(2)}, u32[]{:S(2)}) collective-permute-start(bf16[64,1152]{1,0:T(8,128)(2,1)} %get-tuple-element.65), channel_id=1, source_target_pairs={{0,28},{4,24},{8,20},{12,16},{16,12},{20,8},{24,4},{28,0},{1,29},{... | collective-permute-start | bytes 442376 | tf_op jit(solution)/shard_map/ppermute | solution.py:594
  29.6 0.8 collective-permute-start.11
  30.4 2.0 %collective-permute-start.12 = (bf16[64,1152]{1,0:T(8,128)(2,1)}, bf16[64,1152]{1,0:T(8,128)(2,1)S(1)}, u32[]{:S(2)}, u32[]{:S(2)}) collective-permute-start(bf16[64,1152]{1,0:T(8,128)(2,1)} %get-tuple-element.68), channel_id=1, source_target_pairs={{0,16},{4,20},{8,24},{12,28},{16,0},{20,4},{24,8},{28,12},{1,17},{... | collective-permute-start | bytes 442376 | tf_op jit(solution)/shard_map/ppermute | solution.py:594
  32.4 2.4 %collective-permute-start.13 = (bf16[64,1152]{1,0:T(8,128)(2,1)}, bf16[64,1152]{1,0:T(8,128)(2,1)S(1)}, u32[]{:S(2)}, u32[]{:S(2)}) collective-permute-start(bf16[64,1152]{1,0:T(8,128)(2,1)} %get-tuple-element.69), channel_id=1, source_target_pairs={{0,12},{4,8},{8,4},{12,0},{16,28},{20,24},{24,20},{28,16},{1,13},{... | collective-permute-start | bytes 442376 | tf_op jit(solution)/shard_map/ppermute | solution.py:594
  34.8 3.8 %project_halos.1 = (bf16[512,640]{1,0:T(8,128)(2,1)S(1)}, bf16[1280,256]{1,0:T(8,128)(2,1)S(1)}) custom-call(bf16[256,1152]{1,0:T(8,128)(2,1)S(1)} %collective-permute-done.top_ref, bf16[256,1152]{1,0:T(8,128)(2,1)S(1)} %collective-permute-done.1.bot_ref, bf16[1728,1152]{1,0:T(8,128)(2,1)S(1)} %bitcast.8, bf16[1728,1152]{1,0:T(8,128)(2,1)S(1)} %bitcast.9), custom_call_target="tpu_custom_call" | custom-call | flops 2000000000 | bytes 4194304 | tf_op jit(solution)/shard_map/project_halos/pallas_call | solution.py:125
  38.7 1.3 %copy-done.10 = bf16[2560,256]{1,0:T(8,128)(2,1)S(1)} copy-done((bf16[2560,256]{1,0:T(8,128)(2,1)S(1)}, bf16[2560,256]{1,0:T(8,128)(2,1)}, u32[]{:S(2)}) %copy-start.10) | copy-done | bytes 1310744
  40.0 6.5 %spatial_edges.1 = (bf16[1024,1152]{1,0:T(8,128)(2,1)S(1)}, bf16[64,1152]{1,0:T(8,128)(2,1)S(1)}, bf16[64,1152]{1,0:T(8,128)(2,1)S(1)}, bf16[64,1152]{1,0:T(8,12...) custom-call(s32[1,16,9]{2,1,0:T(8,128)S(1)} %copy-done.2, ...), custom_call_target="tpu_custom_call", output_to_operand_aliasing={{0}: (12, {})} | custom-call | flops 6000000000 | bytes 8388608 | tf_op jit(solution)/shard_map/spatial_edges/pallas_call | solution.py:435
  46.6 0.8 collective-permute-start.14
  47.8 4.3 %collective-permute-done.11.refs_3_ = bf16[64,1152]{1,0:T(8,128)(2,1)S(1)} collective-permute-done((bf16[64,1152]{1,0:T(8,128)(2,1)}, bf16[64,1152]{1,0:T(8,128)(2,1)S(1)}, u32[]{:S(2)}, u32[]{:S(2)}) %collective-permute-start.11) | collective-permute-done | bytes 147488 | tf_op jit(solution)/shard_map/ppermute | solution.py:594
  52.1 2.6 %collective-permute-start.2 = (bf16[64,1152]{1,0:T(8,128)(2,1)S(1)}, bf16[64,1152]{1,0:T(8,128)(2,1)S(1)}, u32[]{:S(2)}, u32[]{:S(2)}) collective-permute-start(bf16[64,1152]{1,0:T(8,128)(2,1)S(1)} %get-tuple-element.57), channel_id=1, source_target_pairs={{0,28},{4,24},{8,20},{12,16},{16,12},{20,8},{24,4},{28,0},{1,29},{... | collective-permute-start | bytes 442376 | tf_op jit(solution)/shard_map/ppermute | solution.py:594
  55.0 1.9 %collective-permute-start.3 = (bf16[64,1152]{1,0:T(8,128)(2,1)S(1)}, bf16[64,1152]{1,0:T(8,128)(2,1)S(1)}, u32[]{:S(2)}, u32[]{:S(2)}) collective-permute-start(bf16[64,1152]{1,0:T(8,128)(2,1)S(1)} %get-tuple-element.58), channel_id=1, source_target_pairs={{0,24},{4,28},{8,16},{12,20},{16,8},{20,12},{24,0},{28,4},{1,25},{... | collective-permute-start | bytes 442376 | tf_op jit(solution)/shard_map/ppermute | solution.py:594
  56.9 7.9 %collective-permute-done.14.refs_6_ = bf16[64,1152]{1,0:T(8,128)(2,1)S(1)} collective-permute-done((bf16[64,1152]{1,0:T(8,128)(2,1)S(1)}, bf16[64,1152]{1,0:T(8,128)(2,1)S(1)}, u32[]{:S(2)}, u32[]{:S(2)}) %collective-permute-start.14) | collective-permute-done | bytes 147488 | tf_op jit(solution)/shard_map/ppermute | solution.py:594
  64.8 2.3 %collective-permute-start.6 = (bf16[64,1152]{1,0:T(8,128)(2,1)S(1)}, bf16[64,1152]{1,0:T(8,128)(2,1)S(1)}, u32[]{:S(2)}, u32[]{:S(2)}) collective-permute-start(bf16[64,1152]{1,0:T(8,128)(2,1)S(1)} %get-tuple-element.61), channel_id=1, source_target_pairs={{0,12},{4,8},{8,4},{12,0},{16,28},{20,24},{24,20},{28,16},{1,13},{... | collective-permute-start | bytes 442376 | tf_op jit(solution)/shard_map/ppermute | solution.py:594
  67.2 1.3 %collective-permute-start.8 = (bf16[64,1152]{1,0:T(8,128)(2,1)S(1)}, bf16[64,1152]{1,0:T(8,128)(2,1)S(1)}, u32[]{:S(2)}, u32[]{:S(2)}) collective-permute-start(bf16[64,1152]{1,0:T(8,128)(2,1)S(1)} %get-tuple-element.63), channel_id=1, source_target_pairs={{0,4},{4,0},{8,12},{12,8},{16,20},{20,16},{24,28},{28,24},{1,5},{5... | collective-permute-start | bytes 442376 | tf_op jit(solution)/shard_map/ppermute | solution.py:594
  68.5 5.1 %temporal.2 = (bf16[64,576]{1,0:T(8,128)(2,1)S(1)}, bf16[64,576]{1,0:T(8,128)(2,1)S(1)}, bf16[64,576]{1,0:T(8,128)(2,1)S(1)}, bf16[64,576]{1,0:T(8,128)(2,1)S(1)...) custom-call(bf16[64,1152]{1,0:T(8,128)(2,1)S(1)} %copy-done.11, ...), custom_call_target="tpu_custom_call" | custom-call | flops 4000000000 | bytes 6291456 | tf_op jit(solution)/shard_map/temporal/pallas_call | solution.py:518
  73.6 3.3 %collective-permute-done.4.refs_3_ = bf16[64,1152]{1,0:T(8,128)(2,1)S(1)} collective-permute-done((bf16[64,1152]{1,0:T(8,128)(2,1)S(1)}, bf16[64,1152]{1,0:T(8,128)(2,1)S(1)}, u32[]{:S(2)}, u32[]{:S(2)}) %collective-permute-start.4) | collective-permute-done | bytes 147488 | tf_op jit(solution)/shard_map/ppermute | solution.py:594
  76.9 3.4 %collective-permute-done.5.refs_4_ = bf16[64,1152]{1,0:T(8,128)(2,1)S(1)} collective-permute-done((bf16[64,1152]{1,0:T(8,128)(2,1)S(1)}, bf16[64,1152]{1,0:T(8,128)(2,1)S(1)}, u32[]{:S(2)}, u32[]{:S(2)}) %collective-permute-start.5) | collective-permute-done | bytes 147488 | tf_op jit(solution)/shard_map/ppermute | solution.py:594
  80.3 5.1 %temporal.3 = (bf16[128,576]{1,0:T(8,128)(2,1)S(1)}, bf16[128,576]{1,0:T(8,128)(2,1)S(1)}, bf16[128,576]{1,0:T(8,128)(2,1)S(1)}, bf16[128,576]{1,0:T(8,128)(2,1)...) custom-call(bf16[64,1152]{1,0:T(8,128)(2,1)S(1)} %get-tuple-element., ...), custom_call_target="tpu_custom_call" | custom-call | flops 4000000000 | bytes 6291456 | tf_op jit(solution)/shard_map/temporal/pallas_call | solution.py:518
  85.5 2.0 %collective-permute-start.16 = (bf16[128,576]{1,0:T(8,128)(2,1)S(1)}, bf16[128,576]{1,0:T(8,128)(2,1)S(1)}, u32[]{:S(2)}, u32[]{:S(2)}) collective-permute-start(bf16[128,576]{1,0:T(8,128)(2,1)S(1)} %get-tuple-element.81), channel_id=1, source_target_pairs={{0,28},{4,24},{8,20},{12,16},{16,12},{20,8},{24,4},{28,0},{1,29},{... | collective-permute-start | bytes 442376 | tf_op jit(solution)/shard_map/ppermute | solution.py:594
  87.5 1.6 %collective-permute-start.17 = (bf16[128,576]{1,0:T(8,128)(2,1)S(1)}, bf16[128,576]{1,0:T(8,128)(2,1)S(1)}, u32[]{:S(2)}, u32[]{:S(2)}) collective-permute-start(bf16[128,576]{1,0:T(8,128)(2,1)S(1)} %get-tuple-element.82), channel_id=1, source_target_pairs={{0,24},{4,28},{8,16},{12,20},{16,8},{20,12},{24,0},{28,4},{1,25},{... | collective-permute-start | bytes 442376 | tf_op jit(solution)/shard_map/ppermute | solution.py:594
  89.0 4.2 %collective-permute-start.19 = (bf16[128,576]{1,0:T(8,128)(2,1)S(1)}, bf16[128,576]{1,0:T(8,128)(2,1)S(1)}, u32[]{:S(2)}, u32[]{:S(2)}) collective-permute-start(bf16[128,576]{1,0:T(8,128)(2,1)S(1)} %get-tuple-element.84), channel_id=1, source_target_pairs={{0,16},{4,20},{8,24},{12,28},{16,0},{20,4},{24,8},{28,12},{1,17},{... | collective-permute-start | bytes 442376 | tf_op jit(solution)/shard_map/ppermute | solution.py:594
  93.2 1.5 %collective-permute-done.16.refs_1_ = bf16[128,576]{1,0:T(8,128)(2,1)S(1)} collective-permute-done((bf16[128,576]{1,0:T(8,128)(2,1)S(1)}, bf16[128,576]{1,0:T(8,128)(2,1)S(1)}, u32[]{:S(2)}, u32[]{:S(2)}) %collective-permute-start.16) | collective-permute-done | bytes 147488 | tf_op jit(solution)/shard_map/ppermute | solution.py:594
  94.9 1.6 %collective-permute-done.17.refs_2_ = bf16[128,576]{1,0:T(8,128)(2,1)S(1)} collective-permute-done((bf16[128,576]{1,0:T(8,128)(2,1)S(1)}, bf16[128,576]{1,0:T(8,128)(2,1)S(1)}, u32[]{:S(2)}, u32[]{:S(2)}) %collective-permute-start.17) | collective-permute-done | bytes 147488 | tf_op jit(solution)/shard_map/ppermute | solution.py:594
  96.5 11.8 %collective-permute-start.22 = (bf16[128,576]{1,0:T(8,128)(2,1)S(1)}, bf16[128,576]{1,0:T(8,128)(2,1)S(1)}, u32[]{:S(2)}, u32[]{:S(2)}) collective-permute-start(bf16[128,576]{1,0:T(8,128)(2,1)S(1)} %get-tuple-element.87), channel_id=1, source_target_pairs={{0,4},{4,0},{8,12},{12,8},{16,20},{20,16},{24,28},{28,24},{1,5},{5... | collective-permute-start | bytes 442376 | tf_op jit(solution)/shard_map/ppermute | solution.py:594
  108.3 4.7 %collective-permute-done.18.refs_3_ = bf16[128,576]{1,0:T(8,128)(2,1)S(1)} collective-permute-done((bf16[128,576]{1,0:T(8,128)(2,1)S(1)}, bf16[128,576]{1,0:T(8,128)(2,1)S(1)}, u32[]{:S(2)}, u32[]{:S(2)}) %collective-permute-start.18) | collective-permute-done | bytes 147488 | tf_op jit(solution)/shard_map/ppermute | solution.py:594
  112.9 3.8 %collective-permute-done.19.refs_4_ = bf16[128,576]{1,0:T(8,128)(2,1)S(1)} collective-permute-done((bf16[128,576]{1,0:T(8,128)(2,1)S(1)}, bf16[128,576]{1,0:T(8,128)(2,1)S(1)}, u32[]{:S(2)}, u32[]{:S(2)}) %collective-permute-start.19) | collective-permute-done | bytes 147488 | tf_op jit(solution)/shard_map/ppermute | solution.py:594
  116.8 3.8 %final.1 = bf16[1024,1152]{1,0:T(8,128)(2,1)} custom-call(bf16[128,576]{1,0:T(8,128)(2,1)S(1)} %get-tuple-element.80.refs_0_, bf16[128,576]{1,0:T(8,128)(2,1)S(1)} %collective-permute-done.16.refs_1_, bf16[128,576]{1,0:T(8,128)(2,1)S(1)} %collective-permute-done.17.refs_2_, bf16[128,576]{1,0:T(8,128)(2,1)S(1)} %collective-permute-done.18.refs_3_, ...), custom_call_target="tpu_custom_call" | custom-call | flops 2000000000 | bytes 6291456 | tf_op jit(solution)/shard_map/final/pallas_call | solution.py:564
  (52 shorter events, 1.3 us)
Async XLA Ops:
  0.0 5.1 %copy-start.12 = (s32[1,16,9]{1,0,2:T(1,128)S(1)}, s32[1,16,9]{1,0,2:T(1,128)}, u32[]{:S(2)}) copy-start(s32[1,16,9]{1,0,2:T(1,128)} %param.12) | copy-start | bytes 1732
  1.4 29.0 %collective-permute-start = (bf16[256,1152]{1,0:T(8,128)(2,1)S(1)}, bf16[256,1152]{1,0:T(8,128)(2,1)S(1)}, u32[]{:S(2)}, u32[]{:S(2)}) collective-permute-start(bf16[256,1152]{1,0:T(8,128)(2,1)S(1)} %bitcast.15), channel_id=1, source_target_pairs={{0,1},{1,2},{2,3},{4,5},{5,6},{6,7},{8,9},{9,10},{10,11},{12,13},{... | collective-permute-start | bytes 1769480 | tf_op jit(solution)/shard_map/ppermute | solution.py:582
  3.8 28.6 %collective-permute-start.1 = (bf16[256,1152]{1,0:T(8,128)(2,1)S(1)}, bf16[256,1152]{1,0:T(8,128)(2,1)S(1)}, u32[]{:S(2)}, u32[]{:S(2)}) collective-permute-start(bf16[256,1152]{1,0:T(8,128)(2,1)S(1)} %bitcast.14), channel_id=1, source_target_pairs={{1,0},{2,1},{3,2},{5,4},{6,5},{7,6},{9,8},{10,9},{11,10},{13,12},{... | collective-permute-start | bytes 1769480 | tf_op jit(solution)/shard_map/ppermute | solution.py:582
  5.8 29.0 %copy-start = (bf16[1152,1728]{0,1:T(8,128)(2,1)S(1)}, bf16[1152,1728]{0,1:T(8,128)(2,1)}, u32[]{:S(2)}) copy-start(bf16[1152,1728]{0,1:T(8,128)(2,1)} %param.8) | copy-start | bytes 11943940
  23.9 22.6 %collective-permute-start.9 = (bf16[64,1152]{1,0:T(8,128)(2,1)}, bf16[64,1152]{1,0:T(8,128)(2,1)S(1)}, u32[]{:S(2)}, u32[]{:S(2)}) collective-permute-start(bf16[64,1152]{1,0:T(8,128)(2,1)} %get-tuple-element.65), channel_id=1, source_target_pairs={{0,28},{4,24},{8,20},{12,16},{16,12},{20,8},{24,4},{28,0},{1,29},{... | collective-permute-start | bytes 442376 | tf_op jit(solution)/shard_map/ppermute | solution.py:594
  29.4 18.0 %collective-permute-start.10 = (bf16[64,1152]{1,0:T(8,128)(2,1)}, bf16[64,1152]{1,0:T(8,128)(2,1)S(1)}, u32[]{:S(2)}, u32[]{:S(2)}) collective-permute-start(bf16[64,1152]{1,0:T(8,128)(2,1)} %get-tuple-element.66), channel_id=1, source_target_pairs={{0,24},{4,28},{8,16},{12,20},{16,8},{20,12},{24,0},{28,4},{1,25},{... | collective-permute-start | bytes 442376 | tf_op jit(solution)/shard_map/ppermute | solution.py:594
  29.6 22.5 %collective-permute-start.11 = (bf16[64,1152]{1,0:T(8,128)(2,1)}, bf16[64,1152]{1,0:T(8,128)(2,1)S(1)}, u32[]{:S(2)}, u32[]{:S(2)}) collective-permute-start(bf16[64,1152]{1,0:T(8,128)(2,1)} %get-tuple-element.67), channel_id=1, source_target_pairs={{0,20},{4,16},{8,28},{12,24},{16,4},{20,0},{24,12},{28,8},{1,21},{... | collective-permute-start | bytes 442376 | tf_op jit(solution)/shard_map/ppermute | solution.py:594
  30.4 24.6 %collective-permute-start.12 = (bf16[64,1152]{1,0:T(8,128)(2,1)}, bf16[64,1152]{1,0:T(8,128)(2,1)S(1)}, u32[]{:S(2)}, u32[]{:S(2)}) collective-permute-start(bf16[64,1152]{1,0:T(8,128)(2,1)} %get-tuple-element.68), channel_id=1, source_target_pairs={{0,16},{4,20},{8,24},{12,28},{16,0},{20,4},{24,8},{28,12},{1,17},{... | collective-permute-start | bytes 442376 | tf_op jit(solution)/shard_map/ppermute | solution.py:594
  32.4 24.5 %collective-permute-start.13 = (bf16[64,1152]{1,0:T(8,128)(2,1)}, bf16[64,1152]{1,0:T(8,128)(2,1)S(1)}, u32[]{:S(2)}, u32[]{:S(2)}) collective-permute-start(bf16[64,1152]{1,0:T(8,128)(2,1)} %get-tuple-element.69), channel_id=1, source_target_pairs={{0,12},{4,8},{8,4},{12,0},{16,28},{20,24},{24,20},{28,16},{1,13},{... | collective-permute-start | bytes 442376 | tf_op jit(solution)/shard_map/ppermute | solution.py:594
  34.7 3.9 %copy-start.6 = (s32[1,16]{1,0:T(1,128)S(1)}, s32[1,16]{1,0:T(1,128)}, u32[]{:S(2)}) copy-start(s32[1,16]{1,0:T(1,128)} %counts_ref.3) | copy-start | bytes 196
  34.8 3.9 %copy-start.7 = (bf16[1024,1152]{1,0:T(8,128)(2,1)S(1)}, bf16[1024,1152]{1,0:T(8,128)(2,1)}, u32[]{:S(2)}) copy-start(bf16[1024,1152]{1,0:T(8,128)(2,1)} %get-tuple-element.55._) | copy-start | bytes 7077892
  40.0 6.6 %copy-start.14 = (bf16[64,1152]{1,0:T(8,128)(2,1)S(1)}, bf16[64,1152]{1,0:T(8,128)(2,1)}, u32[]{:S(2)}) copy-start(bf16[64,1152]{1,0:T(8,128)(2,1)} %get-tuple-element.70) | copy-start | bytes 442372
  40.0 7.4 %copy-start.13 = (bf16[64,1152]{1,0:T(8,128)(2,1)S(1)}, bf16[64,1152]{1,0:T(8,128)(2,1)}, u32[]{:S(2)}) copy-start(bf16[64,1152]{1,0:T(8,128)(2,1)} %get-tuple-element.71) | copy-start | bytes 442372
  40.0 28.5 %copy-start.3 = (bf16[1152,1728]{0,1:T(8,128)(2,1)S(1)}, bf16[1152,1728]{0,1:T(8,128)(2,1)}, u32[]{:S(2)}) copy-start(bf16[1152,1728]{0,1:T(8,128)(2,1)} %param.10) | copy-start | bytes 11943940
  40.0 28.5 %copy-start.11 = (bf16[64,1152]{1,0:T(8,128)(2,1)S(1)}, bf16[64,1152]{1,0:T(8,128)(2,1)}, u32[]{:S(2)}) copy-start(bf16[64,1152]{1,0:T(8,128)(2,1)} %get-tuple-element.64.refs_0_) | copy-start | bytes 442372
  46.6 18.2 %collective-permute-start.14 = (bf16[64,1152]{1,0:T(8,128)(2,1)S(1)}, bf16[64,1152]{1,0:T(8,128)(2,1)S(1)}, u32[]{:S(2)}, u32[]{:S(2)}) collective-permute-start(bf16[64,1152]{1,0:T(8,128)(2,1)S(1)} %copy-done.14), channel_id=1, source_target_pairs={{0,8},{4,12},{8,0},{12,4},{16,24},{20,28},{24,16},{28,20},{1,9},{5... | collective-permute-start | bytes 442376 | tf_op jit(solution)/shard_map/ppermute | solution.py:594
  47.4 17.4 %collective-permute-start.15 = (bf16[64,1152]{1,0:T(8,128)(2,1)S(1)}, bf16[64,1152]{1,0:T(8,128)(2,1)S(1)}, u32[]{:S(2)}, u32[]{:S(2)}) collective-permute-start(bf16[64,1152]{1,0:T(8,128)(2,1)S(1)} %copy-done.13), channel_id=1, source_target_pairs={{0,4},{4,0},{8,12},{12,8},{16,20},{20,16},{24,28},{28,24},{1,5},{5... | collective-permute-start | bytes 442376 | tf_op jit(solution)/shard_map/ppermute | solution.py:594
  52.1 15.0 %collective-permute-start.2 = (bf16[64,1152]{1,0:T(8,128)(2,1)S(1)}, bf16[64,1152]{1,0:T(8,128)(2,1)S(1)}, u32[]{:S(2)}, u32[]{:S(2)}) collective-permute-start(bf16[64,1152]{1,0:T(8,128)(2,1)S(1)} %get-tuple-element.57), channel_id=1, source_target_pairs={{0,28},{4,24},{8,20},{12,16},{16,12},{20,8},{24,4},{28,0},{1,29},{... | collective-permute-start | bytes 442376 | tf_op jit(solution)/shard_map/ppermute | solution.py:594
  55.0 12.2 %collective-permute-start.3 = (bf16[64,1152]{1,0:T(8,128)(2,1)S(1)}, bf16[64,1152]{1,0:T(8,128)(2,1)S(1)}, u32[]{:S(2)}, u32[]{:S(2)}) collective-permute-start(bf16[64,1152]{1,0:T(8,128)(2,1)S(1)} %get-tuple-element.58), channel_id=1, source_target_pairs={{0,24},{4,28},{8,16},{12,20},{16,8},{20,12},{24,0},{28,4},{1,25},{... | collective-permute-start | bytes 442376 | tf_op jit(solution)/shard_map/ppermute | solution.py:594
  56.9 20.0 %collective-permute-start.4 = (bf16[64,1152]{1,0:T(8,128)(2,1)S(1)}, bf16[64,1152]{1,0:T(8,128)(2,1)S(1)}, u32[]{:S(2)}, u32[]{:S(2)}) collective-permute-start(bf16[64,1152]{1,0:T(8,128)(2,1)S(1)} %get-tuple-element.59), channel_id=1, source_target_pairs={{0,20},{4,16},{8,28},{12,24},{16,4},{20,0},{24,12},{28,8},{1,21},{... | collective-permute-start | bytes 442376 | tf_op jit(solution)/shard_map/ppermute | solution.py:594
  64.8 15.5 %collective-permute-start.5 = (bf16[64,1152]{1,0:T(8,128)(2,1)S(1)}, bf16[64,1152]{1,0:T(8,128)(2,1)S(1)}, u32[]{:S(2)}, u32[]{:S(2)}) collective-permute-start(bf16[64,1152]{1,0:T(8,128)(2,1)S(1)} %get-tuple-element.60), channel_id=1, source_target_pairs={{0,16},{4,20},{8,24},{12,28},{16,0},{20,4},{24,8},{28,12},{1,17},{... | collective-permute-start | bytes 442376 | tf_op jit(solution)/shard_map/ppermute | solution.py:594
  64.8 15.5 %collective-permute-start.6 = (bf16[64,1152]{1,0:T(8,128)(2,1)S(1)}, bf16[64,1152]{1,0:T(8,128)(2,1)S(1)}, u32[]{:S(2)}, u32[]{:S(2)}) collective-permute-start(bf16[64,1152]{1,0:T(8,128)(2,1)S(1)} %get-tuple-element.61), channel_id=1, source_target_pairs={{0,12},{4,8},{8,4},{12,0},{16,28},{20,24},{24,20},{28,16},{1,13},{... | collective-permute-start | bytes 442376 | tf_op jit(solution)/shard_map/ppermute | solution.py:594
  67.1 13.2 %collective-permute-start.7 = (bf16[64,1152]{1,0:T(8,128)(2,1)S(1)}, bf16[64,1152]{1,0:T(8,128)(2,1)S(1)}, u32[]{:S(2)}, u32[]{:S(2)}) collective-permute-start(bf16[64,1152]{1,0:T(8,128)(2,1)S(1)} %get-tuple-element.62), channel_id=1, source_target_pairs={{0,8},{4,12},{8,0},{12,4},{16,24},{20,28},{24,16},{28,20},{1,9},{5... | collective-permute-start | bytes 442376 | tf_op jit(solution)/shard_map/ppermute | solution.py:594
  67.2 13.1 %collective-permute-start.8 = (bf16[64,1152]{1,0:T(8,128)(2,1)S(1)}, bf16[64,1152]{1,0:T(8,128)(2,1)S(1)}, u32[]{:S(2)}, u32[]{:S(2)}) collective-permute-start(bf16[64,1152]{1,0:T(8,128)(2,1)S(1)} %get-tuple-element.63), channel_id=1, source_target_pairs={{0,4},{4,0},{8,12},{12,8},{16,20},{20,16},{24,28},{28,24},{1,5},{5... | collective-permute-start | bytes 442376 | tf_op jit(solution)/shard_map/ppermute | solution.py:594
  80.3 36.4 %copy-start.5 = (bf16[576,1152]{1,0:T(8,128)(2,1)S(1)}, bf16[576,1152]{1,0:T(8,128)(2,1)}, u32[]{:S(2)}) copy-start(bf16[576,1152]{1,0:T(8,128)(2,1)} %refs_9_.1) | copy-start | bytes 3981316
  85.5 9.3 %collective-permute-start.16 = (bf16[128,576]{1,0:T(8,128)(2,1)S(1)}, bf16[128,576]{1,0:T(8,128)(2,1)S(1)}, u32[]{:S(2)}, u32[]{:S(2)}) collective-permute-start(bf16[128,576]{1,0:T(8,128)(2,1)S(1)} %get-tuple-element.81), channel_id=1, source_target_pairs={{0,28},{4,24},{8,20},{12,16},{16,12},{20,8},{24,4},{28,0},{1,29},{... | collective-permute-start | bytes 442376 | tf_op jit(solution)/shard_map/ppermute | solution.py:594
  87.5 9.0 %collective-permute-start.17 = (bf16[128,576]{1,0:T(8,128)(2,1)S(1)}, bf16[128,576]{1,0:T(8,128)(2,1)S(1)}, u32[]{:S(2)}, u32[]{:S(2)}) collective-permute-start(bf16[128,576]{1,0:T(8,128)(2,1)S(1)} %get-tuple-element.82), channel_id=1, source_target_pairs={{0,24},{4,28},{8,16},{12,20},{16,8},{20,12},{24,0},{28,4},{1,25},{... | collective-permute-start | bytes 442376 | tf_op jit(solution)/shard_map/ppermute | solution.py:594
  89.0 23.9 %collective-permute-start.18 = (bf16[128,576]{1,0:T(8,128)(2,1)S(1)}, bf16[128,576]{1,0:T(8,128)(2,1)S(1)}, u32[]{:S(2)}, u32[]{:S(2)}) collective-permute-start(bf16[128,576]{1,0:T(8,128)(2,1)S(1)} %get-tuple-element.83), channel_id=1, source_target_pairs={{0,20},{4,16},{8,28},{12,24},{16,4},{20,0},{24,12},{28,8},{1,21},{... | collective-permute-start | bytes 442376 | tf_op jit(solution)/shard_map/ppermute | solution.py:594
  89.0 27.7 %collective-permute-start.19 = (bf16[128,576]{1,0:T(8,128)(2,1)S(1)}, bf16[128,576]{1,0:T(8,128)(2,1)S(1)}, u32[]{:S(2)}, u32[]{:S(2)}) collective-permute-start(bf16[128,576]{1,0:T(8,128)(2,1)S(1)} %get-tuple-element.84), channel_id=1, source_target_pairs={{0,16},{4,20},{8,24},{12,28},{16,0},{20,4},{24,8},{28,12},{1,17},{... | collective-permute-start | bytes 442376 | tf_op jit(solution)/shard_map/ppermute | solution.py:594
  93.2 23.6 %collective-permute-start.20 = (bf16[128,576]{1,0:T(8,128)(2,1)S(1)}, bf16[128,576]{1,0:T(8,128)(2,1)S(1)}, u32[]{:S(2)}, u32[]{:S(2)}) collective-permute-start(bf16[128,576]{1,0:T(8,128)(2,1)S(1)} %get-tuple-element.85), channel_id=1, source_target_pairs={{0,12},{4,8},{8,4},{12,0},{16,28},{20,24},{24,20},{28,16},{1,13},{... | collective-permute-start | bytes 442376 | tf_op jit(solution)/shard_map/ppermute | solution.py:594
  94.7 22.0 %collective-permute-start.21 = (bf16[128,576]{1,0:T(8,128)(2,1)S(1)}, bf16[128,576]{1,0:T(8,128)(2,1)S(1)}, u32[]{:S(2)}, u32[]{:S(2)}) collective-permute-start(bf16[128,576]{1,0:T(8,128)(2,1)S(1)} %get-tuple-element.86), channel_id=1, source_target_pairs={{0,8},{4,12},{8,0},{12,4},{16,24},{20,28},{24,16},{28,20},{1,9},{5... | collective-permute-start | bytes 442376 | tf_op jit(solution)/shard_map/ppermute | solution.py:594
  96.5 20.3 %collective-permute-start.22 = (bf16[128,576]{1,0:T(8,128)(2,1)S(1)}, bf16[128,576]{1,0:T(8,128)(2,1)S(1)}, u32[]{:S(2)}, u32[]{:S(2)}) collective-permute-start(bf16[128,576]{1,0:T(8,128)(2,1)S(1)} %get-tuple-element.87), channel_id=1, source_target_pairs={{0,4},{4,0},{8,12},{12,8},{16,20},{20,16},{24,28},{28,24},{1,5},{5... | collective-permute-start | bytes 442376 | tf_op jit(solution)/shard_map/ppermute | solution.py:594
  (6 other events, 20.8 us)

commit v5 on v4

v5 whole, which is shorter than its diff:
```python
import functools

import jax
import jax.numpy as jnp
from jax import lax
from jax.experimental import pallas as pl
from jax.experimental.pallas import tpu as pltpu
from jax.sharding import PartitionSpec as P

HEADS = 8
HD = 72
TH = 4
TW = 16
LANES = 128
PACK = 16
NORM_EPS = 1e-06
NEG = -1e30
LOG2E = 1.4426950408889634
F32 = jnp.float32
BF16 = jnp.bfloat16
INNER = HEADS * HD
WIDE = -(-INNER // LANES) * LANES
PAIR = 2 * HD
PAIRS = HEADS // 2
PAIR_ROWS = PAIR + PACK
TILE = TH * TW
VMEM_LIMIT = 28 * 1024 * 1024
VMEM_WHOLE = 58 * 1024 * 1024


def params(limit=VMEM_LIMIT):
    return pltpu.CompilerParams(vmem_limit_bytes=limit)


def cost(flops, bytes_accessed):
    return pl.CostEstimate(flops=flops, bytes_accessed=bytes_accessed, transcendentals=0)


def nt_dot(a, b):
    return lax.dot_general(a, b, (((1,), (1,)), ((), ())), preferred_element_type=F32)


def nn_dot(a, b):
    return jnp.dot(a, b, preferred_element_type=F32)


def moments(x):
    x = x.astype(F32)
    mean = jnp.mean(x, axis=-1, keepdims=True)
    centred = x - mean
    spread = jnp.mean(centred * centred, axis=-1, keepdims=True)
    return mean, lax.rsqrt(spread + NORM_EPS)


def as_rows(column):
    return jnp.broadcast_to(column, (column.shape[0], LANES)).T[:1]


def tile_order(rows, columns):
    for col in range(columns // TW):
        for row in range(TH):
            yield (col * TH + row) * TW, row * columns + col * TW


def pair_window(pair):
    return pair * PAIR // LANES * LANES, -(-(pair + 1) * PAIR // LANES) * LANES


def two_heads(queries, pair):
    lo, hi = pair_window(pair)
    lane = lax.broadcasted_iota(jnp.int32, queries.shape, 1) + lo
    start = pair * PAIR
    first = jnp.where((lane >= start) & (lane < start + HD), queries, 0)
    second = jnp.where((lane >= start + HD) & (lane < start + PAIR), queries, 0)
    return jnp.concatenate([first, second], axis=0)


def split_queries_keys(prod):
    keys = prod[:, INNER // LANES * LANES :]
    shift = INNER % LANES
    if shift:
        keys = pltpu.roll(keys, keys.shape[1] - shift, 1)
    return prod[:, :WIDE], keys


def row_sums(w):
    return jnp.sum(w.astype(F32), axis=-1, keepdims=True)


def store_values(v_ref, values, lanes):
    for pair in range(PAIRS):
        at = pair * PAIR_ROWS
        v_ref[at : at + PAIR, lanes] = values[pair * PAIR : (pair + 1) * PAIR]
        v_ref[at + PAIR : at + PAIR_ROWS, lanes] = jnp.ones((PACK, values.shape[1]), BF16)


def packed_keys(slab):
    per = slab // LANES
    full = WIDE // slab * per
    for piece in range(WIDE // LANES):
        lanes = pl.ds(piece * LANES, LANES)
        if piece < full:
            yield pl.ds(0, slab), lanes, pl.ds(piece // per * slab, slab), pl.ds(piece % per * LANES, LANES)
        else:
            rows = slab // per
            for part in range(per):
                to = pl.ds(full // per * slab, rows), pl.ds(part * LANES, LANES)
                yield pl.ds(part * rows, rows), lanes, *to


def unpack_halo(halo_ref, k_ref, v_ref):
    size = v_ref.shape[0]
    v_ref[...] = halo_ref[:size, :]
    for rows, lanes, at, to in packed_keys(k_ref.shape[0]):
        k_ref[rows, lanes] = halo_ref[pl.ds(size + at.start, at.size), to]


def visible_bits(tile, count, global_row, tile_cols, slot_num, targets_ref):
    bits = jnp.int32(0)
    for slot in range(slot_num):
        target = targets_ref[0, tile, slot]
        cand = (lax.div(target, tile_cols) - global_row + 1) * tile_cols + lax.rem(target, tile_cols)
        bits = bits | jnp.where(slot < count, jnp.left_shift(1, cand), 0)
    return bits


def hidden(bits, index):
    return (1 - (jnp.right_shift(bits, index) & 1)).astype(F32) * NEG


def attend_tile_row(
    tile_row, tile_rows, columns, targets_ref, counts_ref, q_ref, k_refs, v_refs, p_ref, acc_ref
):
    slab = q_ref.shape[0]
    tile_cols = columns // TW
    slot_num = targets_ref.shape[2]
    global_row = lax.axis_index("row") * tile_rows + tile_row
    left = lax.broadcasted_iota(jnp.int32, (1, 4 * TILE), 1) % (2 * TILE) < TILE
    for duo in range(tile_cols // 2):
        bits = []
        for tile in (2 * duo, 2 * duo + 1):
            tile = tile_row * tile_cols + tile
            bits.append(
                visible_bits(tile, counts_ref[0, tile], global_row, tile_cols, slot_num, targets_ref)
            )
        lowest, highest = max(2 * duo - 1, 0), min(2 * duo + 2, tile_cols - 1)
        span = range(lowest, highest + 1)
        bias = {}
        for j in range(3):
            for col in span:
                at = j * tile_cols + col
                bias[j, col] = jnp.where(left, hidden(bits[0], at), hidden(bits[1], at))
        for pair in range(PAIRS):
            lo, hi = pair_window(pair)
            queries = two_heads(q_ref[2 * duo * TILE : (2 * duo + 2) * TILE, lo:hi], pair)
            scores = {}
            for j, ref in enumerate(k_refs):
                part = nt_dot(ref[lowest * TILE : (highest + 1) * TILE, lo:hi], queries)
                for col in span:
                    at = (col - lowest) * TILE
                    scores[j, col] = part[at : at + TILE] + bias[j, col]
            top = functools.reduce(jnp.maximum, scores.values())
            top = jnp.max(top, axis=0, keepdims=True)
            for (j, col), score in scores.items():
                at = j * slab + col * TILE
                p_ref[duo * PAIRS + pair, at : at + TILE, :] = jnp.exp2(score - top).astype(BF16)

    for duo in range(tile_cols // 2):
        for pair in range(PAIRS):
            out = sum(
                nn_dot(
                    ref[pair * PAIR_ROWS : (pair + 1) * PAIR_ROWS, :],
                    p_ref[duo * PAIRS + pair, j * slab : (j + 1) * slab, :],
                )
                for j, ref in enumerate(v_refs)
            )
            out = out[:PAIR] * (1.0 / out[PAIR : PAIR + 1])
            lanes = slice(2 * duo * TILE, (2 * duo + 2) * TILE)
            acc_ref[pair * PAIR : pair * PAIR + HD, lanes] = out[:HD, : 2 * TILE]
            acc_ref[pair * PAIR + HD : (pair + 1) * PAIR, lanes] = out[HD:, 2 * TILE :]


def peer_of(slot, peers, xor):
    me, j = lax.axis_index("frame"), (peers - slot) % peers
    return me ^ j if xor else lax.rem(me + j, peers)


def hand_out(send_refs, out_ref, group, xor):
    for slot, ref in enumerate(send_refs):
        peer = peer_of(slot, len(send_refs), xor)
        ref[...] = out_ref[pl.ds(pl.multiple_of(peer * group, PACK), group), :]


def inner_kernel(
    group, peers, xor,
    targets_ref, counts_ref, x_hbm, w_ref, wo_ref, q_hbm, k_hbm, v_hbm, edge_hbm, top_hbm, bot_hbm, mixed_ref,
    *rest,
):
    send_refs, rest = rest[:peers], rest[peers:]
    x_ref, q_ref, k_ref, v_ref, sum_ref, col_ref, p_ref, acc_ref, out_ref, x_sem, out_sem, halo_sem = rest
    step = pl.program_id(0)
    tile_rows, tile_cols = x_ref.shape[:2]
    columns = tile_cols * TW
    feat = x_ref.shape[-1]
    slab = tile_cols * TILE
    v_rows = PAIRS * PAIR_ROWS
    low = INNER // LANES * LANES

    def x_copy(at, col):
        return pltpu.make_async_copy(
            x_hbm.at[pl.ds(at * TH, TH), pl.ds(col * TW, TW), :], x_ref.at[at, col], x_sem.at[at, col]
        )

    def out_copies(at):
        rows, wide = pl.ds(at * slab, slab), pl.ds(at * v_rows, v_rows)
        return (
            pltpu.make_async_copy(q_ref.at[at], q_hbm.at[rows], out_sem.at[0, at]),
            pltpu.make_async_copy(k_ref.at[at], k_hbm.at[rows], out_sem.at[1, at]),
            pltpu.make_async_copy(v_ref.at[at], v_hbm.at[wide], out_sem.at[2, at]),
        )

    def edge_copies():
        for part, at in enumerate((0, tile_rows - 1)):
            yield pltpu.make_async_copy(x_ref.at[at], edge_hbm.at[part], out_sem.at[3, part])

    def halo_copies():
        for part, (at, halo) in enumerate(((0, top_hbm), (tile_rows - 1, bot_hbm))):
            yield pltpu.make_async_copy(v_ref.at[at], halo.at[pl.ds(0, v_rows)], halo_sem.at[part, 0])
            for piece, (rows, lanes, to, lane) in enumerate(packed_keys(slab)):
                to = pl.ds(v_rows + to.start, to.size)
                yield pltpu.make_async_copy(
                    k_ref.at[at, rows, lanes], halo.at[to, lane], halo_sem.at[part, 1 + piece]
                )

    def work(first):
        for col in range(tile_cols):
            x_copy(step, col).wait()
        x = x_ref[step].reshape(slab, feat)
        mean, rstd = moments(x)
        if first:
            rows = jnp.concatenate([x, jnp.ones((PACK, feat), BF16)], axis=0)
            q, k = nt_dot(rows, w_ref[:low, :]), nt_dot(rows, w_ref[low : 2 * INNER, :])
            sum_ref[:, :low], sum_ref[:, low:] = q[slab : slab + 1], k[slab : slab + 1]
            q, k = q[:slab], k[:slab]
        else:
            q, k = nt_dot(x, w_ref[:low, :]), nt_dot(x, w_ref[low : 2 * INNER, :])
        q = (q - mean * sum_ref[:, :low]) * (rstd * (LOG2E * HD**-0.5))
        q_ref[step, :, :low] = q.astype(BF16)
        k = (k - mean * sum_ref[:, low:]) * rstd
        if INNER > low:
            q_ref[step, :, low:] = (k[:, : WIDE - low] * (LOG2E * HD**-0.5)).astype(BF16)
            k = pltpu.roll(k, k.shape[1] - (INNER - low), 1)
        k_ref[step] = k.astype(BF16)
        if first:
            col_ref[...] = row_sums(w_ref[2 * INNER :, :])
        values = nt_dot(w_ref[2 * INNER :, :], x) - col_ref[...] * as_rows(mean)
        store_values(v_ref.at[step], (values * as_rows(rstd)).astype(BF16), slice(None))
        for copy in out_copies(step):
            copy.start()

    @pl.when(step == 0)
    def _():
        for col in range(tile_cols):
            x_copy(0, col).start()
        for at in range(1, tile_rows):
            for col in range(tile_cols):
                x_copy(at, col).start()
        work(True)

    @pl.when((step > 0) & (step < tile_rows))
    def _():
        work(False)

    @pl.when(step == tile_rows)
    def _():
        for copy in (*edge_copies(), *halo_copies()):
            copy.start()
        p_ref[...] = jnp.zeros(p_ref.shape, BF16)

    @pl.when(step >= tile_rows)
    def _():
        tile_row = step - tile_rows + 1
        k_refs = [k_ref.at[tile_row + j] for j in (-1, 0, 1)]
        v_refs = [v_ref.at[tile_row + j] for j in (-1, 0, 1)]
        attend_tile_row(
            tile_row, tile_rows, columns, targets_ref, counts_ref, q_ref.at[tile_row],
            k_refs, v_refs, p_ref, acc_ref,
        )
        branch = nn_dot(acc_ref[...].T.astype(BF16), wo_ref[...])
        mixed = (x_ref[tile_row].reshape(slab, feat).astype(F32) + branch).astype(BF16)
        mixed_ref[...] = mixed
        out_ref[pl.ds(pl.multiple_of((tile_row - 1) * slab, slab), slab), :] = mixed

    @pl.when(step == 2 * tile_rows - 3)
    def _():
        hand_out(send_refs, out_ref, group, xor)
        for at in range(tile_rows):
            for copy in out_copies(at):
                copy.wait()
        for copy in (*edge_copies(), *halo_copies()):
            copy.wait()


def spatial_inner(x, w, wo, targets, counts, peers, xor):
    rows, columns, feat = x.shape
    tile_rows = rows // TH
    slab = TH * columns
    v_rows = PAIRS * PAIR_ROWS
    group = (tile_rows - 2) * slab // peers
    smem = pl.BlockSpec(memory_space=pltpu.SMEM)
    hbm, vmem = pl.BlockSpec(memory_space=pltpu.HBM), pl.BlockSpec(memory_space=pltpu.VMEM)
    outs = pl.pallas_call(
        functools.partial(inner_kernel, group, peers, xor),
        grid=(2 * tile_rows - 2,),
        in_specs=[smem, smem, hbm, vmem, vmem],
        out_specs=[hbm] * 6 + [pl.BlockSpec((slab, feat), lambda i: (jnp.maximum(i - tile_rows, 0), 0))]
        + [pl.BlockSpec((group, feat), lambda i: (0, 0))] * peers,
        out_shape=[
            jax.ShapeDtypeStruct((tile_rows * slab, WIDE), BF16),
            jax.ShapeDtypeStruct((tile_rows * slab, WIDE), BF16),
            jax.ShapeDtypeStruct((tile_rows * v_rows, slab), BF16),
            jax.ShapeDtypeStruct((2, columns // TW, TH, TW, feat), BF16),
            jax.ShapeDtypeStruct((v_rows + WIDE, slab), BF16),
            jax.ShapeDtypeStruct((v_rows + WIDE, slab), BF16),
            jax.ShapeDtypeStruct(((tile_rows - 2) * slab, feat), BF16),
        ]
        + [jax.ShapeDtypeStruct((group, feat), BF16)] * peers,
        scratch_shapes=[
            pltpu.VMEM((tile_rows, columns // TW, TH, TW, feat), BF16),
            pltpu.VMEM((tile_rows, slab, WIDE), BF16),
            pltpu.VMEM((tile_rows, slab, WIDE), BF16),
            pltpu.VMEM((tile_rows, v_rows, slab), BF16),
            pltpu.VMEM((1, 2 * INNER), F32),
            pltpu.VMEM((INNER, 1), F32),
            pltpu.VMEM((columns // TW // 2 * PAIRS, 3 * slab, 4 * TILE), BF16),
            pltpu.VMEM((INNER, slab), F32),
            pltpu.VMEM(((tile_rows - 2) * slab, feat), BF16),
            pltpu.SemaphoreType.DMA((tile_rows, columns // TW)),
            pltpu.SemaphoreType.DMA((4, tile_rows)),
            pltpu.SemaphoreType.DMA((2, 1 + len(list(packed_keys(slab))))),
        ],
        compiler_params=params(VMEM_WHOLE),
        cost_estimate=cost(12 * 10**9, 16 * 2**20),
        name="spatial_inner",
    )(targets, counts, x, w, wo)
    return outs[:3], outs[3].reshape(2 * slab, feat), outs[4:6], outs[6], outs[7:]


def edges_kernel(
    group, peers, xor, tile_rows, columns,
    targets_ref, counts_ref, x_ref, q_ref, k0, k1, k2, v0, v1, v2, top_ref, bot_ref, w_ref, mixed_ref, *rest,
):
    send_refs, rest = rest[:peers], rest[peers:]
    p_ref, acc_ref, out_ref, k_prev, k_next, v_prev, v_next = rest
    step = pl.program_id(0)
    slab = x_ref.shape[0]

    @pl.when(step == 0)
    def _():
        p_ref[...] = jnp.zeros(p_ref.shape, BF16)
        unpack_halo(top_ref, k_prev, v_prev)
        k_next[...] = k2[...]
        v_next[...] = v2[...]

    @pl.when(step != 0)
    def _():
        k_prev[...] = k0[...]
        v_prev[...] = v0[...]
        unpack_halo(bot_ref, k_next, v_next)

    attend_tile_row(
        step * (tile_rows - 1), tile_rows, columns, targets_ref, counts_ref, q_ref,
        (k_prev, k1, k_next), (v_prev, v1, v_next), p_ref, acc_ref,
    )
    branch = nn_dot(acc_ref[...].T.astype(BF16), w_ref[...])
    mixed = (x_ref[...].astype(F32) + branch).astype(BF16)
    mixed_ref[...] = mixed
    out_ref[pl.ds(pl.multiple_of(step * slab, slab), slab), :] = mixed

    @pl.when(step == 1)
    def _():
        hand_out(send_refs, out_ref, group, xor)


def spatial_edges(x, q, k, v, halos, w, targets, counts, slab, columns, peers, xor):
    feat = x.shape[1]
    tile_rows = q.shape[0] // slab
    group = 2 * slab // peers
    v_rows = PAIRS * PAIR_ROWS
    at = lambda i: i * (tile_rows - 1)
    smem = pl.BlockSpec(memory_space=pltpu.SMEM)
    whole = lambda *shape: pl.BlockSpec(shape, lambda i: (0, 0))
    in_specs = [
        smem,
        smem,
        pl.BlockSpec((slab, feat), lambda i: (i, 0)),
        pl.BlockSpec((slab, WIDE), lambda i: (at(i), 0)),
    ]
    for block in ((slab, WIDE), (v_rows, slab)):
        in_specs += [
            pl.BlockSpec(block, lambda i: (tile_rows - 2, 0)),
            pl.BlockSpec(block, lambda i: (at(i), 0)),
            pl.BlockSpec(block, lambda i: (1, 0)),
        ]
    in_specs += [whole(*halo.shape) for halo in halos]
    in_specs.append(whole(*w.shape))
    outs = pl.pallas_call(
        functools.partial(edges_kernel, group, peers, xor, tile_rows, columns),
        grid=(2,),
        in_specs=in_specs,
        out_specs=[pl.BlockSpec((slab, feat), lambda i: (i, 0))]
        + [whole(group, feat)] * peers,
        out_shape=[jax.ShapeDtypeStruct((2 * slab, feat), BF16)]
        + [jax.ShapeDtypeStruct((group, feat), BF16)] * peers,
        scratch_shapes=[
            pltpu.VMEM((columns // TW // 2 * PAIRS, 3 * slab, 4 * TILE), BF16),
            pltpu.VMEM((INNER, slab), F32),
            pltpu.VMEM((2 * slab, feat), BF16),
            pltpu.VMEM((slab, WIDE), BF16),
            pltpu.VMEM((slab, WIDE), BF16),
            pltpu.VMEM((v_rows, slab), BF16),
            pltpu.VMEM((v_rows, slab), BF16),
        ],
        compiler_params=params(),
        cost_estimate=cost(6 * 10**9, 8 * 2**20),
        name="spatial_edges",
    )(targets, counts, x, q, k, k, k, v, v, v, *halos, w)
    return outs[0], outs[1:]


def temporal_kernel(peers, group, early, *refs):
    in_refs, w_ref, early_refs = refs[:peers], refs[peers], refs[peers + 1 : -6 - peers]
    out_refs, (x_ref, q_ref, k_ref, v_ref, p_ref, acc_ref) = refs[-6 - peers : -6], refs[-6:]
    for slot, ref in zip(early, early_refs):
        out_refs[slot][: ref.shape[0], :] = ref[...]
    block = peers * PACK
    parts = group // PACK
    tokens = peers * group

    for part in range(parts):
        for j in range(peers):
            to = pl.ds(part * block + j * PACK, PACK)
            x_ref[to, :] = in_refs[j][pl.ds(part * PACK, PACK), :]
    x_ref[tokens:, :] = jnp.ones((PACK, x_ref.shape[1]), BF16)
    x = x_ref[:tokens, :]
    mean, rstd = moments(x)
    prod = nt_dot(x_ref[...], w_ref[: 2 * INNER, :])
    prod = (prod[:tokens] - mean * prod[tokens : tokens + 1]) * rstd
    q, k = split_queries_keys(prod)
    q_ref[...] = (q * (LOG2E * HD**-0.5)).astype(BF16)
    k_ref[...] = k.astype(BF16)
    w_values = w_ref[2 * INNER :, :]
    values = (nt_dot(w_values, x) - row_sums(w_values) * as_rows(mean)) * as_rows(rstd)
    store_values(v_ref, values.astype(BF16), slice(None))
    row = lax.broadcasted_iota(jnp.int32, (block, 2 * block), 0)
    col = lax.broadcasted_iota(jnp.int32, (block, 2 * block), 1)
    bias = jnp.where(row % PACK == col % PACK, 0.0, NEG).astype(F32)
    for part in range(parts):
        at = part * block
        for pair in range(PAIRS):
            lo, hi = pair_window(pair)
            queries = two_heads(q_ref[at : at + block, lo:hi], pair)
            scores = nt_dot(k_ref[at : at + block, lo:hi], queries) + bias
            expo = jnp.exp2(scores - jnp.max(scores, axis=0, keepdims=True))
            p_ref[part * PAIRS + pair] = expo.astype(BF16)
    for part in range(parts):
        at = part * block
        for pair in range(PAIRS):
            weights = v_ref[pair * PAIR_ROWS : (pair + 1) * PAIR_ROWS, at : at + block]
            out = nn_dot(weights, p_ref[part * PAIRS + pair])
            out = out[:PAIR] * (1.0 / out[PAIR : PAIR + 1])
            acc_ref[pair * PAIR : pair * PAIR + HD, at : at + block] = out[:HD, :block]
            acc_ref[pair * PAIR + HD : (pair + 1) * PAIR, at : at + block] = out[HD:, block:]
    for part in range(parts):
        at = part * block
        heads = acc_ref[:, at : at + block].T.astype(BF16)
        for j in range(peers):
            rows = pl.ds(out_refs[j].shape[0] - group + part * PACK, PACK)
            out_refs[j][rows, :] = heads[j * PACK : (j + 1) * PACK]


def temporal(pieces, w, early=None):
    early = early or {}
    peers = len(pieces)
    group, feat = pieces[0].shape
    tokens = peers * group
    rows = [group + (early[slot].shape[0] if slot in early else 0) for slot in range(peers)]
    return pl.pallas_call(
        functools.partial(temporal_kernel, peers, group, tuple(early)),
        out_shape=[jax.ShapeDtypeStruct((count, INNER), BF16) for count in rows],
        scratch_shapes=[
            pltpu.VMEM((tokens + PACK, feat), BF16),
            pltpu.VMEM((tokens, WIDE), BF16),
            pltpu.VMEM((tokens, WIDE), BF16),
            pltpu.VMEM((PAIRS * PAIR_ROWS, tokens), BF16),
            pltpu.VMEM((group // PACK * PAIRS, peers * PACK, 2 * peers * PACK), BF16),
            pltpu.VMEM((INNER, tokens), F32),
        ],
        compiler_params=params(),
        cost_estimate=cost(4 * 10**9, 6 * 2**20),
        name="temporal",
    )(*pieces, w, *early.values())


def final_kernel(inner, groups, early, xor, columns, *refs):
    in_refs, (first_ref, second_ref, w_ref, out_ref, heads_ref) = refs[:-5], refs[-5:]
    in_refs, early_refs = in_refs[: -len(early)], dict(zip(early, in_refs[-len(early) :]))
    step = pl.program_id(0)
    slab = first_ref.shape[0]
    peers = len(in_refs)

    @pl.when(step == 0)
    def _():
        for slot, ref in enumerate(in_refs):
            peer = peer_of(slot, peers, xor)
            to = pl.ds(pl.multiple_of(peer * groups[0], PACK), groups[0])
            heads_ref[to, :] = early_refs[slot][...] if slot in early_refs else ref[: groups[0], :]
            to = pl.multiple_of(peers * groups[0] + peer * groups[1], PACK)
            heads_ref[pl.ds(to, groups[1]), :] = ref[ref.shape[0] - groups[1] :, :]

    def work(mixed_ref):
        heads = heads_ref[pl.ds(pl.multiple_of(step * slab, slab), slab), :]
        result = mixed_ref[...].astype(F32) + nn_dot(heads, w_ref[...])
        for to, at in tile_order(slab, columns):
            out_ref[pl.ds(at, TW), :] = result[to : to + TW].astype(BF16)

    @pl.when(step < inner)
    def _():
        work(first_ref)

    @pl.when(step >= inner)
    def _():
        work(second_ref)


def final(pieces, early, first, second, w, slab, columns, xor):
    feat = first.shape[1]
    inner = first.shape[0] // slab
    tile_rows = inner + 2
    peers = len(pieces)
    groups = (first.shape[0] // peers, second.shape[0] // peers)
    at = lambda i: jnp.where(i < inner, i + 1, (i - inner) * (tile_rows - 1))
    whole = lambda *shape: pl.BlockSpec(shape, lambda i: (0, 0))
    return pl.pallas_call(
        functools.partial(final_kernel, inner, groups, tuple(early), xor, columns),
        grid=(tile_rows,),
        in_specs=[whole(*piece.shape) for piece in (*pieces, *early.values())]
        + [
            pl.BlockSpec((slab, feat), lambda i: (jnp.minimum(i, inner - 1), 0)),
            pl.BlockSpec((slab, feat), lambda i: (jnp.maximum(i - inner, 0), 0)),
            whole(*w.shape),
        ],
        out_specs=pl.BlockSpec((slab, feat), lambda i: (at(i), 0)),
        out_shape=jax.ShapeDtypeStruct((tile_rows * slab, feat), BF16),
        scratch_shapes=[pltpu.VMEM((tile_rows * slab, INNER), BF16)],
        compiler_params=params(),
        cost_estimate=cost(2 * 10**9, 6 * 2**20),
        name="final",
    )(*pieces, *early.values(), first, second, w)


def neighbours(top, bot):
    size = lax.axis_size("row")
    up = [(i, i + 1) for i in range(size - 1)]
    down = [(j, i) for i, j in up]
    return lax.ppermute(bot, "row", up), lax.ppermute(top, "row", down)


def exchange(pieces, xor, back):
    size = lax.axis_size("frame")
    result = {}
    for slot, piece in pieces.items():
        j = (size - slot) % size
        if xor:
            pairs = [(i, i ^ j) for i in range(size)]
        else:
            pairs = [(i, (i - j if back else i + j) % size) for i in range(size)]
        result[slot] = lax.ppermute(piece, "frame", pairs) if slot else piece
    return result


def by_slot(pieces):
    return dict(enumerate(pieces))


def body(frames_in, spatial_qkv, spatial_out, temporal_qkv, temporal_out, key_tiles, tile_counts):
    _, rows_dev, columns, feat = frames_in.shape
    slab = TH * columns
    peers = lax.axis_size("frame")
    xor = peers & (peers - 1) == 0
    qkv, edges, halos, mixed_a, send_a = spatial_inner(
        frames_in[0], spatial_qkv.T, spatial_out, key_tiles, tile_counts, peers, xor
    )
    got_a = exchange(by_slot(send_a), xor, False)
    halos = neighbours(*halos)
    mixed_b, send_b = spatial_edges(
        edges, *qkv, halos, spatial_out, key_tiles, tile_counts, slab, columns, peers, xor
    )
    got_b = exchange(by_slot(send_b), xor, False)
    heads_a = by_slot(temporal(list(got_a.values()), temporal_qkv.T))
    far = range(1, 1 + peers // 4)
    early = exchange({slot: heads_a.pop(slot) for slot in far}, xor, True)
    heads = by_slot(temporal(list(got_b.values()), temporal_qkv.T, heads_a))
    back = exchange(heads, xor, True)
    out = final(
        list(back.values()), early, mixed_a, mixed_b, temporal_out, slab, columns, xor
    )
    return out.reshape(frames_in.shape)


def solution(mesh):
    in_specs = (
        P("frame", "row", None, None),
        P(),
        P(),
        P(),
        P(),
        P("frame", "row", None),
        P("frame", "row"),
    )
    out_specs = P("frame", "row", None, None)
    return jax.shard_map(body, mesh=mesh, in_specs=in_specs, out_specs=out_specs, check_vma=False)
```

time: 122 us -> 114 us (0.934); the launches traced: 121 us -> 114 us
  Pallas kernels: 42.5 us -> 37.3 us
  starting transfers between devices: 43.5 us -> 39.5 us
  local copies, waits for them, and re-layouts: 3.4 us -> 6.62 us
    pallas_call x4 -> x3, Pallas kernels: 17.8 us -> 13.1 us  [the longest x2 9.3 us: temporal(): pl.pallas_call(functools.partial(temporal_kernel, peers, group, tuple(ear...]
    unnamed x31 -> x27, local copies, waits for them, and re-layouts: 2.04 us -> 6.62 us
    ppermute x23 -> x25, starting transfers between devices: 43.5 us -> 39.5 us  [the longest x23 35.8 us: exchange(): result[slot] = lax.ppermute(piece, 'frame', pairs) if slot else piece]
    slice x1 -> x0, local copies, waits for them, and re-layouts: 1.35 us -> none  [neighbours(): x[:slab]]
    ppermute x23 -> x25, waiting for transfers between devices: 30.9 us -> 30.5 us  [the longest x23 30.5 us: exchange(): result[slot] = lax.ppermute(piece, 'frame', pairs) if slot else piece]
  transfers between devices with their start and end apart: 23 -> 25, of which waited for: 9 -> 8; matrix products, arithmetic and copies ran while one was open for 1% -> 0% of each run, Pallas kernels for 28% -> 14%
where the time goes in v5:
time: 114 us
  starting transfers between devices  39.5 us (35%)
  Pallas kernels  37.3 us (33%)
  waiting for transfers between devices  30.5 us (27%)
  local copies, waits for them, and re-layouts  6.62 us (6%)
    ppermute x23, starting transfers between devices, exchange(): result[slot] = lax.ppermute(piece, 'frame', pairs) if slot else piece  35.8 us
    ppermute x23, waiting for transfers between devices, exchange(): result[slot] = lax.ppermute(piece, 'frame', pairs) if slot else piece  30.5 us
    pallas_call x1, Pallas kernels, spatial_inner(): pl.pallas_call(functools.partial(inner_kernel, group, peers, xor), grid=(...  17.7 us
    pallas_call x2, Pallas kernels, temporal(): pl.pallas_call(functools.partial(temporal_kernel, peers, group, tuple(ear...  9.3 us
    unnamed x27, local copies, waits for them, and re-layouts  6.62 us
    pallas_call x1, Pallas kernels, spatial_edges(): pl.pallas_call(functools.partial(edges_kernel, group, peers, xor, tile_ro...  6.44 us
    pallas_call x1, Pallas kernels, final(): pl.pallas_call(functools.partial(final_kernel, inner, groups, tuple(early...  3.79 us
    ppermute x2, starting transfers between devices, neighbours(): return (lax.ppermute(bot, 'row', up), lax.ppermute(top, 'row', down))  3.69 us
  transfers between devices with their start and end apart: 25, of which 8 were waited for; matrix products, arithmetic and copies ran while one was open for 0% of the time, Pallas kernels for 14%

profile of v5, /device:TPU:0, one launch (start us, length us, event | category | flops | bytes accessed | tf_op | source)
XLA Modules:
  0.0 114.0 jit_solution(14344041930310094545)
XLA Ops:
  0.0 1.4 %copy.9.targets_ref = s32[1,16,9]{2,1,0:T(8,128)} copy(s32[1,16,9]{1,0,2:T(1,128)} %param.12) | data formatting | bytes 1152 | tf_op args[5]
  1.4 17.7 %spatial_inner.1 = (bf16[1024,640]{1,0:T(8,128)(2,1)}, bf16[1024,640]{1,0:T(8,128)(2,1)}, bf16[2560,256]{1,0:T(8,128)(2,1)}, bf16[2,4,4,16,1152]{4,3,2,1,0:T(8,1...) custom-call(s32[1,16,9]{2,1,0:T(8,128)} %copy.9.targets_ref, ...), custom_call_target="tpu_custom_call" | custom-call | flops 12000000000 | bytes 16777216 | tf_op jit(solution)/shard_map/spatial_inner/pallas_call | solution.py:312
  19.1 2.4 %collective-permute-start = (bf16[1280,256]{1,0:T(8,128)(2,1)}, bf16[1280,256]{1,0:T(8,128)(2,1)S(1)}, u32[]{:S(2)}, u32[]{:S(2)}) collective-permute-start(bf16[1280,256]{1,0:T(8,128)(2,1)} %get-tuple-element.49), channel_id=1, source_target_pairs={{0,1},{1,2},{2,3},{4,5},{5,6},{6,7},{8,9},{9,10},{10,11},{12,13},{... | collective-permute-start | bytes 1966088 | tf_op jit(solution)/shard_map/ppermute | solution.py:566
  21.5 1.3 %collective-permute-start.1 = (bf16[1280,256]{1,0:T(8,128)(2,1)}, bf16[1280,256]{1,0:T(8,128)(2,1)S(1)}, u32[]{:S(2)}, u32[]{:S(2)}) collective-permute-start(bf16[1280,256]{1,0:T(8,128)(2,1)} %get-tuple-element.50), channel_id=1, source_target_pairs={{1,0},{2,1},{3,2},{5,4},{6,5},{7,6},{9,8},{10,9},{11,10},{13,12},{... | collective-permute-start | bytes 1966088 | tf_op jit(solution)/shard_map/ppermute | solution.py:566
  22.8 5.4 %collective-permute-start.9 = (bf16[64,1152]{1,0:T(8,128)(2,1)}, bf16[64,1152]{1,0:T(8,128)(2,1)S(1)}, u32[]{:S(2)}, u32[]{:S(2)}) collective-permute-start(bf16[64,1152]{1,0:T(8,128)(2,1)} %get-tuple-element.60), channel_id=1, source_target_pairs={{0,28},{4,24},{8,20},{12,16},{16,12},{20,8},{24,4},{28,0},{1,29},{... | collective-permute-start | bytes 442376 | tf_op jit(solution)/shard_map/ppermute | solution.py:578
  29.2 2.0 %collective-permute-start.12 = (bf16[64,1152]{1,0:T(8,128)(2,1)}, bf16[64,1152]{1,0:T(8,128)(2,1)S(1)}, u32[]{:S(2)}, u32[]{:S(2)}) collective-permute-start(bf16[64,1152]{1,0:T(8,128)(2,1)} %get-tuple-element.63), channel_id=1, source_target_pairs={{0,16},{4,20},{8,24},{12,28},{16,0},{20,4},{24,8},{28,12},{1,17},{... | collective-permute-start | bytes 442376 | tf_op jit(solution)/shard_map/ppermute | solution.py:578
  31.2 2.4 %collective-permute-start.13 = (bf16[64,1152]{1,0:T(8,128)(2,1)}, bf16[64,1152]{1,0:T(8,128)(2,1)S(1)}, u32[]{:S(2)}, u32[]{:S(2)}) collective-permute-start(bf16[64,1152]{1,0:T(8,128)(2,1)} %get-tuple-element.64), channel_id=1, source_target_pairs={{0,12},{4,8},{8,4},{12,0},{16,28},{20,24},{24,20},{28,16},{1,13},{... | collective-permute-start | bytes 442376 | tf_op jit(solution)/shard_map/ppermute | solution.py:578
  33.6 1.3 %copy-done.5 = bf16[2,4,4,16,1152]{4,3,2,1,0:T(8,128)(2,1)S(1)} copy-done((bf16[2,4,4,16,1152]{4,3,2,1,0:T(8,128)(2,1)S(1)}, bf16[2,4,4,16,1152]{4,3,2,1,0:T(8,128)(2,1)}, u32[]{:S(2)}) %copy-start.5) | copy-done | bytes 1179672
  34.9 1.3 %copy-done.7 = bf16[1024,640]{1,0:T(8,128)(2,1)S(1)} copy-done((bf16[1024,640]{1,0:T(8,128)(2,1)S(1)}, bf16[1024,640]{1,0:T(8,128)(2,1)}, u32[]{:S(2)}) %copy-start.7) | copy-done | bytes 1310744
  36.2 1.3 %copy-done.8 = bf16[1024,640]{1,0:T(8,128)(2,1)S(1)} copy-done((bf16[1024,640]{1,0:T(8,128)(2,1)S(1)}, bf16[1024,640]{1,0:T(8,128)(2,1)}, u32[]{:S(2)}) %copy-start.8) | copy-done | bytes 1310744
  37.5 1.3 %copy-done.9 = bf16[2560,256]{1,0:T(8,128)(2,1)S(1)} copy-done((bf16[2560,256]{1,0:T(8,128)(2,1)S(1)}, bf16[2560,256]{1,0:T(8,128)(2,1)}, u32[]{:S(2)}) %copy-start.9) | copy-done | bytes 1310744
  38.8 6.4 %spatial_edges.1 = (bf16[512,1152]{1,0:T(8,128)(2,1)S(1)}, bf16[64,1152]{1,0:T(8,128)(2,1)S(1)}, bf16[64,1152]{1,0:T(8,128)(2,1)S(1)}, bf16[64,1152]{1,0:T(8,128...) custom-call(s32[1,16,9]{2,1,0:T(8,128)S(1)} %copy-done, ...), custom_call_target="tpu_custom_call" | custom-call | flops 6000000000 | bytes 8388608 | tf_op jit(solution)/shard_map/spatial_edges/pallas_call | solution.py:407
  45.3 0.8 collective-permute-start.14
  46.5 4.4 %collective-permute-done.11.refs_3_ = bf16[64,1152]{1,0:T(8,128)(2,1)S(1)} collective-permute-done((bf16[64,1152]{1,0:T(8,128)(2,1)}, bf16[64,1152]{1,0:T(8,128)(2,1)S(1)}, u32[]{:S(2)}, u32[]{:S(2)}) %collective-permute-start.11) | collective-permute-done | bytes 147488 | tf_op jit(solution)/shard_map/ppermute | solution.py:578
  51.0 2.7 %collective-permute-start.2 = (bf16[64,1152]{1,0:T(8,128)(2,1)S(1)}, bf16[64,1152]{1,0:T(8,128)(2,1)S(1)}, u32[]{:S(2)}, u32[]{:S(2)}) collective-permute-start(bf16[64,1152]{1,0:T(8,128)(2,1)S(1)} %get-tuple-element.52), channel_id=1, source_target_pairs={{0,28},{4,24},{8,20},{12,16},{16,12},{20,8},{24,4},{28,0},{1,29},{... | collective-permute-start | bytes 442376 | tf_op jit(solution)/shard_map/ppermute | solution.py:578
  53.9 1.9 %collective-permute-start.3 = (bf16[64,1152]{1,0:T(8,128)(2,1)S(1)}, bf16[64,1152]{1,0:T(8,128)(2,1)S(1)}, u32[]{:S(2)}, u32[]{:S(2)}) collective-permute-start(bf16[64,1152]{1,0:T(8,128)(2,1)S(1)} %get-tuple-element.53), channel_id=1, source_target_pairs={{0,24},{4,28},{8,16},{12,20},{16,8},{20,12},{24,0},{28,4},{1,25},{... | collective-permute-start | bytes 442376 | tf_op jit(solution)/shard_map/ppermute | solution.py:578
  55.8 7.5 %collective-permute-done.14.refs_6_ = bf16[64,1152]{1,0:T(8,128)(2,1)S(1)} collective-permute-done((bf16[64,1152]{1,0:T(8,128)(2,1)S(1)}, bf16[64,1152]{1,0:T(8,128)(2,1)S(1)}, u32[]{:S(2)}, u32[]{:S(2)}) %collective-permute-start.14) | collective-permute-done | bytes 147488 | tf_op jit(solution)/shard_map/ppermute | solution.py:578
  63.4 2.5 %collective-permute-start.7 = (bf16[64,1152]{1,0:T(8,128)(2,1)S(1)}, bf16[64,1152]{1,0:T(8,128)(2,1)S(1)}, u32[]{:S(2)}, u32[]{:S(2)}) collective-permute-start(bf16[64,1152]{1,0:T(8,128)(2,1)S(1)} %get-tuple-element.57), channel_id=1, source_target_pairs={{0,8},{4,12},{8,0},{12,4},{16,24},{20,28},{24,16},{28,20},{1,9},{5... | collective-permute-start | bytes 442376 | tf_op jit(solution)/shard_map/ppermute | solution.py:578
  65.9 1.0 collective-permute-start.8
  66.8 4.6 %temporal.2 = (bf16[64,576]{1,0:T(8,128)(2,1)S(1)}, bf16[64,576]{1,0:T(8,128)(2,1)S(1)}, bf16[64,576]{1,0:T(8,128)(2,1)S(1)}, bf16[64,576]{1,0:T(8,128)(2,1)S(1)...) custom-call(bf16[64,1152]{1,0:T(8,128)(2,1)S(1)} %copy-done.10, ...), custom_call_target="tpu_custom_call" | custom-call | flops 4000000000 | bytes 6291456 | tf_op jit(solution)/shard_map/temporal/pallas_call | solution.py:488
  71.5 4.3 %collective-permute-done.4.refs_3_ = bf16[64,1152]{1,0:T(8,128)(2,1)S(1)} collective-permute-done((bf16[64,1152]{1,0:T(8,128)(2,1)S(1)}, bf16[64,1152]{1,0:T(8,128)(2,1)S(1)}, u32[]{:S(2)}, u32[]{:S(2)}) %collective-permute-start.4) | collective-permute-done | bytes 147488 | tf_op jit(solution)/shard_map/ppermute | solution.py:578
  75.8 3.0 %collective-permute-start.23 = (bf16[64,576]{1,0:T(8,128)(2,1)S(1)}, bf16[64,576]{1,0:T(8,128)(2,1)S(1)}, u32[]{:S(2)}, u32[]{:S(2)}) collective-permute-start(bf16[64,576]{1,0:T(8,128)(2,1)S(1)} %get-tuple-element.81), channel_id=1, source_target_pairs={{0,28},{4,24},{8,20},{12,16},{16,12},{20,8},{24,4},{28,0},{1,29},{... | collective-permute-start | bytes 221192 | tf_op jit(solution)/shard_map/ppermute | solution.py:578
  79.2 1.9 %collective-permute-start.24 = (bf16[64,576]{1,0:T(8,128)(2,1)S(1)}, bf16[64,576]{1,0:T(8,128)(2,1)S(1)}, u32[]{:S(2)}, u32[]{:S(2)}) collective-permute-start(bf16[64,576]{1,0:T(8,128)(2,1)S(1)} %get-tuple-element.82), channel_id=1, source_target_pairs={{0,24},{4,28},{8,16},{12,20},{16,8},{20,12},{24,0},{28,4},{1,25},{... | collective-permute-start | bytes 221192 | tf_op jit(solution)/shard_map/ppermute | solution.py:578
  81.2 4.7 %temporal.3 = (bf16[128,576]{1,0:T(8,128)(2,1)S(1)}, bf16[64,576]{1,0:T(8,128)(2,1)S(1)}, bf16[64,576]{1,0:T(8,128)(2,1)S(1)}, bf16[128,576]{1,0:T(8,128)(2,1)S(...) custom-call(bf16[64,1152]{1,0:T(8,128)(2,1)S(1)} %get-tuple-element., ...), custom_call_target="tpu_custom_call" | custom-call | flops 4000000000 | bytes 6291456 | tf_op jit(solution)/shard_map/temporal/pallas_call | solution.py:488
  85.8 1.7 %collective-permute-start.16 = (bf16[64,576]{1,0:T(8,128)(2,1)S(1)}, bf16[64,576]{1,0:T(8,128)(2,1)S(1)}, u32[]{:S(2)}, u32[]{:S(2)}) collective-permute-start(bf16[64,576]{1,0:T(8,128)(2,1)S(1)} %get-tuple-element.74), channel_id=1, source_target_pairs={{0,28},{4,24},{8,20},{12,16},{16,12},{20,8},{24,4},{28,0},{1,29},{... | collective-permute-start | bytes 221192 | tf_op jit(solution)/shard_map/ppermute | solution.py:578
  87.5 2.2 %collective-permute-start.17 = (bf16[64,576]{1,0:T(8,128)(2,1)S(1)}, bf16[64,576]{1,0:T(8,128)(2,1)S(1)}, u32[]{:S(2)}, u32[]{:S(2)}) collective-permute-start(bf16[64,576]{1,0:T(8,128)(2,1)S(1)} %get-tuple-element.75), channel_id=1, source_target_pairs={{0,24},{4,28},{8,16},{12,20},{16,8},{20,12},{24,0},{28,4},{1,25},{... | collective-permute-start | bytes 221192 | tf_op jit(solution)/shard_map/ppermute | solution.py:578
  89.7 3.8 %collective-permute-start.19 = (bf16[128,576]{1,0:T(8,128)(2,1)S(1)}, bf16[128,576]{1,0:T(8,128)(2,1)S(1)}, u32[]{:S(2)}, u32[]{:S(2)}) collective-permute-start(bf16[128,576]{1,0:T(8,128)(2,1)S(1)} %get-tuple-element.77), channel_id=1, source_target_pairs={{0,16},{4,20},{8,24},{12,28},{16,0},{20,4},{24,8},{28,12},{1,17},{... | collective-permute-start | bytes 442376 | tf_op jit(solution)/shard_map/ppermute | solution.py:578
  94.0 1.6 %collective-permute-start.21 = (bf16[128,576]{1,0:T(8,128)(2,1)S(1)}, bf16[128,576]{1,0:T(8,128)(2,1)S(1)}, u32[]{:S(2)}, u32[]{:S(2)}) collective-permute-start(bf16[128,576]{1,0:T(8,128)(2,1)S(1)} %get-tuple-element.79), channel_id=1, source_target_pairs={{0,8},{4,12},{8,0},{12,4},{16,24},{20,28},{24,16},{28,20},{1,9},{5... | collective-permute-start | bytes 442376 | tf_op jit(solution)/shard_map/ppermute | solution.py:578
  95.6 1.5 %collective-permute-start.22 = (bf16[128,576]{1,0:T(8,128)(2,1)S(1)}, bf16[128,576]{1,0:T(8,128)(2,1)S(1)}, u32[]{:S(2)}, u32[]{:S(2)}) collective-permute-start(bf16[128,576]{1,0:T(8,128)(2,1)S(1)} %get-tuple-element.80), channel_id=1, source_target_pairs={{0,4},{4,0},{8,12},{12,8},{16,20},{20,16},{24,28},{28,24},{1,5},{5... | collective-permute-start | bytes 442376 | tf_op jit(solution)/shard_map/ppermute | solution.py:578
  97.1 10.7 %collective-permute-done.18.refs_3_ = bf16[128,576]{1,0:T(8,128)(2,1)S(1)} collective-permute-done((bf16[128,576]{1,0:T(8,128)(2,1)S(1)}, bf16[128,576]{1,0:T(8,128)(2,1)S(1)}, u32[]{:S(2)}, u32[]{:S(2)}) %collective-permute-start.18) | collective-permute-done | bytes 147488 | tf_op jit(solution)/shard_map/ppermute | solution.py:578
  107.7 2.4 %collective-permute-done.19.refs_4_ = bf16[128,576]{1,0:T(8,128)(2,1)S(1)} collective-permute-done((bf16[128,576]{1,0:T(8,128)(2,1)S(1)}, bf16[128,576]{1,0:T(8,128)(2,1)S(1)}, u32[]{:S(2)}, u32[]{:S(2)}) %collective-permute-start.19) | collective-permute-done | bytes 147488 | tf_op jit(solution)/shard_map/ppermute | solution.py:578
  110.2 3.8 %final.1 = bf16[1024,1152]{1,0:T(8,128)(2,1)} custom-call(bf16[128,576]{1,0:T(8,128)(2,1)S(1)} %get-tuple-element.73.refs_0_, bf16[64,576]{1,0:T(8,128)(2,1)S(1)} %collective-permute-done.16.refs_1_, bf16[64,576]{1,0:T(8,128)(2,1)S(1)} %collective-permute-done.17.refs_2_, bf16[128,576]{1,0:T(8,128)(2,1)S(1)} %collective-permute-done.18.refs_3_, ...), custom_call_target="tpu_custom_call" | custom-call | flops 2000000000 | bytes 6291456 | tf_op jit(solution)/shard_map/final/pallas_call | solution.py:544
  (50 shorter events, 2.5 us)
Async XLA Ops:
  1.4 32.2 %copy-start = (s32[1,16,9]{2,1,0:T(8,128)S(1)}, s32[1,16,9]{2,1,0:T(8,128)}, u32[]{:S(2)}) copy-start(s32[1,16,9]{2,1,0:T(8,128)} %copy.9.targets_ref) | copy-start | bytes 1732
  1.4 32.2 %copy-start.2 = (bf16[576,1152]{1,0:T(8,128)(2,1)S(1)}, bf16[576,1152]{1,0:T(8,128)(2,1)}, u32[]{:S(2)}) copy-start(bf16[576,1152]{1,0:T(8,128)(2,1)} %w_ref.1) | copy-start | bytes 3981316
  1.4 32.2 %copy-start.4 = (s32[1,16]{1,0:T(1,128)S(1)}, s32[1,16]{1,0:T(1,128)}, u32[]{:S(2)}) copy-start(s32[1,16]{1,0:T(1,128)} %counts_ref.3) | copy-start | bytes 196
  19.1 10.1 %collective-permute-start = (bf16[1280,256]{1,0:T(8,128)(2,1)}, bf16[1280,256]{1,0:T(8,128)(2,1)S(1)}, u32[]{:S(2)}, u32[]{:S(2)}) collective-permute-start(bf16[1280,256]{1,0:T(8,128)(2,1)} %get-tuple-element.49), channel_id=1, source_target_pairs={{0,1},{1,2},{2,3},{4,5},{5,6},{6,7},{8,9},{9,10},{10,11},{12,13},{... | collective-permute-start | bytes 1966088 | tf_op jit(solution)/shard_map/ppermute | solution.py:566
  21.5 9.7 %collective-permute-start.1 = (bf16[1280,256]{1,0:T(8,128)(2,1)}, bf16[1280,256]{1,0:T(8,128)(2,1)S(1)}, u32[]{:S(2)}, u32[]{:S(2)}) collective-permute-start(bf16[1280,256]{1,0:T(8,128)(2,1)} %get-tuple-element.50), channel_id=1, source_target_pairs={{1,0},{2,1},{3,2},{5,4},{6,5},{7,6},{9,8},{10,9},{11,10},{13,12},{... | collective-permute-start | bytes 1966088 | tf_op jit(solution)/shard_map/ppermute | solution.py:566
  22.8 22.5 %collective-permute-start.9 = (bf16[64,1152]{1,0:T(8,128)(2,1)}, bf16[64,1152]{1,0:T(8,128)(2,1)S(1)}, u32[]{:S(2)}, u32[]{:S(2)}) collective-permute-start(bf16[64,1152]{1,0:T(8,128)(2,1)} %get-tuple-element.60), channel_id=1, source_target_pairs={{0,28},{4,24},{8,20},{12,16},{16,12},{20,8},{24,4},{28,0},{1,29},{... | collective-permute-start | bytes 442376 | tf_op jit(solution)/shard_map/ppermute | solution.py:578
  28.2 17.9 %collective-permute-start.10 = (bf16[64,1152]{1,0:T(8,128)(2,1)}, bf16[64,1152]{1,0:T(8,128)(2,1)S(1)}, u32[]{:S(2)}, u32[]{:S(2)}) collective-permute-start(bf16[64,1152]{1,0:T(8,128)(2,1)} %get-tuple-element.61), channel_id=1, source_target_pairs={{0,24},{4,28},{8,16},{12,20},{16,8},{20,12},{24,0},{28,4},{1,25},{... | collective-permute-start | bytes 442376 | tf_op jit(solution)/shard_map/ppermute | solution.py:578
  28.5 22.5 %collective-permute-start.11 = (bf16[64,1152]{1,0:T(8,128)(2,1)}, bf16[64,1152]{1,0:T(8,128)(2,1)S(1)}, u32[]{:S(2)}, u32[]{:S(2)}) collective-permute-start(bf16[64,1152]{1,0:T(8,128)(2,1)} %get-tuple-element.62), channel_id=1, source_target_pairs={{0,20},{4,16},{8,28},{12,24},{16,4},{20,0},{24,12},{28,8},{1,21},{... | collective-permute-start | bytes 442376 | tf_op jit(solution)/shard_map/ppermute | solution.py:578
  29.2 24.6 %collective-permute-start.12 = (bf16[64,1152]{1,0:T(8,128)(2,1)}, bf16[64,1152]{1,0:T(8,128)(2,1)S(1)}, u32[]{:S(2)}, u32[]{:S(2)}) collective-permute-start(bf16[64,1152]{1,0:T(8,128)(2,1)} %get-tuple-element.63), channel_id=1, source_target_pairs={{0,16},{4,20},{8,24},{12,28},{16,0},{20,4},{24,8},{28,12},{1,17},{... | collective-permute-start | bytes 442376 | tf_op jit(solution)/shard_map/ppermute | solution.py:578
  31.2 24.6 %collective-permute-start.13 = (bf16[64,1152]{1,0:T(8,128)(2,1)}, bf16[64,1152]{1,0:T(8,128)(2,1)S(1)}, u32[]{:S(2)}, u32[]{:S(2)}) collective-permute-start(bf16[64,1152]{1,0:T(8,128)(2,1)} %get-tuple-element.64), channel_id=1, source_target_pairs={{0,12},{4,8},{8,4},{12,0},{16,28},{20,24},{24,20},{28,16},{1,13},{... | collective-permute-start | bytes 442376 | tf_op jit(solution)/shard_map/ppermute | solution.py:578
  38.8 28.0 %copy-start.1 = (bf16[1152,1728]{0,1:T(8,128)(2,1)S(1)}, bf16[1152,1728]{0,1:T(8,128)(2,1)}, u32[]{:S(2)}) copy-start(bf16[1152,1728]{0,1:T(8,128)(2,1)} %param.10) | copy-start | bytes 11943940
  38.8 28.0 %copy-start.10 = (bf16[64,1152]{1,0:T(8,128)(2,1)S(1)}, bf16[64,1152]{1,0:T(8,128)(2,1)}, u32[]{:S(2)}) copy-start(bf16[64,1152]{1,0:T(8,128)(2,1)} %get-tuple-element.59.refs_0_) | copy-start | bytes 442372
  45.3 18.0 %collective-permute-start.14 = (bf16[64,1152]{1,0:T(8,128)(2,1)S(1)}, bf16[64,1152]{1,0:T(8,128)(2,1)S(1)}, u32[]{:S(2)}, u32[]{:S(2)}) collective-permute-start(bf16[64,1152]{1,0:T(8,128)(2,1)S(1)} %copy-done.12), channel_id=1, source_target_pairs={{0,8},{4,12},{8,0},{12,4},{16,24},{20,28},{24,16},{28,20},{1,9},{5... | collective-permute-start | bytes 442376 | tf_op jit(solution)/shard_map/ppermute | solution.py:578
  46.1 17.2 %collective-permute-start.15 = (bf16[64,1152]{1,0:T(8,128)(2,1)S(1)}, bf16[64,1152]{1,0:T(8,128)(2,1)S(1)}, u32[]{:S(2)}, u32[]{:S(2)}) collective-permute-start(bf16[64,1152]{1,0:T(8,128)(2,1)S(1)} %copy-done.11), channel_id=1, source_target_pairs={{0,4},{4,0},{8,12},{12,8},{16,20},{20,16},{24,28},{28,24},{1,5},{5... | collective-permute-start | bytes 442376 | tf_op jit(solution)/shard_map/ppermute | solution.py:578
  51.0 12.4 %collective-permute-start.2 = (bf16[64,1152]{1,0:T(8,128)(2,1)S(1)}, bf16[64,1152]{1,0:T(8,128)(2,1)S(1)}, u32[]{:S(2)}, u32[]{:S(2)}) collective-permute-start(bf16[64,1152]{1,0:T(8,128)(2,1)S(1)} %get-tuple-element.52), channel_id=1, source_target_pairs={{0,28},{4,24},{8,20},{12,16},{16,12},{20,8},{24,4},{28,0},{1,29},{... | collective-permute-start | bytes 442376 | tf_op jit(solution)/shard_map/ppermute | solution.py:578
  53.9 12.0 %collective-permute-start.3 = (bf16[64,1152]{1,0:T(8,128)(2,1)S(1)}, bf16[64,1152]{1,0:T(8,128)(2,1)S(1)}, u32[]{:S(2)}, u32[]{:S(2)}) collective-permute-start(bf16[64,1152]{1,0:T(8,128)(2,1)S(1)} %get-tuple-element.53), channel_id=1, source_target_pairs={{0,24},{4,28},{8,16},{12,20},{16,8},{20,12},{24,0},{28,4},{1,25},{... | collective-permute-start | bytes 442376 | tf_op jit(solution)/shard_map/ppermute | solution.py:578
  55.8 20.0 %collective-permute-start.4 = (bf16[64,1152]{1,0:T(8,128)(2,1)S(1)}, bf16[64,1152]{1,0:T(8,128)(2,1)S(1)}, u32[]{:S(2)}, u32[]{:S(2)}) collective-permute-start(bf16[64,1152]{1,0:T(8,128)(2,1)S(1)} %get-tuple-element.54), channel_id=1, source_target_pairs={{0,20},{4,16},{8,28},{12,24},{16,4},{20,0},{24,12},{28,8},{1,21},{... | collective-permute-start | bytes 442376 | tf_op jit(solution)/shard_map/ppermute | solution.py:578
  63.3 15.9 %collective-permute-start.5 = (bf16[64,1152]{1,0:T(8,128)(2,1)S(1)}, bf16[64,1152]{1,0:T(8,128)(2,1)S(1)}, u32[]{:S(2)}, u32[]{:S(2)}) collective-permute-start(bf16[64,1152]{1,0:T(8,128)(2,1)S(1)} %get-tuple-element.55), channel_id=1, source_target_pairs={{0,16},{4,20},{8,24},{12,28},{16,0},{20,4},{24,8},{28,12},{1,17},{... | collective-permute-start | bytes 442376 | tf_op jit(solution)/shard_map/ppermute | solution.py:578
  63.3 17.8 %collective-permute-start.6 = (bf16[64,1152]{1,0:T(8,128)(2,1)S(1)}, bf16[64,1152]{1,0:T(8,128)(2,1)S(1)}, u32[]{:S(2)}, u32[]{:S(2)}) collective-permute-start(bf16[64,1152]{1,0:T(8,128)(2,1)S(1)} %get-tuple-element.56), channel_id=1, source_target_pairs={{0,12},{4,8},{8,4},{12,0},{16,28},{20,24},{24,20},{28,16},{1,13},{... | collective-permute-start | bytes 442376 | tf_op jit(solution)/shard_map/ppermute | solution.py:578
  63.4 17.8 %collective-permute-start.7 = (bf16[64,1152]{1,0:T(8,128)(2,1)S(1)}, bf16[64,1152]{1,0:T(8,128)(2,1)S(1)}, u32[]{:S(2)}, u32[]{:S(2)}) collective-permute-start(bf16[64,1152]{1,0:T(8,128)(2,1)S(1)} %get-tuple-element.57), channel_id=1, source_target_pairs={{0,8},{4,12},{8,0},{12,4},{16,24},{20,28},{24,16},{28,20},{1,9},{5... | collective-permute-start | bytes 442376 | tf_op jit(solution)/shard_map/ppermute | solution.py:578
  65.9 15.3 %collective-permute-start.8 = (bf16[64,1152]{1,0:T(8,128)(2,1)S(1)}, bf16[64,1152]{1,0:T(8,128)(2,1)S(1)}, u32[]{:S(2)}, u32[]{:S(2)}) collective-permute-start(bf16[64,1152]{1,0:T(8,128)(2,1)S(1)} %get-tuple-element.58), channel_id=1, source_target_pairs={{0,4},{4,0},{8,12},{12,8},{16,20},{20,16},{24,28},{28,24},{1,5},{5... | collective-permute-start | bytes 442376 | tf_op jit(solution)/shard_map/ppermute | solution.py:578
  75.8 13.9 %collective-permute-start.23 = (bf16[64,576]{1,0:T(8,128)(2,1)S(1)}, bf16[64,576]{1,0:T(8,128)(2,1)S(1)}, u32[]{:S(2)}, u32[]{:S(2)}) collective-permute-start(bf16[64,576]{1,0:T(8,128)(2,1)S(1)} %get-tuple-element.81), channel_id=1, source_target_pairs={{0,28},{4,24},{8,20},{12,16},{16,12},{20,8},{24,4},{28,0},{1,29},{... | collective-permute-start | bytes 221192 | tf_op jit(solution)/shard_map/ppermute | solution.py:578
  79.2 14.3 %collective-permute-start.24 = (bf16[64,576]{1,0:T(8,128)(2,1)S(1)}, bf16[64,576]{1,0:T(8,128)(2,1)S(1)}, u32[]{:S(2)}, u32[]{:S(2)}) collective-permute-start(bf16[64,576]{1,0:T(8,128)(2,1)S(1)} %get-tuple-element.82), channel_id=1, source_target_pairs={{0,24},{4,28},{8,16},{12,20},{16,8},{20,12},{24,0},{28,4},{1,25},{... | collective-permute-start | bytes 221192 | tf_op jit(solution)/shard_map/ppermute | solution.py:578
  81.1 29.0 %copy-start.3 = (bf16[576,1152]{1,0:T(8,128)(2,1)S(1)}, bf16[576,1152]{1,0:T(8,128)(2,1)}, u32[]{:S(2)}) copy-start(bf16[576,1152]{1,0:T(8,128)(2,1)} %refs_12_.1) | copy-start | bytes 3981316
  81.2 29.0 %copy-start.6 = (bf16[512,1152]{1,0:T(8,128)(2,1)S(1)}, bf16[512,1152]{1,0:T(8,128)(2,1)}, u32[]{:S(2)}) copy-start(bf16[512,1152]{1,0:T(8,128)(2,1)} %get-tuple-element.83.refs_10_) | copy-start | bytes 3538948
  85.8 8.1 %collective-permute-start.16 = (bf16[64,576]{1,0:T(8,128)(2,1)S(1)}, bf16[64,576]{1,0:T(8,128)(2,1)S(1)}, u32[]{:S(2)}, u32[]{:S(2)}) collective-permute-start(bf16[64,576]{1,0:T(8,128)(2,1)S(1)} %get-tuple-element.74), channel_id=1, source_target_pairs={{0,28},{4,24},{8,20},{12,16},{16,12},{20,8},{24,4},{28,0},{1,29},{... | collective-permute-start | bytes 221192 | tf_op jit(solution)/shard_map/ppermute | solution.py:578
  87.5 8.1 %collective-permute-start.17 = (bf16[64,576]{1,0:T(8,128)(2,1)S(1)}, bf16[64,576]{1,0:T(8,128)(2,1)S(1)}, u32[]{:S(2)}, u32[]{:S(2)}) collective-permute-start(bf16[64,576]{1,0:T(8,128)(2,1)S(1)} %get-tuple-element.75), channel_id=1, source_target_pairs={{0,24},{4,28},{8,16},{12,20},{16,8},{20,12},{24,0},{28,4},{1,25},{... | collective-permute-start | bytes 221192 | tf_op jit(solution)/shard_map/ppermute | solution.py:578
  89.7 18.1 %collective-permute-start.18 = (bf16[128,576]{1,0:T(8,128)(2,1)S(1)}, bf16[128,576]{1,0:T(8,128)(2,1)S(1)}, u32[]{:S(2)}, u32[]{:S(2)}) collective-permute-start(bf16[128,576]{1,0:T(8,128)(2,1)S(1)} %get-tuple-element.76), channel_id=1, source_target_pairs={{0,20},{4,16},{8,28},{12,24},{16,4},{20,0},{24,12},{28,8},{1,21},{... | collective-permute-start | bytes 442376 | tf_op jit(solution)/shard_map/ppermute | solution.py:578
  89.7 20.5 %collective-permute-start.19 = (bf16[128,576]{1,0:T(8,128)(2,1)S(1)}, bf16[128,576]{1,0:T(8,128)(2,1)S(1)}, u32[]{:S(2)}, u32[]{:S(2)}) collective-permute-start(bf16[128,576]{1,0:T(8,128)(2,1)S(1)} %get-tuple-element.77), channel_id=1, source_target_pairs={{0,16},{4,20},{8,24},{12,28},{16,0},{20,4},{24,8},{28,12},{1,17},{... | collective-permute-start | bytes 442376 | tf_op jit(solution)/shard_map/ppermute | solution.py:578
  93.6 16.6 %collective-permute-start.20 = (bf16[128,576]{1,0:T(8,128)(2,1)S(1)}, bf16[128,576]{1,0:T(8,128)(2,1)S(1)}, u32[]{:S(2)}, u32[]{:S(2)}) collective-permute-start(bf16[128,576]{1,0:T(8,128)(2,1)S(1)} %get-tuple-element.78), channel_id=1, source_target_pairs={{0,12},{4,8},{8,4},{12,0},{16,28},{20,24},{24,20},{28,16},{1,13},{... | collective-permute-start | bytes 442376 | tf_op jit(solution)/shard_map/ppermute | solution.py:578
  94.0 16.2 %collective-permute-start.21 = (bf16[128,576]{1,0:T(8,128)(2,1)S(1)}, bf16[128,576]{1,0:T(8,128)(2,1)S(1)}, u32[]{:S(2)}, u32[]{:S(2)}) collective-permute-start(bf16[128,576]{1,0:T(8,128)(2,1)S(1)} %get-tuple-element.79), channel_id=1, source_target_pairs={{0,8},{4,12},{8,0},{12,4},{16,24},{20,28},{24,16},{28,20},{1,9},{5... | collective-permute-start | bytes 442376 | tf_op jit(solution)/shard_map/ppermute | solution.py:578
  95.6 14.6 %collective-permute-start.22 = (bf16[128,576]{1,0:T(8,128)(2,1)S(1)}, bf16[128,576]{1,0:T(8,128)(2,1)S(1)}, u32[]{:S(2)}, u32[]{:S(2)}) collective-permute-start(bf16[128,576]{1,0:T(8,128)(2,1)S(1)} %get-tuple-element.80), channel_id=1, source_target_pairs={{0,4},{4,0},{8,12},{12,8},{16,20},{20,16},{24,28},{28,24},{1,5},{5... | collective-permute-start | bytes 442376 | tf_op jit(solution)/shard_map/ppermute | solution.py:578
  (6 other events, 19.0 us)

commit v6 on v5

--- a/solution.py
+++ b/solution.py
@@ -22,6 +22,7 @@
 WIDE = -(-INNER // LANES) * LANES
 PAIR = 2 * HD
 PAIRS = HEADS // 2
+PACE = 2
 PAIR_ROWS = PAIR + PACK
 TILE = TH * TW
 VMEM_LIMIT = 28 * 1024 * 1024
@@ -118,7 +119,7 @@
 def visible_bits(tile, count, global_row, tile_cols, slot_num, targets_ref):
     bits = jnp.int32(0)
     for slot in range(slot_num):
-        target = targets_ref[0, tile, slot]
+        target = targets_ref[slot, 0, tile]
         cand = (lax.div(target, tile_cols) - global_row + 1) * tile_cols + lax.rem(target, tile_cols)
         bits = bits | jnp.where(slot < count, jnp.left_shift(1, cand), 0)
     return bits
@@ -133,7 +134,7 @@
 ):
     slab = q_ref.shape[0]
     tile_cols = columns // TW
-    slot_num = targets_ref.shape[2]
+    slot_num = targets_ref.shape[0]
     global_row = lax.axis_index("row") * tile_rows + tile_row
     left = lax.broadcasted_iota(jnp.int32, (1, 4 * TILE), 1) % (2 * TILE) < TILE
     for duo in range(tile_cols // 2):
@@ -180,8 +181,14 @@
             acc_ref[pair * PAIR + HD : (pair + 1) * PAIR, lanes] = out[HD:, 2 * TILE :]
 
 
+def reach(peers):
+    far, near = list(range(peers - 1, peers // 2 - 1, -1)), list(range(peers // 2 - 1, 0, -1))
+    half = len(far) // 2
+    return [0] + far[:half] + near[:1] + far[half:] + near[1:]
+
+
 def peer_of(slot, peers, xor):
-    me, j = lax.axis_index("frame"), (peers - slot) % peers
+    me, j = lax.axis_index("frame"), reach(peers)[slot]
     return me ^ j if xor else lax.rem(me + j, peers)
 
 
@@ -204,7 +211,7 @@
     feat = x_ref.shape[-1]
     slab = tile_cols * TILE
     v_rows = PAIRS * PAIR_ROWS
-    low = INNER // LANES * LANES
+    ahead = tile_rows // PACE
 
     def x_copy(at, col):
         return pltpu.make_async_copy(
@@ -233,53 +240,50 @@
                 )
 
     def work(first):
-        for col in range(tile_cols):
-            x_copy(step, col).wait()
-        x = x_ref[step].reshape(slab, feat)
+        for part in range(PACE):
+            for col in range(tile_cols):
+                x_copy(step * PACE + part, col).wait()
+        size = PACE * slab
+        x = x_ref[pl.ds(step * PACE, PACE)].reshape(size, feat)
         mean, rstd = moments(x)
+        rows = x
         if first:
             rows = jnp.concatenate([x, jnp.ones((PACK, feat), BF16)], axis=0)
-            q, k = nt_dot(rows, w_ref[:low, :]), nt_dot(rows, w_ref[low : 2 * INNER, :])
-            sum_ref[:, :low], sum_ref[:, low:] = q[slab : slab + 1], k[slab : slab + 1]
-            q, k = q[:slab], k[:slab]
-        else:
-            q, k = nt_dot(x, w_ref[:low, :]), nt_dot(x, w_ref[low : 2 * INNER, :])
-        q = (q - mean * sum_ref[:, :low]) * (rstd * (LOG2E * HD**-0.5))
-        q_ref[step, :, :low] = q.astype(BF16)
-        k = (k - mean * sum_ref[:, low:]) * rstd
-        if INNER > low:
-            q_ref[step, :, low:] = (k[:, : WIDE - low] * (LOG2E * HD**-0.5)).astype(BF16)
-            k = pltpu.roll(k, k.shape[1] - (INNER - low), 1)
-        k_ref[step] = k.astype(BF16)
+        prod = nt_dot(rows, w_ref[: 2 * INNER, :])
         if first:
+            sum_ref[...] = prod[size : size + 1]
             col_ref[...] = row_sums(w_ref[2 * INNER :, :])
+        q, k = split_queries_keys((prod[:size] - mean * sum_ref[...]) * rstd)
+        q, k = (q * (LOG2E * HD**-0.5)).astype(BF16), k.astype(BF16)
         values = nt_dot(w_ref[2 * INNER :, :], x) - col_ref[...] * as_rows(mean)
-        store_values(v_ref.at[step], (values * as_rows(rstd)).astype(BF16), slice(None))
-        for copy in out_copies(step):
-            copy.start()
+        values = (values * as_rows(rstd)).astype(BF16)
+        for part in range(PACE):
+            at, own = step * PACE + part, slice(part * slab, (part + 1) * slab)
+            q_ref[at], k_ref[at] = q[own], k[own]
+            store_values(v_ref.at[at], values[:, own], slice(None))
+            for copy in out_copies(at):
+                copy.start()
 
     @pl.when(step == 0)
     def _():
-        for col in range(tile_cols):
-            x_copy(0, col).start()
-        for at in range(1, tile_rows):
+        for at in range(tile_rows):
             for col in range(tile_cols):
                 x_copy(at, col).start()
         work(True)
 
-    @pl.when((step > 0) & (step < tile_rows))
+    @pl.when((step > 0) & (step < ahead))
     def _():
         work(False)
 
-    @pl.when(step == tile_rows)
+    @pl.when(step == ahead)
     def _():
         for copy in (*edge_copies(), *halo_copies()):
             copy.start()
         p_ref[...] = jnp.zeros(p_ref.shape, BF16)
 
-    @pl.when(step >= tile_rows)
-    def _():
-        tile_row = step - tile_rows + 1
+    @pl.when(step >= ahead)
+    def _():
+        tile_row = step - ahead + 1
         k_refs = [k_ref.at[tile_row + j] for j in (-1, 0, 1)]
         v_refs = [v_ref.at[tile_row + j] for j in (-1, 0, 1)]
         attend_tile_row(
@@ -291,7 +295,7 @@
         mixed_ref[...] = mixed
         out_ref[pl.ds(pl.multiple_of((tile_row - 1) * slab, slab), slab), :] = mixed
 
-    @pl.when(step == 2 * tile_rows - 3)
+    @pl.when(step == ahead + tile_rows - 3)
     def _():
         hand_out(send_refs, out_ref, group, xor)
         for at in range(tile_rows):
@@ -306,14 +310,15 @@
     tile_rows = rows // TH
     slab = TH * columns
     v_rows = PAIRS * PAIR_ROWS
+    ahead = tile_rows // PACE
     group = (tile_rows - 2) * slab // peers
     smem = pl.BlockSpec(memory_space=pltpu.SMEM)
     hbm, vmem = pl.BlockSpec(memory_space=pltpu.HBM), pl.BlockSpec(memory_space=pltpu.VMEM)
     outs = pl.pallas_call(
         functools.partial(inner_kernel, group, peers, xor),
-        grid=(2 * tile_rows - 2,),
+        grid=(ahead + tile_rows - 2,),
         in_specs=[smem, smem, hbm, vmem, vmem],
-        out_specs=[hbm] * 6 + [pl.BlockSpec((slab, feat), lambda i: (jnp.maximum(i - tile_rows, 0), 0))]
+        out_specs=[hbm] * 6 + [pl.BlockSpec((slab, feat), lambda i: (jnp.maximum(i - ahead, 0), 0))]
         + [pl.BlockSpec((group, feat), lambda i: (0, 0))] * peers,
         out_shape=[
             jax.ShapeDtypeStruct((tile_rows * slab, WIDE), BF16),
@@ -570,7 +575,7 @@
     size = lax.axis_size("frame")
     result = {}
     for slot, piece in pieces.items():
-        j = (size - slot) % size
+        j = reach(size)[slot]
         if xor:
             pairs = [(i, i ^ j) for i in range(size)]
         else:
@@ -586,6 +591,7 @@
 def body(frames_in, spatial_qkv, spatial_out, temporal_qkv, temporal_out, key_tiles, tile_counts):
     _, rows_dev, columns, feat = frames_in.shape
     slab = TH * columns
+    key_tiles = key_tiles.transpose(2, 0, 1)
     peers = lax.axis_size("frame")
     xor = peers & (peers - 1) == 0
     qkv, edges, halos, mixed_a, send_a = spatial_inner(

time: 114 us -> 112 us (0.982)
  waiting for transfers between devices: 30.5 us -> 27.8 us
  starting transfers between devices: 39.5 us -> 40.9 us
  local copies, waits for them, and re-layouts: 6.62 us -> 5.24 us
    ppermute x23, waiting for transfers between devices: 30.5 us -> 27.8 us  [exchange(): result[slot] = lax.ppermute(piece, 'frame', pairs) if slot else piece]
    unnamed x27 -> x26, local copies, waits for them, and re-layouts: 6.62 us -> 5.24 us
    ppermute x23, starting transfers between devices: 35.8 us -> 37.2 us  [exchange(): result[slot] = lax.ppermute(piece, 'frame', pairs) if slot else piece]
  transfers between devices with their start and end apart: 25 -> 25, of which waited for: 8 -> 7; matrix products, arithmetic and copies ran while one was open for 0% -> 0% of each run, Pallas kernels for 14% -> 14%
where the time goes in v6:
time: 112 us; the launch traced here: 111 us
  starting transfers between devices  40.9 us (37%)
  Pallas kernels  37.1 us (33%)
  waiting for transfers between devices  27.8 us (25%)
  local copies, waits for them, and re-layouts  5.24 us (5%)
    ppermute x23, starting transfers between devices, exchange(): result[slot] = lax.ppermute(piece, 'frame', pairs) if slot else piece  37.2 us
    ppermute x23, waiting for transfers between devices, exchange(): result[slot] = lax.ppermute(piece, 'frame', pairs) if slot else piece  27.8 us
    pallas_call x1, Pallas kernels, spatial_inner(): pl.pallas_call(functools.partial(inner_kernel, group, peers, xor), grid=(...  17.6 us
    pallas_call x2, Pallas kernels, temporal(): pl.pallas_call(functools.partial(temporal_kernel, peers, group, tuple(ear...  9.3 us
    pallas_call x1, Pallas kernels, spatial_edges(): pl.pallas_call(functools.partial(edges_kernel, group, peers, xor, tile_ro...  6.39 us
    unnamed x26, local copies, waits for them, and re-layouts  5.24 us
    pallas_call x1, Pallas kernels, final(): pl.pallas_call(functools.partial(final_kernel, inner, groups, tuple(early...  3.78 us
    ppermute x2, starting transfers between devices, neighbours(): return (lax.ppermute(bot, 'row', up), lax.ppermute(top, 'row', down))  3.7 us
  transfers between devices with their start and end apart: 25, of which 7 were waited for; matrix products, arithmetic and copies ran while one was open for 0% of the time, Pallas kernels for 14%

profile of v6, /device:TPU:0, one launch (start us, length us, event | category | flops | bytes accessed | tf_op | source)
XLA Modules:
  0.0 111.2 jit_solution(15184199478486375023)
XLA Ops:
  0.0 17.6 %spatial_inner.1 = (bf16[1024,640]{1,0:T(8,128)(2,1)}, bf16[1024,640]{1,0:T(8,128)(2,1)}, bf16[2560,256]{1,0:T(8,128)(2,1)}, bf16[2,4,4,16,1152]{4,3,2,1,0:T(8,1...) custom-call(s32[9,1,16]{2,1,0:T(1,128)} %bitcast.8, ...), custom_call_target="tpu_custom_call" | custom-call | flops 12000000000 | bytes 16777216 | tf_op jit(solution)/shard_map/spatial_inner/pallas_call | solution.py:317
  17.6 2.4 %collective-permute-start = (bf16[1280,256]{1,0:T(8,128)(2,1)}, bf16[1280,256]{1,0:T(8,128)(2,1)S(1)}, u32[]{:S(2)}, u32[]{:S(2)}) collective-permute-start(bf16[1280,256]{1,0:T(8,128)(2,1)} %get-tuple-element.49), channel_id=1, source_target_pairs={{0,1},{1,2},{2,3},{4,5},{5,6},{6,7},{8,9},{9,10},{10,11},{12,13},{... | collective-permute-start | bytes 1966088 | tf_op jit(solution)/shard_map/ppermute | solution.py:571
  20.1 1.3 %collective-permute-start.1 = (bf16[1280,256]{1,0:T(8,128)(2,1)}, bf16[1280,256]{1,0:T(8,128)(2,1)S(1)}, u32[]{:S(2)}, u32[]{:S(2)}) collective-permute-start(bf16[1280,256]{1,0:T(8,128)(2,1)} %get-tuple-element.50), channel_id=1, source_target_pairs={{1,0},{2,1},{3,2},{5,4},{6,5},{7,6},{9,8},{10,9},{11,10},{13,12},{... | collective-permute-start | bytes 1966088 | tf_op jit(solution)/shard_map/ppermute | solution.py:571
  21.4 5.4 %collective-permute-start.9 = (bf16[64,1152]{1,0:T(8,128)(2,1)}, bf16[64,1152]{1,0:T(8,128)(2,1)S(1)}, u32[]{:S(2)}, u32[]{:S(2)}) collective-permute-start(bf16[64,1152]{1,0:T(8,128)(2,1)} %get-tuple-element.60), channel_id=1, source_target_pairs={{0,28},{4,24},{8,20},{12,16},{16,12},{20,8},{24,4},{28,0},{1,29},{... | collective-permute-start | bytes 442376 | tf_op jit(solution)/shard_map/ppermute | solution.py:583
  27.0 5.1 %collective-permute-start.12 = (bf16[64,1152]{1,0:T(8,128)(2,1)}, bf16[64,1152]{1,0:T(8,128)(2,1)S(1)}, u32[]{:S(2)}, u32[]{:S(2)}) collective-permute-start(bf16[64,1152]{1,0:T(8,128)(2,1)} %get-tuple-element.63), channel_id=1, source_target_pairs={{0,20},{4,16},{8,28},{12,24},{16,4},{20,0},{24,12},{28,8},{1,21},{... | collective-permute-start | bytes 442376 | tf_op jit(solution)/shard_map/ppermute | solution.py:583
  32.1 1.3 %copy-done.5 = bf16[2,4,4,16,1152]{4,3,2,1,0:T(8,128)(2,1)S(1)} copy-done((bf16[2,4,4,16,1152]{4,3,2,1,0:T(8,128)(2,1)S(1)}, bf16[2,4,4,16,1152]{4,3,2,1,0:T(8,128)(2,1)}, u32[]{:S(2)}) %copy-start.5) | copy-done | bytes 1179672
  33.4 1.3 %copy-done.7 = bf16[1024,640]{1,0:T(8,128)(2,1)S(1)} copy-done((bf16[1024,640]{1,0:T(8,128)(2,1)S(1)}, bf16[1024,640]{1,0:T(8,128)(2,1)}, u32[]{:S(2)}) %copy-start.7) | copy-done | bytes 1310744
  34.7 1.3 %copy-done.8 = bf16[1024,640]{1,0:T(8,128)(2,1)S(1)} copy-done((bf16[1024,640]{1,0:T(8,128)(2,1)S(1)}, bf16[1024,640]{1,0:T(8,128)(2,1)}, u32[]{:S(2)}) %copy-start.8) | copy-done | bytes 1310744
  36.0 1.3 %copy-done.9 = bf16[2560,256]{1,0:T(8,128)(2,1)S(1)} copy-done((bf16[2560,256]{1,0:T(8,128)(2,1)S(1)}, bf16[2560,256]{1,0:T(8,128)(2,1)}, u32[]{:S(2)}) %copy-start.9) | copy-done | bytes 1310744
  37.3 6.4 %spatial_edges.1 = (bf16[512,1152]{1,0:T(8,128)(2,1)S(1)}, bf16[64,1152]{1,0:T(8,128)(2,1)S(1)}, bf16[64,1152]{1,0:T(8,128)(2,1)S(1)}, bf16[64,1152]{1,0:T(8,128...) custom-call(s32[9,1,16]{2,1,0:T(1,128)S(1)} %bitcast.9, ...), custom_call_target="tpu_custom_call" | custom-call | flops 6000000000 | bytes 8388608 | tf_op jit(solution)/shard_map/spatial_edges/pallas_call | solution.py:412
  43.8 0.8 collective-permute-start.14
  45.0 4.7 %collective-permute-start.2 = (bf16[64,1152]{1,0:T(8,128)(2,1)S(1)}, bf16[64,1152]{1,0:T(8,128)(2,1)S(1)}, u32[]{:S(2)}, u32[]{:S(2)}) collective-permute-start(bf16[64,1152]{1,0:T(8,128)(2,1)S(1)} %get-tuple-element.52), channel_id=1, source_target_pairs={{0,28},{4,24},{8,20},{12,16},{16,12},{20,8},{24,4},{28,0},{1,29},{... | collective-permute-start | bytes 442376 | tf_op jit(solution)/shard_map/ppermute | solution.py:583
  49.7 1.5 %collective-permute-start.3 = (bf16[64,1152]{1,0:T(8,128)(2,1)S(1)}, bf16[64,1152]{1,0:T(8,128)(2,1)S(1)}, u32[]{:S(2)}, u32[]{:S(2)}) collective-permute-start(bf16[64,1152]{1,0:T(8,128)(2,1)S(1)} %get-tuple-element.53), channel_id=1, source_target_pairs={{0,24},{4,28},{8,16},{12,20},{16,8},{20,12},{24,0},{28,4},{1,25},{... | collective-permute-start | bytes 442376 | tf_op jit(solution)/shard_map/ppermute | solution.py:583
  51.2 2.2 %collective-permute-done.13.refs_5_ = bf16[64,1152]{1,0:T(8,128)(2,1)S(1)} collective-permute-done((bf16[64,1152]{1,0:T(8,128)(2,1)}, bf16[64,1152]{1,0:T(8,128)(2,1)S(1)}, u32[]{:S(2)}, u32[]{:S(2)}) %collective-permute-start.13) | collective-permute-done | bytes 147488 | tf_op jit(solution)/shard_map/ppermute | solution.py:583
  53.4 8.8 %collective-permute-done.14.refs_6_ = bf16[64,1152]{1,0:T(8,128)(2,1)S(1)} collective-permute-done((bf16[64,1152]{1,0:T(8,128)(2,1)S(1)}, bf16[64,1152]{1,0:T(8,128)(2,1)S(1)}, u32[]{:S(2)}, u32[]{:S(2)}) %collective-permute-start.14) | collective-permute-done | bytes 147488 | tf_op jit(solution)/shard_map/ppermute | solution.py:583
  62.2 3.2 %collective-permute-start.6 = (bf16[64,1152]{1,0:T(8,128)(2,1)S(1)}, bf16[64,1152]{1,0:T(8,128)(2,1)S(1)}, u32[]{:S(2)}, u32[]{:S(2)}) collective-permute-start(bf16[64,1152]{1,0:T(8,128)(2,1)S(1)} %get-tuple-element.56), channel_id=1, source_target_pairs={{0,16},{4,20},{8,24},{12,28},{16,0},{20,4},{24,8},{28,12},{1,17},{... | collective-permute-start | bytes 442376 | tf_op jit(solution)/shard_map/ppermute | solution.py:583
  65.4 1.3 %collective-permute-start.8 = (bf16[64,1152]{1,0:T(8,128)(2,1)S(1)}, bf16[64,1152]{1,0:T(8,128)(2,1)S(1)}, u32[]{:S(2)}, u32[]{:S(2)}) collective-permute-start(bf16[64,1152]{1,0:T(8,128)(2,1)S(1)} %get-tuple-element.58), channel_id=1, source_target_pairs={{0,4},{4,0},{8,12},{12,8},{16,20},{20,16},{24,28},{28,24},{1,5},{5... | collective-permute-start | bytes 442376 | tf_op jit(solution)/shard_map/ppermute | solution.py:583
  66.6 4.6 %temporal.2 = (bf16[64,576]{1,0:T(8,128)(2,1)S(1)}, bf16[64,576]{1,0:T(8,128)(2,1)S(1)}, bf16[64,576]{1,0:T(8,128)(2,1)S(1)}, bf16[64,576]{1,0:T(8,128)(2,1)S(1)...) custom-call(bf16[64,1152]{1,0:T(8,128)(2,1)S(1)} %copy-done.10, ...), custom_call_target="tpu_custom_call" | custom-call | flops 4000000000 | bytes 6291456 | tf_op jit(solution)/shard_map/temporal/pallas_call | solution.py:493
  71.3 1.8 %collective-permute-start.23 = (bf16[64,576]{1,0:T(8,128)(2,1)S(1)}, bf16[64,576]{1,0:T(8,128)(2,1)S(1)}, u32[]{:S(2)}, u32[]{:S(2)}) collective-permute-start(bf16[64,576]{1,0:T(8,128)(2,1)S(1)} %get-tuple-element.81), channel_id=1, source_target_pairs={{0,28},{4,24},{8,20},{12,16},{16,12},{20,8},{24,4},{28,0},{1,29},{... | collective-permute-start | bytes 221192 | tf_op jit(solution)/shard_map/ppermute | solution.py:583
  73.1 2.7 %collective-permute-done.5.refs_4_ = bf16[64,1152]{1,0:T(8,128)(2,1)S(1)} collective-permute-done((bf16[64,1152]{1,0:T(8,128)(2,1)S(1)}, bf16[64,1152]{1,0:T(8,128)(2,1)S(1)}, u32[]{:S(2)}, u32[]{:S(2)}) %collective-permute-start.5) | collective-permute-done | bytes 147488 | tf_op jit(solution)/shard_map/ppermute | solution.py:583
  75.8 1.6 %collective-permute-start.24 = (bf16[64,576]{1,0:T(8,128)(2,1)S(1)}, bf16[64,576]{1,0:T(8,128)(2,1)S(1)}, u32[]{:S(2)}, u32[]{:S(2)}) collective-permute-start(bf16[64,576]{1,0:T(8,128)(2,1)S(1)} %get-tuple-element.82), channel_id=1, source_target_pairs={{0,24},{4,28},{8,16},{12,20},{16,8},{20,12},{24,0},{28,4},{1,25},{... | collective-permute-start | bytes 221192 | tf_op jit(solution)/shard_map/ppermute | solution.py:583
  77.4 2.9 %collective-permute-done.6.refs_5_ = bf16[64,1152]{1,0:T(8,128)(2,1)S(1)} collective-permute-done((bf16[64,1152]{1,0:T(8,128)(2,1)S(1)}, bf16[64,1152]{1,0:T(8,128)(2,1)S(1)}, u32[]{:S(2)}, u32[]{:S(2)}) %collective-permute-start.6) | collective-permute-done | bytes 147488 | tf_op jit(solution)/shard_map/ppermute | solution.py:583
  80.3 4.7 %temporal.3 = (bf16[128,576]{1,0:T(8,128)(2,1)S(1)}, bf16[64,576]{1,0:T(8,128)(2,1)S(1)}, bf16[64,576]{1,0:T(8,128)(2,1)S(1)}, bf16[128,576]{1,0:T(8,128)(2,1)S(...) custom-call(bf16[64,1152]{1,0:T(8,128)(2,1)S(1)} %get-tuple-element., ...), custom_call_target="tpu_custom_call" | custom-call | flops 4000000000 | bytes 6291456 | tf_op jit(solution)/shard_map/temporal/pallas_call | solution.py:493
  84.9 2.1 %collective-permute-start.16 = (bf16[64,576]{1,0:T(8,128)(2,1)S(1)}, bf16[64,576]{1,0:T(8,128)(2,1)S(1)}, u32[]{:S(2)}, u32[]{:S(2)}) collective-permute-start(bf16[64,576]{1,0:T(8,128)(2,1)S(1)} %get-tuple-element.74), channel_id=1, source_target_pairs={{0,28},{4,24},{8,20},{12,16},{16,12},{20,8},{24,4},{28,0},{1,29},{... | collective-permute-start | bytes 221192 | tf_op jit(solution)/shard_map/ppermute | solution.py:583
  87.1 2.2 %collective-permute-start.17 = (bf16[64,576]{1,0:T(8,128)(2,1)S(1)}, bf16[64,576]{1,0:T(8,128)(2,1)S(1)}, u32[]{:S(2)}, u32[]{:S(2)}) collective-permute-start(bf16[64,576]{1,0:T(8,128)(2,1)S(1)} %get-tuple-element.75), channel_id=1, source_target_pairs={{0,24},{4,28},{8,16},{12,20},{16,8},{20,12},{24,0},{28,4},{1,25},{... | collective-permute-start | bytes 221192 | tf_op jit(solution)/shard_map/ppermute | solution.py:583
  89.3 3.1 %collective-permute-start.19 = (bf16[128,576]{1,0:T(8,128)(2,1)S(1)}, bf16[128,576]{1,0:T(8,128)(2,1)S(1)}, u32[]{:S(2)}, u32[]{:S(2)}) collective-permute-start(bf16[128,576]{1,0:T(8,128)(2,1)S(1)} %get-tuple-element.77), channel_id=1, source_target_pairs={{0,20},{4,16},{8,28},{12,24},{16,4},{20,0},{24,12},{28,8},{1,21},{... | collective-permute-start | bytes 442376 | tf_op jit(solution)/shard_map/ppermute | solution.py:583
  92.7 2.5 %collective-permute-start.21 = (bf16[128,576]{1,0:T(8,128)(2,1)S(1)}, bf16[128,576]{1,0:T(8,128)(2,1)S(1)}, u32[]{:S(2)}, u32[]{:S(2)}) collective-permute-start(bf16[128,576]{1,0:T(8,128)(2,1)S(1)} %get-tuple-element.79), channel_id=1, source_target_pairs={{0,8},{4,12},{8,0},{12,4},{16,24},{20,28},{24,16},{28,20},{1,9},{5... | collective-permute-start | bytes 442376 | tf_op jit(solution)/shard_map/ppermute | solution.py:583
  95.2 1.0 collective-permute-start.22
  96.2 4.7 %collective-permute-done.18.refs_3_ = bf16[128,576]{1,0:T(8,128)(2,1)S(1)} collective-permute-done((bf16[128,576]{1,0:T(8,128)(2,1)S(1)}, bf16[128,576]{1,0:T(8,128)(2,1)S(1)}, u32[]{:S(2)}, u32[]{:S(2)}) %collective-permute-start.18) | collective-permute-done | bytes 147488 | tf_op jit(solution)/shard_map/ppermute | solution.py:583
  100.8 4.2 %collective-permute-done.19.refs_4_ = bf16[128,576]{1,0:T(8,128)(2,1)S(1)} collective-permute-done((bf16[128,576]{1,0:T(8,128)(2,1)S(1)}, bf16[128,576]{1,0:T(8,128)(2,1)S(1)}, u32[]{:S(2)}, u32[]{:S(2)}) %collective-permute-start.19) | collective-permute-done | bytes 147488 | tf_op jit(solution)/shard_map/ppermute | solution.py:583
  105.0 2.3 %collective-permute-done.20.refs_5_ = bf16[128,576]{1,0:T(8,128)(2,1)S(1)} collective-permute-done((bf16[128,576]{1,0:T(8,128)(2,1)S(1)}, bf16[128,576]{1,0:T(8,128)(2,1)S(1)}, u32[]{:S(2)}, u32[]{:S(2)}) %collective-permute-start.20) | collective-permute-done | bytes 147488 | tf_op jit(solution)/shard_map/ppermute | solution.py:583
  107.4 3.8 %final.1 = bf16[1024,1152]{1,0:T(8,128)(2,1)} custom-call(bf16[128,576]{1,0:T(8,128)(2,1)S(1)} %get-tuple-element.73.refs_0_, bf16[64,576]{1,0:T(8,128)(2,1)S(1)} %collective-permute-done.16.refs_1_, bf16[64,576]{1,0:T(8,128)(2,1)S(1)} %collective-permute-done.17.refs_2_, bf16[128,576]{1,0:T(8,128)(2,1)S(1)} %collective-permute-done.18.refs_3_, ...), custom_call_target="tpu_custom_call" | custom-call | flops 2000000000 | bytes 6291456 | tf_op jit(solution)/shard_map/final/pallas_call | solution.py:549
  (49 shorter events, 1.0 us)
Async XLA Ops:
  0.0 32.1 %copy-start.1 = (bf16[576,1152]{1,0:T(8,128)(2,1)S(1)}, bf16[576,1152]{1,0:T(8,128)(2,1)}, u32[]{:S(2)}) copy-start(bf16[576,1152]{1,0:T(8,128)(2,1)} %w_ref.1) | copy-start | bytes 3981316
  0.0 32.1 %copy-start.3 = (s32[1,16,9]{1,0,2:T(1,128)S(1)}, s32[1,16,9]{1,0,2:T(1,128)}, u32[]{:S(2)}) copy-start(s32[1,16,9]{1,0,2:T(1,128)} %param.12) | copy-start | bytes 1732
  0.0 32.1 %copy-start.4 = (s32[1,16]{1,0:T(1,128)S(1)}, s32[1,16]{1,0:T(1,128)}, u32[]{:S(2)}) copy-start(s32[1,16]{1,0:T(1,128)} %counts_ref.3) | copy-start | bytes 196
  17.6 9.4 %collective-permute-start = (bf16[1280,256]{1,0:T(8,128)(2,1)}, bf16[1280,256]{1,0:T(8,128)(2,1)S(1)}, u32[]{:S(2)}, u32[]{:S(2)}) collective-permute-start(bf16[1280,256]{1,0:T(8,128)(2,1)} %get-tuple-element.49), channel_id=1, source_target_pairs={{0,1},{1,2},{2,3},{4,5},{5,6},{6,7},{8,9},{9,10},{10,11},{12,13},{... | collective-permute-start | bytes 1966088 | tf_op jit(solution)/shard_map/ppermute | solution.py:571
  20.1 12.0 %collective-permute-start.1 = (bf16[1280,256]{1,0:T(8,128)(2,1)}, bf16[1280,256]{1,0:T(8,128)(2,1)S(1)}, u32[]{:S(2)}, u32[]{:S(2)}) collective-permute-start(bf16[1280,256]{1,0:T(8,128)(2,1)} %get-tuple-element.50), channel_id=1, source_target_pairs={{1,0},{2,1},{3,2},{5,4},{6,5},{7,6},{9,8},{10,9},{11,10},{13,12},{... | collective-permute-start | bytes 1966088 | tf_op jit(solution)/shard_map/ppermute | solution.py:571
  21.4 22.4 %collective-permute-start.9 = (bf16[64,1152]{1,0:T(8,128)(2,1)}, bf16[64,1152]{1,0:T(8,128)(2,1)S(1)}, u32[]{:S(2)}, u32[]{:S(2)}) collective-permute-start(bf16[64,1152]{1,0:T(8,128)(2,1)} %get-tuple-element.60), channel_id=1, source_target_pairs={{0,28},{4,24},{8,20},{12,16},{16,12},{20,8},{24,4},{28,0},{1,29},{... | collective-permute-start | bytes 442376 | tf_op jit(solution)/shard_map/ppermute | solution.py:583
  26.8 17.8 %collective-permute-start.10 = (bf16[64,1152]{1,0:T(8,128)(2,1)}, bf16[64,1152]{1,0:T(8,128)(2,1)S(1)}, u32[]{:S(2)}, u32[]{:S(2)}) collective-permute-start(bf16[64,1152]{1,0:T(8,128)(2,1)} %get-tuple-element.61), channel_id=1, source_target_pairs={{0,24},{4,28},{8,16},{12,20},{16,8},{20,12},{24,0},{28,4},{1,25},{... | collective-permute-start | bytes 442376 | tf_op jit(solution)/shard_map/ppermute | solution.py:583
  27.0 18.0 %collective-permute-start.11 = (bf16[64,1152]{1,0:T(8,128)(2,1)}, bf16[64,1152]{1,0:T(8,128)(2,1)S(1)}, u32[]{:S(2)}, u32[]{:S(2)}) collective-permute-start(bf16[64,1152]{1,0:T(8,128)(2,1)} %get-tuple-element.62), channel_id=1, source_target_pairs={{0,12},{4,8},{8,4},{12,0},{16,28},{20,24},{24,20},{28,16},{1,13},{... | collective-permute-start | bytes 442376 | tf_op jit(solution)/shard_map/ppermute | solution.py:583
  27.0 22.7 %collective-permute-start.12 = (bf16[64,1152]{1,0:T(8,128)(2,1)}, bf16[64,1152]{1,0:T(8,128)(2,1)S(1)}, u32[]{:S(2)}, u32[]{:S(2)}) collective-permute-start(bf16[64,1152]{1,0:T(8,128)(2,1)} %get-tuple-element.63), channel_id=1, source_target_pairs={{0,20},{4,16},{8,28},{12,24},{16,4},{20,0},{24,12},{28,8},{1,21},{... | collective-permute-start | bytes 442376 | tf_op jit(solution)/shard_map/ppermute | solution.py:583
  32.1 21.3 %collective-permute-start.13 = (bf16[64,1152]{1,0:T(8,128)(2,1)}, bf16[64,1152]{1,0:T(8,128)(2,1)S(1)}, u32[]{:S(2)}, u32[]{:S(2)}) collective-permute-start(bf16[64,1152]{1,0:T(8,128)(2,1)} %get-tuple-element.64), channel_id=1, source_target_pairs={{0,16},{4,20},{8,24},{12,28},{16,0},{20,4},{24,8},{28,12},{1,17},{... | collective-permute-start | bytes 442376 | tf_op jit(solution)/shard_map/ppermute | solution.py:583
  37.3 29.3 %copy-start = (bf16[1152,1728]{0,1:T(8,128)(2,1)S(1)}, bf16[1152,1728]{0,1:T(8,128)(2,1)}, u32[]{:S(2)}) copy-start(bf16[1152,1728]{0,1:T(8,128)(2,1)} %param.10) | copy-start | bytes 11943940
  37.3 29.3 %copy-start.10 = (bf16[64,1152]{1,0:T(8,128)(2,1)S(1)}, bf16[64,1152]{1,0:T(8,128)(2,1)}, u32[]{:S(2)}) copy-start(bf16[64,1152]{1,0:T(8,128)(2,1)} %get-tuple-element.59.refs_0_) | copy-start | bytes 442372
  43.8 18.4 %collective-permute-start.14 = (bf16[64,1152]{1,0:T(8,128)(2,1)S(1)}, bf16[64,1152]{1,0:T(8,128)(2,1)S(1)}, u32[]{:S(2)}, u32[]{:S(2)}) collective-permute-start(bf16[64,1152]{1,0:T(8,128)(2,1)S(1)} %copy-done.12), channel_id=1, source_target_pairs={{0,8},{4,12},{8,0},{12,4},{16,24},{20,28},{24,16},{28,20},{1,9},{5... | collective-permute-start | bytes 442376 | tf_op jit(solution)/shard_map/ppermute | solution.py:583
  44.6 17.5 %collective-permute-start.15 = (bf16[64,1152]{1,0:T(8,128)(2,1)S(1)}, bf16[64,1152]{1,0:T(8,128)(2,1)S(1)}, u32[]{:S(2)}, u32[]{:S(2)}) collective-permute-start(bf16[64,1152]{1,0:T(8,128)(2,1)S(1)} %copy-done.11), channel_id=1, source_target_pairs={{0,4},{4,0},{8,12},{12,8},{16,20},{20,16},{24,28},{28,24},{1,5},{5... | collective-permute-start | bytes 442376 | tf_op jit(solution)/shard_map/ppermute | solution.py:583
  45.0 20.3 %collective-permute-start.2 = (bf16[64,1152]{1,0:T(8,128)(2,1)S(1)}, bf16[64,1152]{1,0:T(8,128)(2,1)S(1)}, u32[]{:S(2)}, u32[]{:S(2)}) collective-permute-start(bf16[64,1152]{1,0:T(8,128)(2,1)S(1)} %get-tuple-element.52), channel_id=1, source_target_pairs={{0,28},{4,24},{8,20},{12,16},{16,12},{20,8},{24,4},{28,0},{1,29},{... | collective-permute-start | bytes 442376 | tf_op jit(solution)/shard_map/ppermute | solution.py:583
  49.7 15.7 %collective-permute-start.3 = (bf16[64,1152]{1,0:T(8,128)(2,1)S(1)}, bf16[64,1152]{1,0:T(8,128)(2,1)S(1)}, u32[]{:S(2)}, u32[]{:S(2)}) collective-permute-start(bf16[64,1152]{1,0:T(8,128)(2,1)S(1)} %get-tuple-element.53), channel_id=1, source_target_pairs={{0,24},{4,28},{8,16},{12,20},{16,8},{20,12},{24,0},{28,4},{1,25},{... | collective-permute-start | bytes 442376 | tf_op jit(solution)/shard_map/ppermute | solution.py:583
  53.4 17.9 %collective-permute-start.4 = (bf16[64,1152]{1,0:T(8,128)(2,1)S(1)}, bf16[64,1152]{1,0:T(8,128)(2,1)S(1)}, u32[]{:S(2)}, u32[]{:S(2)}) collective-permute-start(bf16[64,1152]{1,0:T(8,128)(2,1)S(1)} %get-tuple-element.54), channel_id=1, source_target_pairs={{0,12},{4,8},{8,4},{12,0},{16,28},{20,24},{24,20},{28,16},{1,13},{... | collective-permute-start | bytes 442376 | tf_op jit(solution)/shard_map/ppermute | solution.py:583
  62.2 13.7 %collective-permute-start.5 = (bf16[64,1152]{1,0:T(8,128)(2,1)S(1)}, bf16[64,1152]{1,0:T(8,128)(2,1)S(1)}, u32[]{:S(2)}, u32[]{:S(2)}) collective-permute-start(bf16[64,1152]{1,0:T(8,128)(2,1)S(1)} %get-tuple-element.55), channel_id=1, source_target_pairs={{0,20},{4,16},{8,28},{12,24},{16,4},{20,0},{24,12},{28,8},{1,21},{... | collective-permute-start | bytes 442376 | tf_op jit(solution)/shard_map/ppermute | solution.py:583
  62.2 18.1 %collective-permute-start.6 = (bf16[64,1152]{1,0:T(8,128)(2,1)S(1)}, bf16[64,1152]{1,0:T(8,128)(2,1)S(1)}, u32[]{:S(2)}, u32[]{:S(2)}) collective-permute-start(bf16[64,1152]{1,0:T(8,128)(2,1)S(1)} %get-tuple-element.56), channel_id=1, source_target_pairs={{0,16},{4,20},{8,24},{12,28},{16,0},{20,4},{24,8},{28,12},{1,17},{... | collective-permute-start | bytes 442376 | tf_op jit(solution)/shard_map/ppermute | solution.py:583
  65.3 14.9 %collective-permute-start.7 = (bf16[64,1152]{1,0:T(8,128)(2,1)S(1)}, bf16[64,1152]{1,0:T(8,128)(2,1)S(1)}, u32[]{:S(2)}, u32[]{:S(2)}) collective-permute-start(bf16[64,1152]{1,0:T(8,128)(2,1)S(1)} %get-tuple-element.57), channel_id=1, source_target_pairs={{0,8},{4,12},{8,0},{12,4},{16,24},{20,28},{24,16},{28,20},{1,9},{5... | collective-permute-start | bytes 442376 | tf_op jit(solution)/shard_map/ppermute | solution.py:583
  65.4 14.9 %collective-permute-start.8 = (bf16[64,1152]{1,0:T(8,128)(2,1)S(1)}, bf16[64,1152]{1,0:T(8,128)(2,1)S(1)}, u32[]{:S(2)}, u32[]{:S(2)}) collective-permute-start(bf16[64,1152]{1,0:T(8,128)(2,1)S(1)} %get-tuple-element.58), channel_id=1, source_target_pairs={{0,4},{4,0},{8,12},{12,8},{16,20},{20,16},{24,28},{28,24},{1,5},{5... | collective-permute-start | bytes 442376 | tf_op jit(solution)/shard_map/ppermute | solution.py:583
  71.3 18.0 %collective-permute-start.23 = (bf16[64,576]{1,0:T(8,128)(2,1)S(1)}, bf16[64,576]{1,0:T(8,128)(2,1)S(1)}, u32[]{:S(2)}, u32[]{:S(2)}) collective-permute-start(bf16[64,576]{1,0:T(8,128)(2,1)S(1)} %get-tuple-element.81), channel_id=1, source_target_pairs={{0,28},{4,24},{8,20},{12,16},{16,12},{20,8},{24,4},{28,0},{1,29},{... | collective-permute-start | bytes 221192 | tf_op jit(solution)/shard_map/ppermute | solution.py:583
  75.8 16.6 %collective-permute-start.24 = (bf16[64,576]{1,0:T(8,128)(2,1)S(1)}, bf16[64,576]{1,0:T(8,128)(2,1)S(1)}, u32[]{:S(2)}, u32[]{:S(2)}) collective-permute-start(bf16[64,576]{1,0:T(8,128)(2,1)S(1)} %get-tuple-element.82), channel_id=1, source_target_pairs={{0,24},{4,28},{8,16},{12,20},{16,8},{20,12},{24,0},{28,4},{1,25},{... | collective-permute-start | bytes 221192 | tf_op jit(solution)/shard_map/ppermute | solution.py:583
  80.3 27.1 %copy-start.2 = (bf16[576,1152]{1,0:T(8,128)(2,1)S(1)}, bf16[576,1152]{1,0:T(8,128)(2,1)}, u32[]{:S(2)}) copy-start(bf16[576,1152]{1,0:T(8,128)(2,1)} %refs_12_.1) | copy-start | bytes 3981316
  80.3 27.1 %copy-start.6 = (bf16[512,1152]{1,0:T(8,128)(2,1)S(1)}, bf16[512,1152]{1,0:T(8,128)(2,1)}, u32[]{:S(2)}) copy-start(bf16[512,1152]{1,0:T(8,128)(2,1)} %get-tuple-element.83.refs_10_) | copy-start | bytes 3538948
  84.9 7.7 %collective-permute-start.16 = (bf16[64,576]{1,0:T(8,128)(2,1)S(1)}, bf16[64,576]{1,0:T(8,128)(2,1)S(1)}, u32[]{:S(2)}, u32[]{:S(2)}) collective-permute-start(bf16[64,576]{1,0:T(8,128)(2,1)S(1)} %get-tuple-element.74), channel_id=1, source_target_pairs={{0,28},{4,24},{8,20},{12,16},{16,12},{20,8},{24,4},{28,0},{1,29},{... | collective-permute-start | bytes 221192 | tf_op jit(solution)/shard_map/ppermute | solution.py:583
  87.1 8.1 %collective-permute-start.17 = (bf16[64,576]{1,0:T(8,128)(2,1)S(1)}, bf16[64,576]{1,0:T(8,128)(2,1)S(1)}, u32[]{:S(2)}, u32[]{:S(2)}) collective-permute-start(bf16[64,576]{1,0:T(8,128)(2,1)S(1)} %get-tuple-element.75), channel_id=1, source_target_pairs={{0,24},{4,28},{8,16},{12,20},{16,8},{20,12},{24,0},{28,4},{1,25},{... | collective-permute-start | bytes 221192 | tf_op jit(solution)/shard_map/ppermute | solution.py:583
  89.3 11.6 %collective-permute-start.18 = (bf16[128,576]{1,0:T(8,128)(2,1)S(1)}, bf16[128,576]{1,0:T(8,128)(2,1)S(1)}, u32[]{:S(2)}, u32[]{:S(2)}) collective-permute-start(bf16[128,576]{1,0:T(8,128)(2,1)S(1)} %get-tuple-element.76), channel_id=1, source_target_pairs={{0,12},{4,8},{8,4},{12,0},{16,28},{20,24},{24,20},{28,16},{1,13},{... | collective-permute-start | bytes 442376 | tf_op jit(solution)/shard_map/ppermute | solution.py:583
  89.3 15.8 %collective-permute-start.19 = (bf16[128,576]{1,0:T(8,128)(2,1)S(1)}, bf16[128,576]{1,0:T(8,128)(2,1)S(1)}, u32[]{:S(2)}, u32[]{:S(2)}) collective-permute-start(bf16[128,576]{1,0:T(8,128)(2,1)S(1)} %get-tuple-element.77), channel_id=1, source_target_pairs={{0,20},{4,16},{8,28},{12,24},{16,4},{20,0},{24,12},{28,8},{1,21},{... | collective-permute-start | bytes 442376 | tf_op jit(solution)/shard_map/ppermute | solution.py:583
  92.4 15.0 %collective-permute-start.20 = (bf16[128,576]{1,0:T(8,128)(2,1)S(1)}, bf16[128,576]{1,0:T(8,128)(2,1)S(1)}, u32[]{:S(2)}, u32[]{:S(2)}) collective-permute-start(bf16[128,576]{1,0:T(8,128)(2,1)S(1)} %get-tuple-element.78), channel_id=1, source_target_pairs={{0,16},{4,20},{8,24},{12,28},{16,0},{20,4},{24,8},{28,12},{1,17},{... | collective-permute-start | bytes 442376 | tf_op jit(solution)/shard_map/ppermute | solution.py:583
  92.7 14.7 %collective-permute-start.21 = (bf16[128,576]{1,0:T(8,128)(2,1)S(1)}, bf16[128,576]{1,0:T(8,128)(2,1)S(1)}, u32[]{:S(2)}, u32[]{:S(2)}) collective-permute-start(bf16[128,576]{1,0:T(8,128)(2,1)S(1)} %get-tuple-element.79), channel_id=1, source_target_pairs={{0,8},{4,12},{8,0},{12,4},{16,24},{20,28},{24,16},{28,20},{1,9},{5... | collective-permute-start | bytes 442376 | tf_op jit(solution)/shard_map/ppermute | solution.py:583
  95.2 12.2 %collective-permute-start.22 = (bf16[128,576]{1,0:T(8,128)(2,1)S(1)}, bf16[128,576]{1,0:T(8,128)(2,1)S(1)}, u32[]{:S(2)}, u32[]{:S(2)}) collective-permute-start(bf16[128,576]{1,0:T(8,128)(2,1)S(1)} %get-tuple-element.80), channel_id=1, source_target_pairs={{0,4},{4,0},{8,12},{12,8},{16,20},{20,16},{24,28},{28,24},{1,5},{5... | collective-permute-start | bytes 442376 | tf_op jit(solution)/shard_map/ppermute | solution.py:583
  (6 other events, 18.9 us)

commit v7 on v6

--- a/solution.py
+++ b/solution.py
@@ -380,7 +380,9 @@
     branch = nn_dot(acc_ref[...].T.astype(BF16), w_ref[...])
     mixed = (x_ref[...].astype(F32) + branch).astype(BF16)
     mixed_ref[...] = mixed
-    out_ref[pl.ds(pl.multiple_of(step * slab, slab), slab), :] = mixed
+    mean, rstd = moments(mixed)
+    normed = ((mixed.astype(F32) - mean) * rstd).astype(BF16)
+    out_ref[pl.ds(pl.multiple_of(step * slab, slab), slab), :] = normed
 
     @pl.when(step == 1)
     def _():
@@ -433,7 +435,7 @@
     return outs[0], outs[1:]
 
 
-def temporal_kernel(peers, group, early, *refs):
+def temporal_kernel(peers, group, normed, early, *refs):
     in_refs, w_ref, early_refs = refs[:peers], refs[peers], refs[peers + 1 : -6 - peers]
     out_refs, (x_ref, q_ref, k_ref, v_ref, p_ref, acc_ref) = refs[-6 - peers : -6], refs[-6:]
     for slot, ref in zip(early, early_refs):
@@ -448,14 +450,18 @@
             x_ref[to, :] = in_refs[j][pl.ds(part * PACK, PACK), :]
     x_ref[tokens:, :] = jnp.ones((PACK, x_ref.shape[1]), BF16)
     x = x_ref[:tokens, :]
-    mean, rstd = moments(x)
-    prod = nt_dot(x_ref[...], w_ref[: 2 * INNER, :])
-    prod = (prod[:tokens] - mean * prod[tokens : tokens + 1]) * rstd
+    w_values = w_ref[2 * INNER :, :]
+    if normed:
+        prod = nt_dot(x, w_ref[: 2 * INNER, :])
+        values = nt_dot(w_values, x)
+    else:
+        mean, rstd = moments(x)
+        prod = nt_dot(x_ref[...], w_ref[: 2 * INNER, :])
+        prod = (prod[:tokens] - mean * prod[tokens : tokens + 1]) * rstd
+        values = (nt_dot(w_values, x) - row_sums(w_values) * as_rows(mean)) * as_rows(rstd)
     q, k = split_queries_keys(prod)
     q_ref[...] = (q * (LOG2E * HD**-0.5)).astype(BF16)
     k_ref[...] = k.astype(BF16)
-    w_values = w_ref[2 * INNER :, :]
-    values = (nt_dot(w_values, x) - row_sums(w_values) * as_rows(mean)) * as_rows(rstd)
     store_values(v_ref, values.astype(BF16), slice(None))
     row = lax.broadcasted_iota(jnp.int32, (block, 2 * block), 0)
     col = lax.broadcasted_iota(jnp.int32, (block, 2 * block), 1)
@@ -484,14 +490,14 @@
             out_refs[j][rows, :] = heads[j * PACK : (j + 1) * PACK]
 
 
-def temporal(pieces, w, early=None):
+def temporal(pieces, w, normed, early=None):
     early = early or {}
     peers = len(pieces)
     group, feat = pieces[0].shape
     tokens = peers * group
     rows = [group + (early[slot].shape[0] if slot in early else 0) for slot in range(peers)]
     return pl.pallas_call(
-        functools.partial(temporal_kernel, peers, group, tuple(early)),
+        functools.partial(temporal_kernel, peers, group, normed, tuple(early)),
         out_shape=[jax.ShapeDtypeStruct((count, INNER), BF16) for count in rows],
         scratch_shapes=[
             pltpu.VMEM((tokens + PACK, feat), BF16),
@@ -507,57 +513,54 @@
     )(*pieces, w, *early.values())
 
 
-def final_kernel(inner, groups, early, xor, columns, *refs):
-    in_refs, (first_ref, second_ref, w_ref, out_ref, heads_ref) = refs[:-5], refs[-5:]
+def final_kernel(groups, early, xor, columns, *refs):
+    in_refs, (first_ref, second_ref, w_ref, out_hbm, heads_ref, out_ref, sem) = refs[:-7], refs[-7:]
     in_refs, early_refs = in_refs[: -len(early)], dict(zip(early, in_refs[-len(early) :]))
-    step = pl.program_id(0)
-    slab = first_ref.shape[0]
     peers = len(in_refs)
-
-    @pl.when(step == 0)
-    def _():
-        for slot, ref in enumerate(in_refs):
-            peer = peer_of(slot, peers, xor)
-            to = pl.ds(pl.multiple_of(peer * groups[0], PACK), groups[0])
-            heads_ref[to, :] = early_refs[slot][...] if slot in early_refs else ref[: groups[0], :]
-            to = pl.multiple_of(peers * groups[0] + peer * groups[1], PACK)
-            heads_ref[pl.ds(to, groups[1]), :] = ref[ref.shape[0] - groups[1] :, :]
-
-    def work(mixed_ref):
-        heads = heads_ref[pl.ds(pl.multiple_of(step * slab, slab), slab), :]
-        result = mixed_ref[...].astype(F32) + nn_dot(heads, w_ref[...])
-        for to, at in tile_order(slab, columns):
-            out_ref[pl.ds(at, TW), :] = result[to : to + TW].astype(BF16)
-
-    @pl.when(step < inner)
-    def _():
-        work(first_ref)
-
-    @pl.when(step >= inner)
-    def _():
-        work(second_ref)
+    slab = TH * columns
+    tile_rows = out_ref.shape[0]
+    for slot, ref in enumerate(in_refs):
+        peer = peer_of(slot, peers, xor)
+        to = pl.ds(pl.multiple_of(peer * groups[0], PACK), groups[0])
+        heads_ref[to, :] = early_refs[slot][...] if slot in early_refs else ref[: groups[0], :]
+        to = pl.multiple_of(peers * groups[0] + peer * groups[1], PACK)
+        heads_ref[pl.ds(to, groups[1]), :] = ref[ref.shape[0] - groups[1] :, :]
+
+    copies = []
+    begin = 0
+    for mixed_ref, rows in ((first_ref, range(1, tile_rows - 1)), (second_ref, (0, tile_rows - 1))):
+        end = begin + mixed_ref.shape[0]
+        result = mixed_ref[...].astype(F32) + nn_dot(heads_ref[begin:end, :], w_ref[...])
+        result = result.astype(BF16)
+        begin = end
+        for part, row in enumerate(rows):
+            for to, at in tile_order(slab, columns):
+                to += part * slab
+                out_ref[row, pl.ds(at, TW), :] = result[to : to + TW]
+            copies.append(
+                pltpu.make_async_copy(out_ref.at[row], out_hbm.at[pl.ds(row * slab, slab)], sem.at[row])
+            )
+            copies[-1].start()
+    for copy in copies:
+        copy.wait()
 
 
 def final(pieces, early, first, second, w, slab, columns, xor):
     feat = first.shape[1]
-    inner = first.shape[0] // slab
-    tile_rows = inner + 2
+    tile_rows = (first.shape[0] + second.shape[0]) // slab
     peers = len(pieces)
     groups = (first.shape[0] // peers, second.shape[0] // peers)
-    at = lambda i: jnp.where(i < inner, i + 1, (i - inner) * (tile_rows - 1))
-    whole = lambda *shape: pl.BlockSpec(shape, lambda i: (0, 0))
+    vmem = pl.BlockSpec(memory_space=pltpu.VMEM)
     return pl.pallas_call(
-        functools.partial(final_kernel, inner, groups, tuple(early), xor, columns),
-        grid=(tile_rows,),
-        in_specs=[whole(*piece.shape) for piece in (*pieces, *early.values())]
-        + [
-            pl.BlockSpec((slab, feat), lambda i: (jnp.minimum(i, inner - 1), 0)),
-            pl.BlockSpec((slab, feat), lambda i: (jnp.maximum(i - inner, 0), 0)),
-            whole(*w.shape),
+        functools.partial(final_kernel, groups, tuple(early), xor, columns),
+        in_specs=[vmem] * (peers + len(early) + 3),
+        out_specs=pl.BlockSpec(memory_space=pltpu.HBM),
+        out_shape=jax.ShapeDtypeStruct((tile_rows * slab, feat), BF16),
+        scratch_shapes=[
+            pltpu.VMEM((tile_rows * slab, INNER), BF16),
+            pltpu.VMEM((tile_rows, slab, feat), BF16),
+            pltpu.SemaphoreType.DMA((tile_rows,)),
         ],
-        out_specs=pl.BlockSpec((slab, feat), lambda i: (at(i), 0)),
-        out_shape=jax.ShapeDtypeStruct((tile_rows * slab, feat), BF16),
-        scratch_shapes=[pltpu.VMEM((tile_rows * slab, INNER), BF16)],
         compiler_params=params(),
         cost_estimate=cost(2 * 10**9, 6 * 2**20),
         name="final",
@@ -603,10 +606,10 @@
         edges, *qkv, halos, spatial_out, key_tiles, tile_counts, slab, columns, peers, xor
     )
     got_b = exchange(by_slot(send_b), xor, False)
-    heads_a = by_slot(temporal(list(got_a.values()), temporal_qkv.T))
+    heads_a = by_slot(temporal(list(got_a.values()), temporal_qkv.T, False))
     far = range(1, 1 + peers // 4)
     early = exchange({slot: heads_a.pop(slot) for slot in far}, xor, True)
-    heads = by_slot(temporal(list(got_b.values()), temporal_qkv.T, heads_a))
+    heads = by_slot(temporal(list(got_b.values()), temporal_qkv.T, True, heads_a))
     back = exchange(heads, xor, True)
     out = final(
         list(back.values()), early, mixed_a, mixed_b, temporal_out, slab, columns, xor

time: 112 us -> 111 us (level)
    pallas_call x3, Pallas kernels: 13.1 us -> 11.8 us  [the longest x2 8.5 us: temporal(): pl.pallas_call(functools.partial(temporal_kernel, peers, group, normed, t...]
where the time goes in v7:
time: 111 us
  starting transfers between devices  40.5 us (36%)
  Pallas kernels  36.3 us (33%)
  waiting for transfers between devices  28.3 us (25%)
  local copies, waits for them, and re-layouts  5.24 us (5%)
    ppermute x23, starting transfers between devices, exchange(): result[slot] = lax.ppermute(piece, 'frame', pairs) if slot else piece  36.6 us
    ppermute x23, waiting for transfers between devices, exchange(): result[slot] = lax.ppermute(piece, 'frame', pairs) if slot else piece  28.3 us
    pallas_call x1, Pallas kernels, spatial_inner(): pl.pallas_call(functools.partial(inner_kernel, group, peers, xor), grid=(...  17.6 us
    pallas_call x2, Pallas kernels, temporal(): pl.pallas_call(functools.partial(temporal_kernel, peers, group, normed, t...  8.5 us
    pallas_call x1, Pallas kernels, spatial_edges(): pl.pallas_call(functools.partial(edges_kernel, group, peers, xor, tile_ro...  6.86 us
    unnamed x26, local copies, waits for them, and re-layouts  5.24 us
    ppermute x2, starting transfers between devices, neighbours(): return (lax.ppermute(bot, 'row', up), lax.ppermute(top, 'row', down))  3.89 us
    pallas_call x1, Pallas kernels, final(): pl.pallas_call(functools.partial(final_kernel, groups, tuple(early), xor,...  3.32 us
  transfers between devices with their start and end apart: 25, of which 7 were waited for; matrix products, arithmetic and copies ran while one was open for 0% of the time, Pallas kernels for 14%

profile of v7, /device:TPU:0, one launch (start us, length us, event | category | flops | bytes accessed | tf_op | source)
XLA Modules:
  0.0 110.6 jit_solution(10098629929056035294)
XLA Ops:
  0.0 17.6 %spatial_inner.1 = (bf16[1024,640]{1,0:T(8,128)(2,1)}, bf16[1024,640]{1,0:T(8,128)(2,1)}, bf16[2560,256]{1,0:T(8,128)(2,1)}, bf16[2,4,4,16,1152]{4,3,2,1,0:T(8,1...) custom-call(s32[9,1,16]{2,1,0:T(1,128)} %bitcast.8, ...), custom_call_target="tpu_custom_call" | custom-call | flops 12000000000 | bytes 16777216 | tf_op jit(solution)/shard_map/spatial_inner/pallas_call | solution.py:317
  17.6 2.4 %collective-permute-start = (bf16[1280,256]{1,0:T(8,128)(2,1)}, bf16[1280,256]{1,0:T(8,128)(2,1)S(1)}, u32[]{:S(2)}, u32[]{:S(2)}) collective-permute-start(bf16[1280,256]{1,0:T(8,128)(2,1)} %get-tuple-element.49), channel_id=1, source_target_pairs={{0,1},{1,2},{2,3},{4,5},{5,6},{6,7},{8,9},{9,10},{10,11},{12,13},{... | collective-permute-start | bytes 1966088 | tf_op jit(solution)/shard_map/ppermute | solution.py:574
  20.1 1.5 %collective-permute-start.1 = (bf16[1280,256]{1,0:T(8,128)(2,1)}, bf16[1280,256]{1,0:T(8,128)(2,1)S(1)}, u32[]{:S(2)}, u32[]{:S(2)}) collective-permute-start(bf16[1280,256]{1,0:T(8,128)(2,1)} %get-tuple-element.50), channel_id=1, source_target_pairs={{1,0},{2,1},{3,2},{5,4},{6,5},{7,6},{9,8},{10,9},{11,10},{13,12},{... | collective-permute-start | bytes 1966088 | tf_op jit(solution)/shard_map/ppermute | solution.py:574
  21.5 5.4 %collective-permute-start.9 = (bf16[64,1152]{1,0:T(8,128)(2,1)}, bf16[64,1152]{1,0:T(8,128)(2,1)S(1)}, u32[]{:S(2)}, u32[]{:S(2)}) collective-permute-start(bf16[64,1152]{1,0:T(8,128)(2,1)} %get-tuple-element.60), channel_id=1, source_target_pairs={{0,28},{4,24},{8,20},{12,16},{16,12},{20,8},{24,4},{28,0},{1,29},{... | collective-permute-start | bytes 442376 | tf_op jit(solution)/shard_map/ppermute | solution.py:586
  27.2 5.1 %collective-permute-start.12 = (bf16[64,1152]{1,0:T(8,128)(2,1)}, bf16[64,1152]{1,0:T(8,128)(2,1)S(1)}, u32[]{:S(2)}, u32[]{:S(2)}) collective-permute-start(bf16[64,1152]{1,0:T(8,128)(2,1)} %get-tuple-element.63), channel_id=1, source_target_pairs={{0,20},{4,16},{8,28},{12,24},{16,4},{20,0},{24,12},{28,8},{1,21},{... | collective-permute-start | bytes 442376 | tf_op jit(solution)/shard_map/ppermute | solution.py:586
  32.3 1.3 %copy-done.5 = bf16[2,4,4,16,1152]{4,3,2,1,0:T(8,128)(2,1)S(1)} copy-done((bf16[2,4,4,16,1152]{4,3,2,1,0:T(8,128)(2,1)S(1)}, bf16[2,4,4,16,1152]{4,3,2,1,0:T(8,128)(2,1)}, u32[]{:S(2)}) %copy-start.5) | copy-done | bytes 1179672
  33.6 1.3 %copy-done.7 = bf16[1024,640]{1,0:T(8,128)(2,1)S(1)} copy-done((bf16[1024,640]{1,0:T(8,128)(2,1)S(1)}, bf16[1024,640]{1,0:T(8,128)(2,1)}, u32[]{:S(2)}) %copy-start.7) | copy-done | bytes 1310744
  34.9 1.3 %copy-done.8 = bf16[1024,640]{1,0:T(8,128)(2,1)S(1)} copy-done((bf16[1024,640]{1,0:T(8,128)(2,1)S(1)}, bf16[1024,640]{1,0:T(8,128)(2,1)}, u32[]{:S(2)}) %copy-start.8) | copy-done | bytes 1310744
  36.2 1.3 %copy-done.9 = bf16[2560,256]{1,0:T(8,128)(2,1)S(1)} copy-done((bf16[2560,256]{1,0:T(8,128)(2,1)S(1)}, bf16[2560,256]{1,0:T(8,128)(2,1)}, u32[]{:S(2)}) %copy-start.9) | copy-done | bytes 1310744
  37.5 6.9 %spatial_edges.1 = (bf16[512,1152]{1,0:T(8,128)(2,1)S(1)}, bf16[64,1152]{1,0:T(8,128)(2,1)S(1)}, bf16[64,1152]{1,0:T(8,128)(2,1)S(1)}, bf16[64,1152]{1,0:T(8,128...) custom-call(s32[9,1,16]{2,1,0:T(1,128)S(1)} %bitcast.9, ...), custom_call_target="tpu_custom_call" | custom-call | flops 6000000000 | bytes 8388608 | tf_op jit(solution)/shard_map/spatial_edges/pallas_call | solution.py:414
  44.4 0.8 collective-permute-start.14
  45.7 4.6 %collective-permute-start.2 = (bf16[64,1152]{1,0:T(8,128)(2,1)S(1)}, bf16[64,1152]{1,0:T(8,128)(2,1)S(1)}, u32[]{:S(2)}, u32[]{:S(2)}) collective-permute-start(bf16[64,1152]{1,0:T(8,128)(2,1)S(1)} %get-tuple-element.52), channel_id=1, source_target_pairs={{0,28},{4,24},{8,20},{12,16},{16,12},{20,8},{24,4},{28,0},{1,29},{... | collective-permute-start | bytes 442376 | tf_op jit(solution)/shard_map/ppermute | solution.py:586
  50.3 1.0 collective-permute-start.3
  51.4 1.7 %collective-permute-done.13.refs_5_ = bf16[64,1152]{1,0:T(8,128)(2,1)S(1)} collective-permute-done((bf16[64,1152]{1,0:T(8,128)(2,1)}, bf16[64,1152]{1,0:T(8,128)(2,1)S(1)}, u32[]{:S(2)}, u32[]{:S(2)}) %collective-permute-start.13) | collective-permute-done | bytes 147488 | tf_op jit(solution)/shard_map/ppermute | solution.py:586
  53.1 9.7 %collective-permute-done.14.refs_6_ = bf16[64,1152]{1,0:T(8,128)(2,1)S(1)} collective-permute-done((bf16[64,1152]{1,0:T(8,128)(2,1)S(1)}, bf16[64,1152]{1,0:T(8,128)(2,1)S(1)}, u32[]{:S(2)}, u32[]{:S(2)}) %collective-permute-start.14) | collective-permute-done | bytes 147488 | tf_op jit(solution)/shard_map/ppermute | solution.py:586
  62.8 2.9 %collective-permute-start.6 = (bf16[64,1152]{1,0:T(8,128)(2,1)S(1)}, bf16[64,1152]{1,0:T(8,128)(2,1)S(1)}, u32[]{:S(2)}, u32[]{:S(2)}) collective-permute-start(bf16[64,1152]{1,0:T(8,128)(2,1)S(1)} %get-tuple-element.56), channel_id=1, source_target_pairs={{0,16},{4,20},{8,24},{12,28},{16,0},{20,4},{24,8},{28,12},{1,17},{... | collective-permute-start | bytes 442376 | tf_op jit(solution)/shard_map/ppermute | solution.py:586
  65.7 1.5 %collective-permute-start.8 = (bf16[64,1152]{1,0:T(8,128)(2,1)S(1)}, bf16[64,1152]{1,0:T(8,128)(2,1)S(1)}, u32[]{:S(2)}, u32[]{:S(2)}) collective-permute-start(bf16[64,1152]{1,0:T(8,128)(2,1)S(1)} %get-tuple-element.58), channel_id=1, source_target_pairs={{0,4},{4,0},{8,12},{12,8},{16,20},{20,16},{24,28},{28,24},{1,5},{5... | collective-permute-start | bytes 442376 | tf_op jit(solution)/shard_map/ppermute | solution.py:586
  67.3 4.6 %temporal.2 = (bf16[64,576]{1,0:T(8,128)(2,1)S(1)}, bf16[64,576]{1,0:T(8,128)(2,1)S(1)}, bf16[64,576]{1,0:T(8,128)(2,1)S(1)}, bf16[64,576]{1,0:T(8,128)(2,1)S(1)...) custom-call(bf16[64,1152]{1,0:T(8,128)(2,1)S(1)} %copy-done.10, ...), custom_call_target="tpu_custom_call" | custom-call | flops 4000000000 | bytes 6291456 | tf_op jit(solution)/shard_map/temporal/pallas_call | solution.py:499
  71.9 1.5 %collective-permute-start.23 = (bf16[64,576]{1,0:T(8,128)(2,1)S(1)}, bf16[64,576]{1,0:T(8,128)(2,1)S(1)}, u32[]{:S(2)}, u32[]{:S(2)}) collective-permute-start(bf16[64,576]{1,0:T(8,128)(2,1)S(1)} %get-tuple-element.81), channel_id=1, source_target_pairs={{0,28},{4,24},{8,20},{12,16},{16,12},{20,8},{24,4},{28,0},{1,29},{... | collective-permute-start | bytes 221192 | tf_op jit(solution)/shard_map/ppermute | solution.py:586
  73.4 2.6 %collective-permute-done.5.refs_4_ = bf16[64,1152]{1,0:T(8,128)(2,1)S(1)} collective-permute-done((bf16[64,1152]{1,0:T(8,128)(2,1)S(1)}, bf16[64,1152]{1,0:T(8,128)(2,1)S(1)}, u32[]{:S(2)}, u32[]{:S(2)}) %collective-permute-start.5) | collective-permute-done | bytes 147488 | tf_op jit(solution)/shard_map/ppermute | solution.py:586
  76.0 1.8 %collective-permute-start.24 = (bf16[64,576]{1,0:T(8,128)(2,1)S(1)}, bf16[64,576]{1,0:T(8,128)(2,1)S(1)}, u32[]{:S(2)}, u32[]{:S(2)}) collective-permute-start(bf16[64,576]{1,0:T(8,128)(2,1)S(1)} %get-tuple-element.82), channel_id=1, source_target_pairs={{0,24},{4,28},{8,16},{12,20},{16,8},{20,12},{24,0},{28,4},{1,25},{... | collective-permute-start | bytes 221192 | tf_op jit(solution)/shard_map/ppermute | solution.py:586
  77.8 2.7 %collective-permute-done.6.refs_5_ = bf16[64,1152]{1,0:T(8,128)(2,1)S(1)} collective-permute-done((bf16[64,1152]{1,0:T(8,128)(2,1)S(1)}, bf16[64,1152]{1,0:T(8,128)(2,1)S(1)}, u32[]{:S(2)}, u32[]{:S(2)}) %collective-permute-start.6) | collective-permute-done | bytes 147488 | tf_op jit(solution)/shard_map/ppermute | solution.py:586
  80.5 3.9 %temporal.3 = (bf16[128,576]{1,0:T(8,128)(2,1)S(1)}, bf16[64,576]{1,0:T(8,128)(2,1)S(1)}, bf16[64,576]{1,0:T(8,128)(2,1)S(1)}, bf16[128,576]{1,0:T(8,128)(2,1)S(...) custom-call(bf16[64,1152]{1,0:T(8,128)(2,1)S(1)} %get-tuple-element., ...), custom_call_target="tpu_custom_call" | custom-call | flops 4000000000 | bytes 6291456 | tf_op jit(solution)/shard_map/temporal/pallas_call | solution.py:499
  84.4 2.2 %collective-permute-start.16 = (bf16[64,576]{1,0:T(8,128)(2,1)S(1)}, bf16[64,576]{1,0:T(8,128)(2,1)S(1)}, u32[]{:S(2)}, u32[]{:S(2)}) collective-permute-start(bf16[64,576]{1,0:T(8,128)(2,1)S(1)} %get-tuple-element.74), channel_id=1, source_target_pairs={{0,28},{4,24},{8,20},{12,16},{16,12},{20,8},{24,4},{28,0},{1,29},{... | collective-permute-start | bytes 221192 | tf_op jit(solution)/shard_map/ppermute | solution.py:586
  86.7 2.0 %collective-permute-start.17 = (bf16[64,576]{1,0:T(8,128)(2,1)S(1)}, bf16[64,576]{1,0:T(8,128)(2,1)S(1)}, u32[]{:S(2)}, u32[]{:S(2)}) collective-permute-start(bf16[64,576]{1,0:T(8,128)(2,1)S(1)} %get-tuple-element.75), channel_id=1, source_target_pairs={{0,24},{4,28},{8,16},{12,20},{16,8},{20,12},{24,0},{28,4},{1,25},{... | collective-permute-start | bytes 221192 | tf_op jit(solution)/shard_map/ppermute | solution.py:586
  88.7 3.3 %collective-permute-start.19 = (bf16[128,576]{1,0:T(8,128)(2,1)S(1)}, bf16[128,576]{1,0:T(8,128)(2,1)S(1)}, u32[]{:S(2)}, u32[]{:S(2)}) collective-permute-start(bf16[128,576]{1,0:T(8,128)(2,1)S(1)} %get-tuple-element.77), channel_id=1, source_target_pairs={{0,20},{4,16},{8,28},{12,24},{16,4},{20,0},{24,12},{28,8},{1,21},{... | collective-permute-start | bytes 442376 | tf_op jit(solution)/shard_map/ppermute | solution.py:586
  92.1 2.4 %collective-permute-start.21 = (bf16[128,576]{1,0:T(8,128)(2,1)S(1)}, bf16[128,576]{1,0:T(8,128)(2,1)S(1)}, u32[]{:S(2)}, u32[]{:S(2)}) collective-permute-start(bf16[128,576]{1,0:T(8,128)(2,1)S(1)} %get-tuple-element.79), channel_id=1, source_target_pairs={{0,8},{4,12},{8,0},{12,4},{16,24},{20,28},{24,16},{28,20},{1,9},{5... | collective-permute-start | bytes 442376 | tf_op jit(solution)/shard_map/ppermute | solution.py:586
  94.5 1.1 collective-permute-start.22
  95.6 4.9 %collective-permute-done.18.refs_3_ = bf16[128,576]{1,0:T(8,128)(2,1)S(1)} collective-permute-done((bf16[128,576]{1,0:T(8,128)(2,1)S(1)}, bf16[128,576]{1,0:T(8,128)(2,1)S(1)}, u32[]{:S(2)}, u32[]{:S(2)}) %collective-permute-start.18) | collective-permute-done | bytes 147488 | tf_op jit(solution)/shard_map/ppermute | solution.py:586
  100.5 4.4 %collective-permute-done.19.refs_4_ = bf16[128,576]{1,0:T(8,128)(2,1)S(1)} collective-permute-done((bf16[128,576]{1,0:T(8,128)(2,1)S(1)}, bf16[128,576]{1,0:T(8,128)(2,1)S(1)}, u32[]{:S(2)}, u32[]{:S(2)}) %collective-permute-start.19) | collective-permute-done | bytes 147488 | tf_op jit(solution)/shard_map/ppermute | solution.py:586
  104.9 2.2 %collective-permute-done.20.refs_5_ = bf16[128,576]{1,0:T(8,128)(2,1)S(1)} collective-permute-done((bf16[128,576]{1,0:T(8,128)(2,1)S(1)}, bf16[128,576]{1,0:T(8,128)(2,1)S(1)}, u32[]{:S(2)}, u32[]{:S(2)}) %collective-permute-start.20) | collective-permute-done | bytes 147488 | tf_op jit(solution)/shard_map/ppermute | solution.py:586
  107.1 3.3 %final.1 = bf16[1024,1152]{1,0:T(8,128)(2,1)} custom-call(bf16[128,576]{1,0:T(8,128)(2,1)S(1)} %get-tuple-element.73.refs_0_, bf16[64,576]{1,0:T(8,128)(2,1)S(1)} %collective-permute-done.16.refs_1_, bf16[64,576]{1,0:T(8,128)(2,1)S(1)} %collective-permute-done.17.refs_2_, bf16[128,576]{1,0:T(8,128)(2,1)S(1)} %collective-permute-done.18.refs_3_, ...), custom_call_target="tpu_custom_call" | custom-call | flops 2000000000 | bytes 6291456 | tf_op jit(solution)/shard_map/final/pallas_call | solution.py:554
  (49 shorter events, 0.9 us)
Async XLA Ops:
  0.0 32.3 %copy-start.1 = (bf16[576,1152]{1,0:T(8,128)(2,1)S(1)}, bf16[576,1152]{1,0:T(8,128)(2,1)}, u32[]{:S(2)}) copy-start(bf16[576,1152]{1,0:T(8,128)(2,1)} %w_ref.1) | copy-start | bytes 3981316
  0.0 32.3 %copy-start.3 = (s32[1,16,9]{1,0,2:T(1,128)S(1)}, s32[1,16,9]{1,0,2:T(1,128)}, u32[]{:S(2)}) copy-start(s32[1,16,9]{1,0,2:T(1,128)} %param.12) | copy-start | bytes 1732
  0.0 32.3 %copy-start.4 = (s32[1,16]{1,0:T(1,128)S(1)}, s32[1,16]{1,0:T(1,128)}, u32[]{:S(2)}) copy-start(s32[1,16]{1,0:T(1,128)} %counts_ref.3) | copy-start | bytes 196
  17.6 9.6 %collective-permute-start = (bf16[1280,256]{1,0:T(8,128)(2,1)}, bf16[1280,256]{1,0:T(8,128)(2,1)S(1)}, u32[]{:S(2)}, u32[]{:S(2)}) collective-permute-start(bf16[1280,256]{1,0:T(8,128)(2,1)} %get-tuple-element.49), channel_id=1, source_target_pairs={{0,1},{1,2},{2,3},{4,5},{5,6},{6,7},{8,9},{9,10},{10,11},{12,13},{... | collective-permute-start | bytes 1966088 | tf_op jit(solution)/shard_map/ppermute | solution.py:574
  20.1 12.2 %collective-permute-start.1 = (bf16[1280,256]{1,0:T(8,128)(2,1)}, bf16[1280,256]{1,0:T(8,128)(2,1)S(1)}, u32[]{:S(2)}, u32[]{:S(2)}) collective-permute-start(bf16[1280,256]{1,0:T(8,128)(2,1)} %get-tuple-element.50), channel_id=1, source_target_pairs={{1,0},{2,1},{3,2},{5,4},{6,5},{7,6},{9,8},{10,9},{11,10},{13,12},{... | collective-permute-start | bytes 1966088 | tf_op jit(solution)/shard_map/ppermute | solution.py:574
  21.5 22.9 %collective-permute-start.9 = (bf16[64,1152]{1,0:T(8,128)(2,1)}, bf16[64,1152]{1,0:T(8,128)(2,1)S(1)}, u32[]{:S(2)}, u32[]{:S(2)}) collective-permute-start(bf16[64,1152]{1,0:T(8,128)(2,1)} %get-tuple-element.60), channel_id=1, source_target_pairs={{0,28},{4,24},{8,20},{12,16},{16,12},{20,8},{24,4},{28,0},{1,29},{... | collective-permute-start | bytes 442376 | tf_op jit(solution)/shard_map/ppermute | solution.py:586
  27.0 18.3 %collective-permute-start.10 = (bf16[64,1152]{1,0:T(8,128)(2,1)}, bf16[64,1152]{1,0:T(8,128)(2,1)S(1)}, u32[]{:S(2)}, u32[]{:S(2)}) collective-permute-start(bf16[64,1152]{1,0:T(8,128)(2,1)} %get-tuple-element.61), channel_id=1, source_target_pairs={{0,24},{4,28},{8,16},{12,20},{16,8},{20,12},{24,0},{28,4},{1,25},{... | collective-permute-start | bytes 442376 | tf_op jit(solution)/shard_map/ppermute | solution.py:586
  27.2 18.5 %collective-permute-start.11 = (bf16[64,1152]{1,0:T(8,128)(2,1)}, bf16[64,1152]{1,0:T(8,128)(2,1)S(1)}, u32[]{:S(2)}, u32[]{:S(2)}) collective-permute-start(bf16[64,1152]{1,0:T(8,128)(2,1)} %get-tuple-element.62), channel_id=1, source_target_pairs={{0,12},{4,8},{8,4},{12,0},{16,28},{20,24},{24,20},{28,16},{1,13},{... | collective-permute-start | bytes 442376 | tf_op jit(solution)/shard_map/ppermute | solution.py:586
  27.2 23.1 %collective-permute-start.12 = (bf16[64,1152]{1,0:T(8,128)(2,1)}, bf16[64,1152]{1,0:T(8,128)(2,1)S(1)}, u32[]{:S(2)}, u32[]{:S(2)}) collective-permute-start(bf16[64,1152]{1,0:T(8,128)(2,1)} %get-tuple-element.63), channel_id=1, source_target_pairs={{0,20},{4,16},{8,28},{12,24},{16,4},{20,0},{24,12},{28,8},{1,21},{... | collective-permute-start | bytes 442376 | tf_op jit(solution)/shard_map/ppermute | solution.py:586
  32.3 20.8 %collective-permute-start.13 = (bf16[64,1152]{1,0:T(8,128)(2,1)}, bf16[64,1152]{1,0:T(8,128)(2,1)S(1)}, u32[]{:S(2)}, u32[]{:S(2)}) collective-permute-start(bf16[64,1152]{1,0:T(8,128)(2,1)} %get-tuple-element.64), channel_id=1, source_target_pairs={{0,16},{4,20},{8,24},{12,28},{16,0},{20,4},{24,8},{28,12},{1,17},{... | collective-permute-start | bytes 442376 | tf_op jit(solution)/shard_map/ppermute | solution.py:586
  37.5 29.8 %copy-start = (bf16[1152,1728]{0,1:T(8,128)(2,1)S(1)}, bf16[1152,1728]{0,1:T(8,128)(2,1)}, u32[]{:S(2)}) copy-start(bf16[1152,1728]{0,1:T(8,128)(2,1)} %param.10) | copy-start | bytes 11943940
  37.5 29.8 %copy-start.10 = (bf16[64,1152]{1,0:T(8,128)(2,1)S(1)}, bf16[64,1152]{1,0:T(8,128)(2,1)}, u32[]{:S(2)}) copy-start(bf16[64,1152]{1,0:T(8,128)(2,1)} %get-tuple-element.59.refs_0_) | copy-start | bytes 442372
  44.4 18.4 %collective-permute-start.14 = (bf16[64,1152]{1,0:T(8,128)(2,1)S(1)}, bf16[64,1152]{1,0:T(8,128)(2,1)S(1)}, u32[]{:S(2)}, u32[]{:S(2)}) collective-permute-start(bf16[64,1152]{1,0:T(8,128)(2,1)S(1)} %copy-done.12), channel_id=1, source_target_pairs={{0,8},{4,12},{8,0},{12,4},{16,24},{20,28},{24,16},{28,20},{1,9},{5... | collective-permute-start | bytes 442376 | tf_op jit(solution)/shard_map/ppermute | solution.py:586
  45.2 17.6 %collective-permute-start.15 = (bf16[64,1152]{1,0:T(8,128)(2,1)S(1)}, bf16[64,1152]{1,0:T(8,128)(2,1)S(1)}, u32[]{:S(2)}, u32[]{:S(2)}) collective-permute-start(bf16[64,1152]{1,0:T(8,128)(2,1)S(1)} %copy-done.11), channel_id=1, source_target_pairs={{0,4},{4,0},{8,12},{12,8},{16,20},{20,16},{24,28},{28,24},{1,5},{5... | collective-permute-start | bytes 442376 | tf_op jit(solution)/shard_map/ppermute | solution.py:586
  45.7 20.0 %collective-permute-start.2 = (bf16[64,1152]{1,0:T(8,128)(2,1)S(1)}, bf16[64,1152]{1,0:T(8,128)(2,1)S(1)}, u32[]{:S(2)}, u32[]{:S(2)}) collective-permute-start(bf16[64,1152]{1,0:T(8,128)(2,1)S(1)} %get-tuple-element.52), channel_id=1, source_target_pairs={{0,28},{4,24},{8,20},{12,16},{16,12},{20,8},{24,4},{28,0},{1,29},{... | collective-permute-start | bytes 442376 | tf_op jit(solution)/shard_map/ppermute | solution.py:586
  50.3 15.4 %collective-permute-start.3 = (bf16[64,1152]{1,0:T(8,128)(2,1)S(1)}, bf16[64,1152]{1,0:T(8,128)(2,1)S(1)}, u32[]{:S(2)}, u32[]{:S(2)}) collective-permute-start(bf16[64,1152]{1,0:T(8,128)(2,1)S(1)} %get-tuple-element.53), channel_id=1, source_target_pairs={{0,24},{4,28},{8,16},{12,20},{16,8},{20,12},{24,0},{28,4},{1,25},{... | collective-permute-start | bytes 442376 | tf_op jit(solution)/shard_map/ppermute | solution.py:586
  53.1 18.9 %collective-permute-start.4 = (bf16[64,1152]{1,0:T(8,128)(2,1)S(1)}, bf16[64,1152]{1,0:T(8,128)(2,1)S(1)}, u32[]{:S(2)}, u32[]{:S(2)}) collective-permute-start(bf16[64,1152]{1,0:T(8,128)(2,1)S(1)} %get-tuple-element.54), channel_id=1, source_target_pairs={{0,12},{4,8},{8,4},{12,0},{16,28},{20,24},{24,20},{28,16},{1,13},{... | collective-permute-start | bytes 442376 | tf_op jit(solution)/shard_map/ppermute | solution.py:586
  62.8 13.2 %collective-permute-start.5 = (bf16[64,1152]{1,0:T(8,128)(2,1)S(1)}, bf16[64,1152]{1,0:T(8,128)(2,1)S(1)}, u32[]{:S(2)}, u32[]{:S(2)}) collective-permute-start(bf16[64,1152]{1,0:T(8,128)(2,1)S(1)} %get-tuple-element.55), channel_id=1, source_target_pairs={{0,20},{4,16},{8,28},{12,24},{16,4},{20,0},{24,12},{28,8},{1,21},{... | collective-permute-start | bytes 442376 | tf_op jit(solution)/shard_map/ppermute | solution.py:586
  62.8 17.7 %collective-permute-start.6 = (bf16[64,1152]{1,0:T(8,128)(2,1)S(1)}, bf16[64,1152]{1,0:T(8,128)(2,1)S(1)}, u32[]{:S(2)}, u32[]{:S(2)}) collective-permute-start(bf16[64,1152]{1,0:T(8,128)(2,1)S(1)} %get-tuple-element.56), channel_id=1, source_target_pairs={{0,16},{4,20},{8,24},{12,28},{16,0},{20,4},{24,8},{28,12},{1,17},{... | collective-permute-start | bytes 442376 | tf_op jit(solution)/shard_map/ppermute | solution.py:586
  65.7 14.8 %collective-permute-start.7 = (bf16[64,1152]{1,0:T(8,128)(2,1)S(1)}, bf16[64,1152]{1,0:T(8,128)(2,1)S(1)}, u32[]{:S(2)}, u32[]{:S(2)}) collective-permute-start(bf16[64,1152]{1,0:T(8,128)(2,1)S(1)} %get-tuple-element.57), channel_id=1, source_target_pairs={{0,8},{4,12},{8,0},{12,4},{16,24},{20,28},{24,16},{28,20},{1,9},{5... | collective-permute-start | bytes 442376 | tf_op jit(solution)/shard_map/ppermute | solution.py:586
  65.7 14.8 %collective-permute-start.8 = (bf16[64,1152]{1,0:T(8,128)(2,1)S(1)}, bf16[64,1152]{1,0:T(8,128)(2,1)S(1)}, u32[]{:S(2)}, u32[]{:S(2)}) collective-permute-start(bf16[64,1152]{1,0:T(8,128)(2,1)S(1)} %get-tuple-element.58), channel_id=1, source_target_pairs={{0,4},{4,0},{8,12},{12,8},{16,20},{20,16},{24,28},{28,24},{1,5},{5... | collective-permute-start | bytes 442376 | tf_op jit(solution)/shard_map/ppermute | solution.py:586
  71.9 16.7 %collective-permute-start.23 = (bf16[64,576]{1,0:T(8,128)(2,1)S(1)}, bf16[64,576]{1,0:T(8,128)(2,1)S(1)}, u32[]{:S(2)}, u32[]{:S(2)}) collective-permute-start(bf16[64,576]{1,0:T(8,128)(2,1)S(1)} %get-tuple-element.81), channel_id=1, source_target_pairs={{0,28},{4,24},{8,20},{12,16},{16,12},{20,8},{24,4},{28,0},{1,29},{... | collective-permute-start | bytes 221192 | tf_op jit(solution)/shard_map/ppermute | solution.py:586
  76.0 15.9 %collective-permute-start.24 = (bf16[64,576]{1,0:T(8,128)(2,1)S(1)}, bf16[64,576]{1,0:T(8,128)(2,1)S(1)}, u32[]{:S(2)}, u32[]{:S(2)}) collective-permute-start(bf16[64,576]{1,0:T(8,128)(2,1)S(1)} %get-tuple-element.82), channel_id=1, source_target_pairs={{0,24},{4,28},{8,16},{12,20},{16,8},{20,12},{24,0},{28,4},{1,25},{... | collective-permute-start | bytes 221192 | tf_op jit(solution)/shard_map/ppermute | solution.py:586
  80.5 26.6 %copy-start.2 = (bf16[576,1152]{1,0:T(8,128)(2,1)S(1)}, bf16[576,1152]{1,0:T(8,128)(2,1)}, u32[]{:S(2)}) copy-start(bf16[576,1152]{1,0:T(8,128)(2,1)} %refs_12_.1) | copy-start | bytes 3981316
  80.5 26.6 %copy-start.6 = (bf16[512,1152]{1,0:T(8,128)(2,1)S(1)}, bf16[512,1152]{1,0:T(8,128)(2,1)}, u32[]{:S(2)}) copy-start(bf16[512,1152]{1,0:T(8,128)(2,1)} %get-tuple-element.83.refs_10_) | copy-start | bytes 3538948
  84.4 7.7 %collective-permute-start.16 = (bf16[64,576]{1,0:T(8,128)(2,1)S(1)}, bf16[64,576]{1,0:T(8,128)(2,1)S(1)}, u32[]{:S(2)}, u32[]{:S(2)}) collective-permute-start(bf16[64,576]{1,0:T(8,128)(2,1)S(1)} %get-tuple-element.74), channel_id=1, source_target_pairs={{0,28},{4,24},{8,20},{12,16},{16,12},{20,8},{24,4},{28,0},{1,29},{... | collective-permute-start | bytes 221192 | tf_op jit(solution)/shard_map/ppermute | solution.py:586
  86.7 7.9 %collective-permute-start.17 = (bf16[64,576]{1,0:T(8,128)(2,1)S(1)}, bf16[64,576]{1,0:T(8,128)(2,1)S(1)}, u32[]{:S(2)}, u32[]{:S(2)}) collective-permute-start(bf16[64,576]{1,0:T(8,128)(2,1)S(1)} %get-tuple-element.75), channel_id=1, source_target_pairs={{0,24},{4,28},{8,16},{12,20},{16,8},{20,12},{24,0},{28,4},{1,25},{... | collective-permute-start | bytes 221192 | tf_op jit(solution)/shard_map/ppermute | solution.py:586
  88.7 11.8 %collective-permute-start.18 = (bf16[128,576]{1,0:T(8,128)(2,1)S(1)}, bf16[128,576]{1,0:T(8,128)(2,1)S(1)}, u32[]{:S(2)}, u32[]{:S(2)}) collective-permute-start(bf16[128,576]{1,0:T(8,128)(2,1)S(1)} %get-tuple-element.76), channel_id=1, source_target_pairs={{0,12},{4,8},{8,4},{12,0},{16,28},{20,24},{24,20},{28,16},{1,13},{... | collective-permute-start | bytes 442376 | tf_op jit(solution)/shard_map/ppermute | solution.py:586
  88.7 16.2 %collective-permute-start.19 = (bf16[128,576]{1,0:T(8,128)(2,1)S(1)}, bf16[128,576]{1,0:T(8,128)(2,1)S(1)}, u32[]{:S(2)}, u32[]{:S(2)}) collective-permute-start(bf16[128,576]{1,0:T(8,128)(2,1)S(1)} %get-tuple-element.77), channel_id=1, source_target_pairs={{0,20},{4,16},{8,28},{12,24},{16,4},{20,0},{24,12},{28,8},{1,21},{... | collective-permute-start | bytes 442376 | tf_op jit(solution)/shard_map/ppermute | solution.py:586
  92.0 15.1 %collective-permute-start.20 = (bf16[128,576]{1,0:T(8,128)(2,1)S(1)}, bf16[128,576]{1,0:T(8,128)(2,1)S(1)}, u32[]{:S(2)}, u32[]{:S(2)}) collective-permute-start(bf16[128,576]{1,0:T(8,128)(2,1)S(1)} %get-tuple-element.78), channel_id=1, source_target_pairs={{0,16},{4,20},{8,24},{12,28},{16,0},{20,4},{24,8},{28,12},{1,17},{... | collective-permute-start | bytes 442376 | tf_op jit(solution)/shard_map/ppermute | solution.py:586
  92.1 14.9 %collective-permute-start.21 = (bf16[128,576]{1,0:T(8,128)(2,1)S(1)}, bf16[128,576]{1,0:T(8,128)(2,1)S(1)}, u32[]{:S(2)}, u32[]{:S(2)}) collective-permute-start(bf16[128,576]{1,0:T(8,128)(2,1)S(1)} %get-tuple-element.79), channel_id=1, source_target_pairs={{0,8},{4,12},{8,0},{12,4},{16,24},{20,28},{24,16},{28,20},{1,9},{5... | collective-permute-start | bytes 442376 | tf_op jit(solution)/shard_map/ppermute | solution.py:586
  94.5 12.5 %collective-permute-start.22 = (bf16[128,576]{1,0:T(8,128)(2,1)S(1)}, bf16[128,576]{1,0:T(8,128)(2,1)S(1)}, u32[]{:S(2)}, u32[]{:S(2)}) collective-permute-start(bf16[128,576]{1,0:T(8,128)(2,1)S(1)} %get-tuple-element.80), channel_id=1, source_target_pairs={{0,4},{4,0},{8,12},{12,8},{16,20},{20,16},{24,28},{28,24},{1,5},{5... | collective-permute-start | bytes 442376 | tf_op jit(solution)/shard_map/ppermute | solution.py:586
  (6 other events, 19.8 us)

commit v8 on v7

--- a/solution.py
+++ b/solution.py
@@ -530,17 +530,17 @@
     begin = 0
     for mixed_ref, rows in ((first_ref, range(1, tile_rows - 1)), (second_ref, (0, tile_rows - 1))):
         end = begin + mixed_ref.shape[0]
-        result = mixed_ref[...].astype(F32) + nn_dot(heads_ref[begin:end, :], w_ref[...])
-        result = result.astype(BF16)
-        begin = end
         for part, row in enumerate(rows):
+            own = slice(part * slab, (part + 1) * slab)
+            heads = heads_ref[begin + own.start : begin + own.stop, :]
+            result = (mixed_ref[own, :].astype(F32) + nn_dot(heads, w_ref[...])).astype(BF16)
             for to, at in tile_order(slab, columns):
-                to += part * slab
                 out_ref[row, pl.ds(at, TW), :] = result[to : to + TW]
             copies.append(
                 pltpu.make_async_copy(out_ref.at[row], out_hbm.at[pl.ds(row * slab, slab)], sem.at[row])
             )
             copies[-1].start()
+        begin = end
     for copy in copies:
         copy.wait()
 

time: 111 us -> 111 us (level)
  no operation moved by 1% of the time
where the time goes in v8:
time: 111 us; the launch traced here: 110 us
  starting transfers between devices  40.5 us (36%)
  Pallas kernels  36.1 us (33%)
  waiting for transfers between devices  28.3 us (25%)
  local copies, waits for them, and re-layouts  5.24 us (5%)
    ppermute x23, starting transfers between devices, exchange(): result[slot] = lax.ppermute(piece, 'frame', pairs) if slot else piece  36.6 us
    ppermute x23, waiting for transfers between devices, exchange(): result[slot] = lax.ppermute(piece, 'frame', pairs) if slot else piece  28.3 us
    pallas_call x1, Pallas kernels, spatial_inner(): pl.pallas_call(functools.partial(inner_kernel, group, peers, xor), grid=(...  17.6 us
    pallas_call x2, Pallas kernels, temporal(): pl.pallas_call(functools.partial(temporal_kernel, peers, group, normed, t...  8.5 us
    pallas_call x1, Pallas kernels, spatial_edges(): pl.pallas_call(functools.partial(edges_kernel, group, peers, xor, tile_ro...  6.86 us
    unnamed x26, local copies, waits for them, and re-layouts  5.24 us
    ppermute x2, starting transfers between devices, neighbours(): return (lax.ppermute(bot, 'row', up), lax.ppermute(top, 'row', down))  3.89 us
    pallas_call x1, Pallas kernels, final(): pl.pallas_call(functools.partial(final_kernel, groups, tuple(early), xor,...  3.1 us
  transfers between devices with their start and end apart: 25, of which 7 were waited for; matrix products, arithmetic and copies ran while one was open for 0% of the time, Pallas kernels for 14%

profile of v8, /device:TPU:0, one launch (start us, length us, event | category | flops | bytes accessed | tf_op | source)
XLA Modules:
  0.0 110.4 jit_solution(6676163611754318755)
XLA Ops:
  0.0 17.6 %spatial_inner.1 = (bf16[1024,640]{1,0:T(8,128)(2,1)}, bf16[1024,640]{1,0:T(8,128)(2,1)}, bf16[2560,256]{1,0:T(8,128)(2,1)}, bf16[2,4,4,16,1152]{4,3,2,1,0:T(8,1...) custom-call(s32[9,1,16]{2,1,0:T(1,128)} %bitcast.8, ...), custom_call_target="tpu_custom_call" | custom-call | flops 12000000000 | bytes 16777216 | tf_op jit(solution)/shard_map/spatial_inner/pallas_call | solution.py:317
  17.6 2.4 %collective-permute-start = (bf16[1280,256]{1,0:T(8,128)(2,1)}, bf16[1280,256]{1,0:T(8,128)(2,1)S(1)}, u32[]{:S(2)}, u32[]{:S(2)}) collective-permute-start(bf16[1280,256]{1,0:T(8,128)(2,1)} %get-tuple-element.49), channel_id=1, source_target_pairs={{0,1},{1,2},{2,3},{4,5},{5,6},{6,7},{8,9},{9,10},{10,11},{12,13},{... | collective-permute-start | bytes 1966088 | tf_op jit(solution)/shard_map/ppermute | solution.py:574
  20.1 1.5 %collective-permute-start.1 = (bf16[1280,256]{1,0:T(8,128)(2,1)}, bf16[1280,256]{1,0:T(8,128)(2,1)S(1)}, u32[]{:S(2)}, u32[]{:S(2)}) collective-permute-start(bf16[1280,256]{1,0:T(8,128)(2,1)} %get-tuple-element.50), channel_id=1, source_target_pairs={{1,0},{2,1},{3,2},{5,4},{6,5},{7,6},{9,8},{10,9},{11,10},{13,12},{... | collective-permute-start | bytes 1966088 | tf_op jit(solution)/shard_map/ppermute | solution.py:574
  21.5 5.4 %collective-permute-start.9 = (bf16[64,1152]{1,0:T(8,128)(2,1)}, bf16[64,1152]{1,0:T(8,128)(2,1)S(1)}, u32[]{:S(2)}, u32[]{:S(2)}) collective-permute-start(bf16[64,1152]{1,0:T(8,128)(2,1)} %get-tuple-element.60), channel_id=1, source_target_pairs={{0,28},{4,24},{8,20},{12,16},{16,12},{20,8},{24,4},{28,0},{1,29},{... | collective-permute-start | bytes 442376 | tf_op jit(solution)/shard_map/ppermute | solution.py:586
  27.2 5.1 %collective-permute-start.12 = (bf16[64,1152]{1,0:T(8,128)(2,1)}, bf16[64,1152]{1,0:T(8,128)(2,1)S(1)}, u32[]{:S(2)}, u32[]{:S(2)}) collective-permute-start(bf16[64,1152]{1,0:T(8,128)(2,1)} %get-tuple-element.63), channel_id=1, source_target_pairs={{0,20},{4,16},{8,28},{12,24},{16,4},{20,0},{24,12},{28,8},{1,21},{... | collective-permute-start | bytes 442376 | tf_op jit(solution)/shard_map/ppermute | solution.py:586
  32.3 1.3 %copy-done.5 = bf16[2,4,4,16,1152]{4,3,2,1,0:T(8,128)(2,1)S(1)} copy-done((bf16[2,4,4,16,1152]{4,3,2,1,0:T(8,128)(2,1)S(1)}, bf16[2,4,4,16,1152]{4,3,2,1,0:T(8,128)(2,1)}, u32[]{:S(2)}) %copy-start.5) | copy-done | bytes 1179672
  33.6 1.3 %copy-done.7 = bf16[1024,640]{1,0:T(8,128)(2,1)S(1)} copy-done((bf16[1024,640]{1,0:T(8,128)(2,1)S(1)}, bf16[1024,640]{1,0:T(8,128)(2,1)}, u32[]{:S(2)}) %copy-start.7) | copy-done | bytes 1310744
  34.9 1.3 %copy-done.8 = bf16[1024,640]{1,0:T(8,128)(2,1)S(1)} copy-done((bf16[1024,640]{1,0:T(8,128)(2,1)S(1)}, bf16[1024,640]{1,0:T(8,128)(2,1)}, u32[]{:S(2)}) %copy-start.8) | copy-done | bytes 1310744
  36.2 1.3 %copy-done.9 = bf16[2560,256]{1,0:T(8,128)(2,1)S(1)} copy-done((bf16[2560,256]{1,0:T(8,128)(2,1)S(1)}, bf16[2560,256]{1,0:T(8,128)(2,1)}, u32[]{:S(2)}) %copy-start.9) | copy-done | bytes 1310744
  37.5 6.9 %spatial_edges.1 = (bf16[512,1152]{1,0:T(8,128)(2,1)S(1)}, bf16[64,1152]{1,0:T(8,128)(2,1)S(1)}, bf16[64,1152]{1,0:T(8,128)(2,1)S(1)}, bf16[64,1152]{1,0:T(8,128...) custom-call(s32[9,1,16]{2,1,0:T(1,128)S(1)} %bitcast.9, ...), custom_call_target="tpu_custom_call" | custom-call | flops 6000000000 | bytes 8388608 | tf_op jit(solution)/shard_map/spatial_edges/pallas_call | solution.py:414
  44.4 0.8 collective-permute-start.14
  45.7 4.6 %collective-permute-start.2 = (bf16[64,1152]{1,0:T(8,128)(2,1)S(1)}, bf16[64,1152]{1,0:T(8,128)(2,1)S(1)}, u32[]{:S(2)}, u32[]{:S(2)}) collective-permute-start(bf16[64,1152]{1,0:T(8,128)(2,1)S(1)} %get-tuple-element.52), channel_id=1, source_target_pairs={{0,28},{4,24},{8,20},{12,16},{16,12},{20,8},{24,4},{28,0},{1,29},{... | collective-permute-start | bytes 442376 | tf_op jit(solution)/shard_map/ppermute | solution.py:586
  50.3 1.0 collective-permute-start.3
  51.4 1.7 %collective-permute-done.13.refs_5_ = bf16[64,1152]{1,0:T(8,128)(2,1)S(1)} collective-permute-done((bf16[64,1152]{1,0:T(8,128)(2,1)}, bf16[64,1152]{1,0:T(8,128)(2,1)S(1)}, u32[]{:S(2)}, u32[]{:S(2)}) %collective-permute-start.13) | collective-permute-done | bytes 147488 | tf_op jit(solution)/shard_map/ppermute | solution.py:586
  53.1 9.7 %collective-permute-done.14.refs_6_ = bf16[64,1152]{1,0:T(8,128)(2,1)S(1)} collective-permute-done((bf16[64,1152]{1,0:T(8,128)(2,1)S(1)}, bf16[64,1152]{1,0:T(8,128)(2,1)S(1)}, u32[]{:S(2)}, u32[]{:S(2)}) %collective-permute-start.14) | collective-permute-done | bytes 147488 | tf_op jit(solution)/shard_map/ppermute | solution.py:586
  62.8 2.9 %collective-permute-start.6 = (bf16[64,1152]{1,0:T(8,128)(2,1)S(1)}, bf16[64,1152]{1,0:T(8,128)(2,1)S(1)}, u32[]{:S(2)}, u32[]{:S(2)}) collective-permute-start(bf16[64,1152]{1,0:T(8,128)(2,1)S(1)} %get-tuple-element.56), channel_id=1, source_target_pairs={{0,16},{4,20},{8,24},{12,28},{16,0},{20,4},{24,8},{28,12},{1,17},{... | collective-permute-start | bytes 442376 | tf_op jit(solution)/shard_map/ppermute | solution.py:586
  65.7 1.5 %collective-permute-start.8 = (bf16[64,1152]{1,0:T(8,128)(2,1)S(1)}, bf16[64,1152]{1,0:T(8,128)(2,1)S(1)}, u32[]{:S(2)}, u32[]{:S(2)}) collective-permute-start(bf16[64,1152]{1,0:T(8,128)(2,1)S(1)} %get-tuple-element.58), channel_id=1, source_target_pairs={{0,4},{4,0},{8,12},{12,8},{16,20},{20,16},{24,28},{28,24},{1,5},{5... | collective-permute-start | bytes 442376 | tf_op jit(solution)/shard_map/ppermute | solution.py:586
  67.3 4.6 %temporal.2 = (bf16[64,576]{1,0:T(8,128)(2,1)S(1)}, bf16[64,576]{1,0:T(8,128)(2,1)S(1)}, bf16[64,576]{1,0:T(8,128)(2,1)S(1)}, bf16[64,576]{1,0:T(8,128)(2,1)S(1)...) custom-call(bf16[64,1152]{1,0:T(8,128)(2,1)S(1)} %copy-done.10, ...), custom_call_target="tpu_custom_call" | custom-call | flops 4000000000 | bytes 6291456 | tf_op jit(solution)/shard_map/temporal/pallas_call | solution.py:499
  71.9 1.5 %collective-permute-start.23 = (bf16[64,576]{1,0:T(8,128)(2,1)S(1)}, bf16[64,576]{1,0:T(8,128)(2,1)S(1)}, u32[]{:S(2)}, u32[]{:S(2)}) collective-permute-start(bf16[64,576]{1,0:T(8,128)(2,1)S(1)} %get-tuple-element.81), channel_id=1, source_target_pairs={{0,28},{4,24},{8,20},{12,16},{16,12},{20,8},{24,4},{28,0},{1,29},{... | collective-permute-start | bytes 221192 | tf_op jit(solution)/shard_map/ppermute | solution.py:586
  73.4 2.6 %collective-permute-done.5.refs_4_ = bf16[64,1152]{1,0:T(8,128)(2,1)S(1)} collective-permute-done((bf16[64,1152]{1,0:T(8,128)(2,1)S(1)}, bf16[64,1152]{1,0:T(8,128)(2,1)S(1)}, u32[]{:S(2)}, u32[]{:S(2)}) %collective-permute-start.5) | collective-permute-done | bytes 147488 | tf_op jit(solution)/shard_map/ppermute | solution.py:586
  76.0 1.8 %collective-permute-start.24 = (bf16[64,576]{1,0:T(8,128)(2,1)S(1)}, bf16[64,576]{1,0:T(8,128)(2,1)S(1)}, u32[]{:S(2)}, u32[]{:S(2)}) collective-permute-start(bf16[64,576]{1,0:T(8,128)(2,1)S(1)} %get-tuple-element.82), channel_id=1, source_target_pairs={{0,24},{4,28},{8,16},{12,20},{16,8},{20,12},{24,0},{28,4},{1,25},{... | collective-permute-start | bytes 221192 | tf_op jit(solution)/shard_map/ppermute | solution.py:586
  77.8 2.7 %collective-permute-done.6.refs_5_ = bf16[64,1152]{1,0:T(8,128)(2,1)S(1)} collective-permute-done((bf16[64,1152]{1,0:T(8,128)(2,1)S(1)}, bf16[64,1152]{1,0:T(8,128)(2,1)S(1)}, u32[]{:S(2)}, u32[]{:S(2)}) %collective-permute-start.6) | collective-permute-done | bytes 147488 | tf_op jit(solution)/shard_map/ppermute | solution.py:586
  80.5 3.9 %temporal.3 = (bf16[128,576]{1,0:T(8,128)(2,1)S(1)}, bf16[64,576]{1,0:T(8,128)(2,1)S(1)}, bf16[64,576]{1,0:T(8,128)(2,1)S(1)}, bf16[128,576]{1,0:T(8,128)(2,1)S(...) custom-call(bf16[64,1152]{1,0:T(8,128)(2,1)S(1)} %get-tuple-element., ...), custom_call_target="tpu_custom_call" | custom-call | flops 4000000000 | bytes 6291456 | tf_op jit(solution)/shard_map/temporal/pallas_call | solution.py:499
  84.4 2.2 %collective-permute-start.16 = (bf16[64,576]{1,0:T(8,128)(2,1)S(1)}, bf16[64,576]{1,0:T(8,128)(2,1)S(1)}, u32[]{:S(2)}, u32[]{:S(2)}) collective-permute-start(bf16[64,576]{1,0:T(8,128)(2,1)S(1)} %get-tuple-element.74), channel_id=1, source_target_pairs={{0,28},{4,24},{8,20},{12,16},{16,12},{20,8},{24,4},{28,0},{1,29},{... | collective-permute-start | bytes 221192 | tf_op jit(solution)/shard_map/ppermute | solution.py:586
  86.7 2.0 %collective-permute-start.17 = (bf16[64,576]{1,0:T(8,128)(2,1)S(1)}, bf16[64,576]{1,0:T(8,128)(2,1)S(1)}, u32[]{:S(2)}, u32[]{:S(2)}) collective-permute-start(bf16[64,576]{1,0:T(8,128)(2,1)S(1)} %get-tuple-element.75), channel_id=1, source_target_pairs={{0,24},{4,28},{8,16},{12,20},{16,8},{20,12},{24,0},{28,4},{1,25},{... | collective-permute-start | bytes 221192 | tf_op jit(solution)/shard_map/ppermute | solution.py:586
  88.7 3.3 %collective-permute-start.19 = (bf16[128,576]{1,0:T(8,128)(2,1)S(1)}, bf16[128,576]{1,0:T(8,128)(2,1)S(1)}, u32[]{:S(2)}, u32[]{:S(2)}) collective-permute-start(bf16[128,576]{1,0:T(8,128)(2,1)S(1)} %get-tuple-element.77), channel_id=1, source_target_pairs={{0,20},{4,16},{8,28},{12,24},{16,4},{20,0},{24,12},{28,8},{1,21},{... | collective-permute-start | bytes 442376 | tf_op jit(solution)/shard_map/ppermute | solution.py:586
  92.1 2.4 %collective-permute-start.21 = (bf16[128,576]{1,0:T(8,128)(2,1)S(1)}, bf16[128,576]{1,0:T(8,128)(2,1)S(1)}, u32[]{:S(2)}, u32[]{:S(2)}) collective-permute-start(bf16[128,576]{1,0:T(8,128)(2,1)S(1)} %get-tuple-element.79), channel_id=1, source_target_pairs={{0,8},{4,12},{8,0},{12,4},{16,24},{20,28},{24,16},{28,20},{1,9},{5... | collective-permute-start | bytes 442376 | tf_op jit(solution)/shard_map/ppermute | solution.py:586
  94.5 1.1 collective-permute-start.22
  95.6 4.9 %collective-permute-done.18.refs_3_ = bf16[128,576]{1,0:T(8,128)(2,1)S(1)} collective-permute-done((bf16[128,576]{1,0:T(8,128)(2,1)S(1)}, bf16[128,576]{1,0:T(8,128)(2,1)S(1)}, u32[]{:S(2)}, u32[]{:S(2)}) %collective-permute-start.18) | collective-permute-done | bytes 147488 | tf_op jit(solution)/shard_map/ppermute | solution.py:586
  100.5 4.4 %collective-permute-done.19.refs_4_ = bf16[128,576]{1,0:T(8,128)(2,1)S(1)} collective-permute-done((bf16[128,576]{1,0:T(8,128)(2,1)S(1)}, bf16[128,576]{1,0:T(8,128)(2,1)S(1)}, u32[]{:S(2)}, u32[]{:S(2)}) %collective-permute-start.19) | collective-permute-done | bytes 147488 | tf_op jit(solution)/shard_map/ppermute | solution.py:586
  104.9 2.2 %collective-permute-done.20.refs_5_ = bf16[128,576]{1,0:T(8,128)(2,1)S(1)} collective-permute-done((bf16[128,576]{1,0:T(8,128)(2,1)S(1)}, bf16[128,576]{1,0:T(8,128)(2,1)S(1)}, u32[]{:S(2)}, u32[]{:S(2)}) %collective-permute-start.20) | collective-permute-done | bytes 147488 | tf_op jit(solution)/shard_map/ppermute | solution.py:586
  107.1 3.1 %final.1 = bf16[1024,1152]{1,0:T(8,128)(2,1)} custom-call(bf16[128,576]{1,0:T(8,128)(2,1)S(1)} %get-tuple-element.73.refs_0_, bf16[64,576]{1,0:T(8,128)(2,1)S(1)} %collective-permute-done.16.refs_1_, bf16[64,576]{1,0:T(8,128)(2,1)S(1)} %collective-permute-done.17.refs_2_, bf16[128,576]{1,0:T(8,128)(2,1)S(1)} %collective-permute-done.18.refs_3_, ...), custom_call_target="tpu_custom_call" | custom-call | flops 2000000000 | bytes 6291456 | tf_op jit(solution)/shard_map/final/pallas_call | solution.py:554
  (49 shorter events, 0.9 us)
Async XLA Ops:
  0.0 32.3 %copy-start.1 = (bf16[576,1152]{1,0:T(8,128)(2,1)S(1)}, bf16[576,1152]{1,0:T(8,128)(2,1)}, u32[]{:S(2)}) copy-start(bf16[576,1152]{1,0:T(8,128)(2,1)} %w_ref.1) | copy-start | bytes 3981316
  0.0 32.3 %copy-start.3 = (s32[1,16,9]{1,0,2:T(1,128)S(1)}, s32[1,16,9]{1,0,2:T(1,128)}, u32[]{:S(2)}) copy-start(s32[1,16,9]{1,0,2:T(1,128)} %param.12) | copy-start | bytes 1732
  0.0 32.3 %copy-start.4 = (s32[1,16]{1,0:T(1,128)S(1)}, s32[1,16]{1,0:T(1,128)}, u32[]{:S(2)}) copy-start(s32[1,16]{1,0:T(1,128)} %counts_ref.3) | copy-start | bytes 196
  17.6 9.6 %collective-permute-start = (bf16[1280,256]{1,0:T(8,128)(2,1)}, bf16[1280,256]{1,0:T(8,128)(2,1)S(1)}, u32[]{:S(2)}, u32[]{:S(2)}) collective-permute-start(bf16[1280,256]{1,0:T(8,128)(2,1)} %get-tuple-element.49), channel_id=1, source_target_pairs={{0,1},{1,2},{2,3},{4,5},{5,6},{6,7},{8,9},{9,10},{10,11},{12,13},{... | collective-permute-start | bytes 1966088 | tf_op jit(solution)/shard_map/ppermute | solution.py:574
  20.1 12.2 %collective-permute-start.1 = (bf16[1280,256]{1,0:T(8,128)(2,1)}, bf16[1280,256]{1,0:T(8,128)(2,1)S(1)}, u32[]{:S(2)}, u32[]{:S(2)}) collective-permute-start(bf16[1280,256]{1,0:T(8,128)(2,1)} %get-tuple-element.50), channel_id=1, source_target_pairs={{1,0},{2,1},{3,2},{5,4},{6,5},{7,6},{9,8},{10,9},{11,10},{13,12},{... | collective-permute-start | bytes 1966088 | tf_op jit(solution)/shard_map/ppermute | solution.py:574
  21.5 22.9 %collective-permute-start.9 = (bf16[64,1152]{1,0:T(8,128)(2,1)}, bf16[64,1152]{1,0:T(8,128)(2,1)S(1)}, u32[]{:S(2)}, u32[]{:S(2)}) collective-permute-start(bf16[64,1152]{1,0:T(8,128)(2,1)} %get-tuple-element.60), channel_id=1, source_target_pairs={{0,28},{4,24},{8,20},{12,16},{16,12},{20,8},{24,4},{28,0},{1,29},{... | collective-permute-start | bytes 442376 | tf_op jit(solution)/shard_map/ppermute | solution.py:586
  27.0 18.3 %collective-permute-start.10 = (bf16[64,1152]{1,0:T(8,128)(2,1)}, bf16[64,1152]{1,0:T(8,128)(2,1)S(1)}, u32[]{:S(2)}, u32[]{:S(2)}) collective-permute-start(bf16[64,1152]{1,0:T(8,128)(2,1)} %get-tuple-element.61), channel_id=1, source_target_pairs={{0,24},{4,28},{8,16},{12,20},{16,8},{20,12},{24,0},{28,4},{1,25},{... | collective-permute-start | bytes 442376 | tf_op jit(solution)/shard_map/ppermute | solution.py:586
  27.2 18.5 %collective-permute-start.11 = (bf16[64,1152]{1,0:T(8,128)(2,1)}, bf16[64,1152]{1,0:T(8,128)(2,1)S(1)}, u32[]{:S(2)}, u32[]{:S(2)}) collective-permute-start(bf16[64,1152]{1,0:T(8,128)(2,1)} %get-tuple-element.62), channel_id=1, source_target_pairs={{0,12},{4,8},{8,4},{12,0},{16,28},{20,24},{24,20},{28,16},{1,13},{... | collective-permute-start | bytes 442376 | tf_op jit(solution)/shard_map/ppermute | solution.py:586
  27.2 23.1 %collective-permute-start.12 = (bf16[64,1152]{1,0:T(8,128)(2,1)}, bf16[64,1152]{1,0:T(8,128)(2,1)S(1)}, u32[]{:S(2)}, u32[]{:S(2)}) collective-permute-start(bf16[64,1152]{1,0:T(8,128)(2,1)} %get-tuple-element.63), channel_id=1, source_target_pairs={{0,20},{4,16},{8,28},{12,24},{16,4},{20,0},{24,12},{28,8},{1,21},{... | collective-permute-start | bytes 442376 | tf_op jit(solution)/shard_map/ppermute | solution.py:586
  32.3 20.8 %collective-permute-start.13 = (bf16[64,1152]{1,0:T(8,128)(2,1)}, bf16[64,1152]{1,0:T(8,128)(2,1)S(1)}, u32[]{:S(2)}, u32[]{:S(2)}) collective-permute-start(bf16[64,1152]{1,0:T(8,128)(2,1)} %get-tuple-element.64), channel_id=1, source_target_pairs={{0,16},{4,20},{8,24},{12,28},{16,0},{20,4},{24,8},{28,12},{1,17},{... | collective-permute-start | bytes 442376 | tf_op jit(solution)/shard_map/ppermute | solution.py:586
  37.5 29.8 %copy-start = (bf16[1152,1728]{0,1:T(8,128)(2,1)S(1)}, bf16[1152,1728]{0,1:T(8,128)(2,1)}, u32[]{:S(2)}) copy-start(bf16[1152,1728]{0,1:T(8,128)(2,1)} %param.10) | copy-start | bytes 11943940
  37.5 29.8 %copy-start.10 = (bf16[64,1152]{1,0:T(8,128)(2,1)S(1)}, bf16[64,1152]{1,0:T(8,128)(2,1)}, u32[]{:S(2)}) copy-start(bf16[64,1152]{1,0:T(8,128)(2,1)} %get-tuple-element.59.refs_0_) | copy-start | bytes 442372
  44.4 18.4 %collective-permute-start.14 = (bf16[64,1152]{1,0:T(8,128)(2,1)S(1)}, bf16[64,1152]{1,0:T(8,128)(2,1)S(1)}, u32[]{:S(2)}, u32[]{:S(2)}) collective-permute-start(bf16[64,1152]{1,0:T(8,128)(2,1)S(1)} %copy-done.12), channel_id=1, source_target_pairs={{0,8},{4,12},{8,0},{12,4},{16,24},{20,28},{24,16},{28,20},{1,9},{5... | collective-permute-start | bytes 442376 | tf_op jit(solution)/shard_map/ppermute | solution.py:586
  45.2 17.6 %collective-permute-start.15 = (bf16[64,1152]{1,0:T(8,128)(2,1)S(1)}, bf16[64,1152]{1,0:T(8,128)(2,1)S(1)}, u32[]{:S(2)}, u32[]{:S(2)}) collective-permute-start(bf16[64,1152]{1,0:T(8,128)(2,1)S(1)} %copy-done.11), channel_id=1, source_target_pairs={{0,4},{4,0},{8,12},{12,8},{16,20},{20,16},{24,28},{28,24},{1,5},{5... | collective-permute-start | bytes 442376 | tf_op jit(solution)/shard_map/ppermute | solution.py:586
  45.7 20.0 %collective-permute-start.2 = (bf16[64,1152]{1,0:T(8,128)(2,1)S(1)}, bf16[64,1152]{1,0:T(8,128)(2,1)S(1)}, u32[]{:S(2)}, u32[]{:S(2)}) collective-permute-start(bf16[64,1152]{1,0:T(8,128)(2,1)S(1)} %get-tuple-element.52), channel_id=1, source_target_pairs={{0,28},{4,24},{8,20},{12,16},{16,12},{20,8},{24,4},{28,0},{1,29},{... | collective-permute-start | bytes 442376 | tf_op jit(solution)/shard_map/ppermute | solution.py:586
  50.3 15.4 %collective-permute-start.3 = (bf16[64,1152]{1,0:T(8,128)(2,1)S(1)}, bf16[64,1152]{1,0:T(8,128)(2,1)S(1)}, u32[]{:S(2)}, u32[]{:S(2)}) collective-permute-start(bf16[64,1152]{1,0:T(8,128)(2,1)S(1)} %get-tuple-element.53), channel_id=1, source_target_pairs={{0,24},{4,28},{8,16},{12,20},{16,8},{20,12},{24,0},{28,4},{1,25},{... | collective-permute-start | bytes 442376 | tf_op jit(solution)/shard_map/ppermute | solution.py:586
  53.1 18.9 %collective-permute-start.4 = (bf16[64,1152]{1,0:T(8,128)(2,1)S(1)}, bf16[64,1152]{1,0:T(8,128)(2,1)S(1)}, u32[]{:S(2)}, u32[]{:S(2)}) collective-permute-start(bf16[64,1152]{1,0:T(8,128)(2,1)S(1)} %get-tuple-element.54), channel_id=1, source_target_pairs={{0,12},{4,8},{8,4},{12,0},{16,28},{20,24},{24,20},{28,16},{1,13},{... | collective-permute-start | bytes 442376 | tf_op jit(solution)/shard_map/ppermute | solution.py:586
  62.8 13.2 %collective-permute-start.5 = (bf16[64,1152]{1,0:T(8,128)(2,1)S(1)}, bf16[64,1152]{1,0:T(8,128)(2,1)S(1)}, u32[]{:S(2)}, u32[]{:S(2)}) collective-permute-start(bf16[64,1152]{1,0:T(8,128)(2,1)S(1)} %get-tuple-element.55), channel_id=1, source_target_pairs={{0,20},{4,16},{8,28},{12,24},{16,4},{20,0},{24,12},{28,8},{1,21},{... | collective-permute-start | bytes 442376 | tf_op jit(solution)/shard_map/ppermute | solution.py:586
  62.8 17.7 %collective-permute-start.6 = (bf16[64,1152]{1,0:T(8,128)(2,1)S(1)}, bf16[64,1152]{1,0:T(8,128)(2,1)S(1)}, u32[]{:S(2)}, u32[]{:S(2)}) collective-permute-start(bf16[64,1152]{1,0:T(8,128)(2,1)S(1)} %get-tuple-element.56), channel_id=1, source_target_pairs={{0,16},{4,20},{8,24},{12,28},{16,0},{20,4},{24,8},{28,12},{1,17},{... | collective-permute-start | bytes 442376 | tf_op jit(solution)/shard_map/ppermute | solution.py:586
  65.7 14.8 %collective-permute-start.7 = (bf16[64,1152]{1,0:T(8,128)(2,1)S(1)}, bf16[64,1152]{1,0:T(8,128)(2,1)S(1)}, u32[]{:S(2)}, u32[]{:S(2)}) collective-permute-start(bf16[64,1152]{1,0:T(8,128)(2,1)S(1)} %get-tuple-element.57), channel_id=1, source_target_pairs={{0,8},{4,12},{8,0},{12,4},{16,24},{20,28},{24,16},{28,20},{1,9},{5... | collective-permute-start | bytes 442376 | tf_op jit(solution)/shard_map/ppermute | solution.py:586
  65.7 14.8 %collective-permute-start.8 = (bf16[64,1152]{1,0:T(8,128)(2,1)S(1)}, bf16[64,1152]{1,0:T(8,128)(2,1)S(1)}, u32[]{:S(2)}, u32[]{:S(2)}) collective-permute-start(bf16[64,1152]{1,0:T(8,128)(2,1)S(1)} %get-tuple-element.58), channel_id=1, source_target_pairs={{0,4},{4,0},{8,12},{12,8},{16,20},{20,16},{24,28},{28,24},{1,5},{5... | collective-permute-start | bytes 442376 | tf_op jit(solution)/shard_map/ppermute | solution.py:586
  71.9 16.7 %collective-permute-start.23 = (bf16[64,576]{1,0:T(8,128)(2,1)S(1)}, bf16[64,576]{1,0:T(8,128)(2,1)S(1)}, u32[]{:S(2)}, u32[]{:S(2)}) collective-permute-start(bf16[64,576]{1,0:T(8,128)(2,1)S(1)} %get-tuple-element.81), channel_id=1, source_target_pairs={{0,28},{4,24},{8,20},{12,16},{16,12},{20,8},{24,4},{28,0},{1,29},{... | collective-permute-start | bytes 221192 | tf_op jit(solution)/shard_map/ppermute | solution.py:586
  76.0 15.9 %collective-permute-start.24 = (bf16[64,576]{1,0:T(8,128)(2,1)S(1)}, bf16[64,576]{1,0:T(8,128)(2,1)S(1)}, u32[]{:S(2)}, u32[]{:S(2)}) collective-permute-start(bf16[64,576]{1,0:T(8,128)(2,1)S(1)} %get-tuple-element.82), channel_id=1, source_target_pairs={{0,24},{4,28},{8,16},{12,20},{16,8},{20,12},{24,0},{28,4},{1,25},{... | collective-permute-start | bytes 221192 | tf_op jit(solution)/shard_map/ppermute | solution.py:586
  80.5 26.6 %copy-start.2 = (bf16[576,1152]{1,0:T(8,128)(2,1)S(1)}, bf16[576,1152]{1,0:T(8,128)(2,1)}, u32[]{:S(2)}) copy-start(bf16[576,1152]{1,0:T(8,128)(2,1)} %refs_12_.1) | copy-start | bytes 3981316
  80.5 26.6 %copy-start.6 = (bf16[512,1152]{1,0:T(8,128)(2,1)S(1)}, bf16[512,1152]{1,0:T(8,128)(2,1)}, u32[]{:S(2)}) copy-start(bf16[512,1152]{1,0:T(8,128)(2,1)} %get-tuple-element.83.refs_10_) | copy-start | bytes 3538948
  84.4 7.7 %collective-permute-start.16 = (bf16[64,576]{1,0:T(8,128)(2,1)S(1)}, bf16[64,576]{1,0:T(8,128)(2,1)S(1)}, u32[]{:S(2)}, u32[]{:S(2)}) collective-permute-start(bf16[64,576]{1,0:T(8,128)(2,1)S(1)} %get-tuple-element.74), channel_id=1, source_target_pairs={{0,28},{4,24},{8,20},{12,16},{16,12},{20,8},{24,4},{28,0},{1,29},{... | collective-permute-start | bytes 221192 | tf_op jit(solution)/shard_map/ppermute | solution.py:586
  86.7 7.9 %collective-permute-start.17 = (bf16[64,576]{1,0:T(8,128)(2,1)S(1)}, bf16[64,576]{1,0:T(8,128)(2,1)S(1)}, u32[]{:S(2)}, u32[]{:S(2)}) collective-permute-start(bf16[64,576]{1,0:T(8,128)(2,1)S(1)} %get-tuple-element.75), channel_id=1, source_target_pairs={{0,24},{4,28},{8,16},{12,20},{16,8},{20,12},{24,0},{28,4},{1,25},{... | collective-permute-start | bytes 221192 | tf_op jit(solution)/shard_map/ppermute | solution.py:586
  88.7 11.8 %collective-permute-start.18 = (bf16[128,576]{1,0:T(8,128)(2,1)S(1)}, bf16[128,576]{1,0:T(8,128)(2,1)S(1)}, u32[]{:S(2)}, u32[]{:S(2)}) collective-permute-start(bf16[128,576]{1,0:T(8,128)(2,1)S(1)} %get-tuple-element.76), channel_id=1, source_target_pairs={{0,12},{4,8},{8,4},{12,0},{16,28},{20,24},{24,20},{28,16},{1,13},{... | collective-permute-start | bytes 442376 | tf_op jit(solution)/shard_map/ppermute | solution.py:586
  88.7 16.2 %collective-permute-start.19 = (bf16[128,576]{1,0:T(8,128)(2,1)S(1)}, bf16[128,576]{1,0:T(8,128)(2,1)S(1)}, u32[]{:S(2)}, u32[]{:S(2)}) collective-permute-start(bf16[128,576]{1,0:T(8,128)(2,1)S(1)} %get-tuple-element.77), channel_id=1, source_target_pairs={{0,20},{4,16},{8,28},{12,24},{16,4},{20,0},{24,12},{28,8},{1,21},{... | collective-permute-start | bytes 442376 | tf_op jit(solution)/shard_map/ppermute | solution.py:586
  92.0 15.1 %collective-permute-start.20 = (bf16[128,576]{1,0:T(8,128)(2,1)S(1)}, bf16[128,576]{1,0:T(8,128)(2,1)S(1)}, u32[]{:S(2)}, u32[]{:S(2)}) collective-permute-start(bf16[128,576]{1,0:T(8,128)(2,1)S(1)} %get-tuple-element.78), channel_id=1, source_target_pairs={{0,16},{4,20},{8,24},{12,28},{16,0},{20,4},{24,8},{28,12},{1,17},{... | collective-permute-start | bytes 442376 | tf_op jit(solution)/shard_map/ppermute | solution.py:586
  92.1 14.9 %collective-permute-start.21 = (bf16[128,576]{1,0:T(8,128)(2,1)S(1)}, bf16[128,576]{1,0:T(8,128)(2,1)S(1)}, u32[]{:S(2)}, u32[]{:S(2)}) collective-permute-start(bf16[128,576]{1,0:T(8,128)(2,1)S(1)} %get-tuple-element.79), channel_id=1, source_target_pairs={{0,8},{4,12},{8,0},{12,4},{16,24},{20,28},{24,16},{28,20},{1,9},{5... | collective-permute-start | bytes 442376 | tf_op jit(solution)/shard_map/ppermute | solution.py:586
  94.5 12.5 %collective-permute-start.22 = (bf16[128,576]{1,0:T(8,128)(2,1)S(1)}, bf16[128,576]{1,0:T(8,128)(2,1)S(1)}, u32[]{:S(2)}, u32[]{:S(2)}) collective-permute-start(bf16[128,576]{1,0:T(8,128)(2,1)S(1)} %get-tuple-element.80), channel_id=1, source_target_pairs={{0,4},{4,0},{8,12},{12,8},{16,20},{20,16},{24,28},{28,24},{1,5},{5... | collective-permute-start | bytes 442376 | tf_op jit(solution)/shard_map/ppermute | solution.py:586
  (6 other events, 19.8 us)
